TPU v7x, 32 devices: a whole 2x2x4 slice. The times are simulated.
32 devices in a mesh: gx: 4 (over y, x), gy: 8 (over z, core).
Axes of the slice: x: 2, y: 2, z: 4, core: 2. Of those that a mesh axis runs over, the one named last changes fastest.
Arguments:
- field: float32 [3, 16, 256, 1024], P(None, None, 'gx', 'gy'), may hold values from -6 to 6
- masks: int32 [2, 7, 8, 32], P(None, None, 'gx', 'gy'), may hold values 0 or 1
Outputs:
- restored: float32 [3, 16, 256, 1024], P(None, None, 'gx', 'gy')
- coarse: float32 [3, 4, 64, 256], replicated
All inputs are finite; a program needn't handle non-finite values. No bound on the sum of `masks` on one device may be relied on, other than what follows from the above.
Results may differ from a plain program's by a relative error of at most 0.00002.
Values sent between devices are 32-bit elements; how exact they have to be, the bound alone decides.
No kernel may reach another device: no remote copies, remote signals or barrier semaphores. Data moves between devices by JAX's collectives and lax.ppermute only.
A program may use at most 128 MiB of HBM per device.

v0:
```python
import functools

import jax
import jax.numpy as jnp
import ml_dtypes
import numpy as np
from jax import lax
from jax.experimental import pallas as pl
from jax.experimental.pallas import tpu as pltpu
from jax.sharding import PartitionSpec as P

F32 = jnp.float32
BF16 = jnp.bfloat16
VMEM_LIMIT = 32 * 1024 * 1024

NV, NZ, NR, NL = 3, 16, 64, 128


def detail_row(k):
    return {2 * k + 1: 1.0, 2 * k: -0.5, 2 * k + 2: -0.5}


def smooth_row(k):
    row = {2 * k: 1.0}
    for j in (k - 1, k):
        for cell, value in detail_row(j).items():
            row[cell] = row.get(cell, 0.0) + 0.25 * value
    return row


def even_row(k):
    return {("s", k): 1.0, ("d", k - 1): -0.25, ("d", k): -0.25}


def odd_row(k):
    row = {("d", k): 1.0}
    for j in (k, k + 1):
        for name, value in even_row(j).items():
            row[name] = row.get(name, 0.0) + 0.5 * value
    return row


def as_bf16(matrix):
    cast = matrix.astype(ml_dtypes.bfloat16)
    assert (cast.astype(np.float64) == matrix).all()
    return cast


def combine(*terms):
    total = {}
    for factor, row in terms:
        for cell, value in row.items():
            total[cell] = total.get(cell, 0.0) + factor * value
    return total


def level_one_columns():
    names = {("s", k): k for k in range(65)}
    names.update({("d", k): 128 + k for k in range(65)})
    names[("d", -1)] = 128 + 65
    return names


def level_two_columns():
    names = {("s", k): k for k in range(33)}
    names.update({("d", k): 64 + k for k in range(33)})
    names[("d", -1)] = 64 + 33
    return names


def smooth_place(k):
    return k + 2


def beyond(n):
    return {"cell": 24 * n, "after": 24 * n + 8, "before": 24 * n + 16}


BEYOND_SMOOTH = {65: 96, 66: 104, -2: 112, -1: 120}


def own_row(kind, k, n):
    place = {name: 128 + lane for name, lane in beyond(n).items()}
    if kind == "d":
        if k == -1:
            return {place["before"]: 1.0, 0: -0.5}
        if k == 64:
            return {place["after"]: 1.0}
        return {(place["cell"] if y == 128 else y): value for y, value in detail_row(k).items()}
    if k in BEYOND_SMOOTH:
        row = {128 + BEYOND_SMOOTH[k]: 1.0}
        return combine((1.0, row), (1.0, {0: -0.125})) if k == -1 else row
    even = place["cell"] if k == 64 else 2 * k
    return combine((1.0, {even: 1.0}), (0.25, own_row("d", k - 1, n)), (0.25, own_row("d", k, n)))


@functools.lru_cache(maxsize=None)
def weights():
    w = {}
    names = level_one_columns()
    forward = np.zeros((4, 256, 256))
    inverse = np.zeros((256, 128))
    for (kind, k), column in names.items():
        for n in range(4):
            for place, value in own_row(kind, k, n).items():
                forward[n, place, column] += value
    for k in range(64):
        for y, row in ((2 * k, even_row(k)), (2 * k + 1, odd_row(k))):
            for name, value in row.items():
                inverse[names[name], y] += value
    short = np.zeros((144, 256))
    short[:128] = forward[0, :128]
    for i, lane in enumerate(beyond(0).values()):
        short[128 + i] = forward[0, 128 + lane]
    smooth = np.zeros((256, 128))
    for k in range(-2, 67):
        for place, value in own_row("s", k, 0).items():
            smooth[place, smooth_place(k)] += value
    names2 = level_two_columns()
    forward2 = np.zeros((128, 128))
    inverse2 = np.zeros((128, 128))
    for (kind, k), column in names2.items():
        for cell, value in (smooth_row(k) if kind == "s" else detail_row(k)).items():
            forward2[smooth_place(cell), column] += value
    for k in range(33):
        rows = [(2 * k, even_row(k))] + ([(2 * k + 1, odd_row(k))] if k < 32 else [])
        for y, row in rows:
            for name, value in row.items():
                inverse2[names2[name], y] += value
    back = np.zeros((256, 128))
    back[:65] = inverse[:65]
    back[128 : 128 + 65] = inverse[:65]
    spread = np.zeros((3, 128, 2, 128))
    for k in range(64):
        spread[0, k, 0, k] = 1
    spread[1, 0, 0, 64] = 1
    spread[2, 63, 0, 65] = 1
    for k in range(32):
        spread[0, 64 + k, 1, k] = 1
        spread[0, 64 + k, 1, 64 + k] = 1
    for base in (0, 64):
        spread[1, 64, 1, base + 32] = 1
        spread[2, 95, 1, base + 33] = 1
    w["wide"] = np.concatenate([short, spread.reshape(384, 256)], 0)
    own, beside = smooth[:128], smooth[128:]
    w["narrow"] = np.concatenate([inverse, own, own, beside, beside, back, forward2, inverse2], 0)
    edge = np.zeros((4, 128, 128))

    def put(n, lane, row):
        for z in range(8):
            for y, value in row.items():
                j = y - 120 if y >= 120 else y + 8
                edge[n, 16 * z + j, lane + z] += value

    part = {127: 1.0, 126: -0.5}
    for n in range(4):
        put(n, beyond(n)["cell"], {0: 1.0})
        put(n, beyond(n)["after"], detail_row(0))
        put(n, beyond(n)["before"], part)
    put(0, BEYOND_SMOOTH[65], smooth_row(1))
    put(0, BEYOND_SMOOTH[66], smooth_row(2))
    put(0, BEYOND_SMOOTH[-2], smooth_row(62))
    put(0, BEYOND_SMOOTH[-1], combine((1.0, {126: 1.0}), (0.25, detail_row(62)), (0.25, part)))
    w["edge"] = edge.reshape(512, 128)
    expand = np.zeros((2, 4, 128))
    for j in range(4):
        expand[0, j, 16 * j : 16 * j + 16] = 1
        expand[1, j, 64 + 8 * j : 64 + 8 * j + 8] = 1
    twice = combine(*[(value, smooth_row(k)) for k, value in smooth_row(0).items()])
    columns = np.zeros((2, 128, 128))
    for m in range(-1, 34):
        for t, value in twice.items():
            if 0 <= 4 * m + t < NL:
                columns[:, 4 * m + t, m + 1] = value
    rows = np.zeros((4, 32, 2, 64))
    for z in range(4):
        places = {m: m for m in range(16)}
        places.update({16: 16 + 2 * z, 17: 17 + 2 * z, -1: 16 + 15 - z})
        for m, place in places.items():
            for t, value in twice.items():
                if 0 <= 4 * m + t < NR:
                    rows[z, place, :, 4 * m + t] = value
    pad = np.zeros((8, 128))
    w["first"] = np.concatenate([columns.reshape(256, 128), rows.reshape(128, 128), expand.reshape(8, 128), pad], 0)
    return {name: as_bf16(matrix) for name, matrix in w.items()}


def two_terms(x):
    high = x.astype(BF16)
    low = (x - high.astype(F32)).astype(BF16)
    return high, low


def cost(gigaflops):
    return pl.CostEstimate(flops=gigaflops * 10**9, bytes_accessed=8 * 10**6, transcendentals=0)


def dot(a, b):
    return jnp.dot(a, b, preferred_element_type=F32)


def lift_planes(cells):
    half = len(cells) // 2
    even, odd = cells[0::2], cells[1::2]
    detail = [odd[k] - 0.5 * (even[k] + even[min(k + 1, half - 1)]) for k in range(half)]
    smooth = [even[k] + 0.25 * (detail[max(k - 1, 0)] + detail[k]) for k in range(half)]
    return smooth, detail


def unlift_planes(smooth, detail):
    half = len(smooth)
    even = [smooth[k] - 0.25 * (detail[max(k - 1, 0)] + detail[k]) for k in range(half)]
    out = []
    for k in range(half):
        out += [even[k], detail[k] + 0.5 * (even[k] + even[min(k + 1, half - 1)])]
    return out


def lift_rows(load, start):
    even, odd, after = load(start), load(start + 1), load(start + 2)
    before, odd_before = load(start - 2), load(start - 1)
    detail = odd - 0.5 * (even + after)
    detail_before = odd_before - 0.5 * (before + even)
    return even + 0.25 * (detail_before + detail), detail


def unlift_rows(smooth, detail, row):
    here, after = detail(row), detail(row + 1)
    even = smooth(row) - 0.25 * (detail(row - 1) + here)
    next_even = smooth(row + 1) - 0.25 * (here + after)
    return even, here + 0.5 * (even + next_even)


PITCH = 80


def first_kernel(
    field, masks_hbm, table_hbm, lifted, up, down, own_masks, share, cells, twice, masks, table, sems
):
    copies = []
    for v in range(NV):
        for h in range(4):
            part = pl.ds(4 * h, 4)
            copies.append(pltpu.make_async_copy(field.at[v, part], cells.at[v, part], sems.at[4 * v + h]))
    copies.append(pltpu.make_async_copy(masks_hbm, masks, sems.at[4 * NV]))
    copies.append(pltpu.make_async_copy(table_hbm, table, sems.at[4 * NV + 1]))
    for copy in copies:
        copy.start()
    for p in range(NV * NZ):
        lifted[p * PITCH : p * PITCH + 8, :] = jnp.zeros((8, NL), F32)
        lifted[p * PITCH + 72 : p * PITCH + 80, :] = jnp.zeros((8, NL), F32)

    for v in range(NV):
        for copy in copies[4 * v : 4 * v + 4]:
            copy.wait()

        def planes(t, _):
            at = pl.multiple_of(t * 8, 8)
            smooth, detail = lift_planes([cells[v, z, pl.ds(at, 8), :] for z in range(NZ)])
            for k, tile in enumerate(smooth + detail):
                lifted[pl.ds((v * NZ + k) * PITCH + 8 + at, 8), :] = tile
            for k, tile in enumerate(lift_planes(smooth)[0]):
                twice[v * 4 + k, pl.ds(at, 8), :] = tile
            return 0

        lax.fori_loop(0, 8, planes, 0)
        for bz in range(2):

            def row(x):
                return lifted[pl.ds((v * NZ + bz * 8) * PITCH + 8 + x, 8, stride=PITCH), :]

            x = [row(j) for j in range(7 if bz == 0 else 3)]
            first = x[1] - 0.5 * (x[0] + x[2])
            up[v * 6 + bz] = x[0]
            up[v * 6 + 2 + bz] = first
            y = {j: row(j) for j in (range(58, 64) if bz == 0 else (62, 63))}
            part = y[63] - 0.5 * y[62]
            down[v * 4 + bz] = part
            if bz == 0:
                second = x[3] - 0.5 * (x[2] + x[4])
                third = x[5] - 0.5 * (x[4] + x[6])
                up[v * 6 + 4] = x[2] + 0.25 * (first + second)
                up[v * 6 + 5] = x[4] + 0.25 * (second + third)
                before = y[59] - 0.5 * (y[58] + y[60])
                last = y[61] - 0.5 * (y[60] + y[62])
                down[v * 4 + 2] = y[60] + 0.25 * (before + last)
                down[v * 4 + 3] = y[62] + 0.25 * (last + part)

    for copy in copies[4 * NV :]:
        copy.wait()
    for i, out, tile in ((0, up, 18), (1, down, 12)):
        total = jnp.zeros((7, NL), F32)
        for l in range(2):
            flags = masks[l, i].astype(F32).astype(BF16)
            spread = table[384 + 4 * l : 388 + 4 * l, :]
            total += lax.dot_general(flags, spread, (((0,), (0,)), ((), ())), preferred_element_type=F32)
        own_masks[i] = jnp.concatenate([total, jnp.zeros((1, NL), F32)], 0)
        out[tile] = own_masks[i]
    total = jnp.zeros((80, NL), F32)
    for v in range(NV):
        main, extra = [], jnp.zeros((16, NL), F32)
        for z in range(4):
            terms = jnp.concatenate(two_terms(twice[v * 4 + z]), 0)
            part = dot(table[256 + 32 * z : 288 + 32 * z, :], terms)
            main.append(part[:16])
            extra += part[16:]
        terms = jnp.concatenate(two_terms(jnp.concatenate(main + [extra], 0)), 1)
        part = dot(terms, table[0:256, :])
        total += pltpu.roll(part, 35 * v, 1) if v else part
    lane = lax.broadcasted_iota(jnp.int32, (8, NL), 1)
    spare = (lane >= 105) & (lane < 126)
    upper = lax.broadcasted_iota(jnp.int32, (8, NL), 0) < 4
    below, above = total[64:72], total[72:80]
    pieces = [pltpu.roll(above, 105 - 21 * p, 1) for p in range(5)]
    for g in range(8):
        if g < 5:
            extra = pltpu.roll(below, 105 - 21 * g, 1)
        else:
            extra = pltpu.roll(pieces[2 * g - 10], 4, 0)
            extra = jnp.where(upper, extra, pieces[2 * g - 9] if g < 7 else 0.0)
        share[8 * g : 8 * g + 8, :] = jnp.where(spare, extra, total[8 * g : 8 * g + 8])


def in_hbm(x):
    return pltpu.with_memory_space_constraint(x, pltpu.HBM)


def first_step(field, masks):
    vmem = pl.BlockSpec(memory_space=pltpu.VMEM)
    shapes = [(NV * NZ * PITCH, NL), (19, 8, NL), (13, 8, NL), (2, 8, NL), (64, NL)]
    return pl.pallas_call(
        first_kernel,
        out_shape=[jax.ShapeDtypeStruct(s, F32) for s in shapes],
        in_specs=[pl.BlockSpec(memory_space=pltpu.HBM)] * 3,
        out_specs=[vmem] * 5,
        scratch_shapes=[
            pltpu.VMEM((NV, NZ, NR, NL), F32),
            pltpu.VMEM((NV * 4, NR, NL), F32),
            pltpu.VMEM((2, 2, 4, 7), jnp.int32),
            pltpu.VMEM((400, NL), BF16),
            pltpu.SemaphoreType.DMA((4 * NV + 2,)),
        ],
        compiler_params=pltpu.CompilerParams(vmem_limit_bytes=VMEM_LIMIT),
    )(*[in_hbm(x) for x in (field, masks.transpose(0, 2, 3, 1), jnp.asarray(weights()["first"]))])


ROWS = 40


def lift_kernel(lifted, parts):
    def lift(step, _):
        v, bz = step // 2, lax.rem(step, 2)
        for z in range(8):
            start = pl.multiple_of((step * 8 + z) * PITCH, 8)
            for t in range(4):
                pair = lift_rows(lambda s: lifted[pl.ds(start + 16 * t + s, 8, stride=2), :], 8)
                for bx in range(2):
                    plane = (2 * bz + bx) * 24 + v * 8 + z
                    parts[pl.ds(pl.multiple_of(plane * ROWS + 8 * t, 8), 8), :] = pair[bx]
        return 0

    lax.fori_loop(0, NV * 2, lift, 0)


def lift_step(lifted):
    vmem = pl.BlockSpec(memory_space=pltpu.VMEM)
    return pl.pallas_call(
        lift_kernel,
        out_shape=jax.ShapeDtypeStruct((4 * NV * 8 * ROWS, NL), F32),
        in_specs=[vmem],
        out_specs=vmem,
        compiler_params=pltpu.CompilerParams(vmem_limit_bytes=VMEM_LIMIT),
    )(lifted)


def edge_kernel(parts_in, lifted, north, south, own_masks, table, parts, sides, packed):
    for p in range(4 * NV * 8):
        parts[p * ROWS + 32 : p * ROWS + 40, :] = jnp.zeros((8, NL), F32)
    for v in range(NV):
        for bz in range(2):

            def cell(x):
                return lifted[pl.ds((v * NZ + bz * 8) * PITCH + 8 + x, 8, stride=PITCH), :]

            def at(bx, r):
                return pl.ds(((2 * bz + bx) * 24 + v * 8) * ROWS + r, 8, stride=ROWS)

            before, after, detail = north[v * 4 + bz], south[v * 6 + bz], south[v * 6 + 2 + bz]
            start = cell(0)
            last = cell(63) - 0.5 * (cell(62) + after)
            parts[at(0, 0), :] = parts[at(0, 0), :] + 0.25 * before
            parts[at(0, 31), :] = parts[at(0, 31), :] - 0.125 * after
            parts[at(1, 31), :] = parts[at(1, 31), :] - 0.5 * after
            parts[at(0, 32), :] = after + 0.25 * (last + detail)
            parts[at(1, 32), :] = detail
            parts[at(1, 39), :] = before - 0.5 * start
            if bz == 0:
                parts[at(0, 33), :] = south[v * 6 + 4]
                parts[at(0, 34), :] = south[v * 6 + 5]
                parts[at(0, 38), :] = north[v * 4 + 2]
                parts[at(0, 39), :] = north[v * 4 + 3] - 0.125 * start

    lane = lax.broadcasted_iota(jnp.int32, (8, NL), 1) // 16

    def pack(step, _):
        for t in range(5):
            tile = jnp.zeros((8, NL), F32)
            for z in range(8):
                x = parts[pl.ds(pl.multiple_of((step * 8 + z) * ROWS + 8 * t, 8), 8), :]
                tile = jnp.where(lane == z, pltpu.roll(x, (8 + 16 * z) % NL, 1), tile)
            packed[pl.ds(pl.multiple_of(step * ROWS + 8 * t, 8), 8), :] = tile
        return 0

    lax.fori_loop(0, 4 * NV, pack, 0)
    terms = [two_terms(packed[n * 120 : (n + 1) * 120, :]) for n in range(4)]
    high, low = [jnp.concatenate(part, 1) for part in zip(*terms)]
    sides[0:120, :] = dot(high, table[...]) + dot(low, table[...])
    sides[120:128, :] = north[12]
    sides[128:136, :] = own_masks[0]
    sides[136:144, :] = own_masks[1]
    sides[144:152, :] = south[18]


def edge_step(parts, lifted, north, south, own_masks):
    vmem = pl.BlockSpec(memory_space=pltpu.VMEM)
    shapes = [(4 * NV * 8 * ROWS, NL), (152, NL)]
    return pl.pallas_call(
        edge_kernel,
        out_shape=[jax.ShapeDtypeStruct(s, F32) for s in shapes],
        in_specs=[vmem] * 6,
        out_specs=[vmem] * 2,
        input_output_aliases={0: 0},
        cost_estimate=cost(20),
        scratch_shapes=[pltpu.VMEM((480, NL), F32)],
        compiler_params=pltpu.CompilerParams(vmem_limit_bytes=VMEM_LIMIT),
    )(parts, lifted, north, south, own_masks, weights()["edge"])


def join_kernel(*refs):
    shares, out = refs[:-2], refs[-1]
    for n, piece in enumerate(shares):
        out[64 * n : 64 * (n + 1), :] = piece[...]


def join_step(shares, after):
    vmem = pl.BlockSpec(memory_space=pltpu.VMEM)
    return pl.pallas_call(
        join_kernel,
        out_shape=jax.ShapeDtypeStruct((64 * len(shares), NL), F32),
        in_specs=[vmem] * len(shares) + [pl.BlockSpec(memory_space=pl.ANY)],
        out_specs=vmem,
        cost_estimate=cost(20),
        compiler_params=pltpu.CompilerParams(vmem_limit_bytes=VMEM_LIMIT),
    )(*shares, after)


def mask_lanes(west, east, own_masks, north_mask, south_mask, wide):
    masks = [jnp.concatenate([ref[120 + 8 * i : 128 + 8 * i, :] for i in range(4)], 0) for ref in (east, west)]
    own = jnp.concatenate([north_mask[0], own_masks[0], own_masks[1], south_mask[0]], 0)
    flags = jnp.concatenate([own] + masks, 1).astype(BF16)
    return dot(flags, wide[144:528, :])


def beside_terms(west, east, at, count):
    lane = lax.broadcasted_iota(jnp.int32, (count, NL), 1)
    from_west = (lane >= 112) | ((lane < 96) & (lax.rem(lane, 24) >= 16))
    tiles = []
    for v in range(NV):
        rows = slice(v * ROWS + at, v * ROWS + at + count)
        beside = jnp.where(from_west, west[rows, :], east[rows, :])
        tiles += [pltpu.roll(beside, NL - z, 1) if z else beside for z in range(8)]
    return jnp.concatenate(two_terms(jnp.concatenate(tiles, 0)), 1)


def own_terms(planes, at, count):
    return jnp.concatenate(two_terms(planes[:, at : at + count, :].reshape(24 * count, NL)), 1)


def low_kernel(
    parts, west, east, own_masks, north_mask, south_mask, wide, narrow, low_back, gain2, low, second, kept2
):
    smooth_own, smooth_beside = narrow.at[256:512], narrow.at[512:768]
    forward2, inverse2 = narrow.at[1024:1152], narrow.at[1152:1280]
    lanes = mask_lanes(west, east, own_masks, north_mask, south_mask, wide)
    lane64 = lax.broadcasted_iota(jnp.int32, (1, NL), 1) < 64
    forward2_f = forward2[...].astype(F32)
    for ib in range(4):
        for n in range(4):
            b = 8 * ib + 4 * (n // 2) + n % 2 - 1
            smooth_two = lanes[b : b + 1, NL:] if n else jnp.ones((1, NL), F32)
            row = jnp.where(lane64, smooth_two, lanes[b + 2 : b + 3, NL:])
            both = dot((forward2_f * row).astype(BF16), inverse2[...]).astype(BF16)
            gain2[ib, n, 0:128, :] = both
            gain2[ib, n, 128:256, :] = both

    for at, count in ((0, 16), (16, 16), (32, 8)):
        part = dot(own_terms(parts.at[0], at, count), smooth_own[...])
        part += dot(beside_terms(west, east, at, count), smooth_beside[...])
        part = part.reshape(24, count, NL)
        if at < 32:
            low[:, 8 + at : 8 + at + count, :] = part
            if at == 0:
                low[:, 56:64, :] = part[:, 0:8]
        else:
            low[:, 0:8, :] = part
            low[:, 40:48, :] = part
            low[:, 48:56, :] = part

    def rows_two(v, _):
        for t in range(3):
            lifted = [
                lift_rows(lambda s: low[v * 8 + p, pl.ds(16 * t + s, 8, stride=2), :], 8) for p in range(8)
            ]
            for bx in range(2):
                smooth, detail = lift_planes([pair[bx] for pair in lifted])
                for bz, part in ((0, smooth), (1, detail)):
                    for z in range(4):
                        second[2 * bz + bx, t, pl.ds(pl.multiple_of((v * 4 + z) * 8, 8), 8), :] = part[z]
        return 0

    lax.fori_loop(0, NV, rows_two, 0)
    for n in range(4):
        for t in range(3):
            terms = jnp.concatenate(two_terms(second[n, t]), 1)
            if t < 2:
                kept2[n, :, 8 + 8 * t : 16 + 8 * t, :] = dot(terms, gain2[t + 1, n]).reshape(NV * 4, 8, NL)
            else:
                kept2[n, :, 0:8, :] = dot(terms, gain2[0, n]).reshape(NV * 4, 8, NL)
                kept2[n, :, 24:32, :] = dot(terms, gain2[3, n]).reshape(NV * 4, 8, NL)

    def back_two(v, _):
        for t in range(3):
            pairs = {}
            for bz in range(2):
                for z in range(4):
                    p = v * 4 + z
                    if t < 2:
                        pairs[bz, z] = unlift_rows(
                            lambda r: kept2[2 * bz, p, pl.ds(r, 8), :],
                            lambda r: kept2[2 * bz + 1, p, pl.ds(r, 8), :],
                            8 + 8 * t,
                        )
                    else:
                        even = kept2[2 * bz, p, 24:32, :] - 0.25 * (
                            kept2[2 * bz + 1, p, 23:31, :] + kept2[2 * bz + 1, p, 24:32, :]
                        )
                        pairs[bz, z] = (even, even)
            for parity in range(2 if t < 2 else 1):
                planes = unlift_planes([pairs[0, z][parity] for z in range(4)], [pairs[1, z][parity] for z in range(4)])
                for z in range(8):
                    low_back[v * 8 + z, pl.ds(16 * t + parity, 8, stride=2), :] = planes[z]
        return 0

    lax.fori_loop(0, NV, back_two, 0)


def high_kernel(
    parts, west, east, own_masks, north_mask, south_mask, wide, narrow, low_back, kept, gain, sides_wide
):
    inverse, back = narrow.at[0:256], narrow.at[768:1024]
    lanes = mask_lanes(west, east, own_masks, north_mask, south_mask, wide)
    forward_f = wide[0:144, :].astype(F32)
    for ib in range(4):
        sides_wide[ib] = jnp.zeros((NL, 4 * NL), F32)
    for ib in range(4):
        for n in range(4):
            b = 8 * ib + 4 * (n // 2) + n % 2 - 1
            smooth_one = lanes[b : b + 1, 0:NL] if n else jnp.zeros((1, NL), F32)
            row = jnp.concatenate([smooth_one, lanes[b + 2 : b + 3, 0:NL]], 1)
            both = dot((forward_f * row).astype(BF16), inverse[...])
            main = both[0:128].astype(BF16)
            gain[ib, n, 0:128, :] = main
            gain[ib, n, 128:256, :] = main
            for i in range(3):
                at = 24 * n + 8 * i
                sides_wide[ib, at : at + 1, n * NL : (n + 1) * NL] = both[128 + i : 129 + i]

    gain_sides = []
    for ib in range(4):
        side = sides_wide[ib].astype(BF16)
        gain_sides.append(jnp.concatenate([side, side], 0))
    for ib in range(3):
        at, count = 16 * ib, 16 if ib < 2 else 8
        terms = beside_terms(west, east, at, count)
        for place, first in (((8 + at, ib + 1),) if ib < 2 else ((40, 3), (0, 0))):
            product = dot(terms, gain_sides[first])
            for n in range(4):
                kept[n, :, place : place + count, :] = product[:, n * NL : (n + 1) * NL].reshape(24, count, NL)

    def keep(n, _):
        for ib in range(3):
            at, count = 16 * ib, 16 if ib < 2 else 8
            terms = own_terms(parts.at[n], at, count)
            for place, first in (((8 + at, ib + 1),) if ib < 2 else ((40, 3), (0, 0))):
                kept[n, :, place : place + count, :] += dot(terms, gain[first, n]).reshape(24, count, NL)
        return 0

    lax.fori_loop(0, 4, keep, 0)
    for at, count in ((0, 16), (16, 16), (32, 8)):
        kept[0, :, 8 + at : 8 + at + count, :] += dot(own_terms(low_back, at, count), back[...]).reshape(24, count, NL)


def cells_kernel(kept, out, cells, sems):
    def back_one(step, _):
        v, t = step // 4, step % 4
        pairs = {}
        for bz in range(2):
            for z in range(8):
                p = v * 8 + z
                pairs[bz, z] = unlift_rows(
                    lambda r: kept[2 * bz, p, pl.ds(8 * t + r, 8), :],
                    lambda r: kept[2 * bz + 1, p, pl.ds(8 * t + r, 8), :],
                    8,
                )
        for parity in range(2):
            planes = unlift_planes([pairs[0, z][parity] for z in range(8)], [pairs[1, z][parity] for z in range(8)])
            for z in range(NZ):
                cells[v, z, pl.ds(16 * t + parity, 8, stride=2), :] = planes[z]
        return 0

    def one(v, _):
        lax.fori_loop(v * 4, v * 4 + 4, back_one, 0)
        pltpu.make_async_copy(cells.at[v], out.at[v], sems.at[v]).start()
        return 0

    lax.fori_loop(0, NV, one, 0)
    for v in range(NV):
        pltpu.make_async_copy(cells.at[v], out.at[v], sems.at[v]).wait()


def main_specs():
    vmem = pl.BlockSpec(memory_space=pltpu.VMEM)
    return [
        vmem, vmem, vmem, vmem,
        pl.BlockSpec((1, 8, NL), lambda i: (12, 0, 0)), pl.BlockSpec((1, 8, NL), lambda i: (18, 0, 0)),
        vmem, vmem,
    ]


def low_step(*operands):
    w = weights()
    return pl.pallas_call(
        low_kernel,
        grid=(1,),
        out_shape=jax.ShapeDtypeStruct((NV * 8, 48, NL), F32),
        in_specs=main_specs(),
        out_specs=pl.BlockSpec((NV * 8, 48, NL), lambda i: (0, 0, 0)),
        scratch_shapes=[
            pltpu.VMEM((4, 4, 256, NL), BF16),
            pltpu.VMEM((NV * 8, 64, NL), F32),
            pltpu.VMEM((4, 3, NV * 32, NL), F32),
            pltpu.VMEM((4, NV * 4, 40, NL), F32),
        ],
        cost_estimate=cost(4),
        compiler_params=pltpu.CompilerParams(vmem_limit_bytes=VMEM_LIMIT),
    )(*operands, w["wide"], w["narrow"])


def high_step(low_back, *operands):
    w = weights()
    return pl.pallas_call(
        high_kernel,
        grid=(1,),
        out_shape=jax.ShapeDtypeStruct((4, NV * 8, 48, NL), F32),
        in_specs=main_specs() + [pl.BlockSpec((NV * 8, 48, NL), lambda i: (0, 0, 0))],
        out_specs=pl.BlockSpec((4, NV * 8, 48, NL), lambda i: (0, 0, 0, 0)),
        scratch_shapes=[
            pltpu.VMEM((4, 4, 256, NL), BF16),
            pltpu.VMEM((4, NL, 4 * NL), F32),
        ],
        cost_estimate=cost(4),
        compiler_params=pltpu.CompilerParams(vmem_limit_bytes=VMEM_LIMIT),
    )(*operands, w["wide"], w["narrow"], low_back)


def cells_step(kept):
    shape = (NV, NZ, NR, NL)
    return pl.pallas_call(
        cells_kernel,
        out_shape=jax.ShapeDtypeStruct(shape, F32),
        in_specs=[pl.BlockSpec(memory_space=pltpu.VMEM)],
        out_specs=pl.BlockSpec(memory_space=pltpu.HBM),
        scratch_shapes=[pltpu.VMEM(shape, F32), pltpu.SemaphoreType.DMA((NV,))],
        cost_estimate=cost(4),
        compiler_params=pltpu.CompilerParams(vmem_limit_bytes=VMEM_LIMIT),
    )(kept)


def rows_kernel(count_x, count_z, *refs):
    shares, out = refs[:count_x], refs[count_x + 1]
    me, me_y = lax.axis_index("gx"), lax.axis_index("gy")
    row = lax.broadcasted_iota(jnp.int32, (8, NL), 0)
    piece = lax.broadcasted_iota(jnp.int32, (8, NL), 1) // 21
    for r in range(count_x):
        at = pl.multiple_of(16 * (me ^ r), 16)
        for j in range(count_z):
            for z in range(4):
                out[j, z, pl.ds(at, 16), :] = shares[r][64 * j + 16 * z : 64 * j + 16 * z + 16, :]
    for r in range(count_x):
        i = me ^ r
        below = pl.multiple_of(16 * lax.rem(i + 1, count_x), 16)
        above = pl.multiple_of(16 * lax.rem(i + count_x - 1, count_x) + 8, 8)
        for j in range(count_z):
            tiles = [shares[r][64 * j + 8 * g : 64 * j + 8 * g + 8, :] for g in range(8)]
            low, high = jnp.zeros((8, NL), F32), jnp.zeros((8, NL), F32)
            for p in range(5):
                back = (21 * p - 105) % NL
                low = jnp.where(piece == p, pltpu.roll(tiles[p], back, 1), low)
                extra = tiles[5 + p // 2]
                extra = extra if p % 2 else pltpu.roll(extra, 4, 0)
                high = jnp.where(piece == p, pltpu.roll(extra, back, 1), high)
            for z in range(4):
                first = pltpu.roll(low, 8 - 2 * z, 0) if z else low
                last = pltpu.roll(high, z, 0) if z else high
                out[j, z, pl.ds(below, 8), :] += jnp.where(row < 2, first, 0.0)
                out[j, z, pl.ds(above, 8), :] += jnp.where(row == 7, last, 0.0)
    for j in range(count_z):
        place = lax.rem(2 * (lax.shift_right_logical(me_y, 1) ^ j) + lax.rem(me_y, 2), 4)
        turn = lax.rem(32 * place + NL - 1, NL)
        for z in range(4):
            for t in range(2 * count_x):
                rows = slice(8 * t, 8 * t + 8)
                out[j, z, rows, :] = pltpu.roll(out[j, z, rows, :], turn, 1)


def rows_step(pieces, count_z, after):
    vmem = pl.BlockSpec(memory_space=pltpu.VMEM)
    count_x = len(pieces)
    return pl.pallas_call(
        functools.partial(rows_kernel, count_x, count_z),
        out_shape=jax.ShapeDtypeStruct((count_z, 4, 16 * count_x, NL), F32),
        in_specs=[vmem] * count_x + [pl.BlockSpec(memory_space=pl.ANY)],
        out_specs=vmem,
        compiler_params=pltpu.CompilerParams(vmem_limit_bytes=VMEM_LIMIT),
    )(*pieces, after)


def coarse_kernel(count_x, count_y, own, other, out_hbm, out, sems):
    me = lax.axis_index("gy")
    me_z, is_even = lax.shift_right_logical(me, 1), lax.rem(me, 2) == 0
    lane = lax.broadcasted_iota(jnp.int32, (8, NL), 1)
    place = [lax.rem(lane + NL - 35 * v, NL) for v in range(NV)]

    def block(i, _):
        rows = pl.ds(pl.multiple_of(8 * i, 8), 8)
        for z in range(4):
            pieces = []
            for j in range(count_y // 2):
                mine, theirs = own[j ^ me_z, z, rows, :], other[j ^ me_z, z, rows, :]
                pieces += [jnp.where(is_even, mine, theirs), jnp.where(is_even, theirs, mine)]
            for v in range(NV):
                at = place[v]
                for t in range(count_y // 4):
                    total = jnp.where(at < 2, pieces[4 * t - 1], 0.0)
                    total += jnp.where(at == NL - 1, pieces[(4 * t + 4) % count_y], 0.0)
                    for q in range(4):
                        inside = (at >= 32 * q - 1) & (at < 32 * q + 34)
                        total += jnp.where(inside, pieces[4 * t + q], 0.0)
                    out[v, z, rows, NL * t : NL * (t + 1)] = pltpu.roll(total, NL - 35 * v, 1) if v else total
        return 0

    def copy(i):
        rows = pl.ds(pl.multiple_of(16 * i, 16), 16)
        return pltpu.make_async_copy(out.at[:, :, rows], out_hbm.at[:, :, rows], sems.at[i])

    def pair(i, _):
        block(2 * i, 0)
        block(2 * i + 1, 0)
        copy(i).start()
        return 0

    lax.fori_loop(0, count_x, pair, 0)
    for i in range(count_x):
        copy(i).wait()


def coarse_step(own, other, count_x, count_y):
    vmem = pl.BlockSpec(memory_space=pltpu.VMEM)
    shape = (NV, 4, 16 * count_x, 32 * count_y)
    return pl.pallas_call(
        functools.partial(coarse_kernel, count_x, count_y),
        out_shape=jax.ShapeDtypeStruct(shape, F32),
        in_specs=[vmem, vmem],
        out_specs=pl.BlockSpec(memory_space=pltpu.HBM),
        scratch_shapes=[pltpu.VMEM(shape, F32), pltpu.SemaphoreType.DMA((count_x,))],
        compiler_params=pltpu.CompilerParams(vmem_limit_bytes=VMEM_LIMIT),
    )(own, other)


def shifted(x, axis, step):
    count = lax.axis_size(axis)
    return lax.ppermute(x, axis, [(i, (i + step) % count) for i in range(count)])


def swapped(x, axis, distance):
    return lax.ppermute(x, axis, [(i, i ^ distance) for i in range(lax.axis_size(axis))])


def body(field, masks):
    count_x, count_y = lax.axis_size("gx"), lax.axis_size("gy")
    lifted, up, down, own_masks, share = first_step(field, masks)
    south = shifted(up, "gx", -1)
    north = shifted(down, "gx", 1)
    shares = [share] + [swapped(share, "gy", r) for r in range(2, count_y, 2)]
    parts, sides = edge_step(lift_step(lifted), lifted, north, south, own_masks)
    west = shifted(sides, "gy", 1)
    east = shifted(sides, "gy", -1)
    joined = join_step(shares, sides)
    pieces = [joined] + [swapped(joined, "gx", r) for r in range(1, count_x)]
    operands = (parts.reshape(4, NV * 8, ROWS, NL), west, east, own_masks, north, south)
    kept = high_step(low_step(*operands), *operands)
    own = rows_step(pieces, count_y // 2, kept)
    other = swapped(own, "gy", 1)
    return cells_step(kept), coarse_step(own, other, count_x, count_y)


def solution(mesh):
    placed = P(None, None, "gx", "gy")
    return jax.shard_map(
        body,
        mesh=mesh,
        in_specs=(placed, placed),
        out_specs=(placed, P()),
        check_vma=False,
    )
```

profile of v0, /device:TPU:0, one launch (start us, length us, event | category | flops | bytes accessed | tf_op | source)
XLA Modules:
  0.0 30.9 jit_solution(3008077701970923263)
XLA Ops:
  0.6 2.5 %shard_map.77 = (f32[3840,128]{1,0:T(8,128)S(1)}, f32[19,8,128]{2,1,0:T(8,128)S(1)}, f32[13,8,128]{2,1,0:T(8,128)S(1)}, f32[2,8,128]{2,1,0:T(8,128)S(1)}, f32[64,128]{1,0:T(8,128)S(1)}) custom-call(f32[3,16,64,128]{3,2,1,0:T(8,128)} %field.1, s32[2,2,4,7]{3,2,1,0:T(4,128)} %bitcast.4, bf16[400,128]{1,0:T(8,128)(2,1)} %constant.8.clone.table_hbm), custom_call_target="tpu_custom_call" | custom-call | tf_op jit(solution)/shard_map/pallas_call | solution.py:331
  3.1 3.9 %collective-permute-start.1 = (f32[19,8,128]{2,1,0:T(8,128)S(1)}, f32[19,8,128]{2,1,0:T(8,128)S(1)}, u32[]{:S(2)}, u32[]{:S(2)}) collective-permute-start(f32[19,8,128]{2,1,0:T(8,128)S(1)} %get-tuple-element.11), channel_id=1, source_target_pairs={{0,24},{8,0},{16,8},{24,16},{1,25},{9,1},{17,9},{25,17},{2,26},{10... | collective-permute-start | bytes 233480 | tf_op jit(solution)/shard_map/ppermute | solution.py:792
  7.1 1.6 %collective-permute-start.4 = (f32[64,128]{1,0:T(8,128)S(1)}, f32[64,128]{1,0:T(8,128)S(1)}, u32[]{:S(2)}, u32[]{:S(2)}) collective-permute-start(f32[64,128]{1,0:T(8,128)S(1)} %get-tuple-element.15.refs_0_), channel_id=1, source_target_pairs={{0,2},{1,3},{2,0},{3,1},{4,6},{5,7},{6,4},{7,5},{8,10},{9,11},{10,... | collective-permute-start | bytes 98312 | tf_op jit(solution)/shard_map/ppermute | solution.py:796
  8.6 2.6 %collective-permute-start.5 = (f32[64,128]{1,0:T(8,128)S(1)}, f32[64,128]{1,0:T(8,128)S(1)}, u32[]{:S(2)}, u32[]{:S(2)}) collective-permute-start(f32[64,128]{1,0:T(8,128)S(1)} %get-tuple-element.15.refs_0_), channel_id=1, source_target_pairs={{0,4},{1,5},{2,6},{3,7},{4,0},{5,1},{6,2},{7,3},{8,12},{9,13},{10,... | collective-permute-start | bytes 98312 | tf_op jit(solution)/shard_map/ppermute | solution.py:796
  11.2 0.2 collective-permute-start.6
  11.5 0.3 %shard_map.78.parts_in = f32[3840,128]{1,0:T(8,128)S(1)} custom-call(f32[3840,128]{1,0:T(8,128)S(1)} %get-tuple-element.9.lifted), custom_call_target="tpu_custom_call" | custom-call | tf_op jit(solution)/shard_map/pallas_call | solution.py:367
  11.8 0.3 %collective-permute-done.north.north_mask = f32[13,8,128]{2,1,0:T(8,128)S(1)} collective-permute-done((f32[13,8,128]{2,1,0:T(8,128)S(1)}, f32[13,8,128]{2,1,0:T(8,128)S(1)}, u32[]{:S(2)}, u32[]{:S(2)}) %collective-permute-start) | collective-permute-done | bytes 53280 | tf_op jit(solution)/shard_map/ppermute | solution.py:792
  12.1 0.3 copy-done.2
  12.4 1.6 %shard_map.79 = (f32[3840,128]{1,0:T(8,128)S(1)}, f32[152,128]{1,0:T(8,128)S(1)}) custom-call(f32[3840,128]{1,0:T(8,128)S(1)} %shard_map.78.parts_in, f32[3840,128]{1,0:T(8,128)S(1)} %get-tuple-element.9.lifted, f32[13,8,128]{2,1,0:T(8,128)S(1)} %collective-permute-done.north.north_mask, ...), custom_call_target="tpu_custom_call", output_to_operand_aliasing={{0}: (0, {})} | custom-call | flops 20000000000 | bytes 8000000 | tf_op jit(solution)/shard_map/pallas_call | solution.py:427
  14.0 0.0 copy-start
  14.0 0.0 copy-start.1
  14.0 0.1 collective-permute-start.2
  14.1 3.5 %collective-permute-start.3 = (f32[152,128]{1,0:T(8,128)S(1)}, f32[152,128]{1,0:T(8,128)S(1)}, u32[]{:S(2)}, u32[]{:S(2)}) collective-permute-start(f32[152,128]{1,0:T(8,128)S(1)} %get-tuple-element.14.refs_4_), channel_id=1, source_target_pairs={{0,7},{1,0},{2,1},{3,2},{4,3},{5,4},{6,5},{7,6},{8,15},{9,8},{10,9... | collective-permute-start | bytes 233480 | tf_op jit(solution)/shard_map/ppermute | solution.py:792
  17.6 2.0 %collective-permute-start.7 = (f32[256,128]{1,0:T(8,128)S(1)}, f32[256,128]{1,0:T(8,128)S(1)}, u32[]{:S(2)}, u32[]{:S(2)}) collective-permute-start(f32[256,128]{1,0:T(8,128)S(1)} %shard_map.83.refs_0_), channel_id=1, source_target_pairs={{0,8},{8,0},{16,24},{24,16},{1,9},{9,1},{17,25},{25,17},{2,10},{10... | collective-permute-start | bytes 393224 | tf_op jit(solution)/shard_map/ppermute | solution.py:796
  19.7 1.5 %collective-permute-start.8 = (f32[256,128]{1,0:T(8,128)S(1)}, f32[256,128]{1,0:T(8,128)S(1)}, u32[]{:S(2)}, u32[]{:S(2)}) collective-permute-start(f32[256,128]{1,0:T(8,128)S(1)} %shard_map.83.refs_0_), channel_id=1, source_target_pairs={{0,16},{8,24},{16,0},{24,8},{1,17},{9,25},{17,1},{25,9},{2,18},{10... | collective-permute-start | bytes 393224 | tf_op jit(solution)/shard_map/ppermute | solution.py:796
  21.2 0.0 collective-permute-start.9
  21.2 1.4 %shard_map.80.low_back = f32[24,48,128]{2,1,0:T(8,128)S(1)} custom-call(f32[4,24,40,128]{3,2,1,0:T(8,128)S(1)} %bitcast.2, f32[152,128]{1,0:T(8,128)S(1)} %collective-permute-done.2.west, f32[152,128]{1,0:T(8,128)S(1)} %collective-permute-done.3.east, f32[2,8,128]{2,1,0:T(8,128)S(1)} %get-tuple-element.12.own_masks, ...), custom_call_target="tpu_custom_call" | custom-call | flops 4000000000 | bytes 8000000 | tf_op jit(solution)/shard_map/pallas_call | solution.py:642
  22.6 2.5 %shard_map.81.kept.refs_4_ = f32[4,24,48,128]{3,2,1,0:T(8,128)S(1)} custom-call(f32[4,24,40,128]{3,2,1,0:T(8,128)S(1)} %bitcast.3, f32[152,128]{1,0:T(8,128)S(1)} %collective-permute-done.2.west, f32[152,128]{1,0:T(8,128)S(1)} %collective-permute-done.3.east, f32[2,8,128]{2,1,0:T(8,128)S(1)} %get-tuple-element.12.own_masks, ...), custom_call_target="tpu_custom_call" | custom-call | flops 4000000000 | bytes 8000000 | tf_op jit(solution)/shard_map/pallas_call | solution.py:661
  25.2 1.8 %collective-permute-done.9.refs_3_ = f32[256,128]{1,0:T(8,128)S(1)} collective-permute-done((f32[256,128]{1,0:T(8,128)S(1)}, f32[256,128]{1,0:T(8,128)S(1)}, u32[]{:S(2)}, u32[]{:S(2)}) %collective-permute-start.9) | collective-permute-done | bytes 131104 | tf_op jit(solution)/shard_map/ppermute | solution.py:796
  27.0 0.5 %shard_map.84.own = f32[4,4,64,128]{3,2,1,0:T(8,128)S(1)} custom-call(f32[256,128]{1,0:T(8,128)S(1)} %shard_map.83.refs_0_, f32[256,128]{1,0:T(8,128)S(1)} %collective-permute-done.7.refs_1_, f32[256,128]{1,0:T(8,128)S(1)} %collective-permute-done.8.refs_2_, f32[256,128]{1,0:T(8,128)S(1)} %collective-permute-done.9.refs_3_, ...), custom_call_target="tpu_custom_call" | custom-call | tf_op jit(solution)/shard_map/pallas_call | solution.py:729
  27.6 0.1 collective-permute-start.10
  27.7 1.4 %shard_map.82 = f32[3,16,64,128]{3,2,1,0:T(8,128)} custom-call(f32[4,24,48,128]{3,2,1,0:T(8,128)S(1)} %shard_map.81.kept.refs_4_), custom_call_target="tpu_custom_call" | custom-call | flops 4000000000 | bytes 8000000 | tf_op jit(solution)/shard_map/pallas_call | solution.py:678
  29.1 0.4 %collective-permute-done.10.other = f32[4,4,64,128]{3,2,1,0:T(8,128)S(1)} collective-permute-done((f32[4,4,64,128]{3,2,1,0:T(8,128)S(1)}, f32[4,4,64,128]{3,2,1,0:T(8,128)S(1)}, u32[]{:S(2)}, u32[]{:S(2)}) %collective-permute-start.10) | collective-permute-done | bytes 524320 | tf_op jit(solution)/shard_map/ppermute | solution.py:796
  29.6 1.4 %shard_map.85 = f32[3,4,64,256]{3,2,1,0:T(8,128)} custom-call(f32[4,4,64,128]{3,2,1,0:T(8,128)S(1)} %shard_map.84.own, f32[4,4,64,128]{3,2,1,0:T(8,128)S(1)} %collective-permute-done.10.other), custom_call_target="tpu_custom_call" | custom-call | tf_op jit(solution)/shard_map/pallas_call | solution.py:780
  (13 shorter events, 0.0 us)
Async XLA Ops:
  3.1 9.0 %collective-permute-start.1 = (f32[19,8,128]{2,1,0:T(8,128)S(1)}, f32[19,8,128]{2,1,0:T(8,128)S(1)}, u32[]{:S(2)}, u32[]{:S(2)}) collective-permute-start(f32[19,8,128]{2,1,0:T(8,128)S(1)} %get-tuple-element.11), channel_id=1, source_target_pairs={{0,24},{8,0},{16,8},{24,16},{1,25},{9,1},{17,9},{25,17},{2,26},{10... | collective-permute-start | bytes 233480 | tf_op jit(solution)/shard_map/ppermute | solution.py:792
  7.1 5.0 %collective-permute-start = (f32[13,8,128]{2,1,0:T(8,128)S(1)}, f32[13,8,128]{2,1,0:T(8,128)S(1)}, u32[]{:S(2)}, u32[]{:S(2)}) collective-permute-start(f32[13,8,128]{2,1,0:T(8,128)S(1)} %get-tuple-element.10), channel_id=1, source_target_pairs={{0,8},{8,16},{16,24},{24,0},{1,9},{9,17},{17,25},{25,1},{2,10},{10... | collective-permute-start | bytes 159752 | tf_op jit(solution)/shard_map/ppermute | solution.py:792
  7.1 10.5 %collective-permute-start.4 = (f32[64,128]{1,0:T(8,128)S(1)}, f32[64,128]{1,0:T(8,128)S(1)}, u32[]{:S(2)}, u32[]{:S(2)}) collective-permute-start(f32[64,128]{1,0:T(8,128)S(1)} %get-tuple-element.15.refs_0_), channel_id=1, source_target_pairs={{0,2},{1,3},{2,0},{3,1},{4,6},{5,7},{6,4},{7,5},{8,10},{9,11},{10,... | collective-permute-start | bytes 98312 | tf_op jit(solution)/shard_map/ppermute | solution.py:796
  8.6 9.0 %collective-permute-start.5 = (f32[64,128]{1,0:T(8,128)S(1)}, f32[64,128]{1,0:T(8,128)S(1)}, u32[]{:S(2)}, u32[]{:S(2)}) collective-permute-start(f32[64,128]{1,0:T(8,128)S(1)} %get-tuple-element.15.refs_0_), channel_id=1, source_target_pairs={{0,4},{1,5},{2,6},{3,7},{4,0},{5,1},{6,2},{7,3},{8,12},{9,13},{10,... | collective-permute-start | bytes 98312 | tf_op jit(solution)/shard_map/ppermute | solution.py:796
  11.2 6.4 %collective-permute-start.6 = (f32[64,128]{1,0:T(8,128)S(1)}, f32[64,128]{1,0:T(8,128)S(1)}, u32[]{:S(2)}, u32[]{:S(2)}) collective-permute-start(f32[64,128]{1,0:T(8,128)S(1)} %get-tuple-element.15.refs_0_), channel_id=1, source_target_pairs={{0,6},{1,7},{2,4},{3,5},{4,2},{5,3},{6,0},{7,1},{8,14},{9,15},{10,... | collective-permute-start | bytes 98312 | tf_op jit(solution)/shard_map/ppermute | solution.py:796
  11.5 0.9 %copy-start.2 = (bf16[512,128]{1,0:T(8,128)(2,1)S(1)}, bf16[512,128]{1,0:T(8,128)(2,1)}, u32[]{:S(2)}) copy-start(bf16[512,128]{1,0:T(8,128)(2,1)} %constant.9.clone.table) | copy-start | bytes 393220
  14.0 7.2 %copy-start = (bf16[1280,128]{1,0:T(8,128)(2,1)S(1)}, bf16[1280,128]{1,0:T(8,128)(2,1)}, u32[]{:S(2)}) copy-start(bf16[1280,128]{1,0:T(8,128)(2,1)} %constant.11.clone.narrow) | copy-start | bytes 983044
  14.0 7.2 %copy-start.1 = (bf16[528,256]{1,0:T(8,128)(2,1)S(1)}, bf16[528,256]{1,0:T(8,128)(2,1)}, u32[]{:S(2)}) copy-start(bf16[528,256]{1,0:T(8,128)(2,1)} %constant.10.clone.wide) | copy-start | bytes 811012
  14.0 7.2 %collective-permute-start.2 = (f32[152,128]{1,0:T(8,128)S(1)}, f32[152,128]{1,0:T(8,128)S(1)}, u32[]{:S(2)}, u32[]{:S(2)}) collective-permute-start(f32[152,128]{1,0:T(8,128)S(1)} %get-tuple-element.14.refs_4_), channel_id=1, source_target_pairs={{0,1},{1,2},{2,3},{3,4},{4,5},{5,6},{6,7},{7,0},{8,9},{9,10},{10,1... | collective-permute-start | bytes 233480 | tf_op jit(solution)/shard_map/ppermute | solution.py:792
  14.1 7.1 %collective-permute-start.3 = (f32[152,128]{1,0:T(8,128)S(1)}, f32[152,128]{1,0:T(8,128)S(1)}, u32[]{:S(2)}, u32[]{:S(2)}) collective-permute-start(f32[152,128]{1,0:T(8,128)S(1)} %get-tuple-element.14.refs_4_), channel_id=1, source_target_pairs={{0,7},{1,0},{2,1},{3,2},{4,3},{5,4},{6,5},{7,6},{8,15},{9,8},{10,9... | collective-permute-start | bytes 233480 | tf_op jit(solution)/shard_map/ppermute | solution.py:792
  17.6 7.6 %collective-permute-start.7 = (f32[256,128]{1,0:T(8,128)S(1)}, f32[256,128]{1,0:T(8,128)S(1)}, u32[]{:S(2)}, u32[]{:S(2)}) collective-permute-start(f32[256,128]{1,0:T(8,128)S(1)} %shard_map.83.refs_0_), channel_id=1, source_target_pairs={{0,8},{8,0},{16,24},{24,16},{1,9},{9,1},{17,25},{25,17},{2,10},{10... | collective-permute-start | bytes 393224 | tf_op jit(solution)/shard_map/ppermute | solution.py:796
  19.7 5.5 %collective-permute-start.8 = (f32[256,128]{1,0:T(8,128)S(1)}, f32[256,128]{1,0:T(8,128)S(1)}, u32[]{:S(2)}, u32[]{:S(2)}) collective-permute-start(f32[256,128]{1,0:T(8,128)S(1)} %shard_map.83.refs_0_), channel_id=1, source_target_pairs={{0,16},{8,24},{16,0},{24,8},{1,17},{9,25},{17,1},{25,9},{2,18},{10... | collective-permute-start | bytes 393224 | tf_op jit(solution)/shard_map/ppermute | solution.py:796
  21.2 5.9 %collective-permute-start.9 = (f32[256,128]{1,0:T(8,128)S(1)}, f32[256,128]{1,0:T(8,128)S(1)}, u32[]{:S(2)}, u32[]{:S(2)}) collective-permute-start(f32[256,128]{1,0:T(8,128)S(1)} %shard_map.83.refs_0_), channel_id=1, source_target_pairs={{0,24},{8,16},{16,8},{24,0},{1,25},{9,17},{17,9},{25,1},{2,26},{10... | collective-permute-start | bytes 393224 | tf_op jit(solution)/shard_map/ppermute | solution.py:796
  27.6 2.0 %collective-permute-start.10 = (f32[4,4,64,128]{3,2,1,0:T(8,128)S(1)}, f32[4,4,64,128]{3,2,1,0:T(8,128)S(1)}, u32[]{:S(2)}, u32[]{:S(2)}) collective-permute-start(f32[4,4,64,128]{3,2,1,0:T(8,128)S(1)} %shard_map.84.own), channel_id=1, source_target_pairs={{0,1},{1,0},{2,3},{3,2},{4,5},{5,4},{6,7},{7,6},{8,9},{9,8},{10,11... | collective-permute-start | bytes 1572872 | tf_op jit(solution)/shard_map/ppermute | solution.py:796
where the time goes:
time: 31.1 us; the launch traced here: 30.9 us
  starting transfers between devices  15.6 us (50%)
  Pallas kernels  11.7 us (38%)
  waiting for transfers between devices  2.61 us (8%)
  between operations  0.76 us (2%)
    ppermute x7, starting transfers between devices, swapped(): lax.ppermute(x, axis, [(i, i ^ distance) for i in range(lax.axis_size(axi...  8.03 us
    ppermute x4, starting transfers between devices, shifted(): lax.ppermute(x, axis, [(i, (i + step) % count) for i in range(count)])  7.54 us
    pallas_call x1, Pallas kernels, high_step(): pl.pallas_call(high_kernel, grid=(1,), out_shape=jax.ShapeDtypeStruct((4,...  2.54 us
    pallas_call x1, Pallas kernels, first_step(): pl.pallas_call(first_kernel, out_shape=[jax.ShapeDtypeStruct(s, F32) for...  2.48 us
    ppermute x7, waiting for transfers between devices, swapped(): lax.ppermute(x, axis, [(i, i ^ distance) for i in range(lax.axis_size(axi...  2.29 us
    pallas_call x1, Pallas kernels, edge_step(): pl.pallas_call(edge_kernel, out_shape=[jax.ShapeDtypeStruct(s, F32) for s...  1.6 us
    pallas_call x1, Pallas kernels, cells_step(): pl.pallas_call(cells_kernel, out_shape=jax.ShapeDtypeStruct(shape, F32),...  1.45 us
    pallas_call x1, Pallas kernels, low_step(): pl.pallas_call(low_kernel, grid=(1,), out_shape=jax.ShapeDtypeStruct((NV...  1.41 us
  transfers between devices with their start and end apart: 11, of which 3 were waited for; matrix products, arithmetic and copies ran while one was open for 0% of the time, Pallas kernels for 24%

commit v1 on v0

--- a/solution.py
+++ b/solution.py
@@ -237,33 +237,41 @@
 def first_kernel(
     field, masks_hbm, table_hbm, lifted, up, down, own_masks, share, cells, twice, masks, table, sems
 ):
+    small = [
+        pltpu.make_async_copy(masks_hbm, masks, sems.at[0]),
+        pltpu.make_async_copy(table_hbm, table, sems.at[1]),
+    ]
     copies = []
     for v in range(NV):
-        for h in range(4):
-            part = pl.ds(4 * h, 4)
-            copies.append(pltpu.make_async_copy(field.at[v, part], cells.at[v, part], sems.at[4 * v + h]))
-    copies.append(pltpu.make_async_copy(masks_hbm, masks, sems.at[4 * NV]))
-    copies.append(pltpu.make_async_copy(table_hbm, table, sems.at[4 * NV + 1]))
-    for copy in copies:
+        for c in range(4):
+            part = pl.ds(16 * c, 16)
+            copies.append(pltpu.make_async_copy(field.at[v, :, part], cells.at[v, :, part], sems.at[2 + 4 * v + c]))
+    for copy in small + copies:
         copy.start()
     for p in range(NV * NZ):
         lifted[p * PITCH : p * PITCH + 8, :] = jnp.zeros((8, NL), F32)
         lifted[p * PITCH + 72 : p * PITCH + 80, :] = jnp.zeros((8, NL), F32)
+    for copy in small:
+        copy.wait()
+    for i, out, tile in ((0, up, 18), (1, down, 12)):
+        total = jnp.zeros((7, NL), F32)
+        for l in range(2):
+            flags = masks[l, i].astype(F32).astype(BF16)
+            spread = table[384 + 4 * l : 388 + 4 * l, :]
+            total += lax.dot_general(flags, spread, (((0,), (0,)), ((), ())), preferred_element_type=F32)
+        own_masks[i] = jnp.concatenate([total, jnp.zeros((1, NL), F32)], 0)
+        out[tile] = own_masks[i]
 
     for v in range(NV):
-        for copy in copies[4 * v : 4 * v + 4]:
-            copy.wait()
-
-        def planes(t, _):
-            at = pl.multiple_of(t * 8, 8)
-            smooth, detail = lift_planes([cells[v, z, pl.ds(at, 8), :] for z in range(NZ)])
+        for t in range(8):
+            if t % 2 == 0:
+                copies[4 * v + t // 2].wait()
+            smooth, detail = lift_planes([cells[v, z, 8 * t : 8 * t + 8, :] for z in range(NZ)])
             for k, tile in enumerate(smooth + detail):
-                lifted[pl.ds((v * NZ + k) * PITCH + 8 + at, 8), :] = tile
+                start = (v * NZ + k) * PITCH + 8 + 8 * t
+                lifted[start : start + 8, :] = tile
             for k, tile in enumerate(lift_planes(smooth)[0]):
-                twice[v * 4 + k, pl.ds(at, 8), :] = tile
-            return 0
-
-        lax.fori_loop(0, 8, planes, 0)
+                twice[v * 4 + k, 8 * t : 8 * t + 8, :] = tile
         for bz in range(2):
 
             def row(x):
@@ -286,16 +294,6 @@
                 down[v * 4 + 2] = y[60] + 0.25 * (before + last)
                 down[v * 4 + 3] = y[62] + 0.25 * (last + part)
 
-    for copy in copies[4 * NV :]:
-        copy.wait()
-    for i, out, tile in ((0, up, 18), (1, down, 12)):
-        total = jnp.zeros((7, NL), F32)
-        for l in range(2):
-            flags = masks[l, i].astype(F32).astype(BF16)
-            spread = table[384 + 4 * l : 388 + 4 * l, :]
-            total += lax.dot_general(flags, spread, (((0,), (0,)), ((), ())), preferred_element_type=F32)
-        own_masks[i] = jnp.concatenate([total, jnp.zeros((1, NL), F32)], 0)
-        out[tile] = own_masks[i]
     total = jnp.zeros((80, NL), F32)
     for v in range(NV):
         main, extra = [], jnp.zeros((16, NL), F32)
@@ -373,7 +371,9 @@
     )(lifted)
 
 
-def edge_kernel(parts_in, lifted, north, south, own_masks, table, parts, sides, packed):
+def edge_kernel(parts_in, lifted, north, south, own_masks, table_hbm, parts, sides, packed, table, sem):
+    copy = pltpu.make_async_copy(table_hbm, table, sem.at[0])
+    copy.start()
     for p in range(4 * NV * 8):
         parts[p * ROWS + 32 : p * ROWS + 40, :] = jnp.zeros((8, NL), F32)
     for v in range(NV):
@@ -402,16 +402,19 @@
 
     lane = lax.broadcasted_iota(jnp.int32, (8, NL), 1) // 16
 
-    def pack(step, _):
-        for t in range(5):
-            tile = jnp.zeros((8, NL), F32)
-            for z in range(8):
-                x = parts[pl.ds(pl.multiple_of((step * 8 + z) * ROWS + 8 * t, 8), 8), :]
-                tile = jnp.where(lane == z, pltpu.roll(x, (8 + 16 * z) % NL, 1), tile)
-            packed[pl.ds(pl.multiple_of(step * ROWS + 8 * t, 8), 8), :] = tile
+    def pack(v, _):
+        for n in range(4):
+            for t in range(5):
+                tile = jnp.zeros((8, NL), F32)
+                for z in range(8):
+                    start = (n * 24 + v * 8 + z) * ROWS + 8 * t
+                    x = parts[pl.ds(pl.multiple_of(start, 8), 8), :]
+                    tile = jnp.where(lane == z, pltpu.roll(x, (8 + 16 * z) % NL, 1), tile)
+                packed[pl.ds(pl.multiple_of(n * 120 + v * ROWS + 8 * t, 8), 8), :] = tile
         return 0
 
-    lax.fori_loop(0, 4 * NV, pack, 0)
+    lax.fori_loop(0, NV, pack, 0)
+    copy.wait()
     terms = [two_terms(packed[n * 120 : (n + 1) * 120, :]) for n in range(4)]
     high, low = [jnp.concatenate(part, 1) for part in zip(*terms)]
     sides[0:120, :] = dot(high, table[...]) + dot(low, table[...])
@@ -427,13 +430,13 @@
     return pl.pallas_call(
         edge_kernel,
         out_shape=[jax.ShapeDtypeStruct(s, F32) for s in shapes],
-        in_specs=[vmem] * 6,
+        in_specs=[vmem] * 5 + [pl.BlockSpec(memory_space=pltpu.HBM)],
         out_specs=[vmem] * 2,
         input_output_aliases={0: 0},
         cost_estimate=cost(20),
-        scratch_shapes=[pltpu.VMEM((480, NL), F32)],
+        scratch_shapes=[pltpu.VMEM((480, NL), F32), pltpu.VMEM((512, NL), BF16), pltpu.SemaphoreType.DMA((1,))],
         compiler_params=pltpu.CompilerParams(vmem_limit_bytes=VMEM_LIMIT),
-    )(parts, lifted, north, south, own_masks, weights()["edge"])
+    )(parts, lifted, north, south, own_masks, in_hbm(jnp.asarray(weights()["edge"])))
 
 
 def join_kernel(*refs):
@@ -461,7 +464,7 @@
     return dot(flags, wide[144:528, :])
 
 
-def beside_terms(west, east, at, count):
+def beside_tiles(west, east, at, count):
     lane = lax.broadcasted_iota(jnp.int32, (count, NL), 1)
     from_west = (lane >= 112) | ((lane < 96) & (lax.rem(lane, 24) >= 16))
     tiles = []
@@ -469,18 +472,24 @@
         rows = slice(v * ROWS + at, v * ROWS + at + count)
         beside = jnp.where(from_west, west[rows, :], east[rows, :])
         tiles += [pltpu.roll(beside, NL - z, 1) if z else beside for z in range(8)]
-    return jnp.concatenate(two_terms(jnp.concatenate(tiles, 0)), 1)
+    return tiles
+
+
+def beside_terms(west, east, at, count):
+    return jnp.concatenate(two_terms(jnp.concatenate(beside_tiles(west, east, at, count), 0)), 1)
 
 
 def own_terms(planes, at, count):
     return jnp.concatenate(two_terms(planes[:, at : at + count, :].reshape(24 * count, NL)), 1)
 
 
-def low_kernel(
-    parts, west, east, own_masks, north_mask, south_mask, wide, narrow, low_back, gain2, low, second, kept2
+def main_kernel(
+    parts, flat, west, east, own_masks, north_mask, south_mask, wide, narrow,
+    kept,
+    gain2, low, second, kept2, low_back, gain, sides_wide, turned,
 ):
-    smooth_own, smooth_beside = narrow.at[256:512], narrow.at[512:768]
-    forward2, inverse2 = narrow.at[1024:1152], narrow.at[1152:1280]
+    inverse, smooth_own, smooth_beside = narrow.at[0:256], narrow.at[256:512], narrow.at[512:768]
+    back, forward2, inverse2 = narrow.at[768:1024], narrow.at[1024:1152], narrow.at[1152:1280]
     lanes = mask_lanes(west, east, own_masks, north_mask, south_mask, wide)
     lane64 = lax.broadcasted_iota(jnp.int32, (1, NL), 1) < 64
     forward2_f = forward2[...].astype(F32)
@@ -548,17 +557,11 @@
             for parity in range(2 if t < 2 else 1):
                 planes = unlift_planes([pairs[0, z][parity] for z in range(4)], [pairs[1, z][parity] for z in range(4)])
                 for z in range(8):
-                    low_back[v * 8 + z, pl.ds(16 * t + parity, 8, stride=2), :] = planes[z]
+                    low_back[pl.ds((v * 8 + z) * 48 + 16 * t + parity, 8, stride=2), :] = planes[z]
         return 0
 
     lax.fori_loop(0, NV, back_two, 0)
 
-
-def high_kernel(
-    parts, west, east, own_masks, north_mask, south_mask, wide, narrow, low_back, kept, gain, sides_wide
-):
-    inverse, back = narrow.at[0:256], narrow.at[768:1024]
-    lanes = mask_lanes(west, east, own_masks, north_mask, south_mask, wide)
     forward_f = wide[0:144, :].astype(F32)
     for ib in range(4):
         sides_wide[ib] = jnp.zeros((NL, 4 * NL), F32)
@@ -579,25 +582,45 @@
     for ib in range(4):
         side = sides_wide[ib].astype(BF16)
         gain_sides.append(jnp.concatenate([side, side], 0))
-    for ib in range(3):
-        at, count = 16 * ib, 16 if ib < 2 else 8
-        terms = beside_terms(west, east, at, count)
-        for place, first in (((8 + at, ib + 1),) if ib < 2 else ((40, 3), (0, 0))):
-            product = dot(terms, gain_sides[first])
-            for n in range(4):
-                kept[n, :, place : place + count, :] = product[:, n * NL : (n + 1) * NL].reshape(24, count, NL)
+    def put(n, p, at, rows):
+        start = pl.multiple_of((n * 24 + p) * 48 + 8 + at, 8)
+        kept[pl.ds(start, rows.shape[0]), :] = rows
+
+    def row_of(ref, first, pitch):
+        return ref[pl.ds(first, 24, stride=pitch), :]
+
+    for ib in range(2):
+        product = dot(beside_terms(west, east, 16 * ib, 16), gain_sides[ib + 1])
+        for n in range(4):
+            for p in range(24):
+                put(n, p, 16 * ib, product[16 * p : 16 * p + 16, n * NL : (n + 1) * NL])
 
     def keep(n, _):
-        for ib in range(3):
-            at, count = 16 * ib, 16 if ib < 2 else 8
-            terms = own_terms(parts.at[n], at, count)
-            for place, first in (((8 + at, ib + 1),) if ib < 2 else ((40, 3), (0, 0))):
-                kept[n, :, place : place + count, :] += dot(terms, gain[first, n]).reshape(24, count, NL)
+        for ib in range(2):
+            product = dot(own_terms(parts.at[n], 16 * ib, 16), gain[ib + 1, n])
+            for p in range(24):
+                start = pl.ds(pl.multiple_of((n * 24 + p) * 48 + 8 + 16 * ib, 8), 16)
+                kept[start, :] += product[16 * p : 16 * p + 16]
         return 0
 
     lax.fori_loop(0, 4, keep, 0)
-    for at, count in ((0, 16), (16, 16), (32, 8)):
-        kept[0, :, 8 + at : 8 + at + count, :] += dot(own_terms(low_back, at, count), back[...]).reshape(24, count, NL)
+    for ib in range(2):
+        rows = jnp.concatenate([low_back[48 * p + 16 * ib : 48 * p + 16 * ib + 16, :] for p in range(24)], 0)
+        product = dot(jnp.concatenate(two_terms(rows), 1), back[...])
+        for p in range(24):
+            start = 48 * p + 8 + 16 * ib
+            kept[start : start + 16, :] += product[16 * p : 16 * p + 16]
+    tiles = beside_tiles(west, east, 32, 8)
+    for p in range(24):
+        turned[8 * p : 8 * p + 8, :] = tiles[p]
+    for first, ib, place, row in ((0, 3, 40, 32), (7, 0, 7, 39)):
+        beside = dot(jnp.concatenate(two_terms(row_of(turned, first, 8)), 1), gain_sides[ib])
+        for n in range(4) if ib else (1, 3):
+            own = jnp.concatenate(two_terms(row_of(flat, n * 24 * ROWS + row, ROWS)), 1)
+            total = beside[:, n * NL : (n + 1) * NL] + dot(own, gain[ib, n])
+            if n == 0:
+                total += dot(jnp.concatenate(two_terms(row_of(low_back, row, 48)), 1), back[...])
+            kept[pl.ds(n * 24 * 48 + place, 24, stride=48), :] = total
 
 
 def cells_kernel(kept, out, cells, sems):
@@ -618,59 +641,50 @@
                 cells[v, z, pl.ds(16 * t + parity, 8, stride=2), :] = planes[z]
         return 0
 
-    def one(v, _):
-        lax.fori_loop(v * 4, v * 4 + 4, back_one, 0)
-        pltpu.make_async_copy(cells.at[v], out.at[v], sems.at[v]).start()
+    def copy(step):
+        v, rows = step // 4, pl.ds(pl.multiple_of(16 * (step % 4), 16), 16)
+        return pltpu.make_async_copy(cells.at[v, :, rows], out.at[v, :, rows], sems.at[step])
+
+    def one(step, _):
+        back_one(step, 0)
+        copy(step).start()
         return 0
 
-    lax.fori_loop(0, NV, one, 0)
-    for v in range(NV):
-        pltpu.make_async_copy(cells.at[v], out.at[v], sems.at[v]).wait()
+    lax.fori_loop(0, NV * 4, one, 0)
+    for step in range(NV * 4):
+        copy(step).wait()
 
 
 def main_specs():
     vmem = pl.BlockSpec(memory_space=pltpu.VMEM)
     return [
-        vmem, vmem, vmem, vmem,
+        vmem, vmem, vmem, vmem, vmem,
         pl.BlockSpec((1, 8, NL), lambda i: (12, 0, 0)), pl.BlockSpec((1, 8, NL), lambda i: (18, 0, 0)),
         vmem, vmem,
     ]
 
 
-def low_step(*operands):
+def main_step(flat, *operands):
     w = weights()
     return pl.pallas_call(
-        low_kernel,
+        main_kernel,
         grid=(1,),
-        out_shape=jax.ShapeDtypeStruct((NV * 8, 48, NL), F32),
+        out_shape=jax.ShapeDtypeStruct((4 * NV * 8 * 48, NL), F32),
         in_specs=main_specs(),
-        out_specs=pl.BlockSpec((NV * 8, 48, NL), lambda i: (0, 0, 0)),
+        out_specs=pl.BlockSpec((4 * NV * 8 * 48, NL), lambda i: (0, 0)),
         scratch_shapes=[
             pltpu.VMEM((4, 4, 256, NL), BF16),
             pltpu.VMEM((NV * 8, 64, NL), F32),
             pltpu.VMEM((4, 3, NV * 32, NL), F32),
             pltpu.VMEM((4, NV * 4, 40, NL), F32),
-        ],
-        cost_estimate=cost(4),
-        compiler_params=pltpu.CompilerParams(vmem_limit_bytes=VMEM_LIMIT),
-    )(*operands, w["wide"], w["narrow"])
-
-
-def high_step(low_back, *operands):
-    w = weights()
-    return pl.pallas_call(
-        high_kernel,
-        grid=(1,),
-        out_shape=jax.ShapeDtypeStruct((4, NV * 8, 48, NL), F32),
-        in_specs=main_specs() + [pl.BlockSpec((NV * 8, 48, NL), lambda i: (0, 0, 0))],
-        out_specs=pl.BlockSpec((4, NV * 8, 48, NL), lambda i: (0, 0, 0, 0)),
-        scratch_shapes=[
+            pltpu.VMEM((NV * 8 * 48, NL), F32),
             pltpu.VMEM((4, 4, 256, NL), BF16),
             pltpu.VMEM((4, NL, 4 * NL), F32),
+            pltpu.VMEM((NV * 64, NL), F32),
         ],
-        cost_estimate=cost(4),
+        cost_estimate=cost(8),
         compiler_params=pltpu.CompilerParams(vmem_limit_bytes=VMEM_LIMIT),
-    )(*operands, w["wide"], w["narrow"], low_back)
+    )(flat.reshape(4, NV * 8, ROWS, NL), flat, *operands, w["wide"], w["narrow"])
 
 
 def cells_step(kept):
@@ -680,7 +694,7 @@
         out_shape=jax.ShapeDtypeStruct(shape, F32),
         in_specs=[pl.BlockSpec(memory_space=pltpu.VMEM)],
         out_specs=pl.BlockSpec(memory_space=pltpu.HBM),
-        scratch_shapes=[pltpu.VMEM(shape, F32), pltpu.SemaphoreType.DMA((NV,))],
+        scratch_shapes=[pltpu.VMEM(shape, F32), pltpu.SemaphoreType.DMA((NV * 4,))],
         cost_estimate=cost(4),
         compiler_params=pltpu.CompilerParams(vmem_limit_bytes=VMEM_LIMIT),
     )(kept)
@@ -691,11 +705,16 @@
     me, me_y = lax.axis_index("gx"), lax.axis_index("gy")
     row = lax.broadcasted_iota(jnp.int32, (8, NL), 0)
     piece = lax.broadcasted_iota(jnp.int32, (8, NL), 1) // 21
+    turns = []
+    for j in range(count_z):
+        place = lax.rem(2 * (lax.shift_right_logical(me_y, 1) ^ j) + lax.rem(me_y, 2), 4)
+        turns.append(lax.rem(32 * place + NL - 1, NL))
     for r in range(count_x):
         at = pl.multiple_of(16 * (me ^ r), 16)
         for j in range(count_z):
             for z in range(4):
-                out[j, z, pl.ds(at, 16), :] = shares[r][64 * j + 16 * z : 64 * j + 16 * z + 16, :]
+                start = 64 * j + 16 * z
+                out[j, z, pl.ds(at, 16), :] = pltpu.roll(shares[r][start : start + 16, :], turns[j], 1)
     for r in range(count_x):
         i = me ^ r
         below = pl.multiple_of(16 * lax.rem(i + 1, count_x), 16)
@@ -709,18 +728,12 @@
                 extra = tiles[5 + p // 2]
                 extra = extra if p % 2 else pltpu.roll(extra, 4, 0)
                 high = jnp.where(piece == p, pltpu.roll(extra, back, 1), high)
+            low, high = pltpu.roll(low, turns[j], 1), pltpu.roll(high, turns[j], 1)
             for z in range(4):
                 first = pltpu.roll(low, 8 - 2 * z, 0) if z else low
                 last = pltpu.roll(high, z, 0) if z else high
                 out[j, z, pl.ds(below, 8), :] += jnp.where(row < 2, first, 0.0)
                 out[j, z, pl.ds(above, 8), :] += jnp.where(row == 7, last, 0.0)
-    for j in range(count_z):
-        place = lax.rem(2 * (lax.shift_right_logical(me_y, 1) ^ j) + lax.rem(me_y, 2), 4)
-        turn = lax.rem(32 * place + NL - 1, NL)
-        for z in range(4):
-            for t in range(2 * count_x):
-                rows = slice(8 * t, 8 * t + 8)
-                out[j, z, rows, :] = pltpu.roll(out[j, z, rows, :], turn, 1)
 
 
 def rows_step(pieces, count_z, after):
@@ -807,11 +820,10 @@
     east = shifted(sides, "gy", -1)
     joined = join_step(shares, sides)
     pieces = [joined] + [swapped(joined, "gx", r) for r in range(1, count_x)]
-    operands = (parts.reshape(4, NV * 8, ROWS, NL), west, east, own_masks, north, south)
-    kept = high_step(low_step(*operands), *operands)
+    kept = main_step(parts, west, east, own_masks, north, south)
     own = rows_step(pieces, count_y // 2, kept)
     other = swapped(own, "gy", 1)
-    return cells_step(kept), coarse_step(own, other, count_x, count_y)
+    return cells_step(kept.reshape(4, NV * 8, 48, NL)), coarse_step(own, other, count_x, count_y)
 
 
 def solution(mesh):

time: 31.1 us -> 30.4 us (0.977)
  Pallas kernels: 11.7 us -> 10.7 us
  waiting for transfers between devices: 2.61 us -> 3.17 us
    ppermute x7, waiting for transfers between devices: 2.29 us -> 2.85 us  [swapped(): lax.ppermute(x, axis, [(i, i ^ distance) for i in range(lax.axis_size(axi...]
    pallas_call x1, Pallas kernels: 1.6 us -> 1.13 us  [edge_step(): pl.pallas_call(edge_kernel, out_shape=[jax.ShapeDtypeStruct(s, F32) for s...]
    pallas_call x2 -> x1, Pallas kernels: 3.96 us -> 3.56 us  [main_step(): pl.pallas_call(main_kernel, grid=(1,), out_shape=jax.ShapeDtypeStruct((4...]
  transfers between devices with their start and end apart: 11 -> 11, of which waited for: 3 -> 5; matrix products, arithmetic and copies ran while one was open for 0% -> 0% of each run, Pallas kernels for 24% -> 21%
where the time goes in v1:
time: 30.4 us; the launch traced here: 30.2 us
  starting transfers between devices  15.6 us (51%)
  Pallas kernels  10.7 us (35%)
  waiting for transfers between devices  3.17 us (10%)
  between operations  0.74 us (2%)
    ppermute x7, starting transfers between devices, swapped(): lax.ppermute(x, axis, [(i, i ^ distance) for i in range(lax.axis_size(axi...  8.03 us
    ppermute x4, starting transfers between devices, shifted(): lax.ppermute(x, axis, [(i, (i + step) % count) for i in range(count)])  7.54 us
    pallas_call x1, Pallas kernels, main_step(): pl.pallas_call(main_kernel, grid=(1,), out_shape=jax.ShapeDtypeStruct((4...  3.56 us
    ppermute x7, waiting for transfers between devices, swapped(): lax.ppermute(x, axis, [(i, i ^ distance) for i in range(lax.axis_size(axi...  2.85 us
    pallas_call x1, Pallas kernels, first_step(): pl.pallas_call(first_kernel, out_shape=[jax.ShapeDtypeStruct(s, F32) for...  2.26 us
    pallas_call x1, Pallas kernels, coarse_step(): pl.pallas_call(functools.partial(coarse_kernel, count_x, count_y), out_sh...  1.37 us
    pallas_call x1, Pallas kernels, cells_step(): pl.pallas_call(cells_kernel, out_shape=jax.ShapeDtypeStruct(shape, F32),...  1.37 us
    pallas_call x1, Pallas kernels, edge_step(): pl.pallas_call(edge_kernel, out_shape=[jax.ShapeDtypeStruct(s, F32) for s...  1.13 us
  transfers between devices with their start and end apart: 11, of which 5 were waited for; matrix products, arithmetic and copies ran while one was open for 0% of the time, Pallas kernels for 21%

profile of v1, /device:TPU:0, one launch (start us, length us, event | category | flops | bytes accessed | tf_op | source)
XLA Modules:
  0.0 30.2 jit_solution(17940875617289103544)
XLA Ops:
  0.6 2.3 %shard_map.77 = (f32[3840,128]{1,0:T(8,128)S(1)}, f32[19,8,128]{2,1,0:T(8,128)S(1)}, f32[13,8,128]{2,1,0:T(8,128)S(1)}, f32[2,8,128]{2,1,0:T(8,128)S(1)}, f32[64,128]{1,0:T(8,128)S(1)}) custom-call(f32[3,16,64,128]{3,2,1,0:T(8,128)} %field.1, s32[2,2,4,7]{3,2,1,0:T(4,128)} %bitcast.5, bf16[400,128]{1,0:T(8,128)(2,1)} %constant.8.clone.table_hbm), custom_call_target="tpu_custom_call" | custom-call | tf_op jit(solution)/shard_map/pallas_call | solution.py:329
  2.9 3.9 %collective-permute-start.1 = (f32[19,8,128]{2,1,0:T(8,128)S(1)}, f32[19,8,128]{2,1,0:T(8,128)S(1)}, u32[]{:S(2)}, u32[]{:S(2)}) collective-permute-start(f32[19,8,128]{2,1,0:T(8,128)S(1)} %get-tuple-element.11), channel_id=1, source_target_pairs={{0,24},{8,0},{16,8},{24,16},{1,25},{9,1},{17,9},{25,17},{2,26},{10... | collective-permute-start | bytes 233480 | tf_op jit(solution)/shard_map/ppermute | solution.py:805
  6.8 1.6 %collective-permute-start.4 = (f32[64,128]{1,0:T(8,128)S(1)}, f32[64,128]{1,0:T(8,128)S(1)}, u32[]{:S(2)}, u32[]{:S(2)}) collective-permute-start(f32[64,128]{1,0:T(8,128)S(1)} %get-tuple-element.15.refs_0_), channel_id=1, source_target_pairs={{0,2},{1,3},{2,0},{3,1},{4,6},{5,7},{6,4},{7,5},{8,10},{9,11},{10,... | collective-permute-start | bytes 98312 | tf_op jit(solution)/shard_map/ppermute | solution.py:809
  8.4 2.6 %collective-permute-start.5 = (f32[64,128]{1,0:T(8,128)S(1)}, f32[64,128]{1,0:T(8,128)S(1)}, u32[]{:S(2)}, u32[]{:S(2)}) collective-permute-start(f32[64,128]{1,0:T(8,128)S(1)} %get-tuple-element.15.refs_0_), channel_id=1, source_target_pairs={{0,4},{1,5},{2,6},{3,7},{4,0},{5,1},{6,2},{7,3},{8,12},{9,13},{10,... | collective-permute-start | bytes 98312 | tf_op jit(solution)/shard_map/ppermute | solution.py:809
  11.0 0.2 collective-permute-start.6
  11.2 0.3 %shard_map.78.parts_in = f32[3840,128]{1,0:T(8,128)S(1)} custom-call(f32[3840,128]{1,0:T(8,128)S(1)} %get-tuple-element.9.lifted), custom_call_target="tpu_custom_call" | custom-call | tf_op jit(solution)/shard_map/pallas_call | solution.py:365
  11.6 0.3 %collective-permute-done.north.north_mask = f32[13,8,128]{2,1,0:T(8,128)S(1)} collective-permute-done((f32[13,8,128]{2,1,0:T(8,128)S(1)}, f32[13,8,128]{2,1,0:T(8,128)S(1)}, u32[]{:S(2)}, u32[]{:S(2)}) %collective-permute-start) | collective-permute-done | bytes 53280 | tf_op jit(solution)/shard_map/ppermute | solution.py:805
  11.9 1.1 %shard_map.79 = (f32[3840,128]{1,0:T(8,128)S(1)}, f32[152,128]{1,0:T(8,128)S(1)}) custom-call(f32[3840,128]{1,0:T(8,128)S(1)} %shard_map.78.parts_in, f32[3840,128]{1,0:T(8,128)S(1)} %get-tuple-element.9.lifted, f32[13,8,128]{2,1,0:T(8,128)S(1)} %collective-permute-done.north.north_mask, ...), custom_call_target="tpu_custom_call", output_to_operand_aliasing={{0}: (0, {})} | custom-call | flops 20000000000 | bytes 8000000 | tf_op jit(solution)/shard_map/pallas_call | solution.py:430
  13.0 0.0 copy-start
  13.0 0.0 copy-start.1
  13.0 0.1 collective-permute-start.2
  13.1 3.5 %collective-permute-start.3 = (f32[152,128]{1,0:T(8,128)S(1)}, f32[152,128]{1,0:T(8,128)S(1)}, u32[]{:S(2)}, u32[]{:S(2)}) collective-permute-start(f32[152,128]{1,0:T(8,128)S(1)} %get-tuple-element.14.refs_4_), channel_id=1, source_target_pairs={{0,7},{1,0},{2,1},{3,2},{4,3},{5,4},{6,5},{7,6},{8,15},{9,8},{10,9... | collective-permute-start | bytes 233480 | tf_op jit(solution)/shard_map/ppermute | solution.py:805
  16.6 0.1 collective-permute-done.6.refs_3_
  16.7 2.0 %collective-permute-start.7 = (f32[256,128]{1,0:T(8,128)S(1)}, f32[256,128]{1,0:T(8,128)S(1)}, u32[]{:S(2)}, u32[]{:S(2)}) collective-permute-start(f32[256,128]{1,0:T(8,128)S(1)} %shard_map.82.refs_0_), channel_id=1, source_target_pairs={{0,8},{8,0},{16,24},{24,16},{1,9},{9,1},{17,25},{25,17},{2,10},{10... | collective-permute-start | bytes 393224 | tf_op jit(solution)/shard_map/ppermute | solution.py:809
  18.8 1.5 %collective-permute-start.8 = (f32[256,128]{1,0:T(8,128)S(1)}, f32[256,128]{1,0:T(8,128)S(1)}, u32[]{:S(2)}, u32[]{:S(2)}) collective-permute-start(f32[256,128]{1,0:T(8,128)S(1)} %shard_map.82.refs_0_), channel_id=1, source_target_pairs={{0,16},{8,24},{16,0},{24,8},{1,17},{9,25},{17,1},{25,9},{2,18},{10... | collective-permute-start | bytes 393224 | tf_op jit(solution)/shard_map/ppermute | solution.py:809
  20.3 0.0 collective-permute-start.9
  20.3 3.6 %shard_map.80.refs_4_ = f32[4608,128]{1,0:T(8,128)S(1)} custom-call(f32[4,24,40,128]{3,2,1,0:T(8,128)S(1)} %bitcast.4, f32[3840,128]{1,0:T(8,128)S(1)} %get-tuple-element.13.flat, f32[152,128]{1,0:T(8,128)S(1)} %collective-permute-done.2.west, f32[152,128]{1,0:T(8,128)S(1)} %collective-permute-done.3.east, f32[2,8,128]{2,1,0:T(8,128)S(1)} %get-tuple-element.12.own_masks, ...), custom_call_target="tpu_custom_call" | custom-call | flops 8000000000 | bytes 8000000 | tf_op jit(solution)/shard_map/pallas_call | solution.py:669
  23.9 0.3 collective-permute-done.8.refs_2_
  24.2 2.0 %collective-permute-done.9.refs_3_ = f32[256,128]{1,0:T(8,128)S(1)} collective-permute-done((f32[256,128]{1,0:T(8,128)S(1)}, f32[256,128]{1,0:T(8,128)S(1)}, u32[]{:S(2)}, u32[]{:S(2)}) %collective-permute-start.9) | collective-permute-done | bytes 131104 | tf_op jit(solution)/shard_map/ppermute | solution.py:809
  26.2 0.7 %shard_map.83.own = f32[4,4,64,128]{3,2,1,0:T(8,128)S(1)} custom-call(f32[256,128]{1,0:T(8,128)S(1)} %shard_map.82.refs_0_, f32[256,128]{1,0:T(8,128)S(1)} %collective-permute-done.7.refs_1_, f32[256,128]{1,0:T(8,128)S(1)} %collective-permute-done.8.refs_2_, f32[256,128]{1,0:T(8,128)S(1)} %collective-permute-done.9.refs_3_, f32[4608,128]{1,0:T(8,128)S(1)} %shard_map.80.refs_4_), custom_call_target="tpu_custom_call" | custom-call | tf_op jit(solution)/shard_map/pallas_call | solution.py:742
  26.8 0.1 collective-permute-start.10
  26.9 1.4 %shard_map.81 = f32[3,16,64,128]{3,2,1,0:T(8,128)} custom-call(f32[4,24,48,128]{3,2,1,0:T(8,128)S(1)} %bitcast.3), custom_call_target="tpu_custom_call" | custom-call | flops 4000000000 | bytes 8000000 | tf_op jit(solution)/shard_map/pallas_call | solution.py:692
  28.3 0.5 %collective-permute-done.10.other = f32[4,4,64,128]{3,2,1,0:T(8,128)S(1)} collective-permute-done((f32[4,4,64,128]{3,2,1,0:T(8,128)S(1)}, f32[4,4,64,128]{3,2,1,0:T(8,128)S(1)}, u32[]{:S(2)}, u32[]{:S(2)}) %collective-permute-start.10) | collective-permute-done | bytes 524320 | tf_op jit(solution)/shard_map/ppermute | solution.py:809
  28.8 1.4 %shard_map.84 = f32[3,4,64,256]{3,2,1,0:T(8,128)} custom-call(f32[4,4,64,128]{3,2,1,0:T(8,128)S(1)} %shard_map.83.own, f32[4,4,64,128]{3,2,1,0:T(8,128)S(1)} %collective-permute-done.10.other), custom_call_target="tpu_custom_call" | custom-call | tf_op jit(solution)/shard_map/pallas_call | solution.py:793
  (10 shorter events, 0.0 us)
Async XLA Ops:
  2.9 9.0 %collective-permute-start.1 = (f32[19,8,128]{2,1,0:T(8,128)S(1)}, f32[19,8,128]{2,1,0:T(8,128)S(1)}, u32[]{:S(2)}, u32[]{:S(2)}) collective-permute-start(f32[19,8,128]{2,1,0:T(8,128)S(1)} %get-tuple-element.11), channel_id=1, source_target_pairs={{0,24},{8,0},{16,8},{24,16},{1,25},{9,1},{17,9},{25,17},{2,26},{10... | collective-permute-start | bytes 233480 | tf_op jit(solution)/shard_map/ppermute | solution.py:805
  6.8 5.0 %collective-permute-start = (f32[13,8,128]{2,1,0:T(8,128)S(1)}, f32[13,8,128]{2,1,0:T(8,128)S(1)}, u32[]{:S(2)}, u32[]{:S(2)}) collective-permute-start(f32[13,8,128]{2,1,0:T(8,128)S(1)} %get-tuple-element.10), channel_id=1, source_target_pairs={{0,8},{8,16},{16,24},{24,0},{1,9},{9,17},{17,25},{25,1},{2,10},{10... | collective-permute-start | bytes 159752 | tf_op jit(solution)/shard_map/ppermute | solution.py:805
  6.8 9.8 %collective-permute-start.4 = (f32[64,128]{1,0:T(8,128)S(1)}, f32[64,128]{1,0:T(8,128)S(1)}, u32[]{:S(2)}, u32[]{:S(2)}) collective-permute-start(f32[64,128]{1,0:T(8,128)S(1)} %get-tuple-element.15.refs_0_), channel_id=1, source_target_pairs={{0,2},{1,3},{2,0},{3,1},{4,6},{5,7},{6,4},{7,5},{8,10},{9,11},{10,... | collective-permute-start | bytes 98312 | tf_op jit(solution)/shard_map/ppermute | solution.py:809
  8.4 8.2 %collective-permute-start.5 = (f32[64,128]{1,0:T(8,128)S(1)}, f32[64,128]{1,0:T(8,128)S(1)}, u32[]{:S(2)}, u32[]{:S(2)}) collective-permute-start(f32[64,128]{1,0:T(8,128)S(1)} %get-tuple-element.15.refs_0_), channel_id=1, source_target_pairs={{0,4},{1,5},{2,6},{3,7},{4,0},{5,1},{6,2},{7,3},{8,12},{9,13},{10,... | collective-permute-start | bytes 98312 | tf_op jit(solution)/shard_map/ppermute | solution.py:809
  11.0 5.7 %collective-permute-start.6 = (f32[64,128]{1,0:T(8,128)S(1)}, f32[64,128]{1,0:T(8,128)S(1)}, u32[]{:S(2)}, u32[]{:S(2)}) collective-permute-start(f32[64,128]{1,0:T(8,128)S(1)} %get-tuple-element.15.refs_0_), channel_id=1, source_target_pairs={{0,6},{1,7},{2,4},{3,5},{4,2},{5,3},{6,0},{7,1},{8,14},{9,15},{10,... | collective-permute-start | bytes 98312 | tf_op jit(solution)/shard_map/ppermute | solution.py:809
  13.0 7.3 %copy-start = (bf16[1280,128]{1,0:T(8,128)(2,1)S(1)}, bf16[1280,128]{1,0:T(8,128)(2,1)}, u32[]{:S(2)}) copy-start(bf16[1280,128]{1,0:T(8,128)(2,1)} %constant.11.clone.narrow) | copy-start | bytes 983044
  13.0 7.3 %copy-start.1 = (bf16[528,256]{1,0:T(8,128)(2,1)S(1)}, bf16[528,256]{1,0:T(8,128)(2,1)}, u32[]{:S(2)}) copy-start(bf16[528,256]{1,0:T(8,128)(2,1)} %constant.10.clone.wide) | copy-start | bytes 811012
  13.0 7.3 %collective-permute-start.2 = (f32[152,128]{1,0:T(8,128)S(1)}, f32[152,128]{1,0:T(8,128)S(1)}, u32[]{:S(2)}, u32[]{:S(2)}) collective-permute-start(f32[152,128]{1,0:T(8,128)S(1)} %get-tuple-element.14.refs_4_), channel_id=1, source_target_pairs={{0,1},{1,2},{2,3},{3,4},{4,5},{5,6},{6,7},{7,0},{8,9},{9,10},{10,1... | collective-permute-start | bytes 233480 | tf_op jit(solution)/shard_map/ppermute | solution.py:805
  13.1 7.2 %collective-permute-start.3 = (f32[152,128]{1,0:T(8,128)S(1)}, f32[152,128]{1,0:T(8,128)S(1)}, u32[]{:S(2)}, u32[]{:S(2)}) collective-permute-start(f32[152,128]{1,0:T(8,128)S(1)} %get-tuple-element.14.refs_4_), channel_id=1, source_target_pairs={{0,7},{1,0},{2,1},{3,2},{4,3},{5,4},{6,5},{7,6},{8,15},{9,8},{10,9... | collective-permute-start | bytes 233480 | tf_op jit(solution)/shard_map/ppermute | solution.py:805
  16.7 7.2 %collective-permute-start.7 = (f32[256,128]{1,0:T(8,128)S(1)}, f32[256,128]{1,0:T(8,128)S(1)}, u32[]{:S(2)}, u32[]{:S(2)}) collective-permute-start(f32[256,128]{1,0:T(8,128)S(1)} %shard_map.82.refs_0_), channel_id=1, source_target_pairs={{0,8},{8,0},{16,24},{24,16},{1,9},{9,1},{17,25},{25,17},{2,10},{10... | collective-permute-start | bytes 393224 | tf_op jit(solution)/shard_map/ppermute | solution.py:809
  18.8 5.4 %collective-permute-start.8 = (f32[256,128]{1,0:T(8,128)S(1)}, f32[256,128]{1,0:T(8,128)S(1)}, u32[]{:S(2)}, u32[]{:S(2)}) collective-permute-start(f32[256,128]{1,0:T(8,128)S(1)} %shard_map.82.refs_0_), channel_id=1, source_target_pairs={{0,16},{8,24},{16,0},{24,8},{1,17},{9,25},{17,1},{25,9},{2,18},{10... | collective-permute-start | bytes 393224 | tf_op jit(solution)/shard_map/ppermute | solution.py:809
  20.3 5.9 %collective-permute-start.9 = (f32[256,128]{1,0:T(8,128)S(1)}, f32[256,128]{1,0:T(8,128)S(1)}, u32[]{:S(2)}, u32[]{:S(2)}) collective-permute-start(f32[256,128]{1,0:T(8,128)S(1)} %shard_map.82.refs_0_), channel_id=1, source_target_pairs={{0,24},{8,16},{16,8},{24,0},{1,25},{9,17},{17,9},{25,1},{2,26},{10... | collective-permute-start | bytes 393224 | tf_op jit(solution)/shard_map/ppermute | solution.py:809
  26.8 2.0 %collective-permute-start.10 = (f32[4,4,64,128]{3,2,1,0:T(8,128)S(1)}, f32[4,4,64,128]{3,2,1,0:T(8,128)S(1)}, u32[]{:S(2)}, u32[]{:S(2)}) collective-permute-start(f32[4,4,64,128]{3,2,1,0:T(8,128)S(1)} %shard_map.83.own), channel_id=1, source_target_pairs={{0,1},{1,0},{2,3},{3,2},{4,5},{5,4},{6,7},{7,6},{8,9},{9,8},{10,11... | collective-permute-start | bytes 1572872 | tf_op jit(solution)/shard_map/ppermute | solution.py:809

commit v2 on v1

--- a/solution.py
+++ b/solution.py
@@ -234,6 +234,10 @@
 PITCH = 80
 
 
+def lanes_turn(j):
+    return lax.rem(32 * lax.rem(j, 4) + NL - 1, NL)
+
+
 def first_kernel(
     field, masks_hbm, table_hbm, lifted, up, down, own_masks, share, cells, twice, masks, table, sems
 ):
@@ -262,6 +266,7 @@
         own_masks[i] = jnp.concatenate([total, jnp.zeros((1, NL), F32)], 0)
         out[tile] = own_masks[i]
 
+    total = jnp.zeros((80, NL), F32)
     for v in range(NV):
         for t in range(8):
             if t % 2 == 0:
@@ -293,9 +298,6 @@
                 last = y[61] - 0.5 * (y[60] + y[62])
                 down[v * 4 + 2] = y[60] + 0.25 * (before + last)
                 down[v * 4 + 3] = y[62] + 0.25 * (last + part)
-
-    total = jnp.zeros((80, NL), F32)
-    for v in range(NV):
         main, extra = [], jnp.zeros((16, NL), F32)
         for z in range(4):
             terms = jnp.concatenate(two_terms(twice[v * 4 + z]), 0)
@@ -305,6 +307,8 @@
         terms = jnp.concatenate(two_terms(jnp.concatenate(main + [extra], 0)), 1)
         part = dot(terms, table[0:256, :])
         total += pltpu.roll(part, 35 * v, 1) if v else part
+
+    turn = lanes_turn(lax.axis_index("gy"))
     lane = lax.broadcasted_iota(jnp.int32, (8, NL), 1)
     spare = (lane >= 105) & (lane < 126)
     upper = lax.broadcasted_iota(jnp.int32, (8, NL), 0) < 4
@@ -316,7 +320,8 @@
         else:
             extra = pltpu.roll(pieces[2 * g - 10], 4, 0)
             extra = jnp.where(upper, extra, pieces[2 * g - 9] if g < 7 else 0.0)
-        share[8 * g : 8 * g + 8, :] = jnp.where(spare, extra, total[8 * g : 8 * g + 8])
+        tile = jnp.where(spare, extra, total[8 * g : 8 * g + 8])
+        share[8 * g : 8 * g + 8, :] = pltpu.roll(tile, turn, 1)
 
 
 def in_hbm(x):
@@ -457,26 +462,31 @@
     )(*shares, after)
 
 
-def mask_lanes(west, east, own_masks, north_mask, south_mask, wide):
-    masks = [jnp.concatenate([ref[120 + 8 * i : 128 + 8 * i, :] for i in range(4)], 0) for ref in (east, west)]
+def mask_lanes(near, far, own_masks, north_mask, south_mask, wide):
+    near_masks, far_masks = [
+        jnp.concatenate([ref[120 + 8 * i : 128 + 8 * i, :] for i in range(4)], 0) for ref in (near, far)
+    ]
+    is_even = lax.rem(lax.axis_index("gy"), 2) == 0
+    masks = [jnp.where(is_even, near_masks, far_masks), jnp.where(is_even, far_masks, near_masks)]
     own = jnp.concatenate([north_mask[0], own_masks[0], own_masks[1], south_mask[0]], 0)
     flags = jnp.concatenate([own] + masks, 1).astype(BF16)
     return dot(flags, wide[144:528, :])
 
 
-def beside_tiles(west, east, at, count):
+def beside_tiles(near, far, at, count):
     lane = lax.broadcasted_iota(jnp.int32, (count, NL), 1)
-    from_west = (lane >= 112) | ((lane < 96) & (lax.rem(lane, 24) >= 16))
+    from_west = ((lane >= 112) | ((lane < 96) & (lax.rem(lane, 24) >= 16))).astype(jnp.int32)
+    from_near = from_west == lax.rem(lax.axis_index("gy"), 2)
     tiles = []
     for v in range(NV):
         rows = slice(v * ROWS + at, v * ROWS + at + count)
-        beside = jnp.where(from_west, west[rows, :], east[rows, :])
+        beside = jnp.where(from_near, near[rows, :], far[rows, :])
         tiles += [pltpu.roll(beside, NL - z, 1) if z else beside for z in range(8)]
     return tiles
 
 
-def beside_terms(west, east, at, count):
-    return jnp.concatenate(two_terms(jnp.concatenate(beside_tiles(west, east, at, count), 0)), 1)
+def beside_terms(near, far, at, count):
+    return jnp.concatenate(two_terms(jnp.concatenate(beside_tiles(near, far, at, count), 0)), 1)
 
 
 def own_terms(planes, at, count):
@@ -484,13 +494,13 @@
 
 
 def main_kernel(
-    parts, flat, west, east, own_masks, north_mask, south_mask, wide, narrow,
+    parts, flat, near, far, own_masks, north_mask, south_mask, wide, narrow,
     kept,
     gain2, low, second, kept2, low_back, gain, sides_wide, turned,
 ):
     inverse, smooth_own, smooth_beside = narrow.at[0:256], narrow.at[256:512], narrow.at[512:768]
     back, forward2, inverse2 = narrow.at[768:1024], narrow.at[1024:1152], narrow.at[1152:1280]
-    lanes = mask_lanes(west, east, own_masks, north_mask, south_mask, wide)
+    lanes = mask_lanes(near, far, own_masks, north_mask, south_mask, wide)
     lane64 = lax.broadcasted_iota(jnp.int32, (1, NL), 1) < 64
     forward2_f = forward2[...].astype(F32)
     for ib in range(4):
@@ -504,7 +514,7 @@
 
     for at, count in ((0, 16), (16, 16), (32, 8)):
         part = dot(own_terms(parts.at[0], at, count), smooth_own[...])
-        part += dot(beside_terms(west, east, at, count), smooth_beside[...])
+        part += dot(beside_terms(near, far, at, count), smooth_beside[...])
         part = part.reshape(24, count, NL)
         if at < 32:
             low[:, 8 + at : 8 + at + count, :] = part
@@ -590,7 +600,7 @@
         return ref[pl.ds(first, 24, stride=pitch), :]
 
     for ib in range(2):
-        product = dot(beside_terms(west, east, 16 * ib, 16), gain_sides[ib + 1])
+        product = dot(beside_terms(near, far, 16 * ib, 16), gain_sides[ib + 1])
         for n in range(4):
             for p in range(24):
                 put(n, p, 16 * ib, product[16 * p : 16 * p + 16, n * NL : (n + 1) * NL])
@@ -610,7 +620,7 @@
         for p in range(24):
             start = 48 * p + 8 + 16 * ib
             kept[start : start + 16, :] += product[16 * p : 16 * p + 16]
-    tiles = beside_tiles(west, east, 32, 8)
+    tiles = beside_tiles(near, far, 32, 8)
     for p in range(24):
         turned[8 * p : 8 * p + 8, :] = tiles[p]
     for first, ib, place, row in ((0, 3, 40, 32), (7, 0, 7, 39)):
@@ -704,31 +714,29 @@
     shares, out = refs[:count_x], refs[count_x + 1]
     me, me_y = lax.axis_index("gx"), lax.axis_index("gy")
     row = lax.broadcasted_iota(jnp.int32, (8, NL), 0)
-    piece = lax.broadcasted_iota(jnp.int32, (8, NL), 1) // 21
-    turns = []
-    for j in range(count_z):
-        place = lax.rem(2 * (lax.shift_right_logical(me_y, 1) ^ j) + lax.rem(me_y, 2), 4)
-        turns.append(lax.rem(32 * place + NL - 1, NL))
+    lane = lax.broadcasted_iota(jnp.int32, (8, NL), 1)
     for r in range(count_x):
         at = pl.multiple_of(16 * (me ^ r), 16)
         for j in range(count_z):
             for z in range(4):
                 start = 64 * j + 16 * z
-                out[j, z, pl.ds(at, 16), :] = pltpu.roll(shares[r][start : start + 16, :], turns[j], 1)
-    for r in range(count_x):
-        i = me ^ r
-        below = pl.multiple_of(16 * lax.rem(i + 1, count_x), 16)
-        above = pl.multiple_of(16 * lax.rem(i + count_x - 1, count_x) + 8, 8)
-        for j in range(count_z):
+                out[j, z, pl.ds(at, 16), :] = shares[r][start : start + 16, :]
+    for j in range(count_z):
+        turn = lanes_turn(me_y ^ (2 * j))
+        piece = lax.rem(lane + (NL - turn), NL) // 21
+        inside = [piece == p for p in range(5)]
+        for r in range(count_x):
+            i = me ^ r
+            below = pl.multiple_of(16 * lax.rem(i + 1, count_x), 16)
+            above = pl.multiple_of(16 * lax.rem(i + count_x - 1, count_x) + 8, 8)
             tiles = [shares[r][64 * j + 8 * g : 64 * j + 8 * g + 8, :] for g in range(8)]
             low, high = jnp.zeros((8, NL), F32), jnp.zeros((8, NL), F32)
             for p in range(5):
                 back = (21 * p - 105) % NL
-                low = jnp.where(piece == p, pltpu.roll(tiles[p], back, 1), low)
+                low = jnp.where(inside[p], pltpu.roll(tiles[p], back, 1), low)
                 extra = tiles[5 + p // 2]
                 extra = extra if p % 2 else pltpu.roll(extra, 4, 0)
-                high = jnp.where(piece == p, pltpu.roll(extra, back, 1), high)
-            low, high = pltpu.roll(low, turns[j], 1), pltpu.roll(high, turns[j], 1)
+                high = jnp.where(inside[p], pltpu.roll(extra, back, 1), high)
             for z in range(4):
                 first = pltpu.roll(low, 8 - 2 * z, 0) if z else low
                 last = pltpu.roll(high, z, 0) if z else high
@@ -809,6 +817,11 @@
     return lax.ppermute(x, axis, [(i, i ^ distance) for i in range(lax.axis_size(axis))])
 
 
+def crossed(x, axis):
+    count = lax.axis_size(axis)
+    return lax.ppermute(x, axis, [(i, (i + (1 if i % 2 else count - 1)) % count) for i in range(count)])
+
+
 def body(field, masks):
     count_x, count_y = lax.axis_size("gx"), lax.axis_size("gy")
     lifted, up, down, own_masks, share = first_step(field, masks)
@@ -816,11 +829,10 @@
     north = shifted(down, "gx", 1)
     shares = [share] + [swapped(share, "gy", r) for r in range(2, count_y, 2)]
     parts, sides = edge_step(lift_step(lifted), lifted, north, south, own_masks)
-    west = shifted(sides, "gy", 1)
-    east = shifted(sides, "gy", -1)
+    near, far = swapped(sides, "gy", 1), crossed(sides, "gy")
     joined = join_step(shares, sides)
     pieces = [joined] + [swapped(joined, "gx", r) for r in range(1, count_x)]
-    kept = main_step(parts, west, east, own_masks, north, south)
+    kept = main_step(parts, near, far, own_masks, north, south)
     own = rows_step(pieces, count_y // 2, kept)
     other = swapped(own, "gy", 1)
     return cells_step(kept.reshape(4, NV * 8, 48, NL)), coarse_step(own, other, count_x, count_y)

time: 30.4 us -> 30.4 us (level)
    ppermute x0 -> x1, starting transfers between devices: none -> 3.7 us  [crossed(): lax.ppermute(x, axis, [(i, (i + (1 if i % 2 else count - 1)) % count) for...]
    ppermute x4 -> x2, starting transfers between devices: 7.54 us -> 3.95 us  [shifted(): lax.ppermute(x, axis, [(i, (i + step) % count) for i in range(count)])]
    pallas_call x1, Pallas kernels: 2.26 us -> 2.61 us  [first_step(): pl.pallas_call(first_kernel, out_shape=[jax.ShapeDtypeStruct(s, F32) for...]
    pallas_call x1, Pallas kernels: 0.67 us -> 0.32 us  [rows_step(): pl.pallas_call(functools.partial(rows_kernel, count_x, count_z), out_shap...]
    ppermute x7 -> x8, waiting for transfers between devices: 2.85 us -> 2.69 us  [swapped(): lax.ppermute(x, axis, [(i, i ^ distance) for i in range(lax.axis_size(axi...]
    ppermute x7 -> x8, starting transfers between devices: 8.03 us -> 8.08 us  [swapped(): lax.ppermute(x, axis, [(i, i ^ distance) for i in range(lax.axis_size(axi...]
  transfers between devices with their start and end apart: 11 -> 11, of which waited for: 5 -> 4; matrix products, arithmetic and copies ran while one was open for 0% -> 0% of each run, Pallas kernels for 21% -> 21%
where the time goes in v2:
time: 30.4 us; the launch traced here: 30.2 us
  starting transfers between devices  15.7 us (52%)
  Pallas kernels  10.7 us (35%)
  waiting for transfers between devices  3.01 us (10%)
  between operations  0.75 us (2%)
    ppermute x8, starting transfers between devices, swapped(): lax.ppermute(x, axis, [(i, i ^ distance) for i in range(lax.axis_size(axi...  8.08 us
    ppermute x2, starting transfers between devices, shifted(): lax.ppermute(x, axis, [(i, (i + step) % count) for i in range(count)])  3.95 us
    ppermute x1, starting transfers between devices, crossed(): lax.ppermute(x, axis, [(i, (i + (1 if i % 2 else count - 1)) % count) for...  3.7 us
    pallas_call x1, Pallas kernels, main_step(): pl.pallas_call(main_kernel, grid=(1,), out_shape=jax.ShapeDtypeStruct((4...  3.56 us
    ppermute x8, waiting for transfers between devices, swapped(): lax.ppermute(x, axis, [(i, i ^ distance) for i in range(lax.axis_size(axi...  2.69 us
    pallas_call x1, Pallas kernels, first_step(): pl.pallas_call(first_kernel, out_shape=[jax.ShapeDtypeStruct(s, F32) for...  2.61 us
    pallas_call x1, Pallas kernels, coarse_step(): pl.pallas_call(functools.partial(coarse_kernel, count_x, count_y), out_sh...  1.37 us
    pallas_call x1, Pallas kernels, cells_step(): pl.pallas_call(cells_kernel, out_shape=jax.ShapeDtypeStruct(shape, F32),...  1.37 us
  transfers between devices with their start and end apart: 11, of which 4 were waited for; matrix products, arithmetic and copies ran while one was open for 0% of the time, Pallas kernels for 21%

profile of v2, /device:TPU:0, one launch (start us, length us, event | category | flops | bytes accessed | tf_op | source)
XLA Modules:
  0.0 30.2 jit_solution(13840318621294934328)
XLA Ops:
  0.6 2.6 %shard_map.77 = (f32[3840,128]{1,0:T(8,128)S(1)}, f32[19,8,128]{2,1,0:T(8,128)S(1)}, f32[13,8,128]{2,1,0:T(8,128)S(1)}, f32[2,8,128]{2,1,0:T(8,128)S(1)}, f32[64,128]{1,0:T(8,128)S(1)}) custom-call(f32[3,16,64,128]{3,2,1,0:T(8,128)} %field.1, s32[2,2,4,7]{3,2,1,0:T(4,128)} %bitcast.5, bf16[400,128]{1,0:T(8,128)(2,1)} %constant.8.clone.table_hbm), custom_call_target="tpu_custom_call" | custom-call | tf_op jit(solution)/shard_map/pallas_call | solution.py:334
  3.2 3.9 %collective-permute-start.1 = (f32[19,8,128]{2,1,0:T(8,128)S(1)}, f32[19,8,128]{2,1,0:T(8,128)S(1)}, u32[]{:S(2)}, u32[]{:S(2)}) collective-permute-start(f32[19,8,128]{2,1,0:T(8,128)S(1)} %get-tuple-element.11), channel_id=1, source_target_pairs={{0,24},{8,0},{16,8},{24,16},{1,25},{9,1},{17,9},{25,17},{2,26},{10... | collective-permute-start | bytes 233480 | tf_op jit(solution)/shard_map/ppermute | solution.py:813
  7.2 1.6 %collective-permute-start.4 = (f32[64,128]{1,0:T(8,128)S(1)}, f32[64,128]{1,0:T(8,128)S(1)}, u32[]{:S(2)}, u32[]{:S(2)}) collective-permute-start(f32[64,128]{1,0:T(8,128)S(1)} %get-tuple-element.15.refs_0_), channel_id=1, source_target_pairs={{0,2},{1,3},{2,0},{3,1},{4,6},{5,7},{6,4},{7,5},{8,10},{9,11},{10,... | collective-permute-start | bytes 98312 | tf_op jit(solution)/shard_map/ppermute | solution.py:817
  8.8 2.6 %collective-permute-start.5 = (f32[64,128]{1,0:T(8,128)S(1)}, f32[64,128]{1,0:T(8,128)S(1)}, u32[]{:S(2)}, u32[]{:S(2)}) collective-permute-start(f32[64,128]{1,0:T(8,128)S(1)} %get-tuple-element.15.refs_0_), channel_id=1, source_target_pairs={{0,4},{1,5},{2,6},{3,7},{4,0},{5,1},{6,2},{7,3},{8,12},{9,13},{10,... | collective-permute-start | bytes 98312 | tf_op jit(solution)/shard_map/ppermute | solution.py:817
  11.4 0.2 collective-permute-start.6
  11.6 0.3 %shard_map.78.parts_in = f32[3840,128]{1,0:T(8,128)S(1)} custom-call(f32[3840,128]{1,0:T(8,128)S(1)} %get-tuple-element.9.lifted), custom_call_target="tpu_custom_call" | custom-call | tf_op jit(solution)/shard_map/pallas_call | solution.py:370
  11.9 0.3 %collective-permute-done.north.north_mask = f32[13,8,128]{2,1,0:T(8,128)S(1)} collective-permute-done((f32[13,8,128]{2,1,0:T(8,128)S(1)}, f32[13,8,128]{2,1,0:T(8,128)S(1)}, u32[]{:S(2)}, u32[]{:S(2)}) %collective-permute-start) | collective-permute-done | bytes 53280 | tf_op jit(solution)/shard_map/ppermute | solution.py:813
  12.2 0.0 collective-permute-done.1.south.south_mask
  12.2 1.1 %shard_map.79 = (f32[3840,128]{1,0:T(8,128)S(1)}, f32[152,128]{1,0:T(8,128)S(1)}) custom-call(f32[3840,128]{1,0:T(8,128)S(1)} %shard_map.78.parts_in, f32[3840,128]{1,0:T(8,128)S(1)} %get-tuple-element.9.lifted, f32[13,8,128]{2,1,0:T(8,128)S(1)} %collective-permute-done.north.north_mask, ...), custom_call_target="tpu_custom_call", output_to_operand_aliasing={{0}: (0, {})} | custom-call | flops 20000000000 | bytes 8000000 | tf_op jit(solution)/shard_map/pallas_call | solution.py:435
  13.4 0.0 copy-start
  13.4 0.0 copy-start.1
  13.4 0.1 collective-permute-start.2
  13.5 3.7 %collective-permute-start.3 = (f32[152,128]{1,0:T(8,128)S(1)}, f32[152,128]{1,0:T(8,128)S(1)}, u32[]{:S(2)}, u32[]{:S(2)}) collective-permute-start(f32[152,128]{1,0:T(8,128)S(1)} %get-tuple-element.14.refs_4_), channel_id=1, source_target_pairs={{0,7},{1,2},{2,1},{3,4},{4,3},{5,6},{6,5},{7,0},{8,15},{9,10},{10,... | collective-permute-start | bytes 233480 | tf_op jit(solution)/shard_map/ppermute | solution.py:822
  17.2 1.9 %collective-permute-start.7 = (f32[256,128]{1,0:T(8,128)S(1)}, f32[256,128]{1,0:T(8,128)S(1)}, u32[]{:S(2)}, u32[]{:S(2)}) collective-permute-start(f32[256,128]{1,0:T(8,128)S(1)} %shard_map.82.refs_0_), channel_id=1, source_target_pairs={{0,8},{8,0},{16,24},{24,16},{1,9},{9,1},{17,25},{25,17},{2,10},{10... | collective-permute-start | bytes 393224 | tf_op jit(solution)/shard_map/ppermute | solution.py:817
  19.1 1.5 %collective-permute-start.8 = (f32[256,128]{1,0:T(8,128)S(1)}, f32[256,128]{1,0:T(8,128)S(1)}, u32[]{:S(2)}, u32[]{:S(2)}) collective-permute-start(f32[256,128]{1,0:T(8,128)S(1)} %shard_map.82.refs_0_), channel_id=1, source_target_pairs={{0,16},{8,24},{16,0},{24,8},{1,17},{9,25},{17,1},{25,9},{2,18},{10... | collective-permute-start | bytes 393224 | tf_op jit(solution)/shard_map/ppermute | solution.py:817
  20.7 0.1 collective-permute-start.9
  20.8 3.6 %shard_map.80.refs_4_ = f32[4608,128]{1,0:T(8,128)S(1)} custom-call(f32[4,24,40,128]{3,2,1,0:T(8,128)S(1)} %bitcast.4, f32[3840,128]{1,0:T(8,128)S(1)} %get-tuple-element.13.flat, f32[152,128]{1,0:T(8,128)S(1)} %collective-permute-done.2.near, f32[152,128]{1,0:T(8,128)S(1)} %collective-permute-done.3.far, f32[2,8,128]{2,1,0:T(8,128)S(1)} %get-tuple-element.12.own_masks, ...), custom_call_target="tpu_custom_call" | custom-call | flops 8000000000 | bytes 8000000 | tf_op jit(solution)/shard_map/pallas_call | solution.py:679
  24.4 0.1 collective-permute-done.8.refs_2_
  24.5 2.0 %collective-permute-done.9.refs_3_ = f32[256,128]{1,0:T(8,128)S(1)} collective-permute-done((f32[256,128]{1,0:T(8,128)S(1)}, f32[256,128]{1,0:T(8,128)S(1)}, u32[]{:S(2)}, u32[]{:S(2)}) %collective-permute-start.9) | collective-permute-done | bytes 131104 | tf_op jit(solution)/shard_map/ppermute | solution.py:817
  26.5 0.3 %shard_map.83.own = f32[4,4,64,128]{3,2,1,0:T(8,128)S(1)} custom-call(f32[256,128]{1,0:T(8,128)S(1)} %shard_map.82.refs_0_, f32[256,128]{1,0:T(8,128)S(1)} %collective-permute-done.7.refs_1_, f32[256,128]{1,0:T(8,128)S(1)} %collective-permute-done.8.refs_2_, f32[256,128]{1,0:T(8,128)S(1)} %collective-permute-done.9.refs_3_, f32[4608,128]{1,0:T(8,128)S(1)} %shard_map.80.refs_4_), custom_call_target="tpu_custom_call" | custom-call | tf_op jit(solution)/shard_map/pallas_call | solution.py:750
  26.9 0.1 collective-permute-start.10
  26.9 1.4 %shard_map.81 = f32[3,16,64,128]{3,2,1,0:T(8,128)} custom-call(f32[4,24,48,128]{3,2,1,0:T(8,128)S(1)} %bitcast.3), custom_call_target="tpu_custom_call" | custom-call | flops 4000000000 | bytes 8000000 | tf_op jit(solution)/shard_map/pallas_call | solution.py:702
  28.3 0.5 %collective-permute-done.10.other = f32[4,4,64,128]{3,2,1,0:T(8,128)S(1)} collective-permute-done((f32[4,4,64,128]{3,2,1,0:T(8,128)S(1)}, f32[4,4,64,128]{3,2,1,0:T(8,128)S(1)}, u32[]{:S(2)}, u32[]{:S(2)}) %collective-permute-start.10) | collective-permute-done | bytes 524320 | tf_op jit(solution)/shard_map/ppermute | solution.py:817
  28.8 1.4 %shard_map.84 = f32[3,4,64,256]{3,2,1,0:T(8,128)} custom-call(f32[4,4,64,128]{3,2,1,0:T(8,128)S(1)} %shard_map.83.own, f32[4,4,64,128]{3,2,1,0:T(8,128)S(1)} %collective-permute-done.10.other), custom_call_target="tpu_custom_call" | custom-call | tf_op jit(solution)/shard_map/pallas_call | solution.py:801
  (10 shorter events, 0.0 us)
Async XLA Ops:
  3.2 9.0 %collective-permute-start.1 = (f32[19,8,128]{2,1,0:T(8,128)S(1)}, f32[19,8,128]{2,1,0:T(8,128)S(1)}, u32[]{:S(2)}, u32[]{:S(2)}) collective-permute-start(f32[19,8,128]{2,1,0:T(8,128)S(1)} %get-tuple-element.11), channel_id=1, source_target_pairs={{0,24},{8,0},{16,8},{24,16},{1,25},{9,1},{17,9},{25,17},{2,26},{10... | collective-permute-start | bytes 233480 | tf_op jit(solution)/shard_map/ppermute | solution.py:813
  7.2 5.0 %collective-permute-start = (f32[13,8,128]{2,1,0:T(8,128)S(1)}, f32[13,8,128]{2,1,0:T(8,128)S(1)}, u32[]{:S(2)}, u32[]{:S(2)}) collective-permute-start(f32[13,8,128]{2,1,0:T(8,128)S(1)} %get-tuple-element.10), channel_id=1, source_target_pairs={{0,8},{8,16},{16,24},{24,0},{1,9},{9,17},{17,25},{25,1},{2,10},{10... | collective-permute-start | bytes 159752 | tf_op jit(solution)/shard_map/ppermute | solution.py:813
  7.2 10.0 %collective-permute-start.4 = (f32[64,128]{1,0:T(8,128)S(1)}, f32[64,128]{1,0:T(8,128)S(1)}, u32[]{:S(2)}, u32[]{:S(2)}) collective-permute-start(f32[64,128]{1,0:T(8,128)S(1)} %get-tuple-element.15.refs_0_), channel_id=1, source_target_pairs={{0,2},{1,3},{2,0},{3,1},{4,6},{5,7},{6,4},{7,5},{8,10},{9,11},{10,... | collective-permute-start | bytes 98312 | tf_op jit(solution)/shard_map/ppermute | solution.py:817
  8.8 8.4 %collective-permute-start.5 = (f32[64,128]{1,0:T(8,128)S(1)}, f32[64,128]{1,0:T(8,128)S(1)}, u32[]{:S(2)}, u32[]{:S(2)}) collective-permute-start(f32[64,128]{1,0:T(8,128)S(1)} %get-tuple-element.15.refs_0_), channel_id=1, source_target_pairs={{0,4},{1,5},{2,6},{3,7},{4,0},{5,1},{6,2},{7,3},{8,12},{9,13},{10,... | collective-permute-start | bytes 98312 | tf_op jit(solution)/shard_map/ppermute | solution.py:817
  11.4 5.8 %collective-permute-start.6 = (f32[64,128]{1,0:T(8,128)S(1)}, f32[64,128]{1,0:T(8,128)S(1)}, u32[]{:S(2)}, u32[]{:S(2)}) collective-permute-start(f32[64,128]{1,0:T(8,128)S(1)} %get-tuple-element.15.refs_0_), channel_id=1, source_target_pairs={{0,6},{1,7},{2,4},{3,5},{4,2},{5,3},{6,0},{7,1},{8,14},{9,15},{10,... | collective-permute-start | bytes 98312 | tf_op jit(solution)/shard_map/ppermute | solution.py:817
  13.4 7.4 %copy-start = (bf16[1280,128]{1,0:T(8,128)(2,1)S(1)}, bf16[1280,128]{1,0:T(8,128)(2,1)}, u32[]{:S(2)}) copy-start(bf16[1280,128]{1,0:T(8,128)(2,1)} %constant.11.clone.narrow) | copy-start | bytes 983044
  13.4 7.4 %copy-start.1 = (bf16[528,256]{1,0:T(8,128)(2,1)S(1)}, bf16[528,256]{1,0:T(8,128)(2,1)}, u32[]{:S(2)}) copy-start(bf16[528,256]{1,0:T(8,128)(2,1)} %constant.10.clone.wide) | copy-start | bytes 811012
  13.4 7.4 %collective-permute-start.2 = (f32[152,128]{1,0:T(8,128)S(1)}, f32[152,128]{1,0:T(8,128)S(1)}, u32[]{:S(2)}, u32[]{:S(2)}) collective-permute-start(f32[152,128]{1,0:T(8,128)S(1)} %get-tuple-element.14.refs_4_), channel_id=1, source_target_pairs={{0,1},{1,0},{2,3},{3,2},{4,5},{5,4},{6,7},{7,6},{8,9},{9,8},{10,11... | collective-permute-start | bytes 233480 | tf_op jit(solution)/shard_map/ppermute | solution.py:817
  13.5 7.3 %collective-permute-start.3 = (f32[152,128]{1,0:T(8,128)S(1)}, f32[152,128]{1,0:T(8,128)S(1)}, u32[]{:S(2)}, u32[]{:S(2)}) collective-permute-start(f32[152,128]{1,0:T(8,128)S(1)} %get-tuple-element.14.refs_4_), channel_id=1, source_target_pairs={{0,7},{1,2},{2,1},{3,4},{4,3},{5,6},{6,5},{7,0},{8,15},{9,10},{10,... | collective-permute-start | bytes 233480 | tf_op jit(solution)/shard_map/ppermute | solution.py:822
  17.2 7.1 %collective-permute-start.7 = (f32[256,128]{1,0:T(8,128)S(1)}, f32[256,128]{1,0:T(8,128)S(1)}, u32[]{:S(2)}, u32[]{:S(2)}) collective-permute-start(f32[256,128]{1,0:T(8,128)S(1)} %shard_map.82.refs_0_), channel_id=1, source_target_pairs={{0,8},{8,0},{16,24},{24,16},{1,9},{9,1},{17,25},{25,17},{2,10},{10... | collective-permute-start | bytes 393224 | tf_op jit(solution)/shard_map/ppermute | solution.py:817
  19.1 5.4 %collective-permute-start.8 = (f32[256,128]{1,0:T(8,128)S(1)}, f32[256,128]{1,0:T(8,128)S(1)}, u32[]{:S(2)}, u32[]{:S(2)}) collective-permute-start(f32[256,128]{1,0:T(8,128)S(1)} %shard_map.82.refs_0_), channel_id=1, source_target_pairs={{0,16},{8,24},{16,0},{24,8},{1,17},{9,25},{17,1},{25,9},{2,18},{10... | collective-permute-start | bytes 393224 | tf_op jit(solution)/shard_map/ppermute | solution.py:817
  20.7 5.9 %collective-permute-start.9 = (f32[256,128]{1,0:T(8,128)S(1)}, f32[256,128]{1,0:T(8,128)S(1)}, u32[]{:S(2)}, u32[]{:S(2)}) collective-permute-start(f32[256,128]{1,0:T(8,128)S(1)} %shard_map.82.refs_0_), channel_id=1, source_target_pairs={{0,24},{8,16},{16,8},{24,0},{1,25},{9,17},{17,9},{25,1},{2,26},{10... | collective-permute-start | bytes 393224 | tf_op jit(solution)/shard_map/ppermute | solution.py:817
  26.9 2.0 %collective-permute-start.10 = (f32[4,4,64,128]{3,2,1,0:T(8,128)S(1)}, f32[4,4,64,128]{3,2,1,0:T(8,128)S(1)}, u32[]{:S(2)}, u32[]{:S(2)}) collective-permute-start(f32[4,4,64,128]{3,2,1,0:T(8,128)S(1)} %shard_map.83.own), channel_id=1, source_target_pairs={{0,1},{1,0},{2,3},{3,2},{4,5},{5,4},{6,7},{7,6},{8,9},{9,8},{10,11... | collective-permute-start | bytes 1572872 | tf_op jit(solution)/shard_map/ppermute | solution.py:817

commit v3 on v2

--- a/solution.py
+++ b/solution.py
@@ -266,7 +266,6 @@
         own_masks[i] = jnp.concatenate([total, jnp.zeros((1, NL), F32)], 0)
         out[tile] = own_masks[i]
 
-    total = jnp.zeros((80, NL), F32)
     for v in range(NV):
         for t in range(8):
             if t % 2 == 0:
@@ -298,6 +297,9 @@
                 last = y[61] - 0.5 * (y[60] + y[62])
                 down[v * 4 + 2] = y[60] + 0.25 * (before + last)
                 down[v * 4 + 3] = y[62] + 0.25 * (last + part)
+
+    total = jnp.zeros((80, NL), F32)
+    for v in range(NV):
         main, extra = [], jnp.zeros((16, NL), F32)
         for z in range(4):
             terms = jnp.concatenate(two_terms(twice[v * 4 + z]), 0)
@@ -307,7 +309,6 @@
         terms = jnp.concatenate(two_terms(jnp.concatenate(main + [extra], 0)), 1)
         part = dot(terms, table[0:256, :])
         total += pltpu.roll(part, 35 * v, 1) if v else part
-
     turn = lanes_turn(lax.axis_index("gy"))
     lane = lax.broadcasted_iota(jnp.int32, (8, NL), 1)
     spare = (lane >= 105) & (lane < 126)
@@ -445,21 +446,22 @@
 
 
 def join_kernel(*refs):
-    shares, out = refs[:-2], refs[-1]
+    shares, sides, (out, message) = refs[:-3], refs[-3], refs[-2:]
     for n, piece in enumerate(shares):
         out[64 * n : 64 * (n + 1), :] = piece[...]
-
-
-def join_step(shares, after):
+    message[...] = sides[...]
+
+
+def join_step(shares, sides):
     vmem = pl.BlockSpec(memory_space=pltpu.VMEM)
     return pl.pallas_call(
         join_kernel,
-        out_shape=jax.ShapeDtypeStruct((64 * len(shares), NL), F32),
-        in_specs=[vmem] * len(shares) + [pl.BlockSpec(memory_space=pl.ANY)],
-        out_specs=vmem,
+        out_shape=[jax.ShapeDtypeStruct((64 * len(shares), NL), F32), jax.ShapeDtypeStruct(sides.shape, F32)],
+        in_specs=[vmem] * (len(shares) + 1),
+        out_specs=[vmem, vmem],
         cost_estimate=cost(20),
         compiler_params=pltpu.CompilerParams(vmem_limit_bytes=VMEM_LIMIT),
-    )(*shares, after)
+    )(*shares, sides)
 
 
 def mask_lanes(near, far, own_masks, north_mask, south_mask, wide):
@@ -829,8 +831,9 @@
     north = shifted(down, "gx", 1)
     shares = [share] + [swapped(share, "gy", r) for r in range(2, count_y, 2)]
     parts, sides = edge_step(lift_step(lifted), lifted, north, south, own_masks)
-    near, far = swapped(sides, "gy", 1), crossed(sides, "gy")
-    joined = join_step(shares, sides)
+    near = swapped(sides, "gy", 1)
+    joined, message = join_step(shares, sides)
+    far = crossed(message, "gy")
     pieces = [joined] + [swapped(joined, "gx", r) for r in range(1, count_x)]
     kept = main_step(parts, near, far, own_masks, north, south)
     own = rows_step(pieces, count_y // 2, kept)

time: 30.4 us -> 31.3 us (1.030)
  waiting for transfers between devices: 3.01 us -> 7.79 us
  starting transfers between devices: 15.7 us -> 12.1 us
    ppermute x1, starting transfers between devices: 3.7 us -> 0.07 us  [crossed(): lax.ppermute(x, axis, [(i, (i + (1 if i % 2 else count - 1)) % count) for...]
    ppermute x8, waiting for transfers between devices: 2.69 us -> 5.52 us  [swapped(): lax.ppermute(x, axis, [(i, i ^ distance) for i in range(lax.axis_size(axi...]
    ppermute x1, waiting for transfers between devices: 0.01 us -> 1.95 us  [crossed(): lax.ppermute(x, axis, [(i, (i + (1 if i % 2 else count - 1)) % count) for...]
  transfers between devices with their start and end apart: 11 -> 11, of which waited for: 4 -> 6; matrix products, arithmetic and copies ran while one was open for 0% -> 0% of each run, Pallas kernels for 21% -> 21%
where the time goes in v3:
time: 31.3 us; the launch traced here: 31.1 us
  starting transfers between devices  12.1 us (39%)
  Pallas kernels  10.4 us (33%)
  waiting for transfers between devices  7.79 us (25%)
  between operations  0.73 us (2%)
    ppermute x8, starting transfers between devices, swapped(): lax.ppermute(x, axis, [(i, i ^ distance) for i in range(lax.axis_size(axi...  8.1 us
    ppermute x8, waiting for transfers between devices, swapped(): lax.ppermute(x, axis, [(i, i ^ distance) for i in range(lax.axis_size(axi...  5.52 us
    ppermute x2, starting transfers between devices, shifted(): lax.ppermute(x, axis, [(i, (i + step) % count) for i in range(count)])  3.95 us
    pallas_call x1, Pallas kernels, main_step(): pl.pallas_call(main_kernel, grid=(1,), out_shape=jax.ShapeDtypeStruct((4...  3.56 us
    pallas_call x1, Pallas kernels, first_step(): pl.pallas_call(first_kernel, out_shape=[jax.ShapeDtypeStruct(s, F32) for...  2.33 us
    ppermute x1, waiting for transfers between devices, crossed(): lax.ppermute(x, axis, [(i, (i + (1 if i % 2 else count - 1)) % count) for...  1.95 us
    pallas_call x1, Pallas kernels, coarse_step(): pl.pallas_call(functools.partial(coarse_kernel, count_x, count_y), out_sh...  1.37 us
    pallas_call x1, Pallas kernels, cells_step(): pl.pallas_call(cells_kernel, out_shape=jax.ShapeDtypeStruct(shape, F32),...  1.37 us
  transfers between devices with their start and end apart: 11, of which 6 were waited for; matrix products, arithmetic and copies ran while one was open for 0% of the time, Pallas kernels for 21%

profile of v3, /device:TPU:0, one launch (start us, length us, event | category | flops | bytes accessed | tf_op | source)
XLA Modules:
  0.0 31.1 jit_solution(10874581082064365608)
XLA Ops:
  0.6 2.3 %shard_map.77 = (f32[3840,128]{1,0:T(8,128)S(1)}, f32[19,8,128]{2,1,0:T(8,128)S(1)}, f32[13,8,128]{2,1,0:T(8,128)S(1)}, f32[2,8,128]{2,1,0:T(8,128)S(1)}, f32[64,128]{1,0:T(8,128)S(1)}) custom-call(f32[3,16,64,128]{3,2,1,0:T(8,128)} %field.1, s32[2,2,4,7]{3,2,1,0:T(4,128)} %bitcast.5, bf16[400,128]{1,0:T(8,128)(2,1)} %constant.8.clone.table_hbm), custom_call_target="tpu_custom_call" | custom-call | tf_op jit(solution)/shard_map/pallas_call | solution.py:335
  3.0 3.9 %collective-permute-start.1 = (f32[19,8,128]{2,1,0:T(8,128)S(1)}, f32[19,8,128]{2,1,0:T(8,128)S(1)}, u32[]{:S(2)}, u32[]{:S(2)}) collective-permute-start(f32[19,8,128]{2,1,0:T(8,128)S(1)} %get-tuple-element.13), channel_id=1, source_target_pairs={{0,24},{8,0},{16,8},{24,16},{1,25},{9,1},{17,9},{25,17},{2,26},{10... | collective-permute-start | bytes 233480 | tf_op jit(solution)/shard_map/ppermute | solution.py:815
  6.9 0.0 collective-permute-start
  6.9 1.6 %collective-permute-start.3 = (f32[64,128]{1,0:T(8,128)S(1)}, f32[64,128]{1,0:T(8,128)S(1)}, u32[]{:S(2)}, u32[]{:S(2)}) collective-permute-start(f32[64,128]{1,0:T(8,128)S(1)} %get-tuple-element.17.refs_0_), channel_id=1, source_target_pairs={{0,2},{1,3},{2,0},{3,1},{4,6},{5,7},{6,4},{7,5},{8,10},{9,11},{10,... | collective-permute-start | bytes 98312 | tf_op jit(solution)/shard_map/ppermute | solution.py:819
  8.5 2.6 %collective-permute-start.4 = (f32[64,128]{1,0:T(8,128)S(1)}, f32[64,128]{1,0:T(8,128)S(1)}, u32[]{:S(2)}, u32[]{:S(2)}) collective-permute-start(f32[64,128]{1,0:T(8,128)S(1)} %get-tuple-element.17.refs_0_), channel_id=1, source_target_pairs={{0,4},{1,5},{2,6},{3,7},{4,0},{5,1},{6,2},{7,3},{8,12},{9,13},{10,... | collective-permute-start | bytes 98312 | tf_op jit(solution)/shard_map/ppermute | solution.py:819
  11.1 0.2 collective-permute-start.5
  11.3 0.3 %shard_map.78.parts_in = f32[3840,128]{1,0:T(8,128)S(1)} custom-call(f32[3840,128]{1,0:T(8,128)S(1)} %get-tuple-element.11.lifted), custom_call_target="tpu_custom_call" | custom-call | tf_op jit(solution)/shard_map/pallas_call | solution.py:371
  11.6 0.3 %collective-permute-done.north.north_mask = f32[13,8,128]{2,1,0:T(8,128)S(1)} collective-permute-done((f32[13,8,128]{2,1,0:T(8,128)S(1)}, f32[13,8,128]{2,1,0:T(8,128)S(1)}, u32[]{:S(2)}, u32[]{:S(2)}) %collective-permute-start) | collective-permute-done | bytes 53280 | tf_op jit(solution)/shard_map/ppermute | solution.py:815
  12.0 1.1 %shard_map.79 = (f32[3840,128]{1,0:T(8,128)S(1)}, f32[152,128]{1,0:T(8,128)S(1)}) custom-call(f32[3840,128]{1,0:T(8,128)S(1)} %shard_map.78.parts_in, f32[3840,128]{1,0:T(8,128)S(1)} %get-tuple-element.11.lifted, f32[13,8,128]{2,1,0:T(8,128)S(1)} %collective-permute-done.north.north_mask, ...), custom_call_target="tpu_custom_call", output_to_operand_aliasing={{0}: (0, {})} | custom-call | flops 20000000000 | bytes 8000000 | tf_op jit(solution)/shard_map/pallas_call | solution.py:436
  13.1 0.5 %collective-permute-done.4.refs_2_ = f32[64,128]{1,0:T(8,128)S(1)} collective-permute-done((f32[64,128]{1,0:T(8,128)S(1)}, f32[64,128]{1,0:T(8,128)S(1)}, u32[]{:S(2)}, u32[]{:S(2)}) %collective-permute-start.4) | collective-permute-done | bytes 32800 | tf_op jit(solution)/shard_map/ppermute | solution.py:819
  13.6 3.2 %collective-permute-done.5.refs_3_ = f32[64,128]{1,0:T(8,128)S(1)} collective-permute-done((f32[64,128]{1,0:T(8,128)S(1)}, f32[64,128]{1,0:T(8,128)S(1)}, u32[]{:S(2)}, u32[]{:S(2)}) %collective-permute-start.5) | collective-permute-done | bytes 32800 | tf_op jit(solution)/shard_map/ppermute | solution.py:819
  16.8 0.1 collective-permute-start.6
  16.9 0.1 collective-permute-start.2
  17.0 2.0 %collective-permute-start.7 = (f32[256,128]{1,0:T(8,128)S(1)}, f32[256,128]{1,0:T(8,128)S(1)}, u32[]{:S(2)}, u32[]{:S(2)}) collective-permute-start(f32[256,128]{1,0:T(8,128)S(1)} %get-tuple-element.19.refs_0_), channel_id=1, source_target_pairs={{0,8},{8,0},{16,24},{24,16},{1,9},{9,1},{17,25},{25,17},{2,10},{10... | collective-permute-start | bytes 393224 | tf_op jit(solution)/shard_map/ppermute | solution.py:819
  19.0 1.5 %collective-permute-start.8 = (f32[256,128]{1,0:T(8,128)S(1)}, f32[256,128]{1,0:T(8,128)S(1)}, u32[]{:S(2)}, u32[]{:S(2)}) collective-permute-start(f32[256,128]{1,0:T(8,128)S(1)} %get-tuple-element.19.refs_0_), channel_id=1, source_target_pairs={{0,16},{8,24},{16,0},{24,8},{1,17},{9,25},{17,1},{25,9},{2,18},{10... | collective-permute-start | bytes 393224 | tf_op jit(solution)/shard_map/ppermute | solution.py:819
  20.5 0.0 collective-permute-start.9
  20.6 2.0 %collective-permute-done.6.far = f32[152,128]{1,0:T(8,128)S(1)} collective-permute-done((f32[152,128]{1,0:T(8,128)S(1)}, f32[152,128]{1,0:T(8,128)S(1)}, u32[]{:S(2)}, u32[]{:S(2)}) %collective-permute-start.6) | collective-permute-done | bytes 77856 | tf_op jit(solution)/shard_map/ppermute | solution.py:824
  22.5 3.6 %shard_map.81.refs_4_ = f32[4608,128]{1,0:T(8,128)S(1)} custom-call(f32[4,24,40,128]{3,2,1,0:T(8,128)S(1)} %bitcast.4, f32[3840,128]{1,0:T(8,128)S(1)} %get-tuple-element.15.flat, f32[152,128]{1,0:T(8,128)S(1)} %collective-permute-done.2.near, f32[152,128]{1,0:T(8,128)S(1)} %collective-permute-done.6.far, f32[2,8,128]{2,1,0:T(8,128)S(1)} %get-tuple-element.14.own_masks, ...), custom_call_target="tpu_custom_call" | custom-call | flops 8000000000 | bytes 8000000 | tf_op jit(solution)/shard_map/pallas_call | solution.py:681
  26.1 1.3 %collective-permute-done.8.refs_2_ = f32[256,128]{1,0:T(8,128)S(1)} collective-permute-done((f32[256,128]{1,0:T(8,128)S(1)}, f32[256,128]{1,0:T(8,128)S(1)}, u32[]{:S(2)}, u32[]{:S(2)}) %collective-permute-start.8) | collective-permute-done | bytes 131104 | tf_op jit(solution)/shard_map/ppermute | solution.py:819
  27.4 0.3 %shard_map.83.own = f32[4,4,64,128]{3,2,1,0:T(8,128)S(1)} custom-call(f32[256,128]{1,0:T(8,128)S(1)} %get-tuple-element.19.refs_0_, f32[256,128]{1,0:T(8,128)S(1)} %collective-permute-done.7.refs_1_, f32[256,128]{1,0:T(8,128)S(1)} %collective-permute-done.8.refs_2_, f32[256,128]{1,0:T(8,128)S(1)} %collective-permute-done.9.refs_3_, ...), custom_call_target="tpu_custom_call" | custom-call | tf_op jit(solution)/shard_map/pallas_call | solution.py:752
  27.7 0.1 collective-permute-start.10
  27.8 1.4 %shard_map.82 = f32[3,16,64,128]{3,2,1,0:T(8,128)} custom-call(f32[4,24,48,128]{3,2,1,0:T(8,128)S(1)} %bitcast.3), custom_call_target="tpu_custom_call" | custom-call | flops 4000000000 | bytes 8000000 | tf_op jit(solution)/shard_map/pallas_call | solution.py:704
  29.2 0.5 %collective-permute-done.10.other = f32[4,4,64,128]{3,2,1,0:T(8,128)S(1)} collective-permute-done((f32[4,4,64,128]{3,2,1,0:T(8,128)S(1)}, f32[4,4,64,128]{3,2,1,0:T(8,128)S(1)}, u32[]{:S(2)}, u32[]{:S(2)}) %collective-permute-start.10) | collective-permute-done | bytes 524320 | tf_op jit(solution)/shard_map/ppermute | solution.py:819
  29.7 1.4 %shard_map.84 = f32[3,4,64,256]{3,2,1,0:T(8,128)} custom-call(f32[4,4,64,128]{3,2,1,0:T(8,128)S(1)} %shard_map.83.own, f32[4,4,64,128]{3,2,1,0:T(8,128)S(1)} %collective-permute-done.10.other), custom_call_target="tpu_custom_call" | custom-call | tf_op jit(solution)/shard_map/pallas_call | solution.py:803
  (10 shorter events, 0.0 us)
Async XLA Ops:
  3.0 9.0 %collective-permute-start.1 = (f32[19,8,128]{2,1,0:T(8,128)S(1)}, f32[19,8,128]{2,1,0:T(8,128)S(1)}, u32[]{:S(2)}, u32[]{:S(2)}) collective-permute-start(f32[19,8,128]{2,1,0:T(8,128)S(1)} %get-tuple-element.13), channel_id=1, source_target_pairs={{0,24},{8,0},{16,8},{24,16},{1,25},{9,1},{17,9},{25,17},{2,26},{10... | collective-permute-start | bytes 233480 | tf_op jit(solution)/shard_map/ppermute | solution.py:815
  6.9 5.0 %collective-permute-start = (f32[13,8,128]{2,1,0:T(8,128)S(1)}, f32[13,8,128]{2,1,0:T(8,128)S(1)}, u32[]{:S(2)}, u32[]{:S(2)}) collective-permute-start(f32[13,8,128]{2,1,0:T(8,128)S(1)} %get-tuple-element.12), channel_id=1, source_target_pairs={{0,8},{8,16},{16,24},{24,0},{1,9},{9,17},{17,25},{25,1},{2,10},{10... | collective-permute-start | bytes 159752 | tf_op jit(solution)/shard_map/ppermute | solution.py:815
  6.9 6.2 %collective-permute-start.3 = (f32[64,128]{1,0:T(8,128)S(1)}, f32[64,128]{1,0:T(8,128)S(1)}, u32[]{:S(2)}, u32[]{:S(2)}) collective-permute-start(f32[64,128]{1,0:T(8,128)S(1)} %get-tuple-element.17.refs_0_), channel_id=1, source_target_pairs={{0,2},{1,3},{2,0},{3,1},{4,6},{5,7},{6,4},{7,5},{8,10},{9,11},{10,... | collective-permute-start | bytes 98312 | tf_op jit(solution)/shard_map/ppermute | solution.py:819
  8.5 5.1 %collective-permute-start.4 = (f32[64,128]{1,0:T(8,128)S(1)}, f32[64,128]{1,0:T(8,128)S(1)}, u32[]{:S(2)}, u32[]{:S(2)}) collective-permute-start(f32[64,128]{1,0:T(8,128)S(1)} %get-tuple-element.17.refs_0_), channel_id=1, source_target_pairs={{0,4},{1,5},{2,6},{3,7},{4,0},{5,1},{6,2},{7,3},{8,12},{9,13},{10,... | collective-permute-start | bytes 98312 | tf_op jit(solution)/shard_map/ppermute | solution.py:819
  11.1 5.7 %collective-permute-start.5 = (f32[64,128]{1,0:T(8,128)S(1)}, f32[64,128]{1,0:T(8,128)S(1)}, u32[]{:S(2)}, u32[]{:S(2)}) collective-permute-start(f32[64,128]{1,0:T(8,128)S(1)} %get-tuple-element.17.refs_0_), channel_id=1, source_target_pairs={{0,6},{1,7},{2,4},{3,5},{4,2},{5,3},{6,0},{7,1},{8,14},{9,15},{10,... | collective-permute-start | bytes 98312 | tf_op jit(solution)/shard_map/ppermute | solution.py:819
  16.8 5.7 %copy-start = (bf16[1280,128]{1,0:T(8,128)(2,1)S(1)}, bf16[1280,128]{1,0:T(8,128)(2,1)}, u32[]{:S(2)}) copy-start(bf16[1280,128]{1,0:T(8,128)(2,1)} %constant.11.clone.narrow) | copy-start | bytes 983044
  16.8 5.7 %copy-start.1 = (bf16[528,256]{1,0:T(8,128)(2,1)S(1)}, bf16[528,256]{1,0:T(8,128)(2,1)}, u32[]{:S(2)}) copy-start(bf16[528,256]{1,0:T(8,128)(2,1)} %constant.10.clone.wide) | copy-start | bytes 811012
  16.8 5.7 %collective-permute-start.6 = (f32[152,128]{1,0:T(8,128)S(1)}, f32[152,128]{1,0:T(8,128)S(1)}, u32[]{:S(2)}, u32[]{:S(2)}) collective-permute-start(f32[152,128]{1,0:T(8,128)S(1)} %get-tuple-element.18), channel_id=1, source_target_pairs={{0,7},{1,2},{2,1},{3,4},{4,3},{5,6},{6,5},{7,0},{8,15},{9,10},{10,... | collective-permute-start | bytes 233480 | tf_op jit(solution)/shard_map/ppermute | solution.py:824
  16.9 5.6 %collective-permute-start.2 = (f32[152,128]{1,0:T(8,128)S(1)}, f32[152,128]{1,0:T(8,128)S(1)}, u32[]{:S(2)}, u32[]{:S(2)}) collective-permute-start(f32[152,128]{1,0:T(8,128)S(1)} %get-tuple-element.16.refs_4_), channel_id=1, source_target_pairs={{0,1},{1,0},{2,3},{3,2},{4,5},{5,4},{6,7},{7,6},{8,9},{9,8},{10,11... | collective-permute-start | bytes 233480 | tf_op jit(solution)/shard_map/ppermute | solution.py:819
  17.0 9.1 %collective-permute-start.7 = (f32[256,128]{1,0:T(8,128)S(1)}, f32[256,128]{1,0:T(8,128)S(1)}, u32[]{:S(2)}, u32[]{:S(2)}) collective-permute-start(f32[256,128]{1,0:T(8,128)S(1)} %get-tuple-element.19.refs_0_), channel_id=1, source_target_pairs={{0,8},{8,0},{16,24},{24,16},{1,9},{9,1},{17,25},{25,17},{2,10},{10... | collective-permute-start | bytes 393224 | tf_op jit(solution)/shard_map/ppermute | solution.py:819
  19.0 8.4 %collective-permute-start.8 = (f32[256,128]{1,0:T(8,128)S(1)}, f32[256,128]{1,0:T(8,128)S(1)}, u32[]{:S(2)}, u32[]{:S(2)}) collective-permute-start(f32[256,128]{1,0:T(8,128)S(1)} %get-tuple-element.19.refs_0_), channel_id=1, source_target_pairs={{0,16},{8,24},{16,0},{24,8},{1,17},{9,25},{17,1},{25,9},{2,18},{10... | collective-permute-start | bytes 393224 | tf_op jit(solution)/shard_map/ppermute | solution.py:819
  20.5 6.9 %collective-permute-start.9 = (f32[256,128]{1,0:T(8,128)S(1)}, f32[256,128]{1,0:T(8,128)S(1)}, u32[]{:S(2)}, u32[]{:S(2)}) collective-permute-start(f32[256,128]{1,0:T(8,128)S(1)} %get-tuple-element.19.refs_0_), channel_id=1, source_target_pairs={{0,24},{8,16},{16,8},{24,0},{1,25},{9,17},{17,9},{25,1},{2,26},{10... | collective-permute-start | bytes 393224 | tf_op jit(solution)/shard_map/ppermute | solution.py:819
  27.7 2.0 %collective-permute-start.10 = (f32[4,4,64,128]{3,2,1,0:T(8,128)S(1)}, f32[4,4,64,128]{3,2,1,0:T(8,128)S(1)}, u32[]{:S(2)}, u32[]{:S(2)}) collective-permute-start(f32[4,4,64,128]{3,2,1,0:T(8,128)S(1)} %shard_map.83.own), channel_id=1, source_target_pairs={{0,1},{1,0},{2,3},{3,2},{4,5},{5,4},{6,7},{7,6},{8,9},{9,8},{10,11... | collective-permute-start | bytes 1572872 | tf_op jit(solution)/shard_map/ppermute | solution.py:819

commit v4 on v2

--- a/solution.py
+++ b/solution.py
@@ -266,7 +266,6 @@
         own_masks[i] = jnp.concatenate([total, jnp.zeros((1, NL), F32)], 0)
         out[tile] = own_masks[i]
 
-    total = jnp.zeros((80, NL), F32)
     for v in range(NV):
         for t in range(8):
             if t % 2 == 0:
@@ -298,6 +297,9 @@
                 last = y[61] - 0.5 * (y[60] + y[62])
                 down[v * 4 + 2] = y[60] + 0.25 * (before + last)
                 down[v * 4 + 3] = y[62] + 0.25 * (last + part)
+
+    total = jnp.zeros((80, NL), F32)
+    for v in range(NV):
         main, extra = [], jnp.zeros((16, NL), F32)
         for z in range(4):
             terms = jnp.concatenate(two_terms(twice[v * 4 + z]), 0)
@@ -307,7 +309,6 @@
         terms = jnp.concatenate(two_terms(jnp.concatenate(main + [extra], 0)), 1)
         part = dot(terms, table[0:256, :])
         total += pltpu.roll(part, 35 * v, 1) if v else part
-
     turn = lanes_turn(lax.axis_index("gy"))
     lane = lax.broadcasted_iota(jnp.int32, (8, NL), 1)
     spare = (lane >= 105) & (lane < 126)
@@ -442,24 +443,6 @@
         scratch_shapes=[pltpu.VMEM((480, NL), F32), pltpu.VMEM((512, NL), BF16), pltpu.SemaphoreType.DMA((1,))],
         compiler_params=pltpu.CompilerParams(vmem_limit_bytes=VMEM_LIMIT),
     )(parts, lifted, north, south, own_masks, in_hbm(jnp.asarray(weights()["edge"])))
-
-
-def join_kernel(*refs):
-    shares, out = refs[:-2], refs[-1]
-    for n, piece in enumerate(shares):
-        out[64 * n : 64 * (n + 1), :] = piece[...]
-
-
-def join_step(shares, after):
-    vmem = pl.BlockSpec(memory_space=pltpu.VMEM)
-    return pl.pallas_call(
-        join_kernel,
-        out_shape=jax.ShapeDtypeStruct((64 * len(shares), NL), F32),
-        in_specs=[vmem] * len(shares) + [pl.BlockSpec(memory_space=pl.ANY)],
-        out_specs=vmem,
-        cost_estimate=cost(20),
-        compiler_params=pltpu.CompilerParams(vmem_limit_bytes=VMEM_LIMIT),
-    )(*shares, after)
 
 
 def mask_lanes(near, far, own_masks, north_mask, south_mask, wide):
@@ -722,7 +705,7 @@
                 start = 64 * j + 16 * z
                 out[j, z, pl.ds(at, 16), :] = shares[r][start : start + 16, :]
     for j in range(count_z):
-        turn = lanes_turn(me_y ^ (2 * j))
+        turn = lanes_turn(2 * j + lax.rem(me_y, 2))
         piece = lax.rem(lane + (NL - turn), NL) // 21
         inside = [piece == p for p in range(5)]
         for r in range(count_x):
@@ -758,7 +741,7 @@
 
 def coarse_kernel(count_x, count_y, own, other, out_hbm, out, sems):
     me = lax.axis_index("gy")
-    me_z, is_even = lax.shift_right_logical(me, 1), lax.rem(me, 2) == 0
+    is_even = lax.rem(me, 2) == 0
     lane = lax.broadcasted_iota(jnp.int32, (8, NL), 1)
     place = [lax.rem(lane + NL - 35 * v, NL) for v in range(NV)]
 
@@ -767,7 +750,7 @@
         for z in range(4):
             pieces = []
             for j in range(count_y // 2):
-                mine, theirs = own[j ^ me_z, z, rows, :], other[j ^ me_z, z, rows, :]
+                mine, theirs = own[j, z, rows, :], other[j, z, rows, :]
                 pieces += [jnp.where(is_even, mine, theirs), jnp.where(is_even, theirs, mine)]
             for v in range(NV):
                 at = place[v]
@@ -827,10 +810,10 @@
     lifted, up, down, own_masks, share = first_step(field, masks)
     south = shifted(up, "gx", -1)
     north = shifted(down, "gx", 1)
-    shares = [share] + [swapped(share, "gy", r) for r in range(2, count_y, 2)]
+    same_core = [list(range(c, count_y, 2)) for c in range(2)]
+    joined = lax.all_gather(share, "gy", axis=0, tiled=True, axis_index_groups=same_core)
     parts, sides = edge_step(lift_step(lifted), lifted, north, south, own_masks)
     near, far = swapped(sides, "gy", 1), crossed(sides, "gy")
-    joined = join_step(shares, sides)
     pieces = [joined] + [swapped(joined, "gx", r) for r in range(1, count_x)]
     kept = main_step(parts, near, far, own_masks, north, south)
     own = rows_step(pieces, count_y // 2, kept)

time: 30.4 us -> 41.3 us (1.36)
  blocking collectives: 0 us -> 13.4 us
  starting transfers between devices: 15.7 us -> 11.3 us
  waiting for transfers between devices: 3.01 us -> 5.24 us
    all_gather x0 -> x1, blocking collectives: none -> 13.4 us  [body(): lax.all_gather(share, 'gy', axis=0, tiled=True, axis_index_groups=same_core)]
    ppermute x8 -> x5, starting transfers between devices: 8.08 us -> 3.63 us  [swapped(): lax.ppermute(x, axis, [(i, i ^ distance) for i in range(lax.axis_size(axi...]
    ppermute x2, waiting for transfers between devices: 0.32 us -> 4.7 us  [shifted(): lax.ppermute(x, axis, [(i, (i + step) % count) for i in range(count)])]
    ppermute x8 -> x5, waiting for transfers between devices: 2.69 us -> 0.53 us  [swapped(): lax.ppermute(x, axis, [(i, i ^ distance) for i in range(lax.axis_size(axi...]
  transfers between devices with their start and end apart: 11 -> 8, of which waited for: 4 -> 2; matrix products, arithmetic and copies ran while one was open for 0% -> 0% of each run, Pallas kernels for 21% -> 13%
where the time goes in v4:
time: 41.3 us; the launch traced here: 41.1 us
  blocking collectives  13.4 us (32%)
  starting transfers between devices  11.3 us (27%)
  Pallas kernels  10.5 us (25%)
  waiting for transfers between devices  5.24 us (13%)
  between operations  0.73 us (2%)
    all_gather x1, blocking collectives, body(): lax.all_gather(share, 'gy', axis=0, tiled=True, axis_index_groups=same_core)  13.4 us
    ppermute x2, waiting for transfers between devices, shifted(): lax.ppermute(x, axis, [(i, (i + step) % count) for i in range(count)])  4.7 us
    ppermute x2, starting transfers between devices, shifted(): lax.ppermute(x, axis, [(i, (i + step) % count) for i in range(count)])  3.95 us
    ppermute x1, starting transfers between devices, crossed(): lax.ppermute(x, axis, [(i, (i + (1 if i % 2 else count - 1)) % count) for...  3.7 us
    ppermute x5, starting transfers between devices, swapped(): lax.ppermute(x, axis, [(i, i ^ distance) for i in range(lax.axis_size(axi...  3.63 us
    pallas_call x1, Pallas kernels, main_step(): pl.pallas_call(main_kernel, grid=(1,), out_shape=jax.ShapeDtypeStruct((4...  3.57 us
    pallas_call x1, Pallas kernels, first_step(): pl.pallas_call(first_kernel, out_shape=[jax.ShapeDtypeStruct(s, F32) for...  2.33 us
    pallas_call x1, Pallas kernels, cells_step(): pl.pallas_call(cells_kernel, out_shape=jax.ShapeDtypeStruct(shape, F32),...  1.37 us
  transfers between devices with their start and end apart: 8, of which 2 were waited for; matrix products, arithmetic and copies ran while one was open for 0% of the time, Pallas kernels for 13%

profile of v4, /device:TPU:0, one launch (start us, length us, event | category | flops | bytes accessed | tf_op | source)
XLA Modules:
  0.0 41.1 jit_solution(1184995401248730259)
XLA Ops:
  0.6 2.3 %shard_map.77 = (f32[3840,128]{1,0:T(8,128)S(1)}, f32[19,8,128]{2,1,0:T(8,128)S(1)}, f32[13,8,128]{2,1,0:T(8,128)S(1)}, f32[2,8,128]{2,1,0:T(8,128)S(1)}, f32[64,128]{1,0:T(8,128)S(1)}) custom-call(f32[3,16,64,128]{3,2,1,0:T(8,128)} %field.1, s32[2,2,4,7]{3,2,1,0:T(4,128)} %bitcast.5, bf16[400,128]{1,0:T(8,128)(2,1)} %constant.8.clone.table_hbm), custom_call_target="tpu_custom_call" | custom-call | tf_op jit(solution)/shard_map/pallas_call | solution.py:335
  3.0 3.9 %collective-permute-start.1 = (f32[19,8,128]{2,1,0:T(8,128)S(1)}, f32[19,8,128]{2,1,0:T(8,128)S(1)}, u32[]{:S(2)}, u32[]{:S(2)}) collective-permute-start(f32[19,8,128]{2,1,0:T(8,128)S(1)} %get-tuple-element.11), channel_id=1, source_target_pairs={{0,24},{8,0},{16,8},{24,16},{1,25},{9,1},{17,9},{25,17},{2,26},{10... | collective-permute-start | bytes 233480 | tf_op jit(solution)/shard_map/ppermute | solution.py:796
  6.9 0.0 collective-permute-start
  6.9 0.3 shard_map.78.parts_in
  7.2 4.7 %collective-permute-done.north.north_mask = f32[13,8,128]{2,1,0:T(8,128)S(1)} collective-permute-done((f32[13,8,128]{2,1,0:T(8,128)S(1)}, f32[13,8,128]{2,1,0:T(8,128)S(1)}, u32[]{:S(2)}, u32[]{:S(2)}) %collective-permute-start) | collective-permute-done | bytes 53280 | tf_op jit(solution)/shard_map/ppermute | solution.py:796
  11.9 0.0 collective-permute-done.1.south.south_mask
  12.0 1.2 %shard_map.79 = (f32[3840,128]{1,0:T(8,128)S(1)}, f32[152,128]{1,0:T(8,128)S(1)}) custom-call(f32[3840,128]{1,0:T(8,128)S(1)} %shard_map.78.parts_in, f32[3840,128]{1,0:T(8,128)S(1)} %get-tuple-element.9.lifted, f32[13,8,128]{2,1,0:T(8,128)S(1)} %collective-permute-done.north.north_mask, ...), custom_call_target="tpu_custom_call", output_to_operand_aliasing={{0}: (0, {})} | custom-call | flops 20000000000 | bytes 8000000 | tf_op jit(solution)/shard_map/pallas_call | solution.py:436
  13.2 0.1 collective-permute-start.2
  13.2 3.7 %collective-permute-start.3 = (f32[152,128]{1,0:T(8,128)S(1)}, f32[152,128]{1,0:T(8,128)S(1)}, u32[]{:S(2)}, u32[]{:S(2)}) collective-permute-start(f32[152,128]{1,0:T(8,128)S(1)} %get-tuple-element.14), channel_id=1, source_target_pairs={{0,7},{1,2},{2,1},{3,4},{4,3},{5,6},{6,5},{7,0},{8,15},{9,10},{10,... | collective-permute-start | bytes 233480 | tf_op jit(solution)/shard_map/ppermute | solution.py:805
  16.9 13.4 %all_gather.3.refs_0_ = f32[256,128]{1,0:T(8,128)S(1)} all-gather(f32[64,128]{1,0:T(8,128)S(1)} %get-tuple-element.15), channel_id=1, replica_groups={{0,2,4,6},{1,3,5,7},{8,10,12,14},{9,11,13,15},{16,18,20,22},{17,19,21,2..., dimensions={0}, use_global_device_ids=true | all-gather | bytes 163840 | tf_op jit(solution)/shard_map/all_gather | solution.py:814
  30.4 0.2 collective-permute-start.4
  30.6 0.9 %collective-permute-start.5 = (f32[256,128]{1,0:T(8,128)S(1)}, f32[256,128]{1,0:T(8,128)S(1)}, u32[]{:S(2)}, u32[]{:S(2)}) collective-permute-start(f32[256,128]{1,0:T(8,128)S(1)} %all_gather.3.refs_0_), channel_id=1, source_target_pairs={{0,16},{8,24},{16,0},{24,8},{1,17},{9,25},{17,1},{25,9},{2,18},{10... | collective-permute-start | bytes 393224 | tf_op jit(solution)/shard_map/ppermute | solution.py:800
  31.4 2.4 %collective-permute-start.6 = (f32[256,128]{1,0:T(8,128)S(1)}, f32[256,128]{1,0:T(8,128)S(1)}, u32[]{:S(2)}, u32[]{:S(2)}) collective-permute-start(f32[256,128]{1,0:T(8,128)S(1)} %all_gather.3.refs_0_), channel_id=1, source_target_pairs={{0,24},{8,16},{16,8},{24,0},{1,25},{9,17},{17,9},{25,1},{2,26},{10... | collective-permute-start | bytes 393224 | tf_op jit(solution)/shard_map/ppermute | solution.py:800
  33.8 0.0 collective-permute-done.2.near
  33.8 0.0 collective-permute-done.3.far
  33.9 3.6 %shard_map.80.refs_4_ = f32[4608,128]{1,0:T(8,128)S(1)} custom-call(f32[4,24,40,128]{3,2,1,0:T(8,128)S(1)} %bitcast.4, f32[3840,128]{1,0:T(8,128)S(1)} %get-tuple-element.13.flat, f32[152,128]{1,0:T(8,128)S(1)} %collective-permute-done.2.near, f32[152,128]{1,0:T(8,128)S(1)} %collective-permute-done.3.far, f32[2,8,128]{2,1,0:T(8,128)S(1)} %get-tuple-element.12.own_masks, ...), custom_call_target="tpu_custom_call" | custom-call | flops 8000000000 | bytes 8000000 | tf_op jit(solution)/shard_map/pallas_call | solution.py:662
  37.4 0.0 collective-permute-done.4.refs_1_
  37.5 0.0 collective-permute-done.5.refs_2_
  37.5 0.0 collective-permute-done.6.refs_3_
  37.5 0.3 shard_map.82.own
  37.8 0.1 collective-permute-start.7
  37.9 1.4 %shard_map.81 = f32[3,16,64,128]{3,2,1,0:T(8,128)} custom-call(f32[4,24,48,128]{3,2,1,0:T(8,128)S(1)} %bitcast.3), custom_call_target="tpu_custom_call" | custom-call | flops 4000000000 | bytes 8000000 | tf_op jit(solution)/shard_map/pallas_call | solution.py:685
  39.2 0.5 %collective-permute-done.7.other = f32[4,4,64,128]{3,2,1,0:T(8,128)S(1)} collective-permute-done((f32[4,4,64,128]{3,2,1,0:T(8,128)S(1)}, f32[4,4,64,128]{3,2,1,0:T(8,128)S(1)}, u32[]{:S(2)}, u32[]{:S(2)}) %collective-permute-start.7) | collective-permute-done | bytes 524320 | tf_op jit(solution)/shard_map/ppermute | solution.py:800
  39.8 1.4 %shard_map.83 = f32[3,4,64,256]{3,2,1,0:T(8,128)} custom-call(f32[4,4,64,128]{3,2,1,0:T(8,128)S(1)} %shard_map.82.own, f32[4,4,64,128]{3,2,1,0:T(8,128)S(1)} %collective-permute-done.7.other), custom_call_target="tpu_custom_call" | custom-call | tf_op jit(solution)/shard_map/pallas_call | solution.py:784
  (4 shorter events, 0.0 us)
Async XLA Ops:
  3.0 9.0 %collective-permute-start.1 = (f32[19,8,128]{2,1,0:T(8,128)S(1)}, f32[19,8,128]{2,1,0:T(8,128)S(1)}, u32[]{:S(2)}, u32[]{:S(2)}) collective-permute-start(f32[19,8,128]{2,1,0:T(8,128)S(1)} %get-tuple-element.11), channel_id=1, source_target_pairs={{0,24},{8,0},{16,8},{24,16},{1,25},{9,1},{17,9},{25,17},{2,26},{10... | collective-permute-start | bytes 233480 | tf_op jit(solution)/shard_map/ppermute | solution.py:796
  6.9 5.0 %collective-permute-start = (f32[13,8,128]{2,1,0:T(8,128)S(1)}, f32[13,8,128]{2,1,0:T(8,128)S(1)}, u32[]{:S(2)}, u32[]{:S(2)}) collective-permute-start(f32[13,8,128]{2,1,0:T(8,128)S(1)} %get-tuple-element.10), channel_id=1, source_target_pairs={{0,8},{8,16},{16,24},{24,0},{1,9},{9,17},{17,25},{25,1},{2,10},{10... | collective-permute-start | bytes 159752 | tf_op jit(solution)/shard_map/ppermute | solution.py:796
  12.0 21.9 %copy-start = (bf16[1280,128]{1,0:T(8,128)(2,1)S(1)}, bf16[1280,128]{1,0:T(8,128)(2,1)}, u32[]{:S(2)}) copy-start(bf16[1280,128]{1,0:T(8,128)(2,1)} %constant.11.clone.narrow) | copy-start | bytes 983044
  12.0 21.9 %copy-start.1 = (bf16[528,256]{1,0:T(8,128)(2,1)S(1)}, bf16[528,256]{1,0:T(8,128)(2,1)}, u32[]{:S(2)}) copy-start(bf16[528,256]{1,0:T(8,128)(2,1)} %constant.10.clone.wide) | copy-start | bytes 811012
  13.2 20.7 %collective-permute-start.2 = (f32[152,128]{1,0:T(8,128)S(1)}, f32[152,128]{1,0:T(8,128)S(1)}, u32[]{:S(2)}, u32[]{:S(2)}) collective-permute-start(f32[152,128]{1,0:T(8,128)S(1)} %get-tuple-element.14), channel_id=1, source_target_pairs={{0,1},{1,0},{2,3},{3,2},{4,5},{5,4},{6,7},{7,6},{8,9},{9,8},{10,11... | collective-permute-start | bytes 233480 | tf_op jit(solution)/shard_map/ppermute | solution.py:800
  13.2 20.6 %collective-permute-start.3 = (f32[152,128]{1,0:T(8,128)S(1)}, f32[152,128]{1,0:T(8,128)S(1)}, u32[]{:S(2)}, u32[]{:S(2)}) collective-permute-start(f32[152,128]{1,0:T(8,128)S(1)} %get-tuple-element.14), channel_id=1, source_target_pairs={{0,7},{1,2},{2,1},{3,4},{4,3},{5,6},{6,5},{7,0},{8,15},{9,10},{10,... | collective-permute-start | bytes 233480 | tf_op jit(solution)/shard_map/ppermute | solution.py:805
  30.4 7.1 %collective-permute-start.4 = (f32[256,128]{1,0:T(8,128)S(1)}, f32[256,128]{1,0:T(8,128)S(1)}, u32[]{:S(2)}, u32[]{:S(2)}) collective-permute-start(f32[256,128]{1,0:T(8,128)S(1)} %all_gather.3.refs_0_), channel_id=1, source_target_pairs={{0,8},{8,0},{16,24},{24,16},{1,9},{9,1},{17,25},{25,17},{2,10},{10... | collective-permute-start | bytes 393224 | tf_op jit(solution)/shard_map/ppermute | solution.py:800
  30.6 6.9 %collective-permute-start.5 = (f32[256,128]{1,0:T(8,128)S(1)}, f32[256,128]{1,0:T(8,128)S(1)}, u32[]{:S(2)}, u32[]{:S(2)}) collective-permute-start(f32[256,128]{1,0:T(8,128)S(1)} %all_gather.3.refs_0_), channel_id=1, source_target_pairs={{0,16},{8,24},{16,0},{24,8},{1,17},{9,25},{17,1},{25,9},{2,18},{10... | collective-permute-start | bytes 393224 | tf_op jit(solution)/shard_map/ppermute | solution.py:800
  31.4 6.0 %collective-permute-start.6 = (f32[256,128]{1,0:T(8,128)S(1)}, f32[256,128]{1,0:T(8,128)S(1)}, u32[]{:S(2)}, u32[]{:S(2)}) collective-permute-start(f32[256,128]{1,0:T(8,128)S(1)} %all_gather.3.refs_0_), channel_id=1, source_target_pairs={{0,24},{8,16},{16,8},{24,0},{1,25},{9,17},{17,9},{25,1},{2,26},{10... | collective-permute-start | bytes 393224 | tf_op jit(solution)/shard_map/ppermute | solution.py:800
  37.8 2.0 %collective-permute-start.7 = (f32[4,4,64,128]{3,2,1,0:T(8,128)S(1)}, f32[4,4,64,128]{3,2,1,0:T(8,128)S(1)}, u32[]{:S(2)}, u32[]{:S(2)}) collective-permute-start(f32[4,4,64,128]{3,2,1,0:T(8,128)S(1)} %shard_map.82.own), channel_id=1, source_target_pairs={{0,1},{1,0},{2,3},{3,2},{4,5},{5,4},{6,7},{7,6},{8,9},{9,8},{10,11... | collective-permute-start | bytes 1572872 | tf_op jit(solution)/shard_map/ppermute | solution.py:800

commit v5 on v1

--- a/solution.py
+++ b/solution.py
@@ -234,6 +234,10 @@
 PITCH = 80
 
 
+def lanes_turn(j):
+    return lax.rem(32 * lax.rem(j, 4) + NL - 1, NL)
+
+
 def first_kernel(
     field, masks_hbm, table_hbm, lifted, up, down, own_masks, share, cells, twice, masks, table, sems
 ):
@@ -305,6 +309,7 @@
         terms = jnp.concatenate(two_terms(jnp.concatenate(main + [extra], 0)), 1)
         part = dot(terms, table[0:256, :])
         total += pltpu.roll(part, 35 * v, 1) if v else part
+    turn = lanes_turn(lax.axis_index("gy"))
     lane = lax.broadcasted_iota(jnp.int32, (8, NL), 1)
     spare = (lane >= 105) & (lane < 126)
     upper = lax.broadcasted_iota(jnp.int32, (8, NL), 0) < 4
@@ -316,7 +321,8 @@
         else:
             extra = pltpu.roll(pieces[2 * g - 10], 4, 0)
             extra = jnp.where(upper, extra, pieces[2 * g - 9] if g < 7 else 0.0)
-        share[8 * g : 8 * g + 8, :] = jnp.where(spare, extra, total[8 * g : 8 * g + 8])
+        tile = jnp.where(spare, extra, total[8 * g : 8 * g + 8])
+        share[8 * g : 8 * g + 8, :] = pltpu.roll(tile, turn, 1)
 
 
 def in_hbm(x):
@@ -484,7 +490,7 @@
 
 
 def main_kernel(
-    parts, flat, west, east, own_masks, north_mask, south_mask, wide, narrow,
+    parts, flat, east, west, own_masks, north_mask, south_mask, wide, narrow,
     kept,
     gain2, low, second, kept2, low_back, gain, sides_wide, turned,
 ):
@@ -704,31 +710,29 @@
     shares, out = refs[:count_x], refs[count_x + 1]
     me, me_y = lax.axis_index("gx"), lax.axis_index("gy")
     row = lax.broadcasted_iota(jnp.int32, (8, NL), 0)
-    piece = lax.broadcasted_iota(jnp.int32, (8, NL), 1) // 21
-    turns = []
-    for j in range(count_z):
-        place = lax.rem(2 * (lax.shift_right_logical(me_y, 1) ^ j) + lax.rem(me_y, 2), 4)
-        turns.append(lax.rem(32 * place + NL - 1, NL))
+    lane = lax.broadcasted_iota(jnp.int32, (8, NL), 1)
     for r in range(count_x):
         at = pl.multiple_of(16 * (me ^ r), 16)
         for j in range(count_z):
             for z in range(4):
                 start = 64 * j + 16 * z
-                out[j, z, pl.ds(at, 16), :] = pltpu.roll(shares[r][start : start + 16, :], turns[j], 1)
-    for r in range(count_x):
-        i = me ^ r
-        below = pl.multiple_of(16 * lax.rem(i + 1, count_x), 16)
-        above = pl.multiple_of(16 * lax.rem(i + count_x - 1, count_x) + 8, 8)
-        for j in range(count_z):
+                out[j, z, pl.ds(at, 16), :] = shares[r][start : start + 16, :]
+    for j in range(count_z):
+        turn = lanes_turn(me_y ^ (2 * j))
+        piece = lax.rem(lane + (NL - turn), NL) // 21
+        inside = [piece == p for p in range(5)]
+        for r in range(count_x):
+            i = me ^ r
+            below = pl.multiple_of(16 * lax.rem(i + 1, count_x), 16)
+            above = pl.multiple_of(16 * lax.rem(i + count_x - 1, count_x) + 8, 8)
             tiles = [shares[r][64 * j + 8 * g : 64 * j + 8 * g + 8, :] for g in range(8)]
             low, high = jnp.zeros((8, NL), F32), jnp.zeros((8, NL), F32)
             for p in range(5):
                 back = (21 * p - 105) % NL
-                low = jnp.where(piece == p, pltpu.roll(tiles[p], back, 1), low)
+                low = jnp.where(inside[p], pltpu.roll(tiles[p], back, 1), low)
                 extra = tiles[5 + p // 2]
                 extra = extra if p % 2 else pltpu.roll(extra, 4, 0)
-                high = jnp.where(piece == p, pltpu.roll(extra, back, 1), high)
-            low, high = pltpu.roll(low, turns[j], 1), pltpu.roll(high, turns[j], 1)
+                high = jnp.where(inside[p], pltpu.roll(extra, back, 1), high)
             for z in range(4):
                 first = pltpu.roll(low, 8 - 2 * z, 0) if z else low
                 last = pltpu.roll(high, z, 0) if z else high
@@ -816,11 +820,11 @@
     north = shifted(down, "gx", 1)
     shares = [share] + [swapped(share, "gy", r) for r in range(2, count_y, 2)]
     parts, sides = edge_step(lift_step(lifted), lifted, north, south, own_masks)
+    east = shifted(sides, "gy", -1)
     west = shifted(sides, "gy", 1)
-    east = shifted(sides, "gy", -1)
     joined = join_step(shares, sides)
     pieces = [joined] + [swapped(joined, "gx", r) for r in range(1, count_x)]
-    kept = main_step(parts, west, east, own_masks, north, south)
+    kept = main_step(parts, east, west, own_masks, north, south)
     own = rows_step(pieces, count_y // 2, kept)
     other = swapped(own, "gy", 1)
     return cells_step(kept.reshape(4, NV * 8, 48, NL)), coarse_step(own, other, count_x, count_y)

time: 30.4 us -> 30.2 us (level)
  waiting for transfers between devices: 3.17 us -> 5.17 us
  starting transfers between devices: 15.6 us -> 13.7 us
    ppermute x7, waiting for transfers between devices: 2.85 us -> 4.85 us  [swapped(): lax.ppermute(x, axis, [(i, i ^ distance) for i in range(lax.axis_size(axi...]
    ppermute x4, starting transfers between devices: 7.54 us -> 5.63 us  [shifted(): lax.ppermute(x, axis, [(i, (i + step) % count) for i in range(count)])]
    pallas_call x1, Pallas kernels: 0.67 us -> 0.32 us  [rows_step(): pl.pallas_call(functools.partial(rows_kernel, count_x, count_z), out_shap...]
where the time goes in v5:
time: 30.2 us; the launch traced here: 30 us
  starting transfers between devices  13.7 us (45%)
  Pallas kernels  10.4 us (34%)
  waiting for transfers between devices  5.17 us (17%)
  between operations  0.74 us (2%)
    ppermute x7, starting transfers between devices, swapped(): lax.ppermute(x, axis, [(i, i ^ distance) for i in range(lax.axis_size(axi...  8.03 us
    ppermute x4, starting transfers between devices, shifted(): lax.ppermute(x, axis, [(i, (i + step) % count) for i in range(count)])  5.63 us
    ppermute x7, waiting for transfers between devices, swapped(): lax.ppermute(x, axis, [(i, i ^ distance) for i in range(lax.axis_size(axi...  4.85 us
    pallas_call x1, Pallas kernels, main_step(): pl.pallas_call(main_kernel, grid=(1,), out_shape=jax.ShapeDtypeStruct((4...  3.57 us
    pallas_call x1, Pallas kernels, first_step(): pl.pallas_call(first_kernel, out_shape=[jax.ShapeDtypeStruct(s, F32) for...  2.33 us
    pallas_call x1, Pallas kernels, coarse_step(): pl.pallas_call(functools.partial(coarse_kernel, count_x, count_y), out_sh...  1.37 us
    pallas_call x1, Pallas kernels, cells_step(): pl.pallas_call(cells_kernel, out_shape=jax.ShapeDtypeStruct(shape, F32),...  1.37 us
    pallas_call x1, Pallas kernels, edge_step(): pl.pallas_call(edge_kernel, out_shape=[jax.ShapeDtypeStruct(s, F32) for s...  1.14 us
  transfers between devices with their start and end apart: 11, of which 5 were waited for; matrix products, arithmetic and copies ran while one was open for 0% of the time, Pallas kernels for 21%

profile of v5, /device:TPU:0, one launch (start us, length us, event | category | flops | bytes accessed | tf_op | source)
XLA Modules:
  0.0 30.0 jit_solution(16502498045872845882)
XLA Ops:
  0.6 2.3 %shard_map.77 = (f32[3840,128]{1,0:T(8,128)S(1)}, f32[19,8,128]{2,1,0:T(8,128)S(1)}, f32[13,8,128]{2,1,0:T(8,128)S(1)}, f32[2,8,128]{2,1,0:T(8,128)S(1)}, f32[64,128]{1,0:T(8,128)S(1)}) custom-call(f32[3,16,64,128]{3,2,1,0:T(8,128)} %field.1, s32[2,2,4,7]{3,2,1,0:T(4,128)} %bitcast.5, bf16[400,128]{1,0:T(8,128)(2,1)} %constant.8.clone.table_hbm), custom_call_target="tpu_custom_call" | custom-call | tf_op jit(solution)/shard_map/pallas_call | solution.py:335
  3.0 3.9 %collective-permute-start.1 = (f32[19,8,128]{2,1,0:T(8,128)S(1)}, f32[19,8,128]{2,1,0:T(8,128)S(1)}, u32[]{:S(2)}, u32[]{:S(2)}) collective-permute-start(f32[19,8,128]{2,1,0:T(8,128)S(1)} %get-tuple-element.11), channel_id=1, source_target_pairs={{0,24},{8,0},{16,8},{24,16},{1,25},{9,1},{17,9},{25,17},{2,26},{10... | collective-permute-start | bytes 233480 | tf_op jit(solution)/shard_map/ppermute | solution.py:809
  6.9 1.6 %collective-permute-start.4 = (f32[64,128]{1,0:T(8,128)S(1)}, f32[64,128]{1,0:T(8,128)S(1)}, u32[]{:S(2)}, u32[]{:S(2)}) collective-permute-start(f32[64,128]{1,0:T(8,128)S(1)} %get-tuple-element.15.refs_0_), channel_id=1, source_target_pairs={{0,2},{1,3},{2,0},{3,1},{4,6},{5,7},{6,4},{7,5},{8,10},{9,11},{10,... | collective-permute-start | bytes 98312 | tf_op jit(solution)/shard_map/ppermute | solution.py:813
  8.5 2.6 %collective-permute-start.5 = (f32[64,128]{1,0:T(8,128)S(1)}, f32[64,128]{1,0:T(8,128)S(1)}, u32[]{:S(2)}, u32[]{:S(2)}) collective-permute-start(f32[64,128]{1,0:T(8,128)S(1)} %get-tuple-element.15.refs_0_), channel_id=1, source_target_pairs={{0,4},{1,5},{2,6},{3,7},{4,0},{5,1},{6,2},{7,3},{8,12},{9,13},{10,... | collective-permute-start | bytes 98312 | tf_op jit(solution)/shard_map/ppermute | solution.py:813
  11.1 0.2 collective-permute-start.6
  11.3 0.3 %shard_map.78.parts_in = f32[3840,128]{1,0:T(8,128)S(1)} custom-call(f32[3840,128]{1,0:T(8,128)S(1)} %get-tuple-element.9.lifted), custom_call_target="tpu_custom_call" | custom-call | tf_op jit(solution)/shard_map/pallas_call | solution.py:371
  11.6 0.3 %collective-permute-done.north.north_mask = f32[13,8,128]{2,1,0:T(8,128)S(1)} collective-permute-done((f32[13,8,128]{2,1,0:T(8,128)S(1)}, f32[13,8,128]{2,1,0:T(8,128)S(1)}, u32[]{:S(2)}, u32[]{:S(2)}) %collective-permute-start) | collective-permute-done | bytes 53280 | tf_op jit(solution)/shard_map/ppermute | solution.py:809
  12.0 1.1 %shard_map.79 = (f32[3840,128]{1,0:T(8,128)S(1)}, f32[152,128]{1,0:T(8,128)S(1)}) custom-call(f32[3840,128]{1,0:T(8,128)S(1)} %shard_map.78.parts_in, f32[3840,128]{1,0:T(8,128)S(1)} %get-tuple-element.9.lifted, f32[13,8,128]{2,1,0:T(8,128)S(1)} %collective-permute-done.north.north_mask, ...), custom_call_target="tpu_custom_call", output_to_operand_aliasing={{0}: (0, {})} | custom-call | flops 20000000000 | bytes 8000000 | tf_op jit(solution)/shard_map/pallas_call | solution.py:436
  13.1 0.0 copy-start
  13.1 0.0 copy-start.1
  13.1 1.7 %collective-permute-start.2 = (f32[152,128]{1,0:T(8,128)S(1)}, f32[152,128]{1,0:T(8,128)S(1)}, u32[]{:S(2)}, u32[]{:S(2)}) collective-permute-start(f32[152,128]{1,0:T(8,128)S(1)} %get-tuple-element.14.refs_4_), channel_id=1, source_target_pairs={{0,7},{1,0},{2,1},{3,2},{4,3},{5,4},{6,5},{7,6},{8,15},{9,8},{10,9... | collective-permute-start | bytes 233480 | tf_op jit(solution)/shard_map/ppermute | solution.py:809
  14.8 0.0 collective-permute-start.3
  14.8 2.1 %collective-permute-done.6.refs_3_ = f32[64,128]{1,0:T(8,128)S(1)} collective-permute-done((f32[64,128]{1,0:T(8,128)S(1)}, f32[64,128]{1,0:T(8,128)S(1)}, u32[]{:S(2)}, u32[]{:S(2)}) %collective-permute-start.6) | collective-permute-done | bytes 32800 | tf_op jit(solution)/shard_map/ppermute | solution.py:813
  16.9 2.0 %collective-permute-start.7 = (f32[256,128]{1,0:T(8,128)S(1)}, f32[256,128]{1,0:T(8,128)S(1)}, u32[]{:S(2)}, u32[]{:S(2)}) collective-permute-start(f32[256,128]{1,0:T(8,128)S(1)} %shard_map.82.refs_0_), channel_id=1, source_target_pairs={{0,8},{8,0},{16,24},{24,16},{1,9},{9,1},{17,25},{25,17},{2,10},{10... | collective-permute-start | bytes 393224 | tf_op jit(solution)/shard_map/ppermute | solution.py:813
  18.9 1.5 %collective-permute-start.8 = (f32[256,128]{1,0:T(8,128)S(1)}, f32[256,128]{1,0:T(8,128)S(1)}, u32[]{:S(2)}, u32[]{:S(2)}) collective-permute-start(f32[256,128]{1,0:T(8,128)S(1)} %shard_map.82.refs_0_), channel_id=1, source_target_pairs={{0,16},{8,24},{16,0},{24,8},{1,17},{9,25},{17,1},{25,9},{2,18},{10... | collective-permute-start | bytes 393224 | tf_op jit(solution)/shard_map/ppermute | solution.py:813
  20.5 0.0 collective-permute-start.9
  20.5 3.6 %shard_map.80.refs_4_ = f32[4608,128]{1,0:T(8,128)S(1)} custom-call(f32[4,24,40,128]{3,2,1,0:T(8,128)S(1)} %bitcast.4, f32[3840,128]{1,0:T(8,128)S(1)} %get-tuple-element.13.flat, f32[152,128]{1,0:T(8,128)S(1)} %collective-permute-done.2.east, f32[152,128]{1,0:T(8,128)S(1)} %collective-permute-done.3.west, f32[2,8,128]{2,1,0:T(8,128)S(1)} %get-tuple-element.12.own_masks, ...), custom_call_target="tpu_custom_call" | custom-call | flops 8000000000 | bytes 8000000 | tf_op jit(solution)/shard_map/pallas_call | solution.py:675
  24.1 0.1 collective-permute-done.8.refs_2_
  24.2 2.1 %collective-permute-done.9.refs_3_ = f32[256,128]{1,0:T(8,128)S(1)} collective-permute-done((f32[256,128]{1,0:T(8,128)S(1)}, f32[256,128]{1,0:T(8,128)S(1)}, u32[]{:S(2)}, u32[]{:S(2)}) %collective-permute-start.9) | collective-permute-done | bytes 131104 | tf_op jit(solution)/shard_map/ppermute | solution.py:813
  26.3 0.3 %shard_map.83.own = f32[4,4,64,128]{3,2,1,0:T(8,128)S(1)} custom-call(f32[256,128]{1,0:T(8,128)S(1)} %shard_map.82.refs_0_, f32[256,128]{1,0:T(8,128)S(1)} %collective-permute-done.7.refs_1_, f32[256,128]{1,0:T(8,128)S(1)} %collective-permute-done.8.refs_2_, f32[256,128]{1,0:T(8,128)S(1)} %collective-permute-done.9.refs_3_, f32[4608,128]{1,0:T(8,128)S(1)} %shard_map.80.refs_4_), custom_call_target="tpu_custom_call" | custom-call | tf_op jit(solution)/shard_map/pallas_call | solution.py:746
  26.7 0.1 collective-permute-start.10
  26.7 1.4 %shard_map.81 = f32[3,16,64,128]{3,2,1,0:T(8,128)} custom-call(f32[4,24,48,128]{3,2,1,0:T(8,128)S(1)} %bitcast.3), custom_call_target="tpu_custom_call" | custom-call | flops 4000000000 | bytes 8000000 | tf_op jit(solution)/shard_map/pallas_call | solution.py:698
  28.1 0.5 %collective-permute-done.10.other = f32[4,4,64,128]{3,2,1,0:T(8,128)S(1)} collective-permute-done((f32[4,4,64,128]{3,2,1,0:T(8,128)S(1)}, f32[4,4,64,128]{3,2,1,0:T(8,128)S(1)}, u32[]{:S(2)}, u32[]{:S(2)}) %collective-permute-start.10) | collective-permute-done | bytes 524320 | tf_op jit(solution)/shard_map/ppermute | solution.py:813
  28.6 1.4 %shard_map.84 = f32[3,4,64,256]{3,2,1,0:T(8,128)} custom-call(f32[4,4,64,128]{3,2,1,0:T(8,128)S(1)} %shard_map.83.own, f32[4,4,64,128]{3,2,1,0:T(8,128)S(1)} %collective-permute-done.10.other), custom_call_target="tpu_custom_call" | custom-call | tf_op jit(solution)/shard_map/pallas_call | solution.py:797
  (10 shorter events, 0.0 us)
Async XLA Ops:
  3.0 9.0 %collective-permute-start.1 = (f32[19,8,128]{2,1,0:T(8,128)S(1)}, f32[19,8,128]{2,1,0:T(8,128)S(1)}, u32[]{:S(2)}, u32[]{:S(2)}) collective-permute-start(f32[19,8,128]{2,1,0:T(8,128)S(1)} %get-tuple-element.11), channel_id=1, source_target_pairs={{0,24},{8,0},{16,8},{24,16},{1,25},{9,1},{17,9},{25,17},{2,26},{10... | collective-permute-start | bytes 233480 | tf_op jit(solution)/shard_map/ppermute | solution.py:809
  6.9 5.0 %collective-permute-start = (f32[13,8,128]{2,1,0:T(8,128)S(1)}, f32[13,8,128]{2,1,0:T(8,128)S(1)}, u32[]{:S(2)}, u32[]{:S(2)}) collective-permute-start(f32[13,8,128]{2,1,0:T(8,128)S(1)} %get-tuple-element.10), channel_id=1, source_target_pairs={{0,8},{8,16},{16,24},{24,0},{1,9},{9,17},{17,25},{25,1},{2,10},{10... | collective-permute-start | bytes 159752 | tf_op jit(solution)/shard_map/ppermute | solution.py:809
  6.9 7.9 %collective-permute-start.4 = (f32[64,128]{1,0:T(8,128)S(1)}, f32[64,128]{1,0:T(8,128)S(1)}, u32[]{:S(2)}, u32[]{:S(2)}) collective-permute-start(f32[64,128]{1,0:T(8,128)S(1)} %get-tuple-element.15.refs_0_), channel_id=1, source_target_pairs={{0,2},{1,3},{2,0},{3,1},{4,6},{5,7},{6,4},{7,5},{8,10},{9,11},{10,... | collective-permute-start | bytes 98312 | tf_op jit(solution)/shard_map/ppermute | solution.py:813
  8.5 6.3 %collective-permute-start.5 = (f32[64,128]{1,0:T(8,128)S(1)}, f32[64,128]{1,0:T(8,128)S(1)}, u32[]{:S(2)}, u32[]{:S(2)}) collective-permute-start(f32[64,128]{1,0:T(8,128)S(1)} %get-tuple-element.15.refs_0_), channel_id=1, source_target_pairs={{0,4},{1,5},{2,6},{3,7},{4,0},{5,1},{6,2},{7,3},{8,12},{9,13},{10,... | collective-permute-start | bytes 98312 | tf_op jit(solution)/shard_map/ppermute | solution.py:813
  11.1 5.8 %collective-permute-start.6 = (f32[64,128]{1,0:T(8,128)S(1)}, f32[64,128]{1,0:T(8,128)S(1)}, u32[]{:S(2)}, u32[]{:S(2)}) collective-permute-start(f32[64,128]{1,0:T(8,128)S(1)} %get-tuple-element.15.refs_0_), channel_id=1, source_target_pairs={{0,6},{1,7},{2,4},{3,5},{4,2},{5,3},{6,0},{7,1},{8,14},{9,15},{10,... | collective-permute-start | bytes 98312 | tf_op jit(solution)/shard_map/ppermute | solution.py:813
  13.1 7.4 %copy-start = (bf16[1280,128]{1,0:T(8,128)(2,1)S(1)}, bf16[1280,128]{1,0:T(8,128)(2,1)}, u32[]{:S(2)}) copy-start(bf16[1280,128]{1,0:T(8,128)(2,1)} %constant.11.clone.narrow) | copy-start | bytes 983044
  13.1 7.4 %copy-start.1 = (bf16[528,256]{1,0:T(8,128)(2,1)S(1)}, bf16[528,256]{1,0:T(8,128)(2,1)}, u32[]{:S(2)}) copy-start(bf16[528,256]{1,0:T(8,128)(2,1)} %constant.10.clone.wide) | copy-start | bytes 811012
  13.1 7.4 %collective-permute-start.2 = (f32[152,128]{1,0:T(8,128)S(1)}, f32[152,128]{1,0:T(8,128)S(1)}, u32[]{:S(2)}, u32[]{:S(2)}) collective-permute-start(f32[152,128]{1,0:T(8,128)S(1)} %get-tuple-element.14.refs_4_), channel_id=1, source_target_pairs={{0,7},{1,0},{2,1},{3,2},{4,3},{5,4},{6,5},{7,6},{8,15},{9,8},{10,9... | collective-permute-start | bytes 233480 | tf_op jit(solution)/shard_map/ppermute | solution.py:809
  14.8 5.7 %collective-permute-start.3 = (f32[152,128]{1,0:T(8,128)S(1)}, f32[152,128]{1,0:T(8,128)S(1)}, u32[]{:S(2)}, u32[]{:S(2)}) collective-permute-start(f32[152,128]{1,0:T(8,128)S(1)} %get-tuple-element.14.refs_4_), channel_id=1, source_target_pairs={{0,1},{1,2},{2,3},{3,4},{4,5},{5,6},{6,7},{7,0},{8,9},{9,10},{10,1... | collective-permute-start | bytes 233480 | tf_op jit(solution)/shard_map/ppermute | solution.py:809
  16.9 7.2 %collective-permute-start.7 = (f32[256,128]{1,0:T(8,128)S(1)}, f32[256,128]{1,0:T(8,128)S(1)}, u32[]{:S(2)}, u32[]{:S(2)}) collective-permute-start(f32[256,128]{1,0:T(8,128)S(1)} %shard_map.82.refs_0_), channel_id=1, source_target_pairs={{0,8},{8,0},{16,24},{24,16},{1,9},{9,1},{17,25},{25,17},{2,10},{10... | collective-permute-start | bytes 393224 | tf_op jit(solution)/shard_map/ppermute | solution.py:813
  18.9 5.3 %collective-permute-start.8 = (f32[256,128]{1,0:T(8,128)S(1)}, f32[256,128]{1,0:T(8,128)S(1)}, u32[]{:S(2)}, u32[]{:S(2)}) collective-permute-start(f32[256,128]{1,0:T(8,128)S(1)} %shard_map.82.refs_0_), channel_id=1, source_target_pairs={{0,16},{8,24},{16,0},{24,8},{1,17},{9,25},{17,1},{25,9},{2,18},{10... | collective-permute-start | bytes 393224 | tf_op jit(solution)/shard_map/ppermute | solution.py:813
  20.5 5.9 %collective-permute-start.9 = (f32[256,128]{1,0:T(8,128)S(1)}, f32[256,128]{1,0:T(8,128)S(1)}, u32[]{:S(2)}, u32[]{:S(2)}) collective-permute-start(f32[256,128]{1,0:T(8,128)S(1)} %shard_map.82.refs_0_), channel_id=1, source_target_pairs={{0,24},{8,16},{16,8},{24,0},{1,25},{9,17},{17,9},{25,1},{2,26},{10... | collective-permute-start | bytes 393224 | tf_op jit(solution)/shard_map/ppermute | solution.py:813
  26.7 2.0 %collective-permute-start.10 = (f32[4,4,64,128]{3,2,1,0:T(8,128)S(1)}, f32[4,4,64,128]{3,2,1,0:T(8,128)S(1)}, u32[]{:S(2)}, u32[]{:S(2)}) collective-permute-start(f32[4,4,64,128]{3,2,1,0:T(8,128)S(1)} %shard_map.83.own), channel_id=1, source_target_pairs={{0,1},{1,0},{2,3},{3,2},{4,5},{5,4},{6,7},{7,6},{8,9},{9,8},{10,11... | collective-permute-start | bytes 1572872 | tf_op jit(solution)/shard_map/ppermute | solution.py:813

commit v6 on v5

--- a/solution.py
+++ b/solution.py
@@ -446,7 +446,7 @@
 
 
 def join_kernel(*refs):
-    shares, out = refs[:-2], refs[-1]
+    shares, out = refs[-3::-1], refs[-1]
     for n, piece in enumerate(shares):
         out[64 * n : 64 * (n + 1), :] = piece[...]
 
@@ -460,7 +460,7 @@
         out_specs=vmem,
         cost_estimate=cost(20),
         compiler_params=pltpu.CompilerParams(vmem_limit_bytes=VMEM_LIMIT),
-    )(*shares, after)
+    )(*shares[::-1], after)
 
 
 def mask_lanes(west, east, own_masks, north_mask, south_mask, wide):
@@ -498,15 +498,19 @@
     back, forward2, inverse2 = narrow.at[768:1024], narrow.at[1024:1152], narrow.at[1152:1280]
     lanes = mask_lanes(west, east, own_masks, north_mask, south_mask, wide)
     lane64 = lax.broadcasted_iota(jnp.int32, (1, NL), 1) < 64
-    forward2_f = forward2[...].astype(F32)
-    for ib in range(4):
-        for n in range(4):
-            b = 8 * ib + 4 * (n // 2) + n % 2 - 1
-            smooth_two = lanes[b : b + 1, NL:] if n else jnp.ones((1, NL), F32)
-            row = jnp.where(lane64, smooth_two, lanes[b + 2 : b + 3, NL:])
-            both = dot((forward2_f * row).astype(BF16), inverse2[...]).astype(BF16)
-            gain2[ib, n, 0:128, :] = both
-            gain2[ib, n, 128:256, :] = both
+    needed = [(ib, n) for ib in range(4) for n in range(4) if ib or n % 2]
+    forward2_f = forward2[0:80, :].astype(F32)
+    masked = []
+    for ib, n in needed:
+        b = 8 * ib + 4 * (n // 2) + n % 2 - 1
+        smooth_two = lanes[b : b + 1, NL:] if n else jnp.ones((1, NL), F32)
+        row = jnp.where(lane64, smooth_two, lanes[b + 2 : b + 3, NL:])
+        masked.append((forward2_f * row).astype(BF16))
+    both = dot(jnp.concatenate(masked, 0), inverse2[...]).astype(BF16)
+    for i, (ib, n) in enumerate(needed):
+        for half in (0, 128):
+            gain2[ib, n, half : half + 80, :] = both[80 * i : 80 * i + 80]
+            gain2[ib, n, half + 80 : half + 128, :] = jnp.zeros((48, NL), BF16)
 
     for at, count in ((0, 16), (16, 16), (32, 8)):
         part = dot(own_terms(parts.at[0], at, count), smooth_own[...])
@@ -540,7 +544,8 @@
             if t < 2:
                 kept2[n, :, 8 + 8 * t : 16 + 8 * t, :] = dot(terms, gain2[t + 1, n]).reshape(NV * 4, 8, NL)
             else:
-                kept2[n, :, 0:8, :] = dot(terms, gain2[0, n]).reshape(NV * 4, 8, NL)
+                if n % 2:
+                    kept2[n, :, 0:8, :] = dot(terms, gain2[0, n]).reshape(NV * 4, 8, NL)
                 kept2[n, :, 24:32, :] = dot(terms, gain2[3, n]).reshape(NV * 4, 8, NL)
 
     def back_two(v, _):
@@ -571,18 +576,20 @@
     forward_f = wide[0:144, :].astype(F32)
     for ib in range(4):
         sides_wide[ib] = jnp.zeros((NL, 4 * NL), F32)
-    for ib in range(4):
-        for n in range(4):
-            b = 8 * ib + 4 * (n // 2) + n % 2 - 1
-            smooth_one = lanes[b : b + 1, 0:NL] if n else jnp.zeros((1, NL), F32)
-            row = jnp.concatenate([smooth_one, lanes[b + 2 : b + 3, 0:NL]], 1)
-            both = dot((forward_f * row).astype(BF16), inverse[...])
-            main = both[0:128].astype(BF16)
-            gain[ib, n, 0:128, :] = main
-            gain[ib, n, 128:256, :] = main
-            for i in range(3):
-                at = 24 * n + 8 * i
-                sides_wide[ib, at : at + 1, n * NL : (n + 1) * NL] = both[128 + i : 129 + i]
+    masked = []
+    for ib, n in needed:
+        b = 8 * ib + 4 * (n // 2) + n % 2 - 1
+        smooth_one = lanes[b : b + 1, 0:NL] if n else jnp.zeros((1, NL), F32)
+        row = jnp.concatenate([smooth_one, lanes[b + 2 : b + 3, 0:NL]], 1)
+        masked.append((forward_f * row).astype(BF16))
+    both = dot(jnp.concatenate(masked, 0), inverse[...])
+    for i, (ib, n) in enumerate(needed):
+        main = both[144 * i : 144 * i + 128].astype(BF16)
+        gain[ib, n, 0:128, :] = main
+        gain[ib, n, 128:256, :] = main
+        for j in range(3):
+            at = 24 * n + 8 * j
+            sides_wide[ib, at : at + 1, n * NL : (n + 1) * NL] = both[144 * i + 128 + j : 144 * i + 129 + j]
 
     gain_sides = []
     for ib in range(4):
@@ -707,7 +714,7 @@
 
 
 def rows_kernel(count_x, count_z, *refs):
-    shares, out = refs[:count_x], refs[count_x + 1]
+    shares, out = refs[count_x - 1 :: -1], refs[count_x + 1]
     me, me_y = lax.axis_index("gx"), lax.axis_index("gy")
     row = lax.broadcasted_iota(jnp.int32, (8, NL), 0)
     lane = lax.broadcasted_iota(jnp.int32, (8, NL), 1)
@@ -749,7 +756,7 @@
         in_specs=[vmem] * count_x + [pl.BlockSpec(memory_space=pl.ANY)],
         out_specs=vmem,
         compiler_params=pltpu.CompilerParams(vmem_limit_bytes=VMEM_LIMIT),
-    )(*pieces, after)
+    )(*pieces[::-1], after)
 
 
 def coarse_kernel(count_x, count_y, own, other, out_hbm, out, sems):

time: 30.2 us -> 28 us (0.927)
  waiting for transfers between devices: 5.17 us -> 2.84 us
    ppermute x7, waiting for transfers between devices: 4.85 us -> 1.09 us  [swapped(): lax.ppermute(x, axis, [(i, i ^ distance) for i in range(lax.axis_size(axi...]
    ppermute x4, waiting for transfers between devices: 0.32 us -> 1.75 us  [shifted(): lax.ppermute(x, axis, [(i, (i + step) % count) for i in range(count)])]
  transfers between devices with their start and end apart: 11 -> 11, of which waited for: 5 -> 4; matrix products, arithmetic and copies ran while one was open for 0% -> 0% of each run, Pallas kernels for 21% -> 23%
where the time goes in v6:
time: 28 us; the launch traced here: 27.8 us
  starting transfers between devices  13.7 us (49%)
  Pallas kernels  10.5 us (38%)
  waiting for transfers between devices  2.84 us (10%)
  between operations  0.72 us (3%)
    ppermute x7, starting transfers between devices, swapped(): lax.ppermute(x, axis, [(i, i ^ distance) for i in range(lax.axis_size(axi...  8.09 us
    ppermute x4, starting transfers between devices, shifted(): lax.ppermute(x, axis, [(i, (i + step) % count) for i in range(count)])  5.63 us
    pallas_call x1, Pallas kernels, main_step(): pl.pallas_call(main_kernel, grid=(1,), out_shape=jax.ShapeDtypeStruct((4...  3.66 us
    pallas_call x1, Pallas kernels, first_step(): pl.pallas_call(first_kernel, out_shape=[jax.ShapeDtypeStruct(s, F32) for...  2.33 us
    ppermute x4, waiting for transfers between devices, shifted(): lax.ppermute(x, axis, [(i, (i + step) % count) for i in range(count)])  1.75 us
    pallas_call x1, Pallas kernels, coarse_step(): pl.pallas_call(functools.partial(coarse_kernel, count_x, count_y), out_sh...  1.37 us
    pallas_call x1, Pallas kernels, cells_step(): pl.pallas_call(cells_kernel, out_shape=jax.ShapeDtypeStruct(shape, F32),...  1.37 us
    pallas_call x1, Pallas kernels, edge_step(): pl.pallas_call(edge_kernel, out_shape=[jax.ShapeDtypeStruct(s, F32) for s...  1.14 us
  transfers between devices with their start and end apart: 11, of which 4 were waited for; matrix products, arithmetic and copies ran while one was open for 0% of the time, Pallas kernels for 23%

profile of v6, /device:TPU:0, one launch (start us, length us, event | category | flops | bytes accessed | tf_op | source)
XLA Modules:
  0.0 27.8 jit_solution(2688207143307793444)
XLA Ops:
  0.6 2.3 %shard_map.77 = (f32[3840,128]{1,0:T(8,128)S(1)}, f32[19,8,128]{2,1,0:T(8,128)S(1)}, f32[13,8,128]{2,1,0:T(8,128)S(1)}, f32[2,8,128]{2,1,0:T(8,128)S(1)}, f32[64,128]{1,0:T(8,128)S(1)}) custom-call(f32[3,16,64,128]{3,2,1,0:T(8,128)} %field.1, s32[2,2,4,7]{3,2,1,0:T(4,128)} %bitcast.5, bf16[400,128]{1,0:T(8,128)(2,1)} %constant.8.clone.table_hbm), custom_call_target="tpu_custom_call" | custom-call | tf_op jit(solution)/shard_map/pallas_call | solution.py:335
  3.0 3.9 %collective-permute-start.1 = (f32[19,8,128]{2,1,0:T(8,128)S(1)}, f32[19,8,128]{2,1,0:T(8,128)S(1)}, u32[]{:S(2)}, u32[]{:S(2)}) collective-permute-start(f32[19,8,128]{2,1,0:T(8,128)S(1)} %get-tuple-element.11), channel_id=1, source_target_pairs={{0,24},{8,0},{16,8},{24,16},{1,25},{9,1},{17,9},{25,17},{2,26},{10... | collective-permute-start | bytes 233480 | tf_op jit(solution)/shard_map/ppermute | solution.py:816
  6.9 0.0 collective-permute-start
  6.9 3.6 %collective-permute-start.4 = (f32[64,128]{1,0:T(8,128)S(1)}, f32[64,128]{1,0:T(8,128)S(1)}, u32[]{:S(2)}, u32[]{:S(2)}) collective-permute-start(f32[64,128]{1,0:T(8,128)S(1)} %get-tuple-element.15.refs_3_), channel_id=1, source_target_pairs={{0,6},{1,7},{2,4},{3,5},{4,2},{5,3},{6,0},{7,1},{8,14},{9,15},{10,... | collective-permute-start | bytes 98312 | tf_op jit(solution)/shard_map/ppermute | solution.py:820
  10.5 0.0 collective-permute-start.5
  10.5 0.8 %collective-permute-start.6 = (f32[64,128]{1,0:T(8,128)S(1)}, f32[64,128]{1,0:T(8,128)S(1)}, u32[]{:S(2)}, u32[]{:S(2)}) collective-permute-start(f32[64,128]{1,0:T(8,128)S(1)} %get-tuple-element.15.refs_3_), channel_id=1, source_target_pairs={{0,2},{1,3},{2,0},{3,1},{4,6},{5,7},{6,4},{7,5},{8,10},{9,11},{10,... | collective-permute-start | bytes 98312 | tf_op jit(solution)/shard_map/ppermute | solution.py:820
  11.3 0.3 %shard_map.78.parts_in = f32[3840,128]{1,0:T(8,128)S(1)} custom-call(f32[3840,128]{1,0:T(8,128)S(1)} %get-tuple-element.9.lifted), custom_call_target="tpu_custom_call" | custom-call | tf_op jit(solution)/shard_map/pallas_call | solution.py:371
  11.6 0.3 %collective-permute-done.north.north_mask = f32[13,8,128]{2,1,0:T(8,128)S(1)} collective-permute-done((f32[13,8,128]{2,1,0:T(8,128)S(1)}, f32[13,8,128]{2,1,0:T(8,128)S(1)}, u32[]{:S(2)}, u32[]{:S(2)}) %collective-permute-start) | collective-permute-done | bytes 53280 | tf_op jit(solution)/shard_map/ppermute | solution.py:816
  12.0 1.1 %shard_map.79 = (f32[3840,128]{1,0:T(8,128)S(1)}, f32[152,128]{1,0:T(8,128)S(1)}) custom-call(f32[3840,128]{1,0:T(8,128)S(1)} %shard_map.78.parts_in, f32[3840,128]{1,0:T(8,128)S(1)} %get-tuple-element.9.lifted, f32[13,8,128]{2,1,0:T(8,128)S(1)} %collective-permute-done.north.north_mask, ...), custom_call_target="tpu_custom_call", output_to_operand_aliasing={{0}: (0, {})} | custom-call | flops 20000000000 | bytes 8000000 | tf_op jit(solution)/shard_map/pallas_call | solution.py:436
  13.1 0.0 copy-start
  13.1 0.0 copy-start.1
  13.1 1.7 %collective-permute-start.2 = (f32[152,128]{1,0:T(8,128)S(1)}, f32[152,128]{1,0:T(8,128)S(1)}, u32[]{:S(2)}, u32[]{:S(2)}) collective-permute-start(f32[152,128]{1,0:T(8,128)S(1)} %get-tuple-element.14.refs_4_), channel_id=1, source_target_pairs={{0,7},{1,0},{2,1},{3,2},{4,3},{5,4},{6,5},{7,6},{8,15},{9,8},{10,9... | collective-permute-start | bytes 233480 | tf_op jit(solution)/shard_map/ppermute | solution.py:816
  14.8 0.5 %collective-permute-done.5.refs_1_ = f32[64,128]{1,0:T(8,128)S(1)} collective-permute-done((f32[64,128]{1,0:T(8,128)S(1)}, f32[64,128]{1,0:T(8,128)S(1)}, u32[]{:S(2)}, u32[]{:S(2)}) %collective-permute-start.5) | collective-permute-done | bytes 32800 | tf_op jit(solution)/shard_map/ppermute | solution.py:820
  15.4 3.0 %collective-permute-start.7 = (f32[256,128]{1,0:T(8,128)S(1)}, f32[256,128]{1,0:T(8,128)S(1)}, u32[]{:S(2)}, u32[]{:S(2)}) collective-permute-start(f32[256,128]{1,0:T(8,128)S(1)} %shard_map.82.refs_3_), channel_id=1, source_target_pairs={{0,24},{8,16},{16,8},{24,0},{1,25},{9,17},{17,9},{25,1},{2,26},{10... | collective-permute-start | bytes 393224 | tf_op jit(solution)/shard_map/ppermute | solution.py:820
  18.3 0.5 %collective-permute-start.8 = (f32[256,128]{1,0:T(8,128)S(1)}, f32[256,128]{1,0:T(8,128)S(1)}, u32[]{:S(2)}, u32[]{:S(2)}) collective-permute-start(f32[256,128]{1,0:T(8,128)S(1)} %shard_map.82.refs_3_), channel_id=1, source_target_pairs={{0,16},{8,24},{16,0},{24,8},{1,17},{9,25},{17,1},{25,9},{2,18},{10... | collective-permute-start | bytes 393224 | tf_op jit(solution)/shard_map/ppermute | solution.py:820
  18.8 0.1 collective-permute-start.9
  19.0 1.4 %collective-permute-done.3.west = f32[152,128]{1,0:T(8,128)S(1)} collective-permute-done((f32[152,128]{1,0:T(8,128)S(1)}, f32[152,128]{1,0:T(8,128)S(1)}, u32[]{:S(2)}, u32[]{:S(2)}) %collective-permute-start.3) | collective-permute-done | bytes 77856 | tf_op jit(solution)/shard_map/ppermute | solution.py:816
  20.4 3.7 %shard_map.80.refs_4_ = f32[4608,128]{1,0:T(8,128)S(1)} custom-call(f32[4,24,40,128]{3,2,1,0:T(8,128)S(1)} %bitcast.4, f32[3840,128]{1,0:T(8,128)S(1)} %get-tuple-element.13.flat, f32[152,128]{1,0:T(8,128)S(1)} %collective-permute-done.2.east, f32[152,128]{1,0:T(8,128)S(1)} %collective-permute-done.3.west, f32[2,8,128]{2,1,0:T(8,128)S(1)} %get-tuple-element.12.own_masks, ...), custom_call_target="tpu_custom_call" | custom-call | flops 8000000000 | bytes 8000000 | tf_op jit(solution)/shard_map/pallas_call | solution.py:682
  24.1 0.0 collective-permute-done.8.refs_1_
  24.1 0.3 %shard_map.83.own = f32[4,4,64,128]{3,2,1,0:T(8,128)S(1)} custom-call(f32[256,128]{1,0:T(8,128)S(1)} %collective-permute-done.7.refs_0_, f32[256,128]{1,0:T(8,128)S(1)} %collective-permute-done.8.refs_1_, f32[256,128]{1,0:T(8,128)S(1)} %collective-permute-done.9.refs_2_, f32[256,128]{1,0:T(8,128)S(1)} %shard_map.82.refs_3_, f32[4608,128]{1,0:T(8,128)S(1)} %shard_map.80.refs_4_), custom_call_target="tpu_custom_call" | custom-call | tf_op jit(solution)/shard_map/pallas_call | solution.py:753
  24.5 0.1 collective-permute-start.10
  24.5 1.4 %shard_map.81 = f32[3,16,64,128]{3,2,1,0:T(8,128)} custom-call(f32[4,24,48,128]{3,2,1,0:T(8,128)S(1)} %bitcast.3), custom_call_target="tpu_custom_call" | custom-call | flops 4000000000 | bytes 8000000 | tf_op jit(solution)/shard_map/pallas_call | solution.py:705
  25.9 0.5 %collective-permute-done.10.other = f32[4,4,64,128]{3,2,1,0:T(8,128)S(1)} collective-permute-done((f32[4,4,64,128]{3,2,1,0:T(8,128)S(1)}, f32[4,4,64,128]{3,2,1,0:T(8,128)S(1)}, u32[]{:S(2)}, u32[]{:S(2)}) %collective-permute-start.10) | collective-permute-done | bytes 524320 | tf_op jit(solution)/shard_map/ppermute | solution.py:820
  26.4 1.4 %shard_map.84 = f32[3,4,64,256]{3,2,1,0:T(8,128)} custom-call(f32[4,4,64,128]{3,2,1,0:T(8,128)S(1)} %shard_map.83.own, f32[4,4,64,128]{3,2,1,0:T(8,128)S(1)} %collective-permute-done.10.other), custom_call_target="tpu_custom_call" | custom-call | tf_op jit(solution)/shard_map/pallas_call | solution.py:804
  (10 shorter events, 0.0 us)
Async XLA Ops:
  3.0 9.0 %collective-permute-start.1 = (f32[19,8,128]{2,1,0:T(8,128)S(1)}, f32[19,8,128]{2,1,0:T(8,128)S(1)}, u32[]{:S(2)}, u32[]{:S(2)}) collective-permute-start(f32[19,8,128]{2,1,0:T(8,128)S(1)} %get-tuple-element.11), channel_id=1, source_target_pairs={{0,24},{8,0},{16,8},{24,16},{1,25},{9,1},{17,9},{25,17},{2,26},{10... | collective-permute-start | bytes 233480 | tf_op jit(solution)/shard_map/ppermute | solution.py:816
  6.9 5.0 %collective-permute-start = (f32[13,8,128]{2,1,0:T(8,128)S(1)}, f32[13,8,128]{2,1,0:T(8,128)S(1)}, u32[]{:S(2)}, u32[]{:S(2)}) collective-permute-start(f32[13,8,128]{2,1,0:T(8,128)S(1)} %get-tuple-element.10), channel_id=1, source_target_pairs={{0,8},{8,16},{16,24},{24,0},{1,9},{9,17},{17,25},{25,1},{2,10},{10... | collective-permute-start | bytes 159752 | tf_op jit(solution)/shard_map/ppermute | solution.py:816
  6.9 7.9 %collective-permute-start.4 = (f32[64,128]{1,0:T(8,128)S(1)}, f32[64,128]{1,0:T(8,128)S(1)}, u32[]{:S(2)}, u32[]{:S(2)}) collective-permute-start(f32[64,128]{1,0:T(8,128)S(1)} %get-tuple-element.15.refs_3_), channel_id=1, source_target_pairs={{0,6},{1,7},{2,4},{3,5},{4,2},{5,3},{6,0},{7,1},{8,14},{9,15},{10,... | collective-permute-start | bytes 98312 | tf_op jit(solution)/shard_map/ppermute | solution.py:820
  10.5 4.8 %collective-permute-start.5 = (f32[64,128]{1,0:T(8,128)S(1)}, f32[64,128]{1,0:T(8,128)S(1)}, u32[]{:S(2)}, u32[]{:S(2)}) collective-permute-start(f32[64,128]{1,0:T(8,128)S(1)} %get-tuple-element.15.refs_3_), channel_id=1, source_target_pairs={{0,4},{1,5},{2,6},{3,7},{4,0},{5,1},{6,2},{7,3},{8,12},{9,13},{10,... | collective-permute-start | bytes 98312 | tf_op jit(solution)/shard_map/ppermute | solution.py:820
  10.5 4.8 %collective-permute-start.6 = (f32[64,128]{1,0:T(8,128)S(1)}, f32[64,128]{1,0:T(8,128)S(1)}, u32[]{:S(2)}, u32[]{:S(2)}) collective-permute-start(f32[64,128]{1,0:T(8,128)S(1)} %get-tuple-element.15.refs_3_), channel_id=1, source_target_pairs={{0,2},{1,3},{2,0},{3,1},{4,6},{5,7},{6,4},{7,5},{8,10},{9,11},{10,... | collective-permute-start | bytes 98312 | tf_op jit(solution)/shard_map/ppermute | solution.py:820
  13.1 7.3 %copy-start = (bf16[1280,128]{1,0:T(8,128)(2,1)S(1)}, bf16[1280,128]{1,0:T(8,128)(2,1)}, u32[]{:S(2)}) copy-start(bf16[1280,128]{1,0:T(8,128)(2,1)} %constant.11.clone.narrow) | copy-start | bytes 983044
  13.1 7.3 %copy-start.1 = (bf16[528,256]{1,0:T(8,128)(2,1)S(1)}, bf16[528,256]{1,0:T(8,128)(2,1)}, u32[]{:S(2)}) copy-start(bf16[528,256]{1,0:T(8,128)(2,1)} %constant.10.clone.wide) | copy-start | bytes 811012
  13.1 5.9 %collective-permute-start.2 = (f32[152,128]{1,0:T(8,128)S(1)}, f32[152,128]{1,0:T(8,128)S(1)}, u32[]{:S(2)}, u32[]{:S(2)}) collective-permute-start(f32[152,128]{1,0:T(8,128)S(1)} %get-tuple-element.14.refs_4_), channel_id=1, source_target_pairs={{0,7},{1,0},{2,1},{3,2},{4,3},{5,4},{6,5},{7,6},{8,15},{9,8},{10,9... | collective-permute-start | bytes 233480 | tf_op jit(solution)/shard_map/ppermute | solution.py:816
  14.8 5.6 %collective-permute-start.3 = (f32[152,128]{1,0:T(8,128)S(1)}, f32[152,128]{1,0:T(8,128)S(1)}, u32[]{:S(2)}, u32[]{:S(2)}) collective-permute-start(f32[152,128]{1,0:T(8,128)S(1)} %get-tuple-element.14.refs_4_), channel_id=1, source_target_pairs={{0,1},{1,2},{2,3},{3,4},{4,5},{5,6},{6,7},{7,0},{8,9},{9,10},{10,1... | collective-permute-start | bytes 233480 | tf_op jit(solution)/shard_map/ppermute | solution.py:816
  15.4 8.7 %collective-permute-start.7 = (f32[256,128]{1,0:T(8,128)S(1)}, f32[256,128]{1,0:T(8,128)S(1)}, u32[]{:S(2)}, u32[]{:S(2)}) collective-permute-start(f32[256,128]{1,0:T(8,128)S(1)} %shard_map.82.refs_3_), channel_id=1, source_target_pairs={{0,24},{8,16},{16,8},{24,0},{1,25},{9,17},{17,9},{25,1},{2,26},{10... | collective-permute-start | bytes 393224 | tf_op jit(solution)/shard_map/ppermute | solution.py:820
  18.3 5.8 %collective-permute-start.8 = (f32[256,128]{1,0:T(8,128)S(1)}, f32[256,128]{1,0:T(8,128)S(1)}, u32[]{:S(2)}, u32[]{:S(2)}) collective-permute-start(f32[256,128]{1,0:T(8,128)S(1)} %shard_map.82.refs_3_), channel_id=1, source_target_pairs={{0,16},{8,24},{16,0},{24,8},{1,17},{9,25},{17,1},{25,9},{2,18},{10... | collective-permute-start | bytes 393224 | tf_op jit(solution)/shard_map/ppermute | solution.py:820
  18.8 5.3 %collective-permute-start.9 = (f32[256,128]{1,0:T(8,128)S(1)}, f32[256,128]{1,0:T(8,128)S(1)}, u32[]{:S(2)}, u32[]{:S(2)}) collective-permute-start(f32[256,128]{1,0:T(8,128)S(1)} %shard_map.82.refs_3_), channel_id=1, source_target_pairs={{0,8},{8,0},{16,24},{24,16},{1,9},{9,1},{17,25},{25,17},{2,10},{10... | collective-permute-start | bytes 393224 | tf_op jit(solution)/shard_map/ppermute | solution.py:820
  24.5 2.0 %collective-permute-start.10 = (f32[4,4,64,128]{3,2,1,0:T(8,128)S(1)}, f32[4,4,64,128]{3,2,1,0:T(8,128)S(1)}, u32[]{:S(2)}, u32[]{:S(2)}) collective-permute-start(f32[4,4,64,128]{3,2,1,0:T(8,128)S(1)} %shard_map.83.own), channel_id=1, source_target_pairs={{0,1},{1,0},{2,3},{3,2},{4,5},{5,4},{6,7},{7,6},{8,9},{9,8},{10,11... | collective-permute-start | bytes 1572872 | tf_op jit(solution)/shard_map/ppermute | solution.py:820

commit v7 on v5

--- a/solution.py
+++ b/solution.py
@@ -257,7 +257,7 @@
         lifted[p * PITCH + 72 : p * PITCH + 80, :] = jnp.zeros((8, NL), F32)
     for copy in small:
         copy.wait()
-    for i, out, tile in ((0, up, 18), (1, down, 12)):
+    for i, out, tile in ((0, up, 15), (1, down, 9)):
         total = jnp.zeros((7, NL), F32)
         for l in range(2):
             flags = masks[l, i].astype(F32).astype(BF16)
@@ -283,20 +283,18 @@
 
             x = [row(j) for j in range(7 if bz == 0 else 3)]
             first = x[1] - 0.5 * (x[0] + x[2])
-            up[v * 6 + bz] = x[0]
-            up[v * 6 + 2 + bz] = first
+            up[v * 5 + bz] = x[0]
+            up[v * 5 + 2 + bz] = first
             y = {j: row(j) for j in (range(58, 64) if bz == 0 else (62, 63))}
             part = y[63] - 0.5 * y[62]
-            down[v * 4 + bz] = part
+            down[v * 3 + bz] = part
             if bz == 0:
                 second = x[3] - 0.5 * (x[2] + x[4])
                 third = x[5] - 0.5 * (x[4] + x[6])
-                up[v * 6 + 4] = x[2] + 0.25 * (first + second)
-                up[v * 6 + 5] = x[4] + 0.25 * (second + third)
+                up[v * 5 + 4] = x[2] + 0.25 * (first + second) - 0.5 * (x[4] + 0.25 * (second + third))
                 before = y[59] - 0.5 * (y[58] + y[60])
                 last = y[61] - 0.5 * (y[60] + y[62])
-                down[v * 4 + 2] = y[60] + 0.25 * (before + last)
-                down[v * 4 + 3] = y[62] + 0.25 * (last + part)
+                down[v * 3 + 2] = y[62] + 0.25 * (last + part) - 0.5 * (y[60] + 0.25 * (before + last))
 
     total = jnp.zeros((80, NL), F32)
     for v in range(NV):
@@ -331,7 +329,7 @@
 
 def first_step(field, masks):
     vmem = pl.BlockSpec(memory_space=pltpu.VMEM)
-    shapes = [(NV * NZ * PITCH, NL), (19, 8, NL), (13, 8, NL), (2, 8, NL), (64, NL)]
+    shapes = [(NV * NZ * PITCH, NL), (16, 8, NL), (10, 8, NL), (2, 8, NL), (64, NL)]
     return pl.pallas_call(
         first_kernel,
         out_shape=[jax.ShapeDtypeStruct(s, F32) for s in shapes],
@@ -391,7 +389,7 @@
             def at(bx, r):
                 return pl.ds(((2 * bz + bx) * 24 + v * 8) * ROWS + r, 8, stride=ROWS)
 
-            before, after, detail = north[v * 4 + bz], south[v * 6 + bz], south[v * 6 + 2 + bz]
+            before, after, detail = north[v * 3 + bz], south[v * 5 + bz], south[v * 5 + 2 + bz]
             start = cell(0)
             last = cell(63) - 0.5 * (cell(62) + after)
             parts[at(0, 0), :] = parts[at(0, 0), :] + 0.25 * before
@@ -401,10 +399,8 @@
             parts[at(1, 32), :] = detail
             parts[at(1, 39), :] = before - 0.5 * start
             if bz == 0:
-                parts[at(0, 33), :] = south[v * 6 + 4]
-                parts[at(0, 34), :] = south[v * 6 + 5]
-                parts[at(0, 38), :] = north[v * 4 + 2]
-                parts[at(0, 39), :] = north[v * 4 + 3] - 0.125 * start
+                parts[at(0, 33), :] = south[v * 5 + 4]
+                parts[at(0, 39), :] = north[v * 3 + 2] - 0.125 * start
 
     lane = lax.broadcasted_iota(jnp.int32, (8, NL), 1) // 16
 
@@ -424,10 +420,10 @@
     terms = [two_terms(packed[n * 120 : (n + 1) * 120, :]) for n in range(4)]
     high, low = [jnp.concatenate(part, 1) for part in zip(*terms)]
     sides[0:120, :] = dot(high, table[...]) + dot(low, table[...])
-    sides[120:128, :] = north[12]
+    sides[120:128, :] = north[9]
     sides[128:136, :] = own_masks[0]
     sides[136:144, :] = own_masks[1]
-    sides[144:152, :] = south[18]
+    sides[144:152, :] = south[15]
 
 
 def edge_step(parts, lifted, north, south, own_masks):
@@ -446,7 +442,7 @@
 
 
 def join_kernel(*refs):
-    shares, out = refs[:-2], refs[-1]
+    shares, out = refs[-3::-1], refs[-1]
     for n, piece in enumerate(shares):
         out[64 * n : 64 * (n + 1), :] = piece[...]
 
@@ -460,7 +456,7 @@
         out_specs=vmem,
         cost_estimate=cost(20),
         compiler_params=pltpu.CompilerParams(vmem_limit_bytes=VMEM_LIMIT),
-    )(*shares, after)
+    )(*shares[::-1], after)
 
 
 def mask_lanes(west, east, own_masks, north_mask, south_mask, wide):
@@ -500,7 +496,7 @@
     lane64 = lax.broadcasted_iota(jnp.int32, (1, NL), 1) < 64
     forward2_f = forward2[...].astype(F32)
     for ib in range(4):
-        for n in range(4):
+        for n in range(4) if ib else (1, 3):
             b = 8 * ib + 4 * (n // 2) + n % 2 - 1
             smooth_two = lanes[b : b + 1, NL:] if n else jnp.ones((1, NL), F32)
             row = jnp.where(lane64, smooth_two, lanes[b + 2 : b + 3, NL:])
@@ -540,7 +536,8 @@
             if t < 2:
                 kept2[n, :, 8 + 8 * t : 16 + 8 * t, :] = dot(terms, gain2[t + 1, n]).reshape(NV * 4, 8, NL)
             else:
-                kept2[n, :, 0:8, :] = dot(terms, gain2[0, n]).reshape(NV * 4, 8, NL)
+                if n % 2:
+                    kept2[n, :, 0:8, :] = dot(terms, gain2[0, n]).reshape(NV * 4, 8, NL)
                 kept2[n, :, 24:32, :] = dot(terms, gain2[3, n]).reshape(NV * 4, 8, NL)
 
     def back_two(v, _):
@@ -572,7 +569,7 @@
     for ib in range(4):
         sides_wide[ib] = jnp.zeros((NL, 4 * NL), F32)
     for ib in range(4):
-        for n in range(4):
+        for n in range(4) if ib else (1, 3):
             b = 8 * ib + 4 * (n // 2) + n % 2 - 1
             smooth_one = lanes[b : b + 1, 0:NL] if n else jnp.zeros((1, NL), F32)
             row = jnp.concatenate([smooth_one, lanes[b + 2 : b + 3, 0:NL]], 1)
@@ -665,7 +662,7 @@
     vmem = pl.BlockSpec(memory_space=pltpu.VMEM)
     return [
         vmem, vmem, vmem, vmem, vmem,
-        pl.BlockSpec((1, 8, NL), lambda i: (12, 0, 0)), pl.BlockSpec((1, 8, NL), lambda i: (18, 0, 0)),
+        pl.BlockSpec((1, 8, NL), lambda i: (9, 0, 0)), pl.BlockSpec((1, 8, NL), lambda i: (15, 0, 0)),
         vmem, vmem,
     ]
 
@@ -707,7 +704,7 @@
 
 
 def rows_kernel(count_x, count_z, *refs):
-    shares, out = refs[:count_x], refs[count_x + 1]
+    shares, out = refs[count_x - 1 :: -1], refs[count_x + 1]
     me, me_y = lax.axis_index("gx"), lax.axis_index("gy")
     row = lax.broadcasted_iota(jnp.int32, (8, NL), 0)
     lane = lax.broadcasted_iota(jnp.int32, (8, NL), 1)
@@ -749,7 +746,7 @@
         in_specs=[vmem] * count_x + [pl.BlockSpec(memory_space=pl.ANY)],
         out_specs=vmem,
         compiler_params=pltpu.CompilerParams(vmem_limit_bytes=VMEM_LIMIT),
-    )(*pieces, after)
+    )(*pieces[::-1], after)
 
 
 def coarse_kernel(count_x, count_y, own, other, out_hbm, out, sems):

time: 30.2 us -> 27.9 us (0.924)
  waiting for transfers between devices: 5.17 us -> 2.77 us
    ppermute x7, waiting for transfers between devices: 4.85 us -> 1.14 us  [swapped(): lax.ppermute(x, axis, [(i, i ^ distance) for i in range(lax.axis_size(axi...]
    ppermute x4, waiting for transfers between devices: 0.32 us -> 1.62 us  [shifted(): lax.ppermute(x, axis, [(i, (i + step) % count) for i in range(count)])]
  transfers between devices with their start and end apart: 11 -> 11, of which waited for: 5 -> 5; matrix products, arithmetic and copies ran while one was open for 0% -> 0% of each run, Pallas kernels for 21% -> 23%
where the time goes in v7:
time: 27.9 us; the launch traced here: 27.7 us
  starting transfers between devices  13.9 us (50%)
  Pallas kernels  10.3 us (37%)
  waiting for transfers between devices  2.77 us (10%)
  between operations  0.72 us (3%)
    ppermute x7, starting transfers between devices, swapped(): lax.ppermute(x, axis, [(i, i ^ distance) for i in range(lax.axis_size(axi...  8.09 us
    ppermute x4, starting transfers between devices, shifted(): lax.ppermute(x, axis, [(i, (i + step) % count) for i in range(count)])  5.76 us
    pallas_call x1, Pallas kernels, main_step(): pl.pallas_call(main_kernel, grid=(1,), out_shape=jax.ShapeDtypeStruct((4...  3.47 us
    pallas_call x1, Pallas kernels, first_step(): pl.pallas_call(first_kernel, out_shape=[jax.ShapeDtypeStruct(s, F32) for...  2.33 us
    ppermute x4, waiting for transfers between devices, shifted(): lax.ppermute(x, axis, [(i, (i + step) % count) for i in range(count)])  1.62 us
    pallas_call x1, Pallas kernels, coarse_step(): pl.pallas_call(functools.partial(coarse_kernel, count_x, count_y), out_sh...  1.37 us
    pallas_call x1, Pallas kernels, cells_step(): pl.pallas_call(cells_kernel, out_shape=jax.ShapeDtypeStruct(shape, F32),...  1.37 us
    ppermute x7, waiting for transfers between devices, swapped(): lax.ppermute(x, axis, [(i, i ^ distance) for i in range(lax.axis_size(axi...  1.14 us
  transfers between devices with their start and end apart: 11, of which 5 were waited for; matrix products, arithmetic and copies ran while one was open for 0% of the time, Pallas kernels for 23%

profile of v7, /device:TPU:0, one launch (start us, length us, event | category | flops | bytes accessed | tf_op | source)
XLA Modules:
  0.0 27.7 jit_solution(8124895926593563807)
XLA Ops:
  0.6 2.3 %shard_map.77 = (f32[3840,128]{1,0:T(8,128)S(1)}, f32[16,8,128]{2,1,0:T(8,128)S(1)}, f32[10,8,128]{2,1,0:T(8,128)S(1)}, f32[2,8,128]{2,1,0:T(8,128)S(1)}, f32[64,128]{1,0:T(8,128)S(1)}) custom-call(f32[3,16,64,128]{3,2,1,0:T(8,128)} %field.1, s32[2,2,4,7]{3,2,1,0:T(4,128)} %bitcast.5, bf16[400,128]{1,0:T(8,128)(2,1)} %constant.8.clone.table_hbm), custom_call_target="tpu_custom_call" | custom-call | tf_op jit(solution)/shard_map/pallas_call | solution.py:333
  3.0 3.9 %collective-permute-start.1 = (f32[16,8,128]{2,1,0:T(8,128)S(1)}, f32[16,8,128]{2,1,0:T(8,128)S(1)}, u32[]{:S(2)}, u32[]{:S(2)}) collective-permute-start(f32[16,8,128]{2,1,0:T(8,128)S(1)} %get-tuple-element.11), channel_id=1, source_target_pairs={{0,24},{8,0},{16,8},{24,16},{1,25},{9,1},{17,9},{25,17},{2,26},{10... | collective-permute-start | bytes 196616 | tf_op jit(solution)/shard_map/ppermute | solution.py:806
  6.9 3.6 %collective-permute-start.4 = (f32[64,128]{1,0:T(8,128)S(1)}, f32[64,128]{1,0:T(8,128)S(1)}, u32[]{:S(2)}, u32[]{:S(2)}) collective-permute-start(f32[64,128]{1,0:T(8,128)S(1)} %get-tuple-element.15.refs_3_), channel_id=1, source_target_pairs={{0,6},{1,7},{2,4},{3,5},{4,2},{5,3},{6,0},{7,1},{8,14},{9,15},{10,... | collective-permute-start | bytes 98312 | tf_op jit(solution)/shard_map/ppermute | solution.py:810
  10.5 0.0 collective-permute-start.5
  10.5 0.8 %collective-permute-start.6 = (f32[64,128]{1,0:T(8,128)S(1)}, f32[64,128]{1,0:T(8,128)S(1)}, u32[]{:S(2)}, u32[]{:S(2)}) collective-permute-start(f32[64,128]{1,0:T(8,128)S(1)} %get-tuple-element.15.refs_3_), channel_id=1, source_target_pairs={{0,2},{1,3},{2,0},{3,1},{4,6},{5,7},{6,4},{7,5},{8,10},{9,11},{10,... | collective-permute-start | bytes 98312 | tf_op jit(solution)/shard_map/ppermute | solution.py:810
  11.3 0.3 %shard_map.78.parts_in = f32[3840,128]{1,0:T(8,128)S(1)} custom-call(f32[3840,128]{1,0:T(8,128)S(1)} %get-tuple-element.9.lifted), custom_call_target="tpu_custom_call" | custom-call | tf_op jit(solution)/shard_map/pallas_call | solution.py:369
  11.6 0.2 collective-permute-done.north.north_mask
  11.8 1.1 %shard_map.79 = (f32[3840,128]{1,0:T(8,128)S(1)}, f32[152,128]{1,0:T(8,128)S(1)}) custom-call(f32[3840,128]{1,0:T(8,128)S(1)} %shard_map.78.parts_in, f32[3840,128]{1,0:T(8,128)S(1)} %get-tuple-element.9.lifted, f32[10,8,128]{2,1,0:T(8,128)S(1)} %collective-permute-done.north.north_mask, ...), custom_call_target="tpu_custom_call", output_to_operand_aliasing={{0}: (0, {})} | custom-call | flops 20000000000 | bytes 8000000 | tf_op jit(solution)/shard_map/pallas_call | solution.py:432
  13.0 0.0 copy-start
  13.0 0.0 copy-start.1
  13.0 1.8 %collective-permute-start.2 = (f32[152,128]{1,0:T(8,128)S(1)}, f32[152,128]{1,0:T(8,128)S(1)}, u32[]{:S(2)}, u32[]{:S(2)}) collective-permute-start(f32[152,128]{1,0:T(8,128)S(1)} %get-tuple-element.14.refs_4_), channel_id=1, source_target_pairs={{0,7},{1,0},{2,1},{3,2},{4,3},{5,4},{6,5},{7,6},{8,15},{9,8},{10,9... | collective-permute-start | bytes 233480 | tf_op jit(solution)/shard_map/ppermute | solution.py:806
  14.8 0.0 collective-permute-start.3
  14.8 0.5 %collective-permute-done.5.refs_1_ = f32[64,128]{1,0:T(8,128)S(1)} collective-permute-done((f32[64,128]{1,0:T(8,128)S(1)}, f32[64,128]{1,0:T(8,128)S(1)}, u32[]{:S(2)}, u32[]{:S(2)}) %collective-permute-start.5) | collective-permute-done | bytes 32800 | tf_op jit(solution)/shard_map/ppermute | solution.py:810
  15.4 3.0 %collective-permute-start.7 = (f32[256,128]{1,0:T(8,128)S(1)}, f32[256,128]{1,0:T(8,128)S(1)}, u32[]{:S(2)}, u32[]{:S(2)}) collective-permute-start(f32[256,128]{1,0:T(8,128)S(1)} %shard_map.82.refs_3_), channel_id=1, source_target_pairs={{0,24},{8,16},{16,8},{24,0},{1,25},{9,17},{17,9},{25,1},{2,26},{10... | collective-permute-start | bytes 393224 | tf_op jit(solution)/shard_map/ppermute | solution.py:810
  18.3 0.5 %collective-permute-start.8 = (f32[256,128]{1,0:T(8,128)S(1)}, f32[256,128]{1,0:T(8,128)S(1)}, u32[]{:S(2)}, u32[]{:S(2)}) collective-permute-start(f32[256,128]{1,0:T(8,128)S(1)} %shard_map.82.refs_3_), channel_id=1, source_target_pairs={{0,16},{8,24},{16,0},{24,8},{1,17},{9,25},{17,1},{25,9},{2,18},{10... | collective-permute-start | bytes 393224 | tf_op jit(solution)/shard_map/ppermute | solution.py:810
  18.8 0.1 collective-permute-start.9
  19.0 1.4 %collective-permute-done.3.west = f32[152,128]{1,0:T(8,128)S(1)} collective-permute-done((f32[152,128]{1,0:T(8,128)S(1)}, f32[152,128]{1,0:T(8,128)S(1)}, u32[]{:S(2)}, u32[]{:S(2)}) %collective-permute-start.3) | collective-permute-done | bytes 77856 | tf_op jit(solution)/shard_map/ppermute | solution.py:806
  20.4 3.5 %shard_map.80.refs_4_ = f32[4608,128]{1,0:T(8,128)S(1)} custom-call(f32[4,24,40,128]{3,2,1,0:T(8,128)S(1)} %bitcast.4, f32[3840,128]{1,0:T(8,128)S(1)} %get-tuple-element.13.flat, f32[152,128]{1,0:T(8,128)S(1)} %collective-permute-done.2.east, f32[152,128]{1,0:T(8,128)S(1)} %collective-permute-done.3.west, f32[2,8,128]{2,1,0:T(8,128)S(1)} %get-tuple-element.12.own_masks, ...), custom_call_target="tpu_custom_call" | custom-call | flops 8000000000 | bytes 8000000 | tf_op jit(solution)/shard_map/pallas_call | solution.py:672
  23.9 0.1 collective-permute-done.8.refs_1_
  24.0 0.3 %shard_map.83.own = f32[4,4,64,128]{3,2,1,0:T(8,128)S(1)} custom-call(f32[256,128]{1,0:T(8,128)S(1)} %collective-permute-done.7.refs_0_, f32[256,128]{1,0:T(8,128)S(1)} %collective-permute-done.8.refs_1_, f32[256,128]{1,0:T(8,128)S(1)} %collective-permute-done.9.refs_2_, f32[256,128]{1,0:T(8,128)S(1)} %shard_map.82.refs_3_, f32[4608,128]{1,0:T(8,128)S(1)} %shard_map.80.refs_4_), custom_call_target="tpu_custom_call" | custom-call | tf_op jit(solution)/shard_map/pallas_call | solution.py:743
  24.3 0.1 collective-permute-start.10
  24.4 1.4 %shard_map.81 = f32[3,16,64,128]{3,2,1,0:T(8,128)} custom-call(f32[4,24,48,128]{3,2,1,0:T(8,128)S(1)} %bitcast.3), custom_call_target="tpu_custom_call" | custom-call | flops 4000000000 | bytes 8000000 | tf_op jit(solution)/shard_map/pallas_call | solution.py:695
  25.8 0.5 %collective-permute-done.10.other = f32[4,4,64,128]{3,2,1,0:T(8,128)S(1)} collective-permute-done((f32[4,4,64,128]{3,2,1,0:T(8,128)S(1)}, f32[4,4,64,128]{3,2,1,0:T(8,128)S(1)}, u32[]{:S(2)}, u32[]{:S(2)}) %collective-permute-start.10) | collective-permute-done | bytes 524320 | tf_op jit(solution)/shard_map/ppermute | solution.py:810
  26.3 1.4 %shard_map.84 = f32[3,4,64,256]{3,2,1,0:T(8,128)} custom-call(f32[4,4,64,128]{3,2,1,0:T(8,128)S(1)} %shard_map.83.own, f32[4,4,64,128]{3,2,1,0:T(8,128)S(1)} %collective-permute-done.10.other), custom_call_target="tpu_custom_call" | custom-call | tf_op jit(solution)/shard_map/pallas_call | solution.py:794
  (10 shorter events, 0.0 us)
Async XLA Ops:
  3.0 8.9 %collective-permute-start.1 = (f32[16,8,128]{2,1,0:T(8,128)S(1)}, f32[16,8,128]{2,1,0:T(8,128)S(1)}, u32[]{:S(2)}, u32[]{:S(2)}) collective-permute-start(f32[16,8,128]{2,1,0:T(8,128)S(1)} %get-tuple-element.11), channel_id=1, source_target_pairs={{0,24},{8,0},{16,8},{24,16},{1,25},{9,1},{17,9},{25,17},{2,26},{10... | collective-permute-start | bytes 196616 | tf_op jit(solution)/shard_map/ppermute | solution.py:806
  6.9 4.9 %collective-permute-start = (f32[10,8,128]{2,1,0:T(8,128)S(1)}, f32[10,8,128]{2,1,0:T(8,128)S(1)}, u32[]{:S(2)}, u32[]{:S(2)}) collective-permute-start(f32[10,8,128]{2,1,0:T(8,128)S(1)} %get-tuple-element.10), channel_id=1, source_target_pairs={{0,8},{8,16},{16,24},{24,0},{1,9},{9,17},{17,25},{25,1},{2,10},{10... | collective-permute-start | bytes 122888 | tf_op jit(solution)/shard_map/ppermute | solution.py:806
  6.9 7.9 %collective-permute-start.4 = (f32[64,128]{1,0:T(8,128)S(1)}, f32[64,128]{1,0:T(8,128)S(1)}, u32[]{:S(2)}, u32[]{:S(2)}) collective-permute-start(f32[64,128]{1,0:T(8,128)S(1)} %get-tuple-element.15.refs_3_), channel_id=1, source_target_pairs={{0,6},{1,7},{2,4},{3,5},{4,2},{5,3},{6,0},{7,1},{8,14},{9,15},{10,... | collective-permute-start | bytes 98312 | tf_op jit(solution)/shard_map/ppermute | solution.py:810
  10.5 4.8 %collective-permute-start.5 = (f32[64,128]{1,0:T(8,128)S(1)}, f32[64,128]{1,0:T(8,128)S(1)}, u32[]{:S(2)}, u32[]{:S(2)}) collective-permute-start(f32[64,128]{1,0:T(8,128)S(1)} %get-tuple-element.15.refs_3_), channel_id=1, source_target_pairs={{0,4},{1,5},{2,6},{3,7},{4,0},{5,1},{6,2},{7,3},{8,12},{9,13},{10,... | collective-permute-start | bytes 98312 | tf_op jit(solution)/shard_map/ppermute | solution.py:810
  10.5 4.8 %collective-permute-start.6 = (f32[64,128]{1,0:T(8,128)S(1)}, f32[64,128]{1,0:T(8,128)S(1)}, u32[]{:S(2)}, u32[]{:S(2)}) collective-permute-start(f32[64,128]{1,0:T(8,128)S(1)} %get-tuple-element.15.refs_3_), channel_id=1, source_target_pairs={{0,2},{1,3},{2,0},{3,1},{4,6},{5,7},{6,4},{7,5},{8,10},{9,11},{10,... | collective-permute-start | bytes 98312 | tf_op jit(solution)/shard_map/ppermute | solution.py:810
  13.0 7.5 %copy-start = (bf16[1280,128]{1,0:T(8,128)(2,1)S(1)}, bf16[1280,128]{1,0:T(8,128)(2,1)}, u32[]{:S(2)}) copy-start(bf16[1280,128]{1,0:T(8,128)(2,1)} %constant.11.clone.narrow) | copy-start | bytes 983044
  13.0 7.5 %copy-start.1 = (bf16[528,256]{1,0:T(8,128)(2,1)S(1)}, bf16[528,256]{1,0:T(8,128)(2,1)}, u32[]{:S(2)}) copy-start(bf16[528,256]{1,0:T(8,128)(2,1)} %constant.10.clone.wide) | copy-start | bytes 811012
  13.0 6.0 %collective-permute-start.2 = (f32[152,128]{1,0:T(8,128)S(1)}, f32[152,128]{1,0:T(8,128)S(1)}, u32[]{:S(2)}, u32[]{:S(2)}) collective-permute-start(f32[152,128]{1,0:T(8,128)S(1)} %get-tuple-element.14.refs_4_), channel_id=1, source_target_pairs={{0,7},{1,0},{2,1},{3,2},{4,3},{5,4},{6,5},{7,6},{8,15},{9,8},{10,9... | collective-permute-start | bytes 233480 | tf_op jit(solution)/shard_map/ppermute | solution.py:806
  14.8 5.6 %collective-permute-start.3 = (f32[152,128]{1,0:T(8,128)S(1)}, f32[152,128]{1,0:T(8,128)S(1)}, u32[]{:S(2)}, u32[]{:S(2)}) collective-permute-start(f32[152,128]{1,0:T(8,128)S(1)} %get-tuple-element.14.refs_4_), channel_id=1, source_target_pairs={{0,1},{1,2},{2,3},{3,4},{4,5},{5,6},{6,7},{7,0},{8,9},{9,10},{10,1... | collective-permute-start | bytes 233480 | tf_op jit(solution)/shard_map/ppermute | solution.py:806
  15.4 8.6 %collective-permute-start.7 = (f32[256,128]{1,0:T(8,128)S(1)}, f32[256,128]{1,0:T(8,128)S(1)}, u32[]{:S(2)}, u32[]{:S(2)}) collective-permute-start(f32[256,128]{1,0:T(8,128)S(1)} %shard_map.82.refs_3_), channel_id=1, source_target_pairs={{0,24},{8,16},{16,8},{24,0},{1,25},{9,17},{17,9},{25,1},{2,26},{10... | collective-permute-start | bytes 393224 | tf_op jit(solution)/shard_map/ppermute | solution.py:810
  18.3 5.7 %collective-permute-start.8 = (f32[256,128]{1,0:T(8,128)S(1)}, f32[256,128]{1,0:T(8,128)S(1)}, u32[]{:S(2)}, u32[]{:S(2)}) collective-permute-start(f32[256,128]{1,0:T(8,128)S(1)} %shard_map.82.refs_3_), channel_id=1, source_target_pairs={{0,16},{8,24},{16,0},{24,8},{1,17},{9,25},{17,1},{25,9},{2,18},{10... | collective-permute-start | bytes 393224 | tf_op jit(solution)/shard_map/ppermute | solution.py:810
  18.8 5.2 %collective-permute-start.9 = (f32[256,128]{1,0:T(8,128)S(1)}, f32[256,128]{1,0:T(8,128)S(1)}, u32[]{:S(2)}, u32[]{:S(2)}) collective-permute-start(f32[256,128]{1,0:T(8,128)S(1)} %shard_map.82.refs_3_), channel_id=1, source_target_pairs={{0,8},{8,0},{16,24},{24,16},{1,9},{9,1},{17,25},{25,17},{2,10},{10... | collective-permute-start | bytes 393224 | tf_op jit(solution)/shard_map/ppermute | solution.py:810
  24.3 2.0 %collective-permute-start.10 = (f32[4,4,64,128]{3,2,1,0:T(8,128)S(1)}, f32[4,4,64,128]{3,2,1,0:T(8,128)S(1)}, u32[]{:S(2)}, u32[]{:S(2)}) collective-permute-start(f32[4,4,64,128]{3,2,1,0:T(8,128)S(1)} %shard_map.83.own), channel_id=1, source_target_pairs={{0,1},{1,0},{2,3},{3,2},{4,5},{5,4},{6,7},{7,6},{8,9},{9,8},{10,11... | collective-permute-start | bytes 1572872 | tf_op jit(solution)/shard_map/ppermute | solution.py:810

commit v8 on v7

--- a/solution.py
+++ b/solution.py
@@ -73,10 +73,11 @@
 
 
 def beyond(n):
-    return {"cell": 24 * n, "after": 24 * n + 8, "before": 24 * n + 16}
-
-
-BEYOND_SMOOTH = {65: 96, 66: 104, -2: 112, -1: 120}
+    return {"cell": 40 + 16 * n, "after": 48 + 16 * n, "before": 8 * n}
+
+
+BEYOND_SMOOTH = {65: 104, -1: 32}
+FROM_WEST = 40
 
 
 def own_row(kind, k, n):
@@ -87,6 +88,8 @@
         if k == 64:
             return {place["after"]: 1.0}
         return {(place["cell"] if y == 128 else y): value for y, value in detail_row(k).items()}
+    if k in (-2, 66):
+        return {}
     if k in BEYOND_SMOOTH:
         row = {128 + BEYOND_SMOOTH[k]: 1.0}
         return combine((1.0, row), (1.0, {0: -0.125})) if k == -1 else row
@@ -133,14 +136,15 @@
     spread = np.zeros((3, 128, 2, 128))
     for k in range(64):
         spread[0, k, 0, k] = 1
-    spread[1, 0, 0, 64] = 1
-    spread[2, 63, 0, 65] = 1
     for k in range(32):
         spread[0, 64 + k, 1, k] = 1
         spread[0, 64 + k, 1, 64 + k] = 1
-    for base in (0, 64):
-        spread[1, 64, 1, base + 32] = 1
-        spread[2, 95, 1, base + 33] = 1
+    for at in range(0, 16, 4):
+        spread[1, at, 0, 64] = 1
+        spread[2, at + 1, 0, 65] = 1
+        for base in (0, 64):
+            spread[1, at + 2, 1, base + 32] = 1
+            spread[2, at + 3, 1, base + 33] = 1
     w["wide"] = np.concatenate([short, spread.reshape(384, 256)], 0)
     own, beside = smooth[:128], smooth[128:]
     w["narrow"] = np.concatenate([inverse, own, own, beside, beside, back, forward2, inverse2], 0)
@@ -157,10 +161,9 @@
         put(n, beyond(n)["cell"], {0: 1.0})
         put(n, beyond(n)["after"], detail_row(0))
         put(n, beyond(n)["before"], part)
-    put(0, BEYOND_SMOOTH[65], smooth_row(1))
-    put(0, BEYOND_SMOOTH[66], smooth_row(2))
-    put(0, BEYOND_SMOOTH[-2], smooth_row(62))
-    put(0, BEYOND_SMOOTH[-1], combine((1.0, {126: 1.0}), (0.25, detail_row(62)), (0.25, part)))
+    put(0, BEYOND_SMOOTH[65], combine((1.0, smooth_row(1)), (-0.5, smooth_row(2))))
+    share = combine((1.0, {126: 1.0}), (0.25, detail_row(62)), (0.25, part))
+    put(0, BEYOND_SMOOTH[-1], combine((1.0, share), (-0.5, smooth_row(62))))
     w["edge"] = edge.reshape(512, 128)
     expand = np.zeros((2, 4, 128))
     for j in range(4):
@@ -375,7 +378,7 @@
     )(lifted)
 
 
-def edge_kernel(parts_in, lifted, north, south, own_masks, table_hbm, parts, sides, packed, table, sem):
+def edge_kernel(parts_in, lifted, north, south, own_masks, table_hbm, parts, to_left, to_right, packed, table, sem):
     copy = pltpu.make_async_copy(table_hbm, table, sem.at[0])
     copy.start()
     for p in range(4 * NV * 8):
@@ -419,21 +422,32 @@
     copy.wait()
     terms = [two_terms(packed[n * 120 : (n + 1) * 120, :]) for n in range(4)]
     high, low = [jnp.concatenate(part, 1) for part in zip(*terms)]
-    sides[0:120, :] = dot(high, table[...]) + dot(low, table[...])
-    sides[120:128, :] = north[9]
-    sides[128:136, :] = own_masks[0]
-    sides[136:144, :] = own_masks[1]
-    sides[144:152, :] = south[15]
+    sides = dot(high, table[...]) + dot(low, table[...])
+    lane = lax.broadcasted_iota(jnp.int32, (ROWS, NL), 1)
+    each = [sides[v * ROWS : (v + 1) * ROWS] for v in range(NV)]
+    right = jnp.where(lane < 40, each[0], pltpu.roll(each[1], 40, 1))
+    to_right[0:ROWS, :] = jnp.where(lane < 80, right, pltpu.roll(each[2], 80, 1))
+    last = jnp.where(lane < 32, pltpu.roll(each[2], NL - 40, 1), pltpu.roll(each[2], NL - 72, 1))
+    to_left[0:ROWS, :] = jnp.where(lane < 40, last, each[0])
+    to_left[ROWS : 2 * ROWS, :] = jnp.where(lane < 32, pltpu.roll(each[2], NL - 72, 1), each[1])
+    lane = lax.broadcasted_iota(jnp.int32, (8, NL), 1)
+    ends = jnp.zeros((8, NL), F32)
+    for ib, tile in enumerate((north[9], own_masks[0], own_masks[1], south[15])):
+        for j, source in enumerate((0, 63, 64, 95)):
+            target = 4 * ib + j
+            ends = jnp.where(lane == target, pltpu.roll(tile, (target - source) % NL, 1), ends)
+    to_left[2 * ROWS : 2 * ROWS + 8, :] = ends
+    to_right[ROWS : ROWS + 8, :] = ends
 
 
 def edge_step(parts, lifted, north, south, own_masks):
     vmem = pl.BlockSpec(memory_space=pltpu.VMEM)
-    shapes = [(4 * NV * 8 * ROWS, NL), (152, NL)]
+    shapes = [(4 * NV * 8 * ROWS, NL), (2 * ROWS + 8, NL), (ROWS + 8, NL)]
     return pl.pallas_call(
         edge_kernel,
         out_shape=[jax.ShapeDtypeStruct(s, F32) for s in shapes],
         in_specs=[vmem] * 5 + [pl.BlockSpec(memory_space=pltpu.HBM)],
-        out_specs=[vmem] * 2,
+        out_specs=[vmem] * 3,
         input_output_aliases={0: 0},
         cost_estimate=cost(20),
         scratch_shapes=[pltpu.VMEM((480, NL), F32), pltpu.VMEM((512, NL), BF16), pltpu.SemaphoreType.DMA((1,))],
@@ -460,7 +474,11 @@
 
 
 def mask_lanes(west, east, own_masks, north_mask, south_mask, wide):
-    masks = [jnp.concatenate([ref[120 + 8 * i : 128 + 8 * i, :] for i in range(4)], 0) for ref in (east, west)]
+    group = lax.broadcasted_iota(jnp.int32, (8, NL), 1) // 4
+    masks = [
+        jnp.concatenate([jnp.where(group == ib, tile, 0.0) for ib in range(4)], 0)
+        for tile in (east[2 * ROWS : 2 * ROWS + 8, :], west[ROWS : ROWS + 8, :])
+    ]
     own = jnp.concatenate([north_mask[0], own_masks[0], own_masks[1], south_mask[0]], 0)
     flags = jnp.concatenate([own] + masks, 1).astype(BF16)
     return dot(flags, wide[144:528, :])
@@ -468,11 +486,13 @@
 
 def beside_tiles(west, east, at, count):
     lane = lax.broadcasted_iota(jnp.int32, (count, NL), 1)
-    from_west = (lane >= 112) | ((lane < 96) & (lax.rem(lane, 24) >= 16))
+    left = west[at : at + count, :]
+    first, second = east[at : at + count, :], east[ROWS + at : ROWS + at + count, :]
+    third = jnp.where(lane < 104, pltpu.roll(second, 72, 1), pltpu.roll(first, 72, 1))
+    third = jnp.where(lane < 72, pltpu.roll(first, 40, 1), third)
     tiles = []
-    for v in range(NV):
-        rows = slice(v * ROWS + at, v * ROWS + at + count)
-        beside = jnp.where(from_west, west[rows, :], east[rows, :])
+    for v, right in enumerate((first, second, third)):
+        beside = jnp.where(lane < FROM_WEST, pltpu.roll(left, NL - 40 * v, 1) if v else left, right)
         tiles += [pltpu.roll(beside, NL - z, 1) if z else beside for z in range(8)]
     return tiles
 
@@ -578,7 +598,7 @@
             gain[ib, n, 0:128, :] = main
             gain[ib, n, 128:256, :] = main
             for i in range(3):
-                at = 24 * n + 8 * i
+                at = list(beyond(n).values())[i]
                 sides_wide[ib, at : at + 1, n * NL : (n + 1) * NL] = both[128 + i : 129 + i]
 
     gain_sides = []
@@ -816,10 +836,10 @@
     south = shifted(up, "gx", -1)
     north = shifted(down, "gx", 1)
     shares = [share] + [swapped(share, "gy", r) for r in range(2, count_y, 2)]
-    parts, sides = edge_step(lift_step(lifted), lifted, north, south, own_masks)
-    east = shifted(sides, "gy", -1)
-    west = shifted(sides, "gy", 1)
-    joined = join_step(shares, sides)
+    parts, to_left, to_right = edge_step(lift_step(lifted), lifted, north, south, own_masks)
+    east = shifted(to_left, "gy", -1)
+    west = shifted(to_right, "gy", 1)
+    joined = join_step(shares, to_left)
     pieces = [joined] + [swapped(joined, "gx", r) for r in range(1, count_x)]
     kept = main_step(parts, east, west, own_masks, north, south)
     own = rows_step(pieces, count_y // 2, kept)

time: 27.9 us -> 28 us (level)
    ppermute x4, waiting for transfers between devices: 1.62 us -> 1.11 us  [shifted(): lax.ppermute(x, axis, [(i, (i + step) % count) for i in range(count)])]
    ppermute x7, waiting for transfers between devices: 1.14 us -> 1.62 us  [swapped(): lax.ppermute(x, axis, [(i, i ^ distance) for i in range(lax.axis_size(axi...]
where the time goes in v8:
time: 28 us; the launch traced here: 27.8 us
  starting transfers between devices  13.9 us (50%)
  Pallas kernels  10.5 us (38%)
  waiting for transfers between devices  2.73 us (10%)
  between operations  0.71 us (3%)
    ppermute x7, starting transfers between devices, swapped(): lax.ppermute(x, axis, [(i, i ^ distance) for i in range(lax.axis_size(axi...  8.09 us
    ppermute x4, starting transfers between devices, shifted(): lax.ppermute(x, axis, [(i, (i + step) % count) for i in range(count)])  5.76 us
    pallas_call x1, Pallas kernels, main_step(): pl.pallas_call(main_kernel, grid=(1,), out_shape=jax.ShapeDtypeStruct((4...  3.52 us
    pallas_call x1, Pallas kernels, first_step(): pl.pallas_call(first_kernel, out_shape=[jax.ShapeDtypeStruct(s, F32) for...  2.33 us
    ppermute x7, waiting for transfers between devices, swapped(): lax.ppermute(x, axis, [(i, i ^ distance) for i in range(lax.axis_size(axi...  1.62 us
    pallas_call x1, Pallas kernels, coarse_step(): pl.pallas_call(functools.partial(coarse_kernel, count_x, count_y), out_sh...  1.37 us
    pallas_call x1, Pallas kernels, cells_step(): pl.pallas_call(cells_kernel, out_shape=jax.ShapeDtypeStruct(shape, F32),...  1.37 us
    pallas_call x1, Pallas kernels, edge_step(): pl.pallas_call(edge_kernel, out_shape=[jax.ShapeDtypeStruct(s, F32) for s...  1.21 us
  transfers between devices with their start and end apart: 11, of which 5 were waited for; matrix products, arithmetic and copies ran while one was open for 0% of the time, Pallas kernels for 23%

profile of v8, /device:TPU:0, one launch (start us, length us, event | category | flops | bytes accessed | tf_op | source)
XLA Modules:
  0.0 27.8 jit_solution(4966103009628336291)
XLA Ops:
  0.6 2.3 %shard_map.77 = (f32[3840,128]{1,0:T(8,128)S(1)}, f32[16,8,128]{2,1,0:T(8,128)S(1)}, f32[10,8,128]{2,1,0:T(8,128)S(1)}, f32[2,8,128]{2,1,0:T(8,128)S(1)}, f32[64,128]{1,0:T(8,128)S(1)}) custom-call(f32[3,16,64,128]{3,2,1,0:T(8,128)} %field.1, s32[2,2,4,7]{3,2,1,0:T(4,128)} %bitcast.5, bf16[400,128]{1,0:T(8,128)(2,1)} %constant.8.clone.table_hbm), custom_call_target="tpu_custom_call" | custom-call | tf_op jit(solution)/shard_map/pallas_call | solution.py:336
  3.0 3.9 %collective-permute-start.1 = (f32[16,8,128]{2,1,0:T(8,128)S(1)}, f32[16,8,128]{2,1,0:T(8,128)S(1)}, u32[]{:S(2)}, u32[]{:S(2)}) collective-permute-start(f32[16,8,128]{2,1,0:T(8,128)S(1)} %get-tuple-element.12), channel_id=1, source_target_pairs={{0,24},{8,0},{16,8},{24,16},{1,25},{9,1},{17,9},{25,17},{2,26},{10... | collective-permute-start | bytes 196616 | tf_op jit(solution)/shard_map/ppermute | solution.py:826
  6.9 0.0 collective-permute-start
  6.9 3.6 %collective-permute-start.4 = (f32[64,128]{1,0:T(8,128)S(1)}, f32[64,128]{1,0:T(8,128)S(1)}, u32[]{:S(2)}, u32[]{:S(2)}) collective-permute-start(f32[64,128]{1,0:T(8,128)S(1)} %get-tuple-element.17.refs_3_), channel_id=1, source_target_pairs={{0,6},{1,7},{2,4},{3,5},{4,2},{5,3},{6,0},{7,1},{8,14},{9,15},{10,... | collective-permute-start | bytes 98312 | tf_op jit(solution)/shard_map/ppermute | solution.py:830
  10.5 0.0 collective-permute-start.5
  10.5 0.8 %collective-permute-start.6 = (f32[64,128]{1,0:T(8,128)S(1)}, f32[64,128]{1,0:T(8,128)S(1)}, u32[]{:S(2)}, u32[]{:S(2)}) collective-permute-start(f32[64,128]{1,0:T(8,128)S(1)} %get-tuple-element.17.refs_3_), channel_id=1, source_target_pairs={{0,2},{1,3},{2,0},{3,1},{4,6},{5,7},{6,4},{7,5},{8,10},{9,11},{10,... | collective-permute-start | bytes 98312 | tf_op jit(solution)/shard_map/ppermute | solution.py:830
  11.3 0.3 %shard_map.78.parts_in = f32[3840,128]{1,0:T(8,128)S(1)} custom-call(f32[3840,128]{1,0:T(8,128)S(1)} %get-tuple-element.10.lifted), custom_call_target="tpu_custom_call" | custom-call | tf_op jit(solution)/shard_map/pallas_call | solution.py:372
  11.6 0.2 collective-permute-done.north.north_mask
  11.8 1.2 %shard_map.79 = (f32[3840,128]{1,0:T(8,128)S(1)}, f32[88,128]{1,0:T(8,128)S(1)}, f32[48,128]{1,0:T(8,128)S(1)}) custom-call(f32[3840,128]{1,0:T(8,128)S(1)} %shard_map.78.parts_in, f32[3840,128]{1,0:T(8,128)S(1)} %get-tuple-element.10.lifted, f32[10,8,128]{2,1,0:T(8,128)S(1)} %collective-permute-done.north.north_mask, ...), custom_call_target="tpu_custom_call", output_to_operand_aliasing={{0}: (0, {})} | custom-call | flops 20000000000 | bytes 8000000 | tf_op jit(solution)/shard_map/pallas_call | solution.py:446
  13.0 1.8 %collective-permute-start.2 = (f32[88,128]{1,0:T(8,128)S(1)}, f32[88,128]{1,0:T(8,128)S(1)}, u32[]{:S(2)}, u32[]{:S(2)}) collective-permute-start(f32[88,128]{1,0:T(8,128)S(1)} %get-tuple-element.15.refs_4_), channel_id=1, source_target_pairs={{0,7},{1,0},{2,1},{3,2},{4,3},{5,4},{6,5},{7,6},{8,15},{9,8},{10,9... | collective-permute-start | bytes 135176 | tf_op jit(solution)/shard_map/ppermute | solution.py:826
  14.9 0.5 %collective-permute-done.5.refs_1_ = f32[64,128]{1,0:T(8,128)S(1)} collective-permute-done((f32[64,128]{1,0:T(8,128)S(1)}, f32[64,128]{1,0:T(8,128)S(1)}, u32[]{:S(2)}, u32[]{:S(2)}) %collective-permute-start.5) | collective-permute-done | bytes 32800 | tf_op jit(solution)/shard_map/ppermute | solution.py:830
  15.4 3.0 %collective-permute-start.7 = (f32[256,128]{1,0:T(8,128)S(1)}, f32[256,128]{1,0:T(8,128)S(1)}, u32[]{:S(2)}, u32[]{:S(2)}) collective-permute-start(f32[256,128]{1,0:T(8,128)S(1)} %shard_map.82.refs_3_), channel_id=1, source_target_pairs={{0,24},{8,16},{16,8},{24,0},{1,25},{9,17},{17,9},{25,1},{2,26},{10... | collective-permute-start | bytes 393224 | tf_op jit(solution)/shard_map/ppermute | solution.py:830
  18.3 0.5 %collective-permute-start.8 = (f32[256,128]{1,0:T(8,128)S(1)}, f32[256,128]{1,0:T(8,128)S(1)}, u32[]{:S(2)}, u32[]{:S(2)}) collective-permute-start(f32[256,128]{1,0:T(8,128)S(1)} %shard_map.82.refs_3_), channel_id=1, source_target_pairs={{0,16},{8,24},{16,0},{24,8},{1,17},{9,25},{17,1},{25,9},{2,18},{10... | collective-permute-start | bytes 393224 | tf_op jit(solution)/shard_map/ppermute | solution.py:830
  18.8 0.1 collective-permute-start.9
  19.0 0.9 %collective-permute-done.3.west = f32[48,128]{1,0:T(8,128)S(1)} collective-permute-done((f32[48,128]{1,0:T(8,128)S(1)}, f32[48,128]{1,0:T(8,128)S(1)}, u32[]{:S(2)}, u32[]{:S(2)}) %collective-permute-start.3) | collective-permute-done | bytes 24608 | tf_op jit(solution)/shard_map/ppermute | solution.py:826
  19.9 0.0 collective-permute-done.2.east
  19.9 3.5 %shard_map.80.refs_4_ = f32[4608,128]{1,0:T(8,128)S(1)} custom-call(f32[4,24,40,128]{3,2,1,0:T(8,128)S(1)} %bitcast.4, f32[3840,128]{1,0:T(8,128)S(1)} %get-tuple-element.14.flat, f32[88,128]{1,0:T(8,128)S(1)} %collective-permute-done.2.east, f32[48,128]{1,0:T(8,128)S(1)} %collective-permute-done.3.west, f32[2,8,128]{2,1,0:T(8,128)S(1)} %get-tuple-element.13.own_masks, ...), custom_call_target="tpu_custom_call" | custom-call | flops 8000000000 | bytes 8000000 | tf_op jit(solution)/shard_map/pallas_call | solution.py:692
  23.5 0.6 %collective-permute-done.8.refs_1_ = f32[256,128]{1,0:T(8,128)S(1)} collective-permute-done((f32[256,128]{1,0:T(8,128)S(1)}, f32[256,128]{1,0:T(8,128)S(1)}, u32[]{:S(2)}, u32[]{:S(2)}) %collective-permute-start.8) | collective-permute-done | bytes 131104 | tf_op jit(solution)/shard_map/ppermute | solution.py:830
  24.1 0.0 collective-permute-done.9.refs_2_
  24.1 0.3 %shard_map.83.own = f32[4,4,64,128]{3,2,1,0:T(8,128)S(1)} custom-call(f32[256,128]{1,0:T(8,128)S(1)} %collective-permute-done.7.refs_0_, f32[256,128]{1,0:T(8,128)S(1)} %collective-permute-done.8.refs_1_, f32[256,128]{1,0:T(8,128)S(1)} %collective-permute-done.9.refs_2_, f32[256,128]{1,0:T(8,128)S(1)} %shard_map.82.refs_3_, f32[4608,128]{1,0:T(8,128)S(1)} %shard_map.80.refs_4_), custom_call_target="tpu_custom_call" | custom-call | tf_op jit(solution)/shard_map/pallas_call | solution.py:763
  24.4 0.1 collective-permute-start.10
  24.5 1.4 %shard_map.81 = f32[3,16,64,128]{3,2,1,0:T(8,128)} custom-call(f32[4,24,48,128]{3,2,1,0:T(8,128)S(1)} %bitcast.3), custom_call_target="tpu_custom_call" | custom-call | flops 4000000000 | bytes 8000000 | tf_op jit(solution)/shard_map/pallas_call | solution.py:715
  25.9 0.5 %collective-permute-done.10.other = f32[4,4,64,128]{3,2,1,0:T(8,128)S(1)} collective-permute-done((f32[4,4,64,128]{3,2,1,0:T(8,128)S(1)}, f32[4,4,64,128]{3,2,1,0:T(8,128)S(1)}, u32[]{:S(2)}, u32[]{:S(2)}) %collective-permute-start.10) | collective-permute-done | bytes 524320 | tf_op jit(solution)/shard_map/ppermute | solution.py:830
  26.4 1.4 %shard_map.84 = f32[3,4,64,256]{3,2,1,0:T(8,128)} custom-call(f32[4,4,64,128]{3,2,1,0:T(8,128)S(1)} %shard_map.83.own, f32[4,4,64,128]{3,2,1,0:T(8,128)S(1)} %collective-permute-done.10.other), custom_call_target="tpu_custom_call" | custom-call | tf_op jit(solution)/shard_map/pallas_call | solution.py:814
  (10 shorter events, 0.0 us)
Async XLA Ops:
  3.0 8.9 %collective-permute-start.1 = (f32[16,8,128]{2,1,0:T(8,128)S(1)}, f32[16,8,128]{2,1,0:T(8,128)S(1)}, u32[]{:S(2)}, u32[]{:S(2)}) collective-permute-start(f32[16,8,128]{2,1,0:T(8,128)S(1)} %get-tuple-element.12), channel_id=1, source_target_pairs={{0,24},{8,0},{16,8},{24,16},{1,25},{9,1},{17,9},{25,17},{2,26},{10... | collective-permute-start | bytes 196616 | tf_op jit(solution)/shard_map/ppermute | solution.py:826
  6.9 4.9 %collective-permute-start = (f32[10,8,128]{2,1,0:T(8,128)S(1)}, f32[10,8,128]{2,1,0:T(8,128)S(1)}, u32[]{:S(2)}, u32[]{:S(2)}) collective-permute-start(f32[10,8,128]{2,1,0:T(8,128)S(1)} %get-tuple-element.11), channel_id=1, source_target_pairs={{0,8},{8,16},{16,24},{24,0},{1,9},{9,17},{17,25},{25,1},{2,10},{10... | collective-permute-start | bytes 122888 | tf_op jit(solution)/shard_map/ppermute | solution.py:826
  6.9 7.9 %collective-permute-start.4 = (f32[64,128]{1,0:T(8,128)S(1)}, f32[64,128]{1,0:T(8,128)S(1)}, u32[]{:S(2)}, u32[]{:S(2)}) collective-permute-start(f32[64,128]{1,0:T(8,128)S(1)} %get-tuple-element.17.refs_3_), channel_id=1, source_target_pairs={{0,6},{1,7},{2,4},{3,5},{4,2},{5,3},{6,0},{7,1},{8,14},{9,15},{10,... | collective-permute-start | bytes 98312 | tf_op jit(solution)/shard_map/ppermute | solution.py:830
  10.5 4.8 %collective-permute-start.5 = (f32[64,128]{1,0:T(8,128)S(1)}, f32[64,128]{1,0:T(8,128)S(1)}, u32[]{:S(2)}, u32[]{:S(2)}) collective-permute-start(f32[64,128]{1,0:T(8,128)S(1)} %get-tuple-element.17.refs_3_), channel_id=1, source_target_pairs={{0,4},{1,5},{2,6},{3,7},{4,0},{5,1},{6,2},{7,3},{8,12},{9,13},{10,... | collective-permute-start | bytes 98312 | tf_op jit(solution)/shard_map/ppermute | solution.py:830
  10.5 4.8 %collective-permute-start.6 = (f32[64,128]{1,0:T(8,128)S(1)}, f32[64,128]{1,0:T(8,128)S(1)}, u32[]{:S(2)}, u32[]{:S(2)}) collective-permute-start(f32[64,128]{1,0:T(8,128)S(1)} %get-tuple-element.17.refs_3_), channel_id=1, source_target_pairs={{0,2},{1,3},{2,0},{3,1},{4,6},{5,7},{6,4},{7,5},{8,10},{9,11},{10,... | collective-permute-start | bytes 98312 | tf_op jit(solution)/shard_map/ppermute | solution.py:830
  13.0 6.9 %collective-permute-start.2 = (f32[88,128]{1,0:T(8,128)S(1)}, f32[88,128]{1,0:T(8,128)S(1)}, u32[]{:S(2)}, u32[]{:S(2)}) collective-permute-start(f32[88,128]{1,0:T(8,128)S(1)} %get-tuple-element.15.refs_4_), channel_id=1, source_target_pairs={{0,7},{1,0},{2,1},{3,2},{4,3},{5,4},{6,5},{7,6},{8,15},{9,8},{10,9... | collective-permute-start | bytes 135176 | tf_op jit(solution)/shard_map/ppermute | solution.py:826
  14.9 5.1 %copy-start = (bf16[1280,128]{1,0:T(8,128)(2,1)S(1)}, bf16[1280,128]{1,0:T(8,128)(2,1)}, u32[]{:S(2)}) copy-start(bf16[1280,128]{1,0:T(8,128)(2,1)} %constant.11.clone.narrow) | copy-start | bytes 983044
  14.9 5.1 %copy-start.1 = (bf16[528,256]{1,0:T(8,128)(2,1)S(1)}, bf16[528,256]{1,0:T(8,128)(2,1)}, u32[]{:S(2)}) copy-start(bf16[528,256]{1,0:T(8,128)(2,1)} %constant.10.clone.wide) | copy-start | bytes 811012
  14.9 5.0 %collective-permute-start.3 = (f32[48,128]{1,0:T(8,128)S(1)}, f32[48,128]{1,0:T(8,128)S(1)}, u32[]{:S(2)}, u32[]{:S(2)}) collective-permute-start(f32[48,128]{1,0:T(8,128)S(1)} %get-tuple-element.16), channel_id=1, source_target_pairs={{0,1},{1,2},{2,3},{3,4},{4,5},{5,6},{6,7},{7,0},{8,9},{9,10},{10,1... | collective-permute-start | bytes 73736 | tf_op jit(solution)/shard_map/ppermute | solution.py:826
  15.4 8.1 %collective-permute-start.7 = (f32[256,128]{1,0:T(8,128)S(1)}, f32[256,128]{1,0:T(8,128)S(1)}, u32[]{:S(2)}, u32[]{:S(2)}) collective-permute-start(f32[256,128]{1,0:T(8,128)S(1)} %shard_map.82.refs_3_), channel_id=1, source_target_pairs={{0,24},{8,16},{16,8},{24,0},{1,25},{9,17},{17,9},{25,1},{2,26},{10... | collective-permute-start | bytes 393224 | tf_op jit(solution)/shard_map/ppermute | solution.py:830
  18.3 5.7 %collective-permute-start.8 = (f32[256,128]{1,0:T(8,128)S(1)}, f32[256,128]{1,0:T(8,128)S(1)}, u32[]{:S(2)}, u32[]{:S(2)}) collective-permute-start(f32[256,128]{1,0:T(8,128)S(1)} %shard_map.82.refs_3_), channel_id=1, source_target_pairs={{0,16},{8,24},{16,0},{24,8},{1,17},{9,25},{17,1},{25,9},{2,18},{10... | collective-permute-start | bytes 393224 | tf_op jit(solution)/shard_map/ppermute | solution.py:830
  18.8 5.2 %collective-permute-start.9 = (f32[256,128]{1,0:T(8,128)S(1)}, f32[256,128]{1,0:T(8,128)S(1)}, u32[]{:S(2)}, u32[]{:S(2)}) collective-permute-start(f32[256,128]{1,0:T(8,128)S(1)} %shard_map.82.refs_3_), channel_id=1, source_target_pairs={{0,8},{8,0},{16,24},{24,16},{1,9},{9,1},{17,25},{25,17},{2,10},{10... | collective-permute-start | bytes 393224 | tf_op jit(solution)/shard_map/ppermute | solution.py:830
  24.4 2.0 %collective-permute-start.10 = (f32[4,4,64,128]{3,2,1,0:T(8,128)S(1)}, f32[4,4,64,128]{3,2,1,0:T(8,128)S(1)}, u32[]{:S(2)}, u32[]{:S(2)}) collective-permute-start(f32[4,4,64,128]{3,2,1,0:T(8,128)S(1)} %shard_map.83.own), channel_id=1, source_target_pairs={{0,1},{1,0},{2,3},{3,2},{4,5},{5,4},{6,7},{7,6},{8,9},{9,8},{10,11... | collective-permute-start | bytes 1572872 | tf_op jit(solution)/shard_map/ppermute | solution.py:830

commit v9 on v8

--- a/solution.py
+++ b/solution.py
@@ -723,8 +723,12 @@
     )(kept)
 
 
+def sent_order(count):
+    return sorted(range(count), key=lambda r: (r == 0, r < 2, r))
+
+
 def rows_kernel(count_x, count_z, *refs):
-    shares, out = refs[count_x - 1 :: -1], refs[count_x + 1]
+    shares, out = [refs[sent_order(count_x).index(r)] for r in range(count_x)], refs[count_x + 1]
     me, me_y = lax.axis_index("gx"), lax.axis_index("gy")
     row = lax.broadcasted_iota(jnp.int32, (8, NL), 0)
     lane = lax.broadcasted_iota(jnp.int32, (8, NL), 1)
@@ -766,7 +770,7 @@
         in_specs=[vmem] * count_x + [pl.BlockSpec(memory_space=pl.ANY)],
         out_specs=vmem,
         compiler_params=pltpu.CompilerParams(vmem_limit_bytes=VMEM_LIMIT),
-    )(*pieces[::-1], after)
+    )(*[pieces[r] for r in sent_order(count_x)], after)
 
 
 def coarse_kernel(count_x, count_y, own, other, out_hbm, out, sems):
@@ -833,8 +837,8 @@
 def body(field, masks):
     count_x, count_y = lax.axis_size("gx"), lax.axis_size("gy")
     lifted, up, down, own_masks, share = first_step(field, masks)
+    north = shifted(down, "gx", 1)
     south = shifted(up, "gx", -1)
-    north = shifted(down, "gx", 1)
     shares = [share] + [swapped(share, "gy", r) for r in range(2, count_y, 2)]
     parts, to_left, to_right = edge_step(lift_step(lifted), lifted, north, south, own_masks)
     east = shifted(to_left, "gy", -1)

time: 28 us -> 28.3 us (1.011)
  waiting for transfers between devices: 2.73 us -> 3.13 us
    ppermute x7, waiting for transfers between devices: 1.62 us -> 1.95 us  [swapped(): lax.ppermute(x, axis, [(i, i ^ distance) for i in range(lax.axis_size(axi...]
  transfers between devices with their start and end apart: 11 -> 11, of which waited for: 5 -> 6; matrix products, arithmetic and copies ran while one was open for 0% -> 0% of each run, Pallas kernels for 23% -> 23%
where the time goes in v9:
time: 28.3 us; the launch traced here: 28.1 us
  starting transfers between devices  13.8 us (49%)
  Pallas kernels  10.4 us (37%)
  waiting for transfers between devices  3.13 us (11%)
  between operations  0.71 us (3%)
    ppermute x7, starting transfers between devices, swapped(): lax.ppermute(x, axis, [(i, i ^ distance) for i in range(lax.axis_size(axi...  8.01 us
    ppermute x4, starting transfers between devices, shifted(): lax.ppermute(x, axis, [(i, (i + step) % count) for i in range(count)])  5.76 us
    pallas_call x1, Pallas kernels, main_step(): pl.pallas_call(main_kernel, grid=(1,), out_shape=jax.ShapeDtypeStruct((4...  3.52 us
    pallas_call x1, Pallas kernels, first_step(): pl.pallas_call(first_kernel, out_shape=[jax.ShapeDtypeStruct(s, F32) for...  2.33 us
    ppermute x7, waiting for transfers between devices, swapped(): lax.ppermute(x, axis, [(i, i ^ distance) for i in range(lax.axis_size(axi...  1.95 us
    pallas_call x1, Pallas kernels, coarse_step(): pl.pallas_call(functools.partial(coarse_kernel, count_x, count_y), out_sh...  1.37 us
    pallas_call x1, Pallas kernels, cells_step(): pl.pallas_call(cells_kernel, out_shape=jax.ShapeDtypeStruct(shape, F32),...  1.37 us
    pallas_call x1, Pallas kernels, edge_step(): pl.pallas_call(edge_kernel, out_shape=[jax.ShapeDtypeStruct(s, F32) for s...  1.21 us
  transfers between devices with their start and end apart: 11, of which 6 were waited for; matrix products, arithmetic and copies ran while one was open for 0% of the time, Pallas kernels for 23%

profile of v9, /device:TPU:0, one launch (start us, length us, event | category | flops | bytes accessed | tf_op | source)
XLA Modules:
  0.0 28.1 jit_solution(11516511673363341483)
XLA Ops:
  0.6 2.3 %shard_map.77 = (f32[3840,128]{1,0:T(8,128)S(1)}, f32[16,8,128]{2,1,0:T(8,128)S(1)}, f32[10,8,128]{2,1,0:T(8,128)S(1)}, f32[2,8,128]{2,1,0:T(8,128)S(1)}, f32[64,128]{1,0:T(8,128)S(1)}) custom-call(f32[3,16,64,128]{3,2,1,0:T(8,128)} %field.1, s32[2,2,4,7]{3,2,1,0:T(4,128)} %bitcast.5, bf16[400,128]{1,0:T(8,128)(2,1)} %constant.8.clone.table_hbm), custom_call_target="tpu_custom_call" | custom-call | tf_op jit(solution)/shard_map/pallas_call | solution.py:336
  3.0 3.9 %collective-permute-start.1 = (f32[16,8,128]{2,1,0:T(8,128)S(1)}, f32[16,8,128]{2,1,0:T(8,128)S(1)}, u32[]{:S(2)}, u32[]{:S(2)}) collective-permute-start(f32[16,8,128]{2,1,0:T(8,128)S(1)} %get-tuple-element.12), channel_id=1, source_target_pairs={{0,24},{8,0},{16,8},{24,16},{1,25},{9,1},{17,9},{25,17},{2,26},{10... | collective-permute-start | bytes 196616 | tf_op jit(solution)/shard_map/ppermute | solution.py:830
  6.9 0.0 collective-permute-start
  6.9 3.6 %collective-permute-start.4 = (f32[64,128]{1,0:T(8,128)S(1)}, f32[64,128]{1,0:T(8,128)S(1)}, u32[]{:S(2)}, u32[]{:S(2)}) collective-permute-start(f32[64,128]{1,0:T(8,128)S(1)} %get-tuple-element.17.refs_3_), channel_id=1, source_target_pairs={{0,6},{1,7},{2,4},{3,5},{4,2},{5,3},{6,0},{7,1},{8,14},{9,15},{10,... | collective-permute-start | bytes 98312 | tf_op jit(solution)/shard_map/ppermute | solution.py:834
  10.5 0.8 %collective-permute-start.6 = (f32[64,128]{1,0:T(8,128)S(1)}, f32[64,128]{1,0:T(8,128)S(1)}, u32[]{:S(2)}, u32[]{:S(2)}) collective-permute-start(f32[64,128]{1,0:T(8,128)S(1)} %get-tuple-element.17.refs_3_), channel_id=1, source_target_pairs={{0,2},{1,3},{2,0},{3,1},{4,6},{5,7},{6,4},{7,5},{8,10},{9,11},{10,... | collective-permute-start | bytes 98312 | tf_op jit(solution)/shard_map/ppermute | solution.py:834
  11.3 0.3 %shard_map.78.parts_in = f32[3840,128]{1,0:T(8,128)S(1)} custom-call(f32[3840,128]{1,0:T(8,128)S(1)} %get-tuple-element.10.lifted), custom_call_target="tpu_custom_call" | custom-call | tf_op jit(solution)/shard_map/pallas_call | solution.py:372
  11.6 0.2 collective-permute-done.north.north_mask
  11.8 0.0 collective-permute-done.1.south.south_mask
  11.8 1.2 %shard_map.79 = (f32[3840,128]{1,0:T(8,128)S(1)}, f32[88,128]{1,0:T(8,128)S(1)}, f32[48,128]{1,0:T(8,128)S(1)}) custom-call(f32[3840,128]{1,0:T(8,128)S(1)} %shard_map.78.parts_in, f32[3840,128]{1,0:T(8,128)S(1)} %get-tuple-element.10.lifted, f32[10,8,128]{2,1,0:T(8,128)S(1)} %collective-permute-done.north.north_mask, ...), custom_call_target="tpu_custom_call", output_to_operand_aliasing={{0}: (0, {})} | custom-call | flops 20000000000 | bytes 8000000 | tf_op jit(solution)/shard_map/pallas_call | solution.py:446
  13.0 1.8 %collective-permute-start.2 = (f32[88,128]{1,0:T(8,128)S(1)}, f32[88,128]{1,0:T(8,128)S(1)}, u32[]{:S(2)}, u32[]{:S(2)}) collective-permute-start(f32[88,128]{1,0:T(8,128)S(1)} %get-tuple-element.15.refs_4_), channel_id=1, source_target_pairs={{0,7},{1,0},{2,1},{3,2},{4,3},{5,4},{6,5},{7,6},{8,15},{9,8},{10,9... | collective-permute-start | bytes 135176 | tf_op jit(solution)/shard_map/ppermute | solution.py:830
  14.9 0.0 collective-permute-start.3
  14.9 0.5 %collective-permute-done.5.refs_1_ = f32[64,128]{1,0:T(8,128)S(1)} collective-permute-done((f32[64,128]{1,0:T(8,128)S(1)}, f32[64,128]{1,0:T(8,128)S(1)}, u32[]{:S(2)}, u32[]{:S(2)}) %collective-permute-start.5) | collective-permute-done | bytes 32800 | tf_op jit(solution)/shard_map/ppermute | solution.py:834
  15.4 1.2 %collective-permute-start.7 = (f32[256,128]{1,0:T(8,128)S(1)}, f32[256,128]{1,0:T(8,128)S(1)}, u32[]{:S(2)}, u32[]{:S(2)}) collective-permute-start(f32[256,128]{1,0:T(8,128)S(1)} %shard_map.82.refs_3_), channel_id=1, source_target_pairs={{0,16},{8,24},{16,0},{24,8},{1,17},{9,25},{17,1},{25,9},{2,18},{10... | collective-permute-start | bytes 393224 | tf_op jit(solution)/shard_map/ppermute | solution.py:834
  16.5 2.3 %collective-permute-start.8 = (f32[256,128]{1,0:T(8,128)S(1)}, f32[256,128]{1,0:T(8,128)S(1)}, u32[]{:S(2)}, u32[]{:S(2)}) collective-permute-start(f32[256,128]{1,0:T(8,128)S(1)} %shard_map.82.refs_3_), channel_id=1, source_target_pairs={{0,24},{8,16},{16,8},{24,0},{1,25},{9,17},{17,9},{25,1},{2,26},{10... | collective-permute-start | bytes 393224 | tf_op jit(solution)/shard_map/ppermute | solution.py:834
  18.8 0.1 collective-permute-start.9
  18.9 1.0 %collective-permute-done.3.west = f32[48,128]{1,0:T(8,128)S(1)} collective-permute-done((f32[48,128]{1,0:T(8,128)S(1)}, f32[48,128]{1,0:T(8,128)S(1)}, u32[]{:S(2)}, u32[]{:S(2)}) %collective-permute-start.3) | collective-permute-done | bytes 24608 | tf_op jit(solution)/shard_map/ppermute | solution.py:830
  19.9 3.5 %shard_map.80.refs_4_ = f32[4608,128]{1,0:T(8,128)S(1)} custom-call(f32[4,24,40,128]{3,2,1,0:T(8,128)S(1)} %bitcast.4, f32[3840,128]{1,0:T(8,128)S(1)} %get-tuple-element.14.flat, f32[88,128]{1,0:T(8,128)S(1)} %collective-permute-done.2.east, f32[48,128]{1,0:T(8,128)S(1)} %collective-permute-done.3.west, f32[2,8,128]{2,1,0:T(8,128)S(1)} %get-tuple-element.13.own_masks, ...), custom_call_target="tpu_custom_call" | custom-call | flops 8000000000 | bytes 8000000 | tf_op jit(solution)/shard_map/pallas_call | solution.py:692
  23.5 0.2 collective-permute-done.8.refs_1_
  23.7 0.7 %collective-permute-done.9.refs_2_ = f32[256,128]{1,0:T(8,128)S(1)} collective-permute-done((f32[256,128]{1,0:T(8,128)S(1)}, f32[256,128]{1,0:T(8,128)S(1)}, u32[]{:S(2)}, u32[]{:S(2)}) %collective-permute-start.9) | collective-permute-done | bytes 131104 | tf_op jit(solution)/shard_map/ppermute | solution.py:834
  24.4 0.3 %shard_map.83.own = f32[4,4,64,128]{3,2,1,0:T(8,128)S(1)} custom-call(f32[256,128]{1,0:T(8,128)S(1)} %collective-permute-done.7.refs_0_, f32[256,128]{1,0:T(8,128)S(1)} %collective-permute-done.8.refs_1_, f32[256,128]{1,0:T(8,128)S(1)} %collective-permute-done.9.refs_2_, f32[256,128]{1,0:T(8,128)S(1)} %shard_map.82.refs_3_, f32[4608,128]{1,0:T(8,128)S(1)} %shard_map.80.refs_4_), custom_call_target="tpu_custom_call" | custom-call | tf_op jit(solution)/shard_map/pallas_call | solution.py:767
  24.7 0.1 collective-permute-start.10
  24.8 1.4 %shard_map.81 = f32[3,16,64,128]{3,2,1,0:T(8,128)} custom-call(f32[4,24,48,128]{3,2,1,0:T(8,128)S(1)} %bitcast.3), custom_call_target="tpu_custom_call" | custom-call | flops 4000000000 | bytes 8000000 | tf_op jit(solution)/shard_map/pallas_call | solution.py:715
  26.2 0.5 %collective-permute-done.10.other = f32[4,4,64,128]{3,2,1,0:T(8,128)S(1)} collective-permute-done((f32[4,4,64,128]{3,2,1,0:T(8,128)S(1)}, f32[4,4,64,128]{3,2,1,0:T(8,128)S(1)}, u32[]{:S(2)}, u32[]{:S(2)}) %collective-permute-start.10) | collective-permute-done | bytes 524320 | tf_op jit(solution)/shard_map/ppermute | solution.py:834
  26.7 1.4 %shard_map.84 = f32[3,4,64,256]{3,2,1,0:T(8,128)} custom-call(f32[4,4,64,128]{3,2,1,0:T(8,128)S(1)} %shard_map.83.own, f32[4,4,64,128]{3,2,1,0:T(8,128)S(1)} %collective-permute-done.10.other), custom_call_target="tpu_custom_call" | custom-call | tf_op jit(solution)/shard_map/pallas_call | solution.py:818
  (10 shorter events, 0.0 us)
Async XLA Ops:
  3.0 8.9 %collective-permute-start.1 = (f32[16,8,128]{2,1,0:T(8,128)S(1)}, f32[16,8,128]{2,1,0:T(8,128)S(1)}, u32[]{:S(2)}, u32[]{:S(2)}) collective-permute-start(f32[16,8,128]{2,1,0:T(8,128)S(1)} %get-tuple-element.12), channel_id=1, source_target_pairs={{0,24},{8,0},{16,8},{24,16},{1,25},{9,1},{17,9},{25,17},{2,26},{10... | collective-permute-start | bytes 196616 | tf_op jit(solution)/shard_map/ppermute | solution.py:830
  6.9 4.9 %collective-permute-start = (f32[10,8,128]{2,1,0:T(8,128)S(1)}, f32[10,8,128]{2,1,0:T(8,128)S(1)}, u32[]{:S(2)}, u32[]{:S(2)}) collective-permute-start(f32[10,8,128]{2,1,0:T(8,128)S(1)} %get-tuple-element.11), channel_id=1, source_target_pairs={{0,8},{8,16},{16,24},{24,0},{1,9},{9,17},{17,25},{25,1},{2,10},{10... | collective-permute-start | bytes 122888 | tf_op jit(solution)/shard_map/ppermute | solution.py:830
  6.9 7.9 %collective-permute-start.4 = (f32[64,128]{1,0:T(8,128)S(1)}, f32[64,128]{1,0:T(8,128)S(1)}, u32[]{:S(2)}, u32[]{:S(2)}) collective-permute-start(f32[64,128]{1,0:T(8,128)S(1)} %get-tuple-element.17.refs_3_), channel_id=1, source_target_pairs={{0,6},{1,7},{2,4},{3,5},{4,2},{5,3},{6,0},{7,1},{8,14},{9,15},{10,... | collective-permute-start | bytes 98312 | tf_op jit(solution)/shard_map/ppermute | solution.py:834
  10.5 4.8 %collective-permute-start.5 = (f32[64,128]{1,0:T(8,128)S(1)}, f32[64,128]{1,0:T(8,128)S(1)}, u32[]{:S(2)}, u32[]{:S(2)}) collective-permute-start(f32[64,128]{1,0:T(8,128)S(1)} %get-tuple-element.17.refs_3_), channel_id=1, source_target_pairs={{0,4},{1,5},{2,6},{3,7},{4,0},{5,1},{6,2},{7,3},{8,12},{9,13},{10,... | collective-permute-start | bytes 98312 | tf_op jit(solution)/shard_map/ppermute | solution.py:834
  10.5 4.8 %collective-permute-start.6 = (f32[64,128]{1,0:T(8,128)S(1)}, f32[64,128]{1,0:T(8,128)S(1)}, u32[]{:S(2)}, u32[]{:S(2)}) collective-permute-start(f32[64,128]{1,0:T(8,128)S(1)} %get-tuple-element.17.refs_3_), channel_id=1, source_target_pairs={{0,2},{1,3},{2,0},{3,1},{4,6},{5,7},{6,4},{7,5},{8,10},{9,11},{10,... | collective-permute-start | bytes 98312 | tf_op jit(solution)/shard_map/ppermute | solution.py:834
  13.0 6.9 %collective-permute-start.2 = (f32[88,128]{1,0:T(8,128)S(1)}, f32[88,128]{1,0:T(8,128)S(1)}, u32[]{:S(2)}, u32[]{:S(2)}) collective-permute-start(f32[88,128]{1,0:T(8,128)S(1)} %get-tuple-element.15.refs_4_), channel_id=1, source_target_pairs={{0,7},{1,0},{2,1},{3,2},{4,3},{5,4},{6,5},{7,6},{8,15},{9,8},{10,9... | collective-permute-start | bytes 135176 | tf_op jit(solution)/shard_map/ppermute | solution.py:830
  14.9 5.1 %copy-start = (bf16[1280,128]{1,0:T(8,128)(2,1)S(1)}, bf16[1280,128]{1,0:T(8,128)(2,1)}, u32[]{:S(2)}) copy-start(bf16[1280,128]{1,0:T(8,128)(2,1)} %constant.11.clone.narrow) | copy-start | bytes 983044
  14.9 5.1 %copy-start.1 = (bf16[528,256]{1,0:T(8,128)(2,1)S(1)}, bf16[528,256]{1,0:T(8,128)(2,1)}, u32[]{:S(2)}) copy-start(bf16[528,256]{1,0:T(8,128)(2,1)} %constant.10.clone.wide) | copy-start | bytes 811012
  14.9 5.0 %collective-permute-start.3 = (f32[48,128]{1,0:T(8,128)S(1)}, f32[48,128]{1,0:T(8,128)S(1)}, u32[]{:S(2)}, u32[]{:S(2)}) collective-permute-start(f32[48,128]{1,0:T(8,128)S(1)} %get-tuple-element.16), channel_id=1, source_target_pairs={{0,1},{1,2},{2,3},{3,4},{4,5},{5,6},{6,7},{7,0},{8,9},{9,10},{10,1... | collective-permute-start | bytes 73736 | tf_op jit(solution)/shard_map/ppermute | solution.py:830
  15.4 8.1 %collective-permute-start.7 = (f32[256,128]{1,0:T(8,128)S(1)}, f32[256,128]{1,0:T(8,128)S(1)}, u32[]{:S(2)}, u32[]{:S(2)}) collective-permute-start(f32[256,128]{1,0:T(8,128)S(1)} %shard_map.82.refs_3_), channel_id=1, source_target_pairs={{0,16},{8,24},{16,0},{24,8},{1,17},{9,25},{17,1},{25,9},{2,18},{10... | collective-permute-start | bytes 393224 | tf_op jit(solution)/shard_map/ppermute | solution.py:834
  16.5 7.2 %collective-permute-start.8 = (f32[256,128]{1,0:T(8,128)S(1)}, f32[256,128]{1,0:T(8,128)S(1)}, u32[]{:S(2)}, u32[]{:S(2)}) collective-permute-start(f32[256,128]{1,0:T(8,128)S(1)} %shard_map.82.refs_3_), channel_id=1, source_target_pairs={{0,24},{8,16},{16,8},{24,0},{1,25},{9,17},{17,9},{25,1},{2,26},{10... | collective-permute-start | bytes 393224 | tf_op jit(solution)/shard_map/ppermute | solution.py:834
  18.8 5.6 %collective-permute-start.9 = (f32[256,128]{1,0:T(8,128)S(1)}, f32[256,128]{1,0:T(8,128)S(1)}, u32[]{:S(2)}, u32[]{:S(2)}) collective-permute-start(f32[256,128]{1,0:T(8,128)S(1)} %shard_map.82.refs_3_), channel_id=1, source_target_pairs={{0,8},{8,0},{16,24},{24,16},{1,9},{9,1},{17,25},{25,17},{2,10},{10... | collective-permute-start | bytes 393224 | tf_op jit(solution)/shard_map/ppermute | solution.py:834
  24.7 2.0 %collective-permute-start.10 = (f32[4,4,64,128]{3,2,1,0:T(8,128)S(1)}, f32[4,4,64,128]{3,2,1,0:T(8,128)S(1)}, u32[]{:S(2)}, u32[]{:S(2)}) collective-permute-start(f32[4,4,64,128]{3,2,1,0:T(8,128)S(1)} %shard_map.83.own), channel_id=1, source_target_pairs={{0,1},{1,0},{2,3},{3,2},{4,5},{5,4},{6,7},{7,6},{8,9},{9,8},{10,11... | collective-permute-start | bytes 1572872 | tf_op jit(solution)/shard_map/ppermute | solution.py:834

commit v10 on v8

--- a/solution.py
+++ b/solution.py
@@ -794,17 +794,16 @@
         return 0
 
     def copy(i):
-        rows = pl.ds(pl.multiple_of(16 * i, 16), 16)
+        rows = pl.ds(pl.multiple_of(8 * i, 8), 8)
         return pltpu.make_async_copy(out.at[:, :, rows], out_hbm.at[:, :, rows], sems.at[i])
 
-    def pair(i, _):
-        block(2 * i, 0)
-        block(2 * i + 1, 0)
+    def one(i, _):
+        block(i, 0)
         copy(i).start()
         return 0
 
-    lax.fori_loop(0, count_x, pair, 0)
-    for i in range(count_x):
+    lax.fori_loop(0, 2 * count_x, one, 0)
+    for i in range(2 * count_x):
         copy(i).wait()
 
 
@@ -816,7 +815,7 @@
         out_shape=jax.ShapeDtypeStruct(shape, F32),
         in_specs=[vmem, vmem],
         out_specs=pl.BlockSpec(memory_space=pltpu.HBM),
-        scratch_shapes=[pltpu.VMEM(shape, F32), pltpu.SemaphoreType.DMA((count_x,))],
+        scratch_shapes=[pltpu.VMEM(shape, F32), pltpu.SemaphoreType.DMA((2 * count_x,))],
         compiler_params=pltpu.CompilerParams(vmem_limit_bytes=VMEM_LIMIT),
     )(own, other)
 

time: 28 us -> 28.3 us (1.011)
  Pallas kernels: 10.5 us -> 10.8 us
    pallas_call x1, Pallas kernels: 1.37 us -> 1.69 us  [coarse_step(): pl.pallas_call(functools.partial(coarse_kernel, count_x, count_y), out_sh...]
where the time goes in v10:
time: 28.3 us; the launch traced here: 28.1 us
  starting transfers between devices  13.9 us (49%)
  Pallas kernels  10.8 us (38%)
  waiting for transfers between devices  2.73 us (10%)
  between operations  0.71 us (3%)
    ppermute x7, starting transfers between devices, swapped(): lax.ppermute(x, axis, [(i, i ^ distance) for i in range(lax.axis_size(axi...  8.09 us
    ppermute x4, starting transfers between devices, shifted(): lax.ppermute(x, axis, [(i, (i + step) % count) for i in range(count)])  5.76 us
    pallas_call x1, Pallas kernels, main_step(): pl.pallas_call(main_kernel, grid=(1,), out_shape=jax.ShapeDtypeStruct((4...  3.52 us
    pallas_call x1, Pallas kernels, first_step(): pl.pallas_call(first_kernel, out_shape=[jax.ShapeDtypeStruct(s, F32) for...  2.33 us
    pallas_call x1, Pallas kernels, coarse_step(): pl.pallas_call(functools.partial(coarse_kernel, count_x, count_y), out_sh...  1.69 us
    ppermute x7, waiting for transfers between devices, swapped(): lax.ppermute(x, axis, [(i, i ^ distance) for i in range(lax.axis_size(axi...  1.62 us
    pallas_call x1, Pallas kernels, cells_step(): pl.pallas_call(cells_kernel, out_shape=jax.ShapeDtypeStruct(shape, F32),...  1.37 us
    pallas_call x1, Pallas kernels, edge_step(): pl.pallas_call(edge_kernel, out_shape=[jax.ShapeDtypeStruct(s, F32) for s...  1.21 us
  transfers between devices with their start and end apart: 11, of which 5 were waited for; matrix products, arithmetic and copies ran while one was open for 0% of the time, Pallas kernels for 23%

profile of v10, /device:TPU:0, one launch (start us, length us, event | category | flops | bytes accessed | tf_op | source)
XLA Modules:
  0.0 28.1 jit_solution(4053202992407454420)
XLA Ops:
  0.6 2.3 %shard_map.77 = (f32[3840,128]{1,0:T(8,128)S(1)}, f32[16,8,128]{2,1,0:T(8,128)S(1)}, f32[10,8,128]{2,1,0:T(8,128)S(1)}, f32[2,8,128]{2,1,0:T(8,128)S(1)}, f32[64,128]{1,0:T(8,128)S(1)}) custom-call(f32[3,16,64,128]{3,2,1,0:T(8,128)} %field.1, s32[2,2,4,7]{3,2,1,0:T(4,128)} %bitcast.5, bf16[400,128]{1,0:T(8,128)(2,1)} %constant.8.clone.table_hbm), custom_call_target="tpu_custom_call" | custom-call | tf_op jit(solution)/shard_map/pallas_call | solution.py:336
  3.0 3.9 %collective-permute-start.1 = (f32[16,8,128]{2,1,0:T(8,128)S(1)}, f32[16,8,128]{2,1,0:T(8,128)S(1)}, u32[]{:S(2)}, u32[]{:S(2)}) collective-permute-start(f32[16,8,128]{2,1,0:T(8,128)S(1)} %get-tuple-element.12), channel_id=1, source_target_pairs={{0,24},{8,0},{16,8},{24,16},{1,25},{9,1},{17,9},{25,17},{2,26},{10... | collective-permute-start | bytes 196616 | tf_op jit(solution)/shard_map/ppermute | solution.py:825
  6.9 0.0 collective-permute-start
  6.9 3.6 %collective-permute-start.4 = (f32[64,128]{1,0:T(8,128)S(1)}, f32[64,128]{1,0:T(8,128)S(1)}, u32[]{:S(2)}, u32[]{:S(2)}) collective-permute-start(f32[64,128]{1,0:T(8,128)S(1)} %get-tuple-element.17.refs_3_), channel_id=1, source_target_pairs={{0,6},{1,7},{2,4},{3,5},{4,2},{5,3},{6,0},{7,1},{8,14},{9,15},{10,... | collective-permute-start | bytes 98312 | tf_op jit(solution)/shard_map/ppermute | solution.py:829
  10.5 0.0 collective-permute-start.5
  10.5 0.8 %collective-permute-start.6 = (f32[64,128]{1,0:T(8,128)S(1)}, f32[64,128]{1,0:T(8,128)S(1)}, u32[]{:S(2)}, u32[]{:S(2)}) collective-permute-start(f32[64,128]{1,0:T(8,128)S(1)} %get-tuple-element.17.refs_3_), channel_id=1, source_target_pairs={{0,2},{1,3},{2,0},{3,1},{4,6},{5,7},{6,4},{7,5},{8,10},{9,11},{10,... | collective-permute-start | bytes 98312 | tf_op jit(solution)/shard_map/ppermute | solution.py:829
  11.3 0.3 %shard_map.78.parts_in = f32[3840,128]{1,0:T(8,128)S(1)} custom-call(f32[3840,128]{1,0:T(8,128)S(1)} %get-tuple-element.10.lifted), custom_call_target="tpu_custom_call" | custom-call | tf_op jit(solution)/shard_map/pallas_call | solution.py:372
  11.6 0.2 collective-permute-done.north.north_mask
  11.8 1.2 %shard_map.79 = (f32[3840,128]{1,0:T(8,128)S(1)}, f32[88,128]{1,0:T(8,128)S(1)}, f32[48,128]{1,0:T(8,128)S(1)}) custom-call(f32[3840,128]{1,0:T(8,128)S(1)} %shard_map.78.parts_in, f32[3840,128]{1,0:T(8,128)S(1)} %get-tuple-element.10.lifted, f32[10,8,128]{2,1,0:T(8,128)S(1)} %collective-permute-done.north.north_mask, ...), custom_call_target="tpu_custom_call", output_to_operand_aliasing={{0}: (0, {})} | custom-call | flops 20000000000 | bytes 8000000 | tf_op jit(solution)/shard_map/pallas_call | solution.py:446
  13.0 1.8 %collective-permute-start.2 = (f32[88,128]{1,0:T(8,128)S(1)}, f32[88,128]{1,0:T(8,128)S(1)}, u32[]{:S(2)}, u32[]{:S(2)}) collective-permute-start(f32[88,128]{1,0:T(8,128)S(1)} %get-tuple-element.15.refs_4_), channel_id=1, source_target_pairs={{0,7},{1,0},{2,1},{3,2},{4,3},{5,4},{6,5},{7,6},{8,15},{9,8},{10,9... | collective-permute-start | bytes 135176 | tf_op jit(solution)/shard_map/ppermute | solution.py:825
  14.9 0.5 %collective-permute-done.5.refs_1_ = f32[64,128]{1,0:T(8,128)S(1)} collective-permute-done((f32[64,128]{1,0:T(8,128)S(1)}, f32[64,128]{1,0:T(8,128)S(1)}, u32[]{:S(2)}, u32[]{:S(2)}) %collective-permute-start.5) | collective-permute-done | bytes 32800 | tf_op jit(solution)/shard_map/ppermute | solution.py:829
  15.4 3.0 %collective-permute-start.7 = (f32[256,128]{1,0:T(8,128)S(1)}, f32[256,128]{1,0:T(8,128)S(1)}, u32[]{:S(2)}, u32[]{:S(2)}) collective-permute-start(f32[256,128]{1,0:T(8,128)S(1)} %shard_map.82.refs_3_), channel_id=1, source_target_pairs={{0,24},{8,16},{16,8},{24,0},{1,25},{9,17},{17,9},{25,1},{2,26},{10... | collective-permute-start | bytes 393224 | tf_op jit(solution)/shard_map/ppermute | solution.py:829
  18.3 0.5 %collective-permute-start.8 = (f32[256,128]{1,0:T(8,128)S(1)}, f32[256,128]{1,0:T(8,128)S(1)}, u32[]{:S(2)}, u32[]{:S(2)}) collective-permute-start(f32[256,128]{1,0:T(8,128)S(1)} %shard_map.82.refs_3_), channel_id=1, source_target_pairs={{0,16},{8,24},{16,0},{24,8},{1,17},{9,25},{17,1},{25,9},{2,18},{10... | collective-permute-start | bytes 393224 | tf_op jit(solution)/shard_map/ppermute | solution.py:829
  18.8 0.1 collective-permute-start.9
  19.0 0.9 %collective-permute-done.3.west = f32[48,128]{1,0:T(8,128)S(1)} collective-permute-done((f32[48,128]{1,0:T(8,128)S(1)}, f32[48,128]{1,0:T(8,128)S(1)}, u32[]{:S(2)}, u32[]{:S(2)}) %collective-permute-start.3) | collective-permute-done | bytes 24608 | tf_op jit(solution)/shard_map/ppermute | solution.py:825
  19.9 0.0 collective-permute-done.2.east
  19.9 3.5 %shard_map.80.refs_4_ = f32[4608,128]{1,0:T(8,128)S(1)} custom-call(f32[4,24,40,128]{3,2,1,0:T(8,128)S(1)} %bitcast.4, f32[3840,128]{1,0:T(8,128)S(1)} %get-tuple-element.14.flat, f32[88,128]{1,0:T(8,128)S(1)} %collective-permute-done.2.east, f32[48,128]{1,0:T(8,128)S(1)} %collective-permute-done.3.west, f32[2,8,128]{2,1,0:T(8,128)S(1)} %get-tuple-element.13.own_masks, ...), custom_call_target="tpu_custom_call" | custom-call | flops 8000000000 | bytes 8000000 | tf_op jit(solution)/shard_map/pallas_call | solution.py:692
  23.5 0.6 %collective-permute-done.8.refs_1_ = f32[256,128]{1,0:T(8,128)S(1)} collective-permute-done((f32[256,128]{1,0:T(8,128)S(1)}, f32[256,128]{1,0:T(8,128)S(1)}, u32[]{:S(2)}, u32[]{:S(2)}) %collective-permute-start.8) | collective-permute-done | bytes 131104 | tf_op jit(solution)/shard_map/ppermute | solution.py:829
  24.1 0.0 collective-permute-done.9.refs_2_
  24.1 0.3 %shard_map.83.own = f32[4,4,64,128]{3,2,1,0:T(8,128)S(1)} custom-call(f32[256,128]{1,0:T(8,128)S(1)} %collective-permute-done.7.refs_0_, f32[256,128]{1,0:T(8,128)S(1)} %collective-permute-done.8.refs_1_, f32[256,128]{1,0:T(8,128)S(1)} %collective-permute-done.9.refs_2_, f32[256,128]{1,0:T(8,128)S(1)} %shard_map.82.refs_3_, f32[4608,128]{1,0:T(8,128)S(1)} %shard_map.80.refs_4_), custom_call_target="tpu_custom_call" | custom-call | tf_op jit(solution)/shard_map/pallas_call | solution.py:763
  24.4 0.1 collective-permute-start.10
  24.5 1.4 %shard_map.81 = f32[3,16,64,128]{3,2,1,0:T(8,128)} custom-call(f32[4,24,48,128]{3,2,1,0:T(8,128)S(1)} %bitcast.3), custom_call_target="tpu_custom_call" | custom-call | flops 4000000000 | bytes 8000000 | tf_op jit(solution)/shard_map/pallas_call | solution.py:715
  25.9 0.5 %collective-permute-done.10.other = f32[4,4,64,128]{3,2,1,0:T(8,128)S(1)} collective-permute-done((f32[4,4,64,128]{3,2,1,0:T(8,128)S(1)}, f32[4,4,64,128]{3,2,1,0:T(8,128)S(1)}, u32[]{:S(2)}, u32[]{:S(2)}) %collective-permute-start.10) | collective-permute-done | bytes 524320 | tf_op jit(solution)/shard_map/ppermute | solution.py:829
  26.4 1.7 %shard_map.84 = f32[3,4,64,256]{3,2,1,0:T(8,128)} custom-call(f32[4,4,64,128]{3,2,1,0:T(8,128)S(1)} %shard_map.83.own, f32[4,4,64,128]{3,2,1,0:T(8,128)S(1)} %collective-permute-done.10.other), custom_call_target="tpu_custom_call" | custom-call | tf_op jit(solution)/shard_map/pallas_call | solution.py:813
  (10 shorter events, 0.0 us)
Async XLA Ops:
  3.0 8.9 %collective-permute-start.1 = (f32[16,8,128]{2,1,0:T(8,128)S(1)}, f32[16,8,128]{2,1,0:T(8,128)S(1)}, u32[]{:S(2)}, u32[]{:S(2)}) collective-permute-start(f32[16,8,128]{2,1,0:T(8,128)S(1)} %get-tuple-element.12), channel_id=1, source_target_pairs={{0,24},{8,0},{16,8},{24,16},{1,25},{9,1},{17,9},{25,17},{2,26},{10... | collective-permute-start | bytes 196616 | tf_op jit(solution)/shard_map/ppermute | solution.py:825
  6.9 4.9 %collective-permute-start = (f32[10,8,128]{2,1,0:T(8,128)S(1)}, f32[10,8,128]{2,1,0:T(8,128)S(1)}, u32[]{:S(2)}, u32[]{:S(2)}) collective-permute-start(f32[10,8,128]{2,1,0:T(8,128)S(1)} %get-tuple-element.11), channel_id=1, source_target_pairs={{0,8},{8,16},{16,24},{24,0},{1,9},{9,17},{17,25},{25,1},{2,10},{10... | collective-permute-start | bytes 122888 | tf_op jit(solution)/shard_map/ppermute | solution.py:825
  6.9 7.9 %collective-permute-start.4 = (f32[64,128]{1,0:T(8,128)S(1)}, f32[64,128]{1,0:T(8,128)S(1)}, u32[]{:S(2)}, u32[]{:S(2)}) collective-permute-start(f32[64,128]{1,0:T(8,128)S(1)} %get-tuple-element.17.refs_3_), channel_id=1, source_target_pairs={{0,6},{1,7},{2,4},{3,5},{4,2},{5,3},{6,0},{7,1},{8,14},{9,15},{10,... | collective-permute-start | bytes 98312 | tf_op jit(solution)/shard_map/ppermute | solution.py:829
  10.5 4.8 %collective-permute-start.5 = (f32[64,128]{1,0:T(8,128)S(1)}, f32[64,128]{1,0:T(8,128)S(1)}, u32[]{:S(2)}, u32[]{:S(2)}) collective-permute-start(f32[64,128]{1,0:T(8,128)S(1)} %get-tuple-element.17.refs_3_), channel_id=1, source_target_pairs={{0,4},{1,5},{2,6},{3,7},{4,0},{5,1},{6,2},{7,3},{8,12},{9,13},{10,... | collective-permute-start | bytes 98312 | tf_op jit(solution)/shard_map/ppermute | solution.py:829
  10.5 4.8 %collective-permute-start.6 = (f32[64,128]{1,0:T(8,128)S(1)}, f32[64,128]{1,0:T(8,128)S(1)}, u32[]{:S(2)}, u32[]{:S(2)}) collective-permute-start(f32[64,128]{1,0:T(8,128)S(1)} %get-tuple-element.17.refs_3_), channel_id=1, source_target_pairs={{0,2},{1,3},{2,0},{3,1},{4,6},{5,7},{6,4},{7,5},{8,10},{9,11},{10,... | collective-permute-start | bytes 98312 | tf_op jit(solution)/shard_map/ppermute | solution.py:829
  13.0 6.9 %collective-permute-start.2 = (f32[88,128]{1,0:T(8,128)S(1)}, f32[88,128]{1,0:T(8,128)S(1)}, u32[]{:S(2)}, u32[]{:S(2)}) collective-permute-start(f32[88,128]{1,0:T(8,128)S(1)} %get-tuple-element.15.refs_4_), channel_id=1, source_target_pairs={{0,7},{1,0},{2,1},{3,2},{4,3},{5,4},{6,5},{7,6},{8,15},{9,8},{10,9... | collective-permute-start | bytes 135176 | tf_op jit(solution)/shard_map/ppermute | solution.py:825
  14.9 5.1 %copy-start = (bf16[1280,128]{1,0:T(8,128)(2,1)S(1)}, bf16[1280,128]{1,0:T(8,128)(2,1)}, u32[]{:S(2)}) copy-start(bf16[1280,128]{1,0:T(8,128)(2,1)} %constant.11.clone.narrow) | copy-start | bytes 983044
  14.9 5.1 %copy-start.1 = (bf16[528,256]{1,0:T(8,128)(2,1)S(1)}, bf16[528,256]{1,0:T(8,128)(2,1)}, u32[]{:S(2)}) copy-start(bf16[528,256]{1,0:T(8,128)(2,1)} %constant.10.clone.wide) | copy-start | bytes 811012
  14.9 5.0 %collective-permute-start.3 = (f32[48,128]{1,0:T(8,128)S(1)}, f32[48,128]{1,0:T(8,128)S(1)}, u32[]{:S(2)}, u32[]{:S(2)}) collective-permute-start(f32[48,128]{1,0:T(8,128)S(1)} %get-tuple-element.16), channel_id=1, source_target_pairs={{0,1},{1,2},{2,3},{3,4},{4,5},{5,6},{6,7},{7,0},{8,9},{9,10},{10,1... | collective-permute-start | bytes 73736 | tf_op jit(solution)/shard_map/ppermute | solution.py:825
  15.4 8.1 %collective-permute-start.7 = (f32[256,128]{1,0:T(8,128)S(1)}, f32[256,128]{1,0:T(8,128)S(1)}, u32[]{:S(2)}, u32[]{:S(2)}) collective-permute-start(f32[256,128]{1,0:T(8,128)S(1)} %shard_map.82.refs_3_), channel_id=1, source_target_pairs={{0,24},{8,16},{16,8},{24,0},{1,25},{9,17},{17,9},{25,1},{2,26},{10... | collective-permute-start | bytes 393224 | tf_op jit(solution)/shard_map/ppermute | solution.py:829
  18.3 5.7 %collective-permute-start.8 = (f32[256,128]{1,0:T(8,128)S(1)}, f32[256,128]{1,0:T(8,128)S(1)}, u32[]{:S(2)}, u32[]{:S(2)}) collective-permute-start(f32[256,128]{1,0:T(8,128)S(1)} %shard_map.82.refs_3_), channel_id=1, source_target_pairs={{0,16},{8,24},{16,0},{24,8},{1,17},{9,25},{17,1},{25,9},{2,18},{10... | collective-permute-start | bytes 393224 | tf_op jit(solution)/shard_map/ppermute | solution.py:829
  18.8 5.2 %collective-permute-start.9 = (f32[256,128]{1,0:T(8,128)S(1)}, f32[256,128]{1,0:T(8,128)S(1)}, u32[]{:S(2)}, u32[]{:S(2)}) collective-permute-start(f32[256,128]{1,0:T(8,128)S(1)} %shard_map.82.refs_3_), channel_id=1, source_target_pairs={{0,8},{8,0},{16,24},{24,16},{1,9},{9,1},{17,25},{25,17},{2,10},{10... | collective-permute-start | bytes 393224 | tf_op jit(solution)/shard_map/ppermute | solution.py:829
  24.4 2.0 %collective-permute-start.10 = (f32[4,4,64,128]{3,2,1,0:T(8,128)S(1)}, f32[4,4,64,128]{3,2,1,0:T(8,128)S(1)}, u32[]{:S(2)}, u32[]{:S(2)}) collective-permute-start(f32[4,4,64,128]{3,2,1,0:T(8,128)S(1)} %shard_map.83.own), channel_id=1, source_target_pairs={{0,1},{1,0},{2,3},{3,2},{4,5},{5,4},{6,7},{7,6},{8,9},{9,8},{10,11... | collective-permute-start | bytes 1572872 | tf_op jit(solution)/shard_map/ppermute | solution.py:829

commit v11 on v10

--- a/solution.py
+++ b/solution.py
@@ -775,9 +775,9 @@
     lane = lax.broadcasted_iota(jnp.int32, (8, NL), 1)
     place = [lax.rem(lane + NL - 35 * v, NL) for v in range(NV)]
 
-    def block(i, _):
-        rows = pl.ds(pl.multiple_of(8 * i, 8), 8)
-        for z in range(4):
+    def plane(z, _):
+        def block(i, _):
+            rows = pl.ds(pl.multiple_of(8 * i, 8), 8)
             pieces = []
             for j in range(count_y // 2):
                 mine, theirs = own[j ^ me_z, z, rows, :], other[j ^ me_z, z, rows, :]
@@ -791,20 +791,25 @@
                         inside = (at >= 32 * q - 1) & (at < 32 * q + 34)
                         total += jnp.where(inside, pieces[4 * t + q], 0.0)
                     out[v, z, rows, NL * t : NL * (t + 1)] = pltpu.roll(total, NL - 35 * v, 1) if v else total
+            return 0
+
+        def four(i, _):
+            for k in range(4):
+                block(4 * i + k, 0)
+            return 0
+
+        lax.fori_loop(0, count_x // 2, four, 0)
+        for v in range(NV):
+            copy(v, z).start()
         return 0
 
-    def copy(i):
-        rows = pl.ds(pl.multiple_of(8 * i, 8), 8)
-        return pltpu.make_async_copy(out.at[:, :, rows], out_hbm.at[:, :, rows], sems.at[i])
-
-    def one(i, _):
-        block(i, 0)
-        copy(i).start()
-        return 0
-
-    lax.fori_loop(0, 2 * count_x, one, 0)
-    for i in range(2 * count_x):
-        copy(i).wait()
+    def copy(v, z):
+        return pltpu.make_async_copy(out.at[v, z], out_hbm.at[v, z], sems.at[v, z])
+
+    lax.fori_loop(0, 4, plane, 0)
+    for v in range(NV):
+        for z in range(4):
+            copy(v, z).wait()
 
 
 def coarse_step(own, other, count_x, count_y):
@@ -815,7 +820,7 @@
         out_shape=jax.ShapeDtypeStruct(shape, F32),
         in_specs=[vmem, vmem],
         out_specs=pl.BlockSpec(memory_space=pltpu.HBM),
-        scratch_shapes=[pltpu.VMEM(shape, F32), pltpu.SemaphoreType.DMA((2 * count_x,))],
+        scratch_shapes=[pltpu.VMEM(shape, F32), pltpu.SemaphoreType.DMA((NV, 4))],
         compiler_params=pltpu.CompilerParams(vmem_limit_bytes=VMEM_LIMIT),
     )(own, other)
 

time: 28.3 us -> 28.3 us (level)
  no operation moved by 1% of the time
where the time goes in v11:
time: 28.3 us; the launch traced here: 28.1 us
  starting transfers between devices  13.9 us (49%)
  Pallas kernels  10.8 us (38%)
  waiting for transfers between devices  2.73 us (10%)
  between operations  0.71 us (3%)
    ppermute x7, starting transfers between devices, swapped(): lax.ppermute(x, axis, [(i, i ^ distance) for i in range(lax.axis_size(axi...  8.09 us
    ppermute x4, starting transfers between devices, shifted(): lax.ppermute(x, axis, [(i, (i + step) % count) for i in range(count)])  5.76 us
    pallas_call x1, Pallas kernels, main_step(): pl.pallas_call(main_kernel, grid=(1,), out_shape=jax.ShapeDtypeStruct((4...  3.52 us
    pallas_call x1, Pallas kernels, first_step(): pl.pallas_call(first_kernel, out_shape=[jax.ShapeDtypeStruct(s, F32) for...  2.33 us
    pallas_call x1, Pallas kernels, coarse_step(): pl.pallas_call(functools.partial(coarse_kernel, count_x, count_y), out_sh...  1.75 us
    ppermute x7, waiting for transfers between devices, swapped(): lax.ppermute(x, axis, [(i, i ^ distance) for i in range(lax.axis_size(axi...  1.62 us
    pallas_call x1, Pallas kernels, cells_step(): pl.pallas_call(cells_kernel, out_shape=jax.ShapeDtypeStruct(shape, F32),...  1.37 us
    pallas_call x1, Pallas kernels, edge_step(): pl.pallas_call(edge_kernel, out_shape=[jax.ShapeDtypeStruct(s, F32) for s...  1.21 us
  transfers between devices with their start and end apart: 11, of which 5 were waited for; matrix products, arithmetic and copies ran while one was open for 0% of the time, Pallas kernels for 23%

profile of v11, /device:TPU:0, one launch (start us, length us, event | category | flops | bytes accessed | tf_op | source)
XLA Modules:
  0.0 28.1 jit_solution(8729634768316750520)
XLA Ops:
  0.6 2.3 %shard_map.77 = (f32[3840,128]{1,0:T(8,128)S(1)}, f32[16,8,128]{2,1,0:T(8,128)S(1)}, f32[10,8,128]{2,1,0:T(8,128)S(1)}, f32[2,8,128]{2,1,0:T(8,128)S(1)}, f32[64,128]{1,0:T(8,128)S(1)}) custom-call(f32[3,16,64,128]{3,2,1,0:T(8,128)} %field.1, s32[2,2,4,7]{3,2,1,0:T(4,128)} %bitcast.5, bf16[400,128]{1,0:T(8,128)(2,1)} %constant.8.clone.table_hbm), custom_call_target="tpu_custom_call" | custom-call | tf_op jit(solution)/shard_map/pallas_call | solution.py:336
  3.0 3.9 %collective-permute-start.1 = (f32[16,8,128]{2,1,0:T(8,128)S(1)}, f32[16,8,128]{2,1,0:T(8,128)S(1)}, u32[]{:S(2)}, u32[]{:S(2)}) collective-permute-start(f32[16,8,128]{2,1,0:T(8,128)S(1)} %get-tuple-element.12), channel_id=1, source_target_pairs={{0,24},{8,0},{16,8},{24,16},{1,25},{9,1},{17,9},{25,17},{2,26},{10... | collective-permute-start | bytes 196616 | tf_op jit(solution)/shard_map/ppermute | solution.py:830
  6.9 0.0 collective-permute-start
  6.9 3.6 %collective-permute-start.4 = (f32[64,128]{1,0:T(8,128)S(1)}, f32[64,128]{1,0:T(8,128)S(1)}, u32[]{:S(2)}, u32[]{:S(2)}) collective-permute-start(f32[64,128]{1,0:T(8,128)S(1)} %get-tuple-element.17.refs_3_), channel_id=1, source_target_pairs={{0,6},{1,7},{2,4},{3,5},{4,2},{5,3},{6,0},{7,1},{8,14},{9,15},{10,... | collective-permute-start | bytes 98312 | tf_op jit(solution)/shard_map/ppermute | solution.py:834
  10.5 0.0 collective-permute-start.5
  10.5 0.8 %collective-permute-start.6 = (f32[64,128]{1,0:T(8,128)S(1)}, f32[64,128]{1,0:T(8,128)S(1)}, u32[]{:S(2)}, u32[]{:S(2)}) collective-permute-start(f32[64,128]{1,0:T(8,128)S(1)} %get-tuple-element.17.refs_3_), channel_id=1, source_target_pairs={{0,2},{1,3},{2,0},{3,1},{4,6},{5,7},{6,4},{7,5},{8,10},{9,11},{10,... | collective-permute-start | bytes 98312 | tf_op jit(solution)/shard_map/ppermute | solution.py:834
  11.3 0.3 %shard_map.78.parts_in = f32[3840,128]{1,0:T(8,128)S(1)} custom-call(f32[3840,128]{1,0:T(8,128)S(1)} %get-tuple-element.10.lifted), custom_call_target="tpu_custom_call" | custom-call | tf_op jit(solution)/shard_map/pallas_call | solution.py:372
  11.6 0.2 collective-permute-done.north.north_mask
  11.8 1.2 %shard_map.79 = (f32[3840,128]{1,0:T(8,128)S(1)}, f32[88,128]{1,0:T(8,128)S(1)}, f32[48,128]{1,0:T(8,128)S(1)}) custom-call(f32[3840,128]{1,0:T(8,128)S(1)} %shard_map.78.parts_in, f32[3840,128]{1,0:T(8,128)S(1)} %get-tuple-element.10.lifted, f32[10,8,128]{2,1,0:T(8,128)S(1)} %collective-permute-done.north.north_mask, ...), custom_call_target="tpu_custom_call", output_to_operand_aliasing={{0}: (0, {})} | custom-call | flops 20000000000 | bytes 8000000 | tf_op jit(solution)/shard_map/pallas_call | solution.py:446
  13.0 1.8 %collective-permute-start.2 = (f32[88,128]{1,0:T(8,128)S(1)}, f32[88,128]{1,0:T(8,128)S(1)}, u32[]{:S(2)}, u32[]{:S(2)}) collective-permute-start(f32[88,128]{1,0:T(8,128)S(1)} %get-tuple-element.15.refs_4_), channel_id=1, source_target_pairs={{0,7},{1,0},{2,1},{3,2},{4,3},{5,4},{6,5},{7,6},{8,15},{9,8},{10,9... | collective-permute-start | bytes 135176 | tf_op jit(solution)/shard_map/ppermute | solution.py:830
  14.9 0.5 %collective-permute-done.5.refs_1_ = f32[64,128]{1,0:T(8,128)S(1)} collective-permute-done((f32[64,128]{1,0:T(8,128)S(1)}, f32[64,128]{1,0:T(8,128)S(1)}, u32[]{:S(2)}, u32[]{:S(2)}) %collective-permute-start.5) | collective-permute-done | bytes 32800 | tf_op jit(solution)/shard_map/ppermute | solution.py:834
  15.4 3.0 %collective-permute-start.7 = (f32[256,128]{1,0:T(8,128)S(1)}, f32[256,128]{1,0:T(8,128)S(1)}, u32[]{:S(2)}, u32[]{:S(2)}) collective-permute-start(f32[256,128]{1,0:T(8,128)S(1)} %shard_map.82.refs_3_), channel_id=1, source_target_pairs={{0,24},{8,16},{16,8},{24,0},{1,25},{9,17},{17,9},{25,1},{2,26},{10... | collective-permute-start | bytes 393224 | tf_op jit(solution)/shard_map/ppermute | solution.py:834
  18.3 0.5 %collective-permute-start.8 = (f32[256,128]{1,0:T(8,128)S(1)}, f32[256,128]{1,0:T(8,128)S(1)}, u32[]{:S(2)}, u32[]{:S(2)}) collective-permute-start(f32[256,128]{1,0:T(8,128)S(1)} %shard_map.82.refs_3_), channel_id=1, source_target_pairs={{0,16},{8,24},{16,0},{24,8},{1,17},{9,25},{17,1},{25,9},{2,18},{10... | collective-permute-start | bytes 393224 | tf_op jit(solution)/shard_map/ppermute | solution.py:834
  18.8 0.1 collective-permute-start.9
  19.0 0.9 %collective-permute-done.3.west = f32[48,128]{1,0:T(8,128)S(1)} collective-permute-done((f32[48,128]{1,0:T(8,128)S(1)}, f32[48,128]{1,0:T(8,128)S(1)}, u32[]{:S(2)}, u32[]{:S(2)}) %collective-permute-start.3) | collective-permute-done | bytes 24608 | tf_op jit(solution)/shard_map/ppermute | solution.py:830
  19.9 0.0 collective-permute-done.2.east
  19.9 3.5 %shard_map.80.refs_4_ = f32[4608,128]{1,0:T(8,128)S(1)} custom-call(f32[4,24,40,128]{3,2,1,0:T(8,128)S(1)} %bitcast.4, f32[3840,128]{1,0:T(8,128)S(1)} %get-tuple-element.14.flat, f32[88,128]{1,0:T(8,128)S(1)} %collective-permute-done.2.east, f32[48,128]{1,0:T(8,128)S(1)} %collective-permute-done.3.west, f32[2,8,128]{2,1,0:T(8,128)S(1)} %get-tuple-element.13.own_masks, ...), custom_call_target="tpu_custom_call" | custom-call | flops 8000000000 | bytes 8000000 | tf_op jit(solution)/shard_map/pallas_call | solution.py:692
  23.5 0.6 %collective-permute-done.8.refs_1_ = f32[256,128]{1,0:T(8,128)S(1)} collective-permute-done((f32[256,128]{1,0:T(8,128)S(1)}, f32[256,128]{1,0:T(8,128)S(1)}, u32[]{:S(2)}, u32[]{:S(2)}) %collective-permute-start.8) | collective-permute-done | bytes 131104 | tf_op jit(solution)/shard_map/ppermute | solution.py:834
  24.1 0.0 collective-permute-done.9.refs_2_
  24.1 0.3 %shard_map.83.own = f32[4,4,64,128]{3,2,1,0:T(8,128)S(1)} custom-call(f32[256,128]{1,0:T(8,128)S(1)} %collective-permute-done.7.refs_0_, f32[256,128]{1,0:T(8,128)S(1)} %collective-permute-done.8.refs_1_, f32[256,128]{1,0:T(8,128)S(1)} %collective-permute-done.9.refs_2_, f32[256,128]{1,0:T(8,128)S(1)} %shard_map.82.refs_3_, f32[4608,128]{1,0:T(8,128)S(1)} %shard_map.80.refs_4_), custom_call_target="tpu_custom_call" | custom-call | tf_op jit(solution)/shard_map/pallas_call | solution.py:763
  24.4 0.1 collective-permute-start.10
  24.5 1.4 %shard_map.81 = f32[3,16,64,128]{3,2,1,0:T(8,128)} custom-call(f32[4,24,48,128]{3,2,1,0:T(8,128)S(1)} %bitcast.3), custom_call_target="tpu_custom_call" | custom-call | flops 4000000000 | bytes 8000000 | tf_op jit(solution)/shard_map/pallas_call | solution.py:715
  25.9 0.5 %collective-permute-done.10.other = f32[4,4,64,128]{3,2,1,0:T(8,128)S(1)} collective-permute-done((f32[4,4,64,128]{3,2,1,0:T(8,128)S(1)}, f32[4,4,64,128]{3,2,1,0:T(8,128)S(1)}, u32[]{:S(2)}, u32[]{:S(2)}) %collective-permute-start.10) | collective-permute-done | bytes 524320 | tf_op jit(solution)/shard_map/ppermute | solution.py:834
  26.4 1.8 %shard_map.84 = f32[3,4,64,256]{3,2,1,0:T(8,128)} custom-call(f32[4,4,64,128]{3,2,1,0:T(8,128)S(1)} %shard_map.83.own, f32[4,4,64,128]{3,2,1,0:T(8,128)S(1)} %collective-permute-done.10.other), custom_call_target="tpu_custom_call" | custom-call | tf_op jit(solution)/shard_map/pallas_call | solution.py:818
  (10 shorter events, 0.0 us)
Async XLA Ops:
  3.0 8.9 %collective-permute-start.1 = (f32[16,8,128]{2,1,0:T(8,128)S(1)}, f32[16,8,128]{2,1,0:T(8,128)S(1)}, u32[]{:S(2)}, u32[]{:S(2)}) collective-permute-start(f32[16,8,128]{2,1,0:T(8,128)S(1)} %get-tuple-element.12), channel_id=1, source_target_pairs={{0,24},{8,0},{16,8},{24,16},{1,25},{9,1},{17,9},{25,17},{2,26},{10... | collective-permute-start | bytes 196616 | tf_op jit(solution)/shard_map/ppermute | solution.py:830
  6.9 4.9 %collective-permute-start = (f32[10,8,128]{2,1,0:T(8,128)S(1)}, f32[10,8,128]{2,1,0:T(8,128)S(1)}, u32[]{:S(2)}, u32[]{:S(2)}) collective-permute-start(f32[10,8,128]{2,1,0:T(8,128)S(1)} %get-tuple-element.11), channel_id=1, source_target_pairs={{0,8},{8,16},{16,24},{24,0},{1,9},{9,17},{17,25},{25,1},{2,10},{10... | collective-permute-start | bytes 122888 | tf_op jit(solution)/shard_map/ppermute | solution.py:830
  6.9 7.9 %collective-permute-start.4 = (f32[64,128]{1,0:T(8,128)S(1)}, f32[64,128]{1,0:T(8,128)S(1)}, u32[]{:S(2)}, u32[]{:S(2)}) collective-permute-start(f32[64,128]{1,0:T(8,128)S(1)} %get-tuple-element.17.refs_3_), channel_id=1, source_target_pairs={{0,6},{1,7},{2,4},{3,5},{4,2},{5,3},{6,0},{7,1},{8,14},{9,15},{10,... | collective-permute-start | bytes 98312 | tf_op jit(solution)/shard_map/ppermute | solution.py:834
  10.5 4.8 %collective-permute-start.5 = (f32[64,128]{1,0:T(8,128)S(1)}, f32[64,128]{1,0:T(8,128)S(1)}, u32[]{:S(2)}, u32[]{:S(2)}) collective-permute-start(f32[64,128]{1,0:T(8,128)S(1)} %get-tuple-element.17.refs_3_), channel_id=1, source_target_pairs={{0,4},{1,5},{2,6},{3,7},{4,0},{5,1},{6,2},{7,3},{8,12},{9,13},{10,... | collective-permute-start | bytes 98312 | tf_op jit(solution)/shard_map/ppermute | solution.py:834
  10.5 4.8 %collective-permute-start.6 = (f32[64,128]{1,0:T(8,128)S(1)}, f32[64,128]{1,0:T(8,128)S(1)}, u32[]{:S(2)}, u32[]{:S(2)}) collective-permute-start(f32[64,128]{1,0:T(8,128)S(1)} %get-tuple-element.17.refs_3_), channel_id=1, source_target_pairs={{0,2},{1,3},{2,0},{3,1},{4,6},{5,7},{6,4},{7,5},{8,10},{9,11},{10,... | collective-permute-start | bytes 98312 | tf_op jit(solution)/shard_map/ppermute | solution.py:834
  13.0 6.9 %collective-permute-start.2 = (f32[88,128]{1,0:T(8,128)S(1)}, f32[88,128]{1,0:T(8,128)S(1)}, u32[]{:S(2)}, u32[]{:S(2)}) collective-permute-start(f32[88,128]{1,0:T(8,128)S(1)} %get-tuple-element.15.refs_4_), channel_id=1, source_target_pairs={{0,7},{1,0},{2,1},{3,2},{4,3},{5,4},{6,5},{7,6},{8,15},{9,8},{10,9... | collective-permute-start | bytes 135176 | tf_op jit(solution)/shard_map/ppermute | solution.py:830
  14.9 5.1 %copy-start = (bf16[1280,128]{1,0:T(8,128)(2,1)S(1)}, bf16[1280,128]{1,0:T(8,128)(2,1)}, u32[]{:S(2)}) copy-start(bf16[1280,128]{1,0:T(8,128)(2,1)} %constant.11.clone.narrow) | copy-start | bytes 983044
  14.9 5.1 %copy-start.1 = (bf16[528,256]{1,0:T(8,128)(2,1)S(1)}, bf16[528,256]{1,0:T(8,128)(2,1)}, u32[]{:S(2)}) copy-start(bf16[528,256]{1,0:T(8,128)(2,1)} %constant.10.clone.wide) | copy-start | bytes 811012
  14.9 5.0 %collective-permute-start.3 = (f32[48,128]{1,0:T(8,128)S(1)}, f32[48,128]{1,0:T(8,128)S(1)}, u32[]{:S(2)}, u32[]{:S(2)}) collective-permute-start(f32[48,128]{1,0:T(8,128)S(1)} %get-tuple-element.16), channel_id=1, source_target_pairs={{0,1},{1,2},{2,3},{3,4},{4,5},{5,6},{6,7},{7,0},{8,9},{9,10},{10,1... | collective-permute-start | bytes 73736 | tf_op jit(solution)/shard_map/ppermute | solution.py:830
  15.4 8.1 %collective-permute-start.7 = (f32[256,128]{1,0:T(8,128)S(1)}, f32[256,128]{1,0:T(8,128)S(1)}, u32[]{:S(2)}, u32[]{:S(2)}) collective-permute-start(f32[256,128]{1,0:T(8,128)S(1)} %shard_map.82.refs_3_), channel_id=1, source_target_pairs={{0,24},{8,16},{16,8},{24,0},{1,25},{9,17},{17,9},{25,1},{2,26},{10... | collective-permute-start | bytes 393224 | tf_op jit(solution)/shard_map/ppermute | solution.py:834
  18.3 5.7 %collective-permute-start.8 = (f32[256,128]{1,0:T(8,128)S(1)}, f32[256,128]{1,0:T(8,128)S(1)}, u32[]{:S(2)}, u32[]{:S(2)}) collective-permute-start(f32[256,128]{1,0:T(8,128)S(1)} %shard_map.82.refs_3_), channel_id=1, source_target_pairs={{0,16},{8,24},{16,0},{24,8},{1,17},{9,25},{17,1},{25,9},{2,18},{10... | collective-permute-start | bytes 393224 | tf_op jit(solution)/shard_map/ppermute | solution.py:834
  18.8 5.2 %collective-permute-start.9 = (f32[256,128]{1,0:T(8,128)S(1)}, f32[256,128]{1,0:T(8,128)S(1)}, u32[]{:S(2)}, u32[]{:S(2)}) collective-permute-start(f32[256,128]{1,0:T(8,128)S(1)} %shard_map.82.refs_3_), channel_id=1, source_target_pairs={{0,8},{8,0},{16,24},{24,16},{1,9},{9,1},{17,25},{25,17},{2,10},{10... | collective-permute-start | bytes 393224 | tf_op jit(solution)/shard_map/ppermute | solution.py:834
  24.4 2.0 %collective-permute-start.10 = (f32[4,4,64,128]{3,2,1,0:T(8,128)S(1)}, f32[4,4,64,128]{3,2,1,0:T(8,128)S(1)}, u32[]{:S(2)}, u32[]{:S(2)}) collective-permute-start(f32[4,4,64,128]{3,2,1,0:T(8,128)S(1)} %shard_map.83.own), channel_id=1, source_target_pairs={{0,1},{1,0},{2,3},{3,2},{4,5},{5,4},{6,7},{7,6},{8,9},{9,8},{10,11... | collective-permute-start | bytes 1572872 | tf_op jit(solution)/shard_map/ppermute | solution.py:834

commit v12 on v8

--- a/solution.py
+++ b/solution.py
@@ -418,7 +418,8 @@
                 packed[pl.ds(pl.multiple_of(n * 120 + v * ROWS + 8 * t, 8), 8), :] = tile
         return 0
 
-    lax.fori_loop(0, NV, pack, 0)
+    for v in range(NV):
+        pack(v, 0)
     copy.wait()
     terms = [two_terms(packed[n * 120 : (n + 1) * 120, :]) for n in range(4)]
     high, low = [jnp.concatenate(part, 1) for part in zip(*terms)]
@@ -549,7 +550,8 @@
                         second[2 * bz + bx, t, pl.ds(pl.multiple_of((v * 4 + z) * 8, 8), 8), :] = part[z]
         return 0
 
-    lax.fori_loop(0, NV, rows_two, 0)
+    for v in range(NV):
+        rows_two(v, 0)
     for n in range(4):
         for t in range(3):
             terms = jnp.concatenate(two_terms(second[n, t]), 1)
@@ -583,7 +585,8 @@
                     low_back[pl.ds((v * 8 + z) * 48 + 16 * t + parity, 8, stride=2), :] = planes[z]
         return 0
 
-    lax.fori_loop(0, NV, back_two, 0)
+    for v in range(NV):
+        back_two(v, 0)
 
     forward_f = wide[0:144, :].astype(F32)
     for ib in range(4):
@@ -626,7 +629,8 @@
                 kept[start, :] += product[16 * p : 16 * p + 16]
         return 0
 
-    lax.fori_loop(0, 4, keep, 0)
+    for n in range(4):
+        keep(n, 0)
     for ib in range(2):
         rows = jnp.concatenate([low_back[48 * p + 16 * ib : 48 * p + 16 * ib + 16, :] for p in range(24)], 0)
         product = dot(jnp.concatenate(two_terms(rows), 1), back[...])
@@ -797,13 +801,16 @@
         rows = pl.ds(pl.multiple_of(16 * i, 16), 16)
         return pltpu.make_async_copy(out.at[:, :, rows], out_hbm.at[:, :, rows], sems.at[i])
 
-    def pair(i, _):
-        block(2 * i, 0)
-        block(2 * i + 1, 0)
-        copy(i).start()
+    group = 4 if count_x % 4 == 0 else 1
+
+    def several(i, _):
+        for k in range(group):
+            block(2 * (group * i + k), 0)
+            block(2 * (group * i + k) + 1, 0)
+            copy(group * i + k).start()
         return 0
 
-    lax.fori_loop(0, count_x, pair, 0)
+    lax.fori_loop(0, count_x // group, several, 0)
     for i in range(count_x):
         copy(i).wait()
 

time: 28 us -> 27.8 us (level)
  Pallas kernels: 10.5 us -> 8.95 us
  waiting for transfers between devices: 2.73 us -> 4.02 us
    pallas_call x1, Pallas kernels: 3.52 us -> 2.23 us  [main_step(): pl.pallas_call(main_kernel, grid=(1,), out_shape=jax.ShapeDtypeStruct((4...]
    ppermute x7, waiting for transfers between devices: 1.62 us -> 2.9 us  [swapped(): lax.ppermute(x, axis, [(i, i ^ distance) for i in range(lax.axis_size(axi...]
  transfers between devices with their start and end apart: 11 -> 11, of which waited for: 5 -> 5; matrix products, arithmetic and copies ran while one was open for 0% -> 0% of each run, Pallas kernels for 23% -> 19%
where the time goes in v12:
time: 27.8 us; the launch traced here: 27.5 us
  starting transfers between devices  13.9 us (50%)
  Pallas kernels  8.95 us (32%)
  waiting for transfers between devices  4.02 us (14%)
  between operations  0.71 us (3%)
    ppermute x7, starting transfers between devices, swapped(): lax.ppermute(x, axis, [(i, i ^ distance) for i in range(lax.axis_size(axi...  8.09 us
    ppermute x4, starting transfers between devices, shifted(): lax.ppermute(x, axis, [(i, (i + step) % count) for i in range(count)])  5.77 us
    ppermute x7, waiting for transfers between devices, swapped(): lax.ppermute(x, axis, [(i, i ^ distance) for i in range(lax.axis_size(axi...  2.9 us
    pallas_call x1, Pallas kernels, first_step(): pl.pallas_call(first_kernel, out_shape=[jax.ShapeDtypeStruct(s, F32) for...  2.33 us
    pallas_call x1, Pallas kernels, main_step(): pl.pallas_call(main_kernel, grid=(1,), out_shape=jax.ShapeDtypeStruct((4...  2.23 us
    pallas_call x1, Pallas kernels, cells_step(): pl.pallas_call(cells_kernel, out_shape=jax.ShapeDtypeStruct(shape, F32),...  1.37 us
    pallas_call x1, Pallas kernels, edge_step(): pl.pallas_call(edge_kernel, out_shape=[jax.ShapeDtypeStruct(s, F32) for s...  1.22 us
    pallas_call x1, Pallas kernels, coarse_step(): pl.pallas_call(functools.partial(coarse_kernel, count_x, count_y), out_sh...  1.15 us
  transfers between devices with their start and end apart: 11, of which 5 were waited for; matrix products, arithmetic and copies ran while one was open for 0% of the time, Pallas kernels for 19%

profile of v12, /device:TPU:0, one launch (start us, length us, event | category | flops | bytes accessed | tf_op | source)
XLA Modules:
  0.0 27.5 jit_solution(1060447404942525029)
XLA Ops:
  0.6 2.3 %shard_map.77 = (f32[3840,128]{1,0:T(8,128)S(1)}, f32[16,8,128]{2,1,0:T(8,128)S(1)}, f32[10,8,128]{2,1,0:T(8,128)S(1)}, f32[2,8,128]{2,1,0:T(8,128)S(1)}, f32[64,128]{1,0:T(8,128)S(1)}) custom-call(f32[3,16,64,128]{3,2,1,0:T(8,128)} %field.1, s32[2,2,4,7]{3,2,1,0:T(4,128)} %bitcast.5, bf16[400,128]{1,0:T(8,128)(2,1)} %constant.8.clone.table_hbm), custom_call_target="tpu_custom_call" | custom-call | tf_op jit(solution)/shard_map/pallas_call | solution.py:336
  3.0 3.9 %collective-permute-start.1 = (f32[16,8,128]{2,1,0:T(8,128)S(1)}, f32[16,8,128]{2,1,0:T(8,128)S(1)}, u32[]{:S(2)}, u32[]{:S(2)}) collective-permute-start(f32[16,8,128]{2,1,0:T(8,128)S(1)} %get-tuple-element.12), channel_id=1, source_target_pairs={{0,24},{8,0},{16,8},{24,16},{1,25},{9,1},{17,9},{25,17},{2,26},{10... | collective-permute-start | bytes 196616 | tf_op jit(solution)/shard_map/ppermute | solution.py:833
  6.9 3.6 %collective-permute-start.4 = (f32[64,128]{1,0:T(8,128)S(1)}, f32[64,128]{1,0:T(8,128)S(1)}, u32[]{:S(2)}, u32[]{:S(2)}) collective-permute-start(f32[64,128]{1,0:T(8,128)S(1)} %get-tuple-element.17.refs_3_), channel_id=1, source_target_pairs={{0,6},{1,7},{2,4},{3,5},{4,2},{5,3},{6,0},{7,1},{8,14},{9,15},{10,... | collective-permute-start | bytes 98312 | tf_op jit(solution)/shard_map/ppermute | solution.py:837
  10.5 0.0 collective-permute-start.5
  10.5 0.8 %collective-permute-start.6 = (f32[64,128]{1,0:T(8,128)S(1)}, f32[64,128]{1,0:T(8,128)S(1)}, u32[]{:S(2)}, u32[]{:S(2)}) collective-permute-start(f32[64,128]{1,0:T(8,128)S(1)} %get-tuple-element.17.refs_3_), channel_id=1, source_target_pairs={{0,2},{1,3},{2,0},{3,1},{4,6},{5,7},{6,4},{7,5},{8,10},{9,11},{10,... | collective-permute-start | bytes 98312 | tf_op jit(solution)/shard_map/ppermute | solution.py:837
  11.3 0.3 %shard_map.78.parts_in = f32[3840,128]{1,0:T(8,128)S(1)} custom-call(f32[3840,128]{1,0:T(8,128)S(1)} %get-tuple-element.10.lifted), custom_call_target="tpu_custom_call" | custom-call | tf_op jit(solution)/shard_map/pallas_call | solution.py:372
  11.6 0.2 collective-permute-done.north.north_mask
  11.8 1.2 %shard_map.79 = (f32[3840,128]{1,0:T(8,128)S(1)}, f32[88,128]{1,0:T(8,128)S(1)}, f32[48,128]{1,0:T(8,128)S(1)}) custom-call(f32[3840,128]{1,0:T(8,128)S(1)} %shard_map.78.parts_in, f32[3840,128]{1,0:T(8,128)S(1)} %get-tuple-element.10.lifted, f32[10,8,128]{2,1,0:T(8,128)S(1)} %collective-permute-done.north.north_mask, ...), custom_call_target="tpu_custom_call", output_to_operand_aliasing={{0}: (0, {})} | custom-call | flops 20000000000 | bytes 8000000 | tf_op jit(solution)/shard_map/pallas_call | solution.py:447
  13.1 1.8 %collective-permute-start.2 = (f32[88,128]{1,0:T(8,128)S(1)}, f32[88,128]{1,0:T(8,128)S(1)}, u32[]{:S(2)}, u32[]{:S(2)}) collective-permute-start(f32[88,128]{1,0:T(8,128)S(1)} %get-tuple-element.15.refs_4_), channel_id=1, source_target_pairs={{0,7},{1,0},{2,1},{3,2},{4,3},{5,4},{6,5},{7,6},{8,15},{9,8},{10,9... | collective-permute-start | bytes 135176 | tf_op jit(solution)/shard_map/ppermute | solution.py:833
  14.9 0.0 collective-permute-start.3
  14.9 0.0 collective-permute-done.4.refs_0_
  14.9 0.5 %collective-permute-done.5.refs_1_ = f32[64,128]{1,0:T(8,128)S(1)} collective-permute-done((f32[64,128]{1,0:T(8,128)S(1)}, f32[64,128]{1,0:T(8,128)S(1)}, u32[]{:S(2)}, u32[]{:S(2)}) %collective-permute-start.5) | collective-permute-done | bytes 32800 | tf_op jit(solution)/shard_map/ppermute | solution.py:837
  15.4 3.0 %collective-permute-start.7 = (f32[256,128]{1,0:T(8,128)S(1)}, f32[256,128]{1,0:T(8,128)S(1)}, u32[]{:S(2)}, u32[]{:S(2)}) collective-permute-start(f32[256,128]{1,0:T(8,128)S(1)} %shard_map.82.refs_3_), channel_id=1, source_target_pairs={{0,24},{8,16},{16,8},{24,0},{1,25},{9,17},{17,9},{25,1},{2,26},{10... | collective-permute-start | bytes 393224 | tf_op jit(solution)/shard_map/ppermute | solution.py:837
  18.3 0.5 %collective-permute-start.8 = (f32[256,128]{1,0:T(8,128)S(1)}, f32[256,128]{1,0:T(8,128)S(1)}, u32[]{:S(2)}, u32[]{:S(2)}) collective-permute-start(f32[256,128]{1,0:T(8,128)S(1)} %shard_map.82.refs_3_), channel_id=1, source_target_pairs={{0,16},{8,24},{16,0},{24,8},{1,17},{9,25},{17,1},{25,9},{2,18},{10... | collective-permute-start | bytes 393224 | tf_op jit(solution)/shard_map/ppermute | solution.py:837
  18.8 0.1 collective-permute-start.9
  19.0 0.9 %collective-permute-done.3.west = f32[48,128]{1,0:T(8,128)S(1)} collective-permute-done((f32[48,128]{1,0:T(8,128)S(1)}, f32[48,128]{1,0:T(8,128)S(1)}, u32[]{:S(2)}, u32[]{:S(2)}) %collective-permute-start.3) | collective-permute-done | bytes 24608 | tf_op jit(solution)/shard_map/ppermute | solution.py:833
  19.9 2.2 %shard_map.80.refs_4_ = f32[4608,128]{1,0:T(8,128)S(1)} custom-call(f32[4,24,40,128]{3,2,1,0:T(8,128)S(1)} %bitcast.4, f32[3840,128]{1,0:T(8,128)S(1)} %get-tuple-element.14.flat, f32[88,128]{1,0:T(8,128)S(1)} %collective-permute-done.2.east, f32[48,128]{1,0:T(8,128)S(1)} %collective-permute-done.3.west, f32[2,8,128]{2,1,0:T(8,128)S(1)} %get-tuple-element.13.own_masks, ...), custom_call_target="tpu_custom_call" | custom-call | flops 8000000000 | bytes 8000000 | tf_op jit(solution)/shard_map/pallas_call | solution.py:696
  22.2 0.0 collective-permute-done.7.refs_0_
  22.2 1.9 %collective-permute-done.8.refs_1_ = f32[256,128]{1,0:T(8,128)S(1)} collective-permute-done((f32[256,128]{1,0:T(8,128)S(1)}, f32[256,128]{1,0:T(8,128)S(1)}, u32[]{:S(2)}, u32[]{:S(2)}) %collective-permute-start.8) | collective-permute-done | bytes 131104 | tf_op jit(solution)/shard_map/ppermute | solution.py:837
  24.1 0.3 %shard_map.83.own = f32[4,4,64,128]{3,2,1,0:T(8,128)S(1)} custom-call(f32[256,128]{1,0:T(8,128)S(1)} %collective-permute-done.7.refs_0_, f32[256,128]{1,0:T(8,128)S(1)} %collective-permute-done.8.refs_1_, f32[256,128]{1,0:T(8,128)S(1)} %collective-permute-done.9.refs_2_, f32[256,128]{1,0:T(8,128)S(1)} %shard_map.82.refs_3_, f32[4608,128]{1,0:T(8,128)S(1)} %shard_map.80.refs_4_), custom_call_target="tpu_custom_call" | custom-call | tf_op jit(solution)/shard_map/pallas_call | solution.py:767
  24.4 0.1 collective-permute-start.10
  24.5 1.4 %shard_map.81 = f32[3,16,64,128]{3,2,1,0:T(8,128)} custom-call(f32[4,24,48,128]{3,2,1,0:T(8,128)S(1)} %bitcast.3), custom_call_target="tpu_custom_call" | custom-call | flops 4000000000 | bytes 8000000 | tf_op jit(solution)/shard_map/pallas_call | solution.py:719
  25.9 0.5 %collective-permute-done.10.other = f32[4,4,64,128]{3,2,1,0:T(8,128)S(1)} collective-permute-done((f32[4,4,64,128]{3,2,1,0:T(8,128)S(1)}, f32[4,4,64,128]{3,2,1,0:T(8,128)S(1)}, u32[]{:S(2)}, u32[]{:S(2)}) %collective-permute-start.10) | collective-permute-done | bytes 524320 | tf_op jit(solution)/shard_map/ppermute | solution.py:837
  26.4 1.1 %shard_map.84 = f32[3,4,64,256]{3,2,1,0:T(8,128)} custom-call(f32[4,4,64,128]{3,2,1,0:T(8,128)S(1)} %shard_map.83.own, f32[4,4,64,128]{3,2,1,0:T(8,128)S(1)} %collective-permute-done.10.other), custom_call_target="tpu_custom_call" | custom-call | tf_op jit(solution)/shard_map/pallas_call | solution.py:821
  (10 shorter events, 0.0 us)
Async XLA Ops:
  3.0 8.9 %collective-permute-start.1 = (f32[16,8,128]{2,1,0:T(8,128)S(1)}, f32[16,8,128]{2,1,0:T(8,128)S(1)}, u32[]{:S(2)}, u32[]{:S(2)}) collective-permute-start(f32[16,8,128]{2,1,0:T(8,128)S(1)} %get-tuple-element.12), channel_id=1, source_target_pairs={{0,24},{8,0},{16,8},{24,16},{1,25},{9,1},{17,9},{25,17},{2,26},{10... | collective-permute-start | bytes 196616 | tf_op jit(solution)/shard_map/ppermute | solution.py:833
  6.9 4.9 %collective-permute-start = (f32[10,8,128]{2,1,0:T(8,128)S(1)}, f32[10,8,128]{2,1,0:T(8,128)S(1)}, u32[]{:S(2)}, u32[]{:S(2)}) collective-permute-start(f32[10,8,128]{2,1,0:T(8,128)S(1)} %get-tuple-element.11), channel_id=1, source_target_pairs={{0,8},{8,16},{16,24},{24,0},{1,9},{9,17},{17,25},{25,1},{2,10},{10... | collective-permute-start | bytes 122888 | tf_op jit(solution)/shard_map/ppermute | solution.py:833
  6.9 8.0 %collective-permute-start.4 = (f32[64,128]{1,0:T(8,128)S(1)}, f32[64,128]{1,0:T(8,128)S(1)}, u32[]{:S(2)}, u32[]{:S(2)}) collective-permute-start(f32[64,128]{1,0:T(8,128)S(1)} %get-tuple-element.17.refs_3_), channel_id=1, source_target_pairs={{0,6},{1,7},{2,4},{3,5},{4,2},{5,3},{6,0},{7,1},{8,14},{9,15},{10,... | collective-permute-start | bytes 98312 | tf_op jit(solution)/shard_map/ppermute | solution.py:837
  10.5 4.8 %collective-permute-start.5 = (f32[64,128]{1,0:T(8,128)S(1)}, f32[64,128]{1,0:T(8,128)S(1)}, u32[]{:S(2)}, u32[]{:S(2)}) collective-permute-start(f32[64,128]{1,0:T(8,128)S(1)} %get-tuple-element.17.refs_3_), channel_id=1, source_target_pairs={{0,4},{1,5},{2,6},{3,7},{4,0},{5,1},{6,2},{7,3},{8,12},{9,13},{10,... | collective-permute-start | bytes 98312 | tf_op jit(solution)/shard_map/ppermute | solution.py:837
  10.5 4.8 %collective-permute-start.6 = (f32[64,128]{1,0:T(8,128)S(1)}, f32[64,128]{1,0:T(8,128)S(1)}, u32[]{:S(2)}, u32[]{:S(2)}) collective-permute-start(f32[64,128]{1,0:T(8,128)S(1)} %get-tuple-element.17.refs_3_), channel_id=1, source_target_pairs={{0,2},{1,3},{2,0},{3,1},{4,6},{5,7},{6,4},{7,5},{8,10},{9,11},{10,... | collective-permute-start | bytes 98312 | tf_op jit(solution)/shard_map/ppermute | solution.py:837
  13.1 6.9 %collective-permute-start.2 = (f32[88,128]{1,0:T(8,128)S(1)}, f32[88,128]{1,0:T(8,128)S(1)}, u32[]{:S(2)}, u32[]{:S(2)}) collective-permute-start(f32[88,128]{1,0:T(8,128)S(1)} %get-tuple-element.15.refs_4_), channel_id=1, source_target_pairs={{0,7},{1,0},{2,1},{3,2},{4,3},{5,4},{6,5},{7,6},{8,15},{9,8},{10,9... | collective-permute-start | bytes 135176 | tf_op jit(solution)/shard_map/ppermute | solution.py:833
  14.9 5.1 %copy-start = (bf16[1280,128]{1,0:T(8,128)(2,1)S(1)}, bf16[1280,128]{1,0:T(8,128)(2,1)}, u32[]{:S(2)}) copy-start(bf16[1280,128]{1,0:T(8,128)(2,1)} %constant.11.clone.narrow) | copy-start | bytes 983044
  14.9 5.1 %copy-start.1 = (bf16[528,256]{1,0:T(8,128)(2,1)S(1)}, bf16[528,256]{1,0:T(8,128)(2,1)}, u32[]{:S(2)}) copy-start(bf16[528,256]{1,0:T(8,128)(2,1)} %constant.10.clone.wide) | copy-start | bytes 811012
  14.9 5.0 %collective-permute-start.3 = (f32[48,128]{1,0:T(8,128)S(1)}, f32[48,128]{1,0:T(8,128)S(1)}, u32[]{:S(2)}, u32[]{:S(2)}) collective-permute-start(f32[48,128]{1,0:T(8,128)S(1)} %get-tuple-element.16), channel_id=1, source_target_pairs={{0,1},{1,2},{2,3},{3,4},{4,5},{5,6},{6,7},{7,0},{8,9},{9,10},{10,1... | collective-permute-start | bytes 73736 | tf_op jit(solution)/shard_map/ppermute | solution.py:833
  15.4 6.8 %collective-permute-start.7 = (f32[256,128]{1,0:T(8,128)S(1)}, f32[256,128]{1,0:T(8,128)S(1)}, u32[]{:S(2)}, u32[]{:S(2)}) collective-permute-start(f32[256,128]{1,0:T(8,128)S(1)} %shard_map.82.refs_3_), channel_id=1, source_target_pairs={{0,24},{8,16},{16,8},{24,0},{1,25},{9,17},{17,9},{25,1},{2,26},{10... | collective-permute-start | bytes 393224 | tf_op jit(solution)/shard_map/ppermute | solution.py:837
  18.3 5.8 %collective-permute-start.8 = (f32[256,128]{1,0:T(8,128)S(1)}, f32[256,128]{1,0:T(8,128)S(1)}, u32[]{:S(2)}, u32[]{:S(2)}) collective-permute-start(f32[256,128]{1,0:T(8,128)S(1)} %shard_map.82.refs_3_), channel_id=1, source_target_pairs={{0,16},{8,24},{16,0},{24,8},{1,17},{9,25},{17,1},{25,9},{2,18},{10... | collective-permute-start | bytes 393224 | tf_op jit(solution)/shard_map/ppermute | solution.py:837
  18.8 5.2 %collective-permute-start.9 = (f32[256,128]{1,0:T(8,128)S(1)}, f32[256,128]{1,0:T(8,128)S(1)}, u32[]{:S(2)}, u32[]{:S(2)}) collective-permute-start(f32[256,128]{1,0:T(8,128)S(1)} %shard_map.82.refs_3_), channel_id=1, source_target_pairs={{0,8},{8,0},{16,24},{24,16},{1,9},{9,1},{17,25},{25,17},{2,10},{10... | collective-permute-start | bytes 393224 | tf_op jit(solution)/shard_map/ppermute | solution.py:837
  24.4 2.0 %collective-permute-start.10 = (f32[4,4,64,128]{3,2,1,0:T(8,128)S(1)}, f32[4,4,64,128]{3,2,1,0:T(8,128)S(1)}, u32[]{:S(2)}, u32[]{:S(2)}) collective-permute-start(f32[4,4,64,128]{3,2,1,0:T(8,128)S(1)} %shard_map.83.own), channel_id=1, source_target_pairs={{0,1},{1,0},{2,3},{3,2},{4,5},{5,4},{6,7},{7,6},{8,9},{9,8},{10,11... | collective-permute-start | bytes 1572872 | tf_op jit(solution)/shard_map/ppermute | solution.py:837

commit v13 on v12

--- a/solution.py
+++ b/solution.py
@@ -727,9 +727,9 @@
     )(kept)
 
 
-def rows_kernel(count_x, count_z, *refs):
+def rows_kernel(count_x, count_z, flip, *refs):
     shares, out = refs[count_x - 1 :: -1], refs[count_x + 1]
-    me, me_y = lax.axis_index("gx"), lax.axis_index("gy")
+    me, me_y = lax.axis_index("gx"), lax.axis_index("gy") ^ flip
     row = lax.broadcasted_iota(jnp.int32, (8, NL), 0)
     lane = lax.broadcasted_iota(jnp.int32, (8, NL), 1)
     for r in range(count_x):
@@ -761,11 +761,11 @@
                 out[j, z, pl.ds(above, 8), :] += jnp.where(row == 7, last, 0.0)
 
 
-def rows_step(pieces, count_z, after):
+def rows_step(pieces, count_z, flip, after):
     vmem = pl.BlockSpec(memory_space=pltpu.VMEM)
     count_x = len(pieces)
     return pl.pallas_call(
-        functools.partial(rows_kernel, count_x, count_z),
+        functools.partial(rows_kernel, count_x, count_z, flip),
         out_shape=jax.ShapeDtypeStruct((count_z, 4, 16 * count_x, NL), F32),
         in_specs=[vmem] * count_x + [pl.BlockSpec(memory_space=pl.ANY)],
         out_specs=vmem,
@@ -849,9 +849,12 @@
     joined = join_step(shares, to_left)
     pieces = [joined] + [swapped(joined, "gx", r) for r in range(1, count_x)]
     kept = main_step(parts, east, west, own_masks, north, south)
-    own = rows_step(pieces, count_y // 2, kept)
-    other = swapped(own, "gy", 1)
-    return cells_step(kept.reshape(4, NV * 8, 48, NL)), coarse_step(own, other, count_x, count_y)
+    restored = cells_step(kept.reshape(4, NV * 8, 48, NL))
+    pieces[-1], restored = lax.optimization_barrier((pieces[-1], restored))
+    others = [swapped(piece, "gy", 1) for piece in pieces]
+    own = rows_step(pieces, count_y // 2, 0, kept)
+    other = rows_step(others, count_y // 2, 1, own)
+    return restored, coarse_step(own, other, count_x, count_y)
 
 
 def solution(mesh):

time: 27.8 us -> 27.4 us (0.986)
  waiting for transfers between devices: 4.02 us -> 2.28 us
  starting transfers between devices: 13.9 us -> 14.9 us
  Pallas kernels: 8.95 us -> 9.27 us
    ppermute x7 -> x10, waiting for transfers between devices: 2.9 us -> 1.16 us  [swapped(): lax.ppermute(x, axis, [(i, i ^ distance) for i in range(lax.axis_size(axi...]
    ppermute x7 -> x10, starting transfers between devices: 8.09 us -> 9.1 us  [swapped(): lax.ppermute(x, axis, [(i, i ^ distance) for i in range(lax.axis_size(axi...]
    pallas_call x1 -> x2, Pallas kernels: 0.32 us -> 0.63 us  [rows_step(): pl.pallas_call(functools.partial(rows_kernel, count_x, count_z, flip), ou...]
  transfers between devices with their start and end apart: 11 -> 14, of which waited for: 5 -> 6; matrix products, arithmetic and copies ran while one was open for 0% -> 0% of each run, Pallas kernels for 19% -> 20%
where the time goes in v13:
time: 27.4 us; the launch traced here: 27.2 us
  starting transfers between devices  14.9 us (54%)
  Pallas kernels  9.27 us (34%)
  waiting for transfers between devices  2.28 us (8%)
  between operations  0.73 us (3%)
    ppermute x10, starting transfers between devices, swapped(): lax.ppermute(x, axis, [(i, i ^ distance) for i in range(lax.axis_size(axi...  9.1 us
    ppermute x4, starting transfers between devices, shifted(): lax.ppermute(x, axis, [(i, (i + step) % count) for i in range(count)])  5.77 us
    pallas_call x1, Pallas kernels, first_step(): pl.pallas_call(first_kernel, out_shape=[jax.ShapeDtypeStruct(s, F32) for...  2.33 us
    pallas_call x1, Pallas kernels, main_step(): pl.pallas_call(main_kernel, grid=(1,), out_shape=jax.ShapeDtypeStruct((4...  2.23 us
    pallas_call x1, Pallas kernels, cells_step(): pl.pallas_call(cells_kernel, out_shape=jax.ShapeDtypeStruct(shape, F32),...  1.37 us
    pallas_call x1, Pallas kernels, edge_step(): pl.pallas_call(edge_kernel, out_shape=[jax.ShapeDtypeStruct(s, F32) for s...  1.22 us
    ppermute x10, waiting for transfers between devices, swapped(): lax.ppermute(x, axis, [(i, i ^ distance) for i in range(lax.axis_size(axi...  1.16 us
    pallas_call x1, Pallas kernels, coarse_step(): pl.pallas_call(functools.partial(coarse_kernel, count_x, count_y), out_sh...  1.15 us
  transfers between devices with their start and end apart: 14, of which 6 were waited for; matrix products, arithmetic and copies ran while one was open for 0% of the time, Pallas kernels for 20%

profile of v13, /device:TPU:0, one launch (start us, length us, event | category | flops | bytes accessed | tf_op | source)
XLA Modules:
  0.0 27.2 jit_solution(9430710265723581705)
XLA Ops:
  0.6 2.3 %shard_map.77 = (f32[3840,128]{1,0:T(8,128)S(1)}, f32[16,8,128]{2,1,0:T(8,128)S(1)}, f32[10,8,128]{2,1,0:T(8,128)S(1)}, f32[2,8,128]{2,1,0:T(8,128)S(1)}, f32[64,128]{1,0:T(8,128)S(1)}) custom-call(f32[3,16,64,128]{3,2,1,0:T(8,128)} %field.1, s32[2,2,4,7]{3,2,1,0:T(4,128)} %bitcast.5, bf16[400,128]{1,0:T(8,128)(2,1)} %constant.8.clone.table_hbm), custom_call_target="tpu_custom_call" | custom-call | tf_op jit(solution)/shard_map/pallas_call | solution.py:336
  3.0 3.9 %collective-permute-start.4 = (f32[16,8,128]{2,1,0:T(8,128)S(1)}, f32[16,8,128]{2,1,0:T(8,128)S(1)}, u32[]{:S(2)}, u32[]{:S(2)}) collective-permute-start(f32[16,8,128]{2,1,0:T(8,128)S(1)} %get-tuple-element.15), channel_id=1, source_target_pairs={{0,24},{8,0},{16,8},{24,16},{1,25},{9,1},{17,9},{25,17},{2,26},{10... | collective-permute-start | bytes 196616 | tf_op jit(solution)/shard_map/ppermute | solution.py:833
  6.9 3.6 %collective-permute-start = (f32[64,128]{1,0:T(8,128)S(1)}, f32[64,128]{1,0:T(8,128)S(1)}, u32[]{:S(2)}, u32[]{:S(2)}) collective-permute-start(f32[64,128]{1,0:T(8,128)S(1)} %get-tuple-element.12.refs_3_), channel_id=1, source_target_pairs={{0,6},{1,7},{2,4},{3,5},{4,2},{5,3},{6,0},{7,1},{8,14},{9,15},{10,... | collective-permute-start | bytes 98312 | tf_op jit(solution)/shard_map/ppermute | solution.py:837
  10.5 0.8 %collective-permute-start.2 = (f32[64,128]{1,0:T(8,128)S(1)}, f32[64,128]{1,0:T(8,128)S(1)}, u32[]{:S(2)}, u32[]{:S(2)}) collective-permute-start(f32[64,128]{1,0:T(8,128)S(1)} %get-tuple-element.12.refs_3_), channel_id=1, source_target_pairs={{0,2},{1,3},{2,0},{3,1},{4,6},{5,7},{6,4},{7,5},{8,10},{9,11},{10,... | collective-permute-start | bytes 98312 | tf_op jit(solution)/shard_map/ppermute | solution.py:837
  11.3 0.3 %shard_map.78.parts_in = f32[3840,128]{1,0:T(8,128)S(1)} custom-call(f32[3840,128]{1,0:T(8,128)S(1)} %get-tuple-element.13.lifted), custom_call_target="tpu_custom_call" | custom-call | tf_op jit(solution)/shard_map/pallas_call | solution.py:372
  11.6 0.2 collective-permute-done.3.north.north_mask
  11.8 1.2 %shard_map.79 = (f32[3840,128]{1,0:T(8,128)S(1)}, f32[88,128]{1,0:T(8,128)S(1)}, f32[48,128]{1,0:T(8,128)S(1)}) custom-call(f32[3840,128]{1,0:T(8,128)S(1)} %shard_map.78.parts_in, f32[3840,128]{1,0:T(8,128)S(1)} %get-tuple-element.13.lifted, f32[10,8,128]{2,1,0:T(8,128)S(1)} %collective-permute-done.3.north.north_mask, ...), custom_call_target="tpu_custom_call", output_to_operand_aliasing={{0}: (0, {})} | custom-call | flops 20000000000 | bytes 8000000 | tf_op jit(solution)/shard_map/pallas_call | solution.py:447
  13.1 1.8 %collective-permute-start.6 = (f32[88,128]{1,0:T(8,128)S(1)}, f32[88,128]{1,0:T(8,128)S(1)}, u32[]{:S(2)}, u32[]{:S(2)}) collective-permute-start(f32[88,128]{1,0:T(8,128)S(1)} %get-tuple-element.17.refs_4_), channel_id=1, source_target_pairs={{0,7},{1,0},{2,1},{3,2},{4,3},{5,4},{6,5},{7,6},{8,15},{9,8},{10,9... | collective-permute-start | bytes 135176 | tf_op jit(solution)/shard_map/ppermute | solution.py:833
  14.9 0.5 %collective-permute-done.1.refs_1_ = f32[64,128]{1,0:T(8,128)S(1)} collective-permute-done((f32[64,128]{1,0:T(8,128)S(1)}, f32[64,128]{1,0:T(8,128)S(1)}, u32[]{:S(2)}, u32[]{:S(2)}) %collective-permute-start.1) | collective-permute-done | bytes 32800 | tf_op jit(solution)/shard_map/ppermute | solution.py:837
  15.4 3.0 %collective-permute-start.5 = (f32[256,128]{1,0:T(8,128)S(1)}, f32[256,128]{1,0:T(8,128)S(1)}, u32[]{:S(2)}, u32[]{:S(2)}) collective-permute-start(f32[256,128]{1,0:T(8,128)S(1)} %shard_map.80.refs_3_), channel_id=1, source_target_pairs={{0,24},{8,16},{16,8},{24,0},{1,25},{9,17},{17,9},{25,1},{2,26},{10... | collective-permute-start | bytes 393224 | tf_op jit(solution)/shard_map/ppermute | solution.py:837
  18.3 0.5 %collective-permute-start.8 = (f32[256,128]{1,0:T(8,128)S(1)}, f32[256,128]{1,0:T(8,128)S(1)}, u32[]{:S(2)}, u32[]{:S(2)}) collective-permute-start(f32[256,128]{1,0:T(8,128)S(1)} %shard_map.80.refs_3_), channel_id=1, source_target_pairs={{0,16},{8,24},{16,0},{24,8},{1,17},{9,25},{17,1},{25,9},{2,18},{10... | collective-permute-start | bytes 393224 | tf_op jit(solution)/shard_map/ppermute | solution.py:837
  18.8 0.1 collective-permute-start.9
  19.0 0.9 %collective-permute-done.7.west = f32[48,128]{1,0:T(8,128)S(1)} collective-permute-done((f32[48,128]{1,0:T(8,128)S(1)}, f32[48,128]{1,0:T(8,128)S(1)}, u32[]{:S(2)}, u32[]{:S(2)}) %collective-permute-start.7) | collective-permute-done | bytes 24608 | tf_op jit(solution)/shard_map/ppermute | solution.py:833
  19.9 2.2 %shard_map.81.refs_4_ = f32[4608,128]{1,0:T(8,128)S(1)} custom-call(f32[4,24,40,128]{3,2,1,0:T(8,128)S(1)} %bitcast.4, f32[3840,128]{1,0:T(8,128)S(1)} %get-tuple-element.18.flat, f32[88,128]{1,0:T(8,128)S(1)} %collective-permute-done.6.east, f32[48,128]{1,0:T(8,128)S(1)} %collective-permute-done.7.west, f32[2,8,128]{2,1,0:T(8,128)S(1)} %get-tuple-element.16.own_masks, ...), custom_call_target="tpu_custom_call" | custom-call | flops 8000000000 | bytes 8000000 | tf_op jit(solution)/shard_map/pallas_call | solution.py:696
  22.2 1.4 %shard_map.82 = f32[3,16,64,128]{3,2,1,0:T(8,128)} custom-call(f32[4,24,48,128]{3,2,1,0:T(8,128)S(1)} %bitcast.3), custom_call_target="tpu_custom_call" | custom-call | flops 4000000000 | bytes 8000000 | tf_op jit(solution)/shard_map/pallas_call | solution.py:719
  23.6 0.6 %collective-permute-start.10 = (f32[256,128]{1,0:T(8,128)S(1)}, f32[256,128]{1,0:T(8,128)S(1)}, u32[]{:S(2)}, u32[]{:S(2)}) collective-permute-start(f32[256,128]{1,0:T(8,128)S(1)} %collective-permute-done.5.refs_0_), channel_id=1, source_target_pairs={{0,1},{1,0},{2,3},{3,2},{4,5},{5,4},{6,7},{7,6},{8,9},{9,8},{10,11... | collective-permute-start | bytes 393224 | tf_op jit(solution)/shard_map/ppermute | solution.py:837
  24.1 0.1 collective-permute-start.11
  24.2 0.4 %collective-permute-start.12 = (f32[256,128]{1,0:T(8,128)S(1)}, f32[256,128]{1,0:T(8,128)S(1)}, u32[]{:S(2)}, u32[]{:S(2)}) collective-permute-start(f32[256,128]{1,0:T(8,128)S(1)} %collective-permute-done.9.refs_2_), channel_id=1, source_target_pairs={{0,1},{1,0},{2,3},{3,2},{4,5},{5,4},{6,7},{7,6},{8,9},{9,8},{10,11... | collective-permute-start | bytes 393224 | tf_op jit(solution)/shard_map/ppermute | solution.py:837
  24.7 0.3 %shard_map.83.refs_4_.own = f32[4,4,64,128]{3,2,1,0:T(8,128)S(1)} custom-call(f32[256,128]{1,0:T(8,128)S(1)} %collective-permute-done.5.refs_0_, f32[256,128]{1,0:T(8,128)S(1)} %collective-permute-done.8.refs_1_, f32[256,128]{1,0:T(8,128)S(1)} %collective-permute-done.9.refs_2_, f32[256,128]{1,0:T(8,128)S(1)} %shard_map.80.refs_3_, ...), custom_call_target="tpu_custom_call" | custom-call | tf_op jit(solution)/shard_map/pallas_call | solution.py:767
  25.0 0.1 collective-permute-done.10.refs_0_
  25.1 0.4 %collective-permute-done.11.refs_1_ = f32[256,128]{1,0:T(8,128)S(1)} collective-permute-done((f32[256,128]{1,0:T(8,128)S(1)}, f32[256,128]{1,0:T(8,128)S(1)}, u32[]{:S(2)}, u32[]{:S(2)}) %collective-permute-start.11) | collective-permute-done | bytes 131104 | tf_op jit(solution)/shard_map/ppermute | solution.py:837
  25.5 0.2 collective-permute-done.12.refs_2_
  25.7 0.3 %shard_map.84.other = f32[4,4,64,128]{3,2,1,0:T(8,128)S(1)} custom-call(f32[256,128]{1,0:T(8,128)S(1)} %collective-permute-done.10.refs_0_, f32[256,128]{1,0:T(8,128)S(1)} %collective-permute-done.11.refs_1_, f32[256,128]{1,0:T(8,128)S(1)} %collective-permute-done.12.refs_2_, f32[256,128]{1,0:T(8,128)S(1)} %collective-permute-done.13.refs_3_, ...), custom_call_target="tpu_custom_call" | custom-call | tf_op jit(solution)/shard_map/pallas_call | solution.py:767
  26.0 1.2 %shard_map.85 = f32[3,4,64,256]{3,2,1,0:T(8,128)} custom-call(f32[4,4,64,128]{3,2,1,0:T(8,128)S(1)} %shard_map.83.refs_4_.own, f32[4,4,64,128]{3,2,1,0:T(8,128)S(1)} %shard_map.84.other), custom_call_target="tpu_custom_call" | custom-call | tf_op jit(solution)/shard_map/pallas_call | solution.py:821
  (17 shorter events, 0.0 us)
Async XLA Ops:
  3.0 8.9 %collective-permute-start.4 = (f32[16,8,128]{2,1,0:T(8,128)S(1)}, f32[16,8,128]{2,1,0:T(8,128)S(1)}, u32[]{:S(2)}, u32[]{:S(2)}) collective-permute-start(f32[16,8,128]{2,1,0:T(8,128)S(1)} %get-tuple-element.15), channel_id=1, source_target_pairs={{0,24},{8,0},{16,8},{24,16},{1,25},{9,1},{17,9},{25,17},{2,26},{10... | collective-permute-start | bytes 196616 | tf_op jit(solution)/shard_map/ppermute | solution.py:833
  6.9 4.9 %collective-permute-start.3 = (f32[10,8,128]{2,1,0:T(8,128)S(1)}, f32[10,8,128]{2,1,0:T(8,128)S(1)}, u32[]{:S(2)}, u32[]{:S(2)}) collective-permute-start(f32[10,8,128]{2,1,0:T(8,128)S(1)} %get-tuple-element.14), channel_id=1, source_target_pairs={{0,8},{8,16},{16,24},{24,0},{1,9},{9,17},{17,25},{25,1},{2,10},{10... | collective-permute-start | bytes 122888 | tf_op jit(solution)/shard_map/ppermute | solution.py:833
  6.9 8.0 %collective-permute-start = (f32[64,128]{1,0:T(8,128)S(1)}, f32[64,128]{1,0:T(8,128)S(1)}, u32[]{:S(2)}, u32[]{:S(2)}) collective-permute-start(f32[64,128]{1,0:T(8,128)S(1)} %get-tuple-element.12.refs_3_), channel_id=1, source_target_pairs={{0,6},{1,7},{2,4},{3,5},{4,2},{5,3},{6,0},{7,1},{8,14},{9,15},{10,... | collective-permute-start | bytes 98312 | tf_op jit(solution)/shard_map/ppermute | solution.py:837
  10.5 4.8 %collective-permute-start.1 = (f32[64,128]{1,0:T(8,128)S(1)}, f32[64,128]{1,0:T(8,128)S(1)}, u32[]{:S(2)}, u32[]{:S(2)}) collective-permute-start(f32[64,128]{1,0:T(8,128)S(1)} %get-tuple-element.12.refs_3_), channel_id=1, source_target_pairs={{0,4},{1,5},{2,6},{3,7},{4,0},{5,1},{6,2},{7,3},{8,12},{9,13},{10,... | collective-permute-start | bytes 98312 | tf_op jit(solution)/shard_map/ppermute | solution.py:837
  10.5 4.8 %collective-permute-start.2 = (f32[64,128]{1,0:T(8,128)S(1)}, f32[64,128]{1,0:T(8,128)S(1)}, u32[]{:S(2)}, u32[]{:S(2)}) collective-permute-start(f32[64,128]{1,0:T(8,128)S(1)} %get-tuple-element.12.refs_3_), channel_id=1, source_target_pairs={{0,2},{1,3},{2,0},{3,1},{4,6},{5,7},{6,4},{7,5},{8,10},{9,11},{10,... | collective-permute-start | bytes 98312 | tf_op jit(solution)/shard_map/ppermute | solution.py:837
  13.1 6.9 %collective-permute-start.6 = (f32[88,128]{1,0:T(8,128)S(1)}, f32[88,128]{1,0:T(8,128)S(1)}, u32[]{:S(2)}, u32[]{:S(2)}) collective-permute-start(f32[88,128]{1,0:T(8,128)S(1)} %get-tuple-element.17.refs_4_), channel_id=1, source_target_pairs={{0,7},{1,0},{2,1},{3,2},{4,3},{5,4},{6,5},{7,6},{8,15},{9,8},{10,9... | collective-permute-start | bytes 135176 | tf_op jit(solution)/shard_map/ppermute | solution.py:833
  14.9 5.1 %copy-start = (bf16[1280,128]{1,0:T(8,128)(2,1)S(1)}, bf16[1280,128]{1,0:T(8,128)(2,1)}, u32[]{:S(2)}) copy-start(bf16[1280,128]{1,0:T(8,128)(2,1)} %constant.11.clone.narrow) | copy-start | bytes 983044
  14.9 5.1 %copy-start.1 = (bf16[528,256]{1,0:T(8,128)(2,1)S(1)}, bf16[528,256]{1,0:T(8,128)(2,1)}, u32[]{:S(2)}) copy-start(bf16[528,256]{1,0:T(8,128)(2,1)} %constant.10.clone.wide) | copy-start | bytes 811012
  14.9 5.0 %collective-permute-start.7 = (f32[48,128]{1,0:T(8,128)S(1)}, f32[48,128]{1,0:T(8,128)S(1)}, u32[]{:S(2)}, u32[]{:S(2)}) collective-permute-start(f32[48,128]{1,0:T(8,128)S(1)} %get-tuple-element.19), channel_id=1, source_target_pairs={{0,1},{1,2},{2,3},{3,4},{4,5},{5,6},{6,7},{7,0},{8,9},{9,10},{10,1... | collective-permute-start | bytes 73736 | tf_op jit(solution)/shard_map/ppermute | solution.py:833
  15.4 8.2 %collective-permute-start.5 = (f32[256,128]{1,0:T(8,128)S(1)}, f32[256,128]{1,0:T(8,128)S(1)}, u32[]{:S(2)}, u32[]{:S(2)}) collective-permute-start(f32[256,128]{1,0:T(8,128)S(1)} %shard_map.80.refs_3_), channel_id=1, source_target_pairs={{0,24},{8,16},{16,8},{24,0},{1,25},{9,17},{17,9},{25,1},{2,26},{10... | collective-permute-start | bytes 393224 | tf_op jit(solution)/shard_map/ppermute | solution.py:837
  18.3 5.8 %collective-permute-start.8 = (f32[256,128]{1,0:T(8,128)S(1)}, f32[256,128]{1,0:T(8,128)S(1)}, u32[]{:S(2)}, u32[]{:S(2)}) collective-permute-start(f32[256,128]{1,0:T(8,128)S(1)} %shard_map.80.refs_3_), channel_id=1, source_target_pairs={{0,16},{8,24},{16,0},{24,8},{1,17},{9,25},{17,1},{25,9},{2,18},{10... | collective-permute-start | bytes 393224 | tf_op jit(solution)/shard_map/ppermute | solution.py:837
  18.8 5.4 %collective-permute-start.9 = (f32[256,128]{1,0:T(8,128)S(1)}, f32[256,128]{1,0:T(8,128)S(1)}, u32[]{:S(2)}, u32[]{:S(2)}) collective-permute-start(f32[256,128]{1,0:T(8,128)S(1)} %shard_map.80.refs_3_), channel_id=1, source_target_pairs={{0,8},{8,0},{16,24},{24,16},{1,9},{9,1},{17,25},{25,17},{2,10},{10... | collective-permute-start | bytes 393224 | tf_op jit(solution)/shard_map/ppermute | solution.py:837
  19.9 5.1 %collective-permute-start.13 = (f32[256,128]{1,0:T(8,128)S(1)}, f32[256,128]{1,0:T(8,128)S(1)}, u32[]{:S(2)}, u32[]{:S(2)}) collective-permute-start(f32[256,128]{1,0:T(8,128)S(1)} %shard_map.80.refs_3_), channel_id=1, source_target_pairs={{0,1},{1,0},{2,3},{3,2},{4,5},{5,4},{6,7},{7,6},{8,9},{9,8},{10,11... | collective-permute-start | bytes 393224 | tf_op jit(solution)/shard_map/ppermute | solution.py:837
  23.6 1.6 %collective-permute-start.10 = (f32[256,128]{1,0:T(8,128)S(1)}, f32[256,128]{1,0:T(8,128)S(1)}, u32[]{:S(2)}, u32[]{:S(2)}) collective-permute-start(f32[256,128]{1,0:T(8,128)S(1)} %collective-permute-done.5.refs_0_), channel_id=1, source_target_pairs={{0,1},{1,0},{2,3},{3,2},{4,5},{5,4},{6,7},{7,6},{8,9},{9,8},{10,11... | collective-permute-start | bytes 393224 | tf_op jit(solution)/shard_map/ppermute | solution.py:837
  24.1 1.3 %collective-permute-start.11 = (f32[256,128]{1,0:T(8,128)S(1)}, f32[256,128]{1,0:T(8,128)S(1)}, u32[]{:S(2)}, u32[]{:S(2)}) collective-permute-start(f32[256,128]{1,0:T(8,128)S(1)} %collective-permute-done.8.refs_1_), channel_id=1, source_target_pairs={{0,1},{1,0},{2,3},{3,2},{4,5},{5,4},{6,7},{7,6},{8,9},{9,8},{10,11... | collective-permute-start | bytes 393224 | tf_op jit(solution)/shard_map/ppermute | solution.py:837
  24.2 1.4 %collective-permute-start.12 = (f32[256,128]{1,0:T(8,128)S(1)}, f32[256,128]{1,0:T(8,128)S(1)}, u32[]{:S(2)}, u32[]{:S(2)}) collective-permute-start(f32[256,128]{1,0:T(8,128)S(1)} %collective-permute-done.9.refs_2_), channel_id=1, source_target_pairs={{0,1},{1,0},{2,3},{3,2},{4,5},{5,4},{6,7},{7,6},{8,9},{9,8},{10,11... | collective-permute-start | bytes 393224 | tf_op jit(solution)/shard_map/ppermute | solution.py:837

commit v14 on v13

--- a/solution.py
+++ b/solution.py
@@ -677,7 +677,12 @@
         copy(step).start()
         return 0
 
-    lax.fori_loop(0, NV * 4, one, 0)
+    def four(v, _):
+        for t in range(4):
+            one(4 * v + t, 0)
+        return 0
+
+    lax.fori_loop(0, NV, four, 0)
     for step in range(NV * 4):
         copy(step).wait()
 

time: 27.4 us -> 27.3 us (level)
  no operation moved by 1% of the time
where the time goes in v14:
time: 27.3 us; the launch traced here: 27.1 us
  starting transfers between devices  14.9 us (55%)
  Pallas kernels  9.19 us (34%)
  waiting for transfers between devices  2.32 us (8%)
  between operations  0.73 us (3%)
    ppermute x10, starting transfers between devices, swapped(): lax.ppermute(x, axis, [(i, i ^ distance) for i in range(lax.axis_size(axi...  9.1 us
    ppermute x4, starting transfers between devices, shifted(): lax.ppermute(x, axis, [(i, (i + step) % count) for i in range(count)])  5.77 us
    pallas_call x1, Pallas kernels, first_step(): pl.pallas_call(first_kernel, out_shape=[jax.ShapeDtypeStruct(s, F32) for...  2.33 us
    pallas_call x1, Pallas kernels, main_step(): pl.pallas_call(main_kernel, grid=(1,), out_shape=jax.ShapeDtypeStruct((4...  2.23 us
    pallas_call x1, Pallas kernels, cells_step(): pl.pallas_call(cells_kernel, out_shape=jax.ShapeDtypeStruct(shape, F32),...  1.28 us
    pallas_call x1, Pallas kernels, edge_step(): pl.pallas_call(edge_kernel, out_shape=[jax.ShapeDtypeStruct(s, F32) for s...  1.22 us
    ppermute x10, waiting for transfers between devices, swapped(): lax.ppermute(x, axis, [(i, i ^ distance) for i in range(lax.axis_size(axi...  1.19 us
    pallas_call x1, Pallas kernels, coarse_step(): pl.pallas_call(functools.partial(coarse_kernel, count_x, count_y), out_sh...  1.15 us
  transfers between devices with their start and end apart: 14, of which 6 were waited for; matrix products, arithmetic and copies ran while one was open for 0% of the time, Pallas kernels for 20%

profile of v14, /device:TPU:0, one launch (start us, length us, event | category | flops | bytes accessed | tf_op | source)
XLA Modules:
  0.0 27.1 jit_solution(13824034264736863852)
XLA Ops:
  0.6 2.3 %shard_map.77 = (f32[3840,128]{1,0:T(8,128)S(1)}, f32[16,8,128]{2,1,0:T(8,128)S(1)}, f32[10,8,128]{2,1,0:T(8,128)S(1)}, f32[2,8,128]{2,1,0:T(8,128)S(1)}, f32[64,128]{1,0:T(8,128)S(1)}) custom-call(f32[3,16,64,128]{3,2,1,0:T(8,128)} %field.1, s32[2,2,4,7]{3,2,1,0:T(4,128)} %bitcast.5, bf16[400,128]{1,0:T(8,128)(2,1)} %constant.8.clone.table_hbm), custom_call_target="tpu_custom_call" | custom-call | tf_op jit(solution)/shard_map/pallas_call | solution.py:336
  3.0 3.9 %collective-permute-start.4 = (f32[16,8,128]{2,1,0:T(8,128)S(1)}, f32[16,8,128]{2,1,0:T(8,128)S(1)}, u32[]{:S(2)}, u32[]{:S(2)}) collective-permute-start(f32[16,8,128]{2,1,0:T(8,128)S(1)} %get-tuple-element.15), channel_id=1, source_target_pairs={{0,24},{8,0},{16,8},{24,16},{1,25},{9,1},{17,9},{25,17},{2,26},{10... | collective-permute-start | bytes 196616 | tf_op jit(solution)/shard_map/ppermute | solution.py:838
  6.9 3.6 %collective-permute-start = (f32[64,128]{1,0:T(8,128)S(1)}, f32[64,128]{1,0:T(8,128)S(1)}, u32[]{:S(2)}, u32[]{:S(2)}) collective-permute-start(f32[64,128]{1,0:T(8,128)S(1)} %get-tuple-element.12.refs_3_), channel_id=1, source_target_pairs={{0,6},{1,7},{2,4},{3,5},{4,2},{5,3},{6,0},{7,1},{8,14},{9,15},{10,... | collective-permute-start | bytes 98312 | tf_op jit(solution)/shard_map/ppermute | solution.py:842
  10.5 0.8 %collective-permute-start.2 = (f32[64,128]{1,0:T(8,128)S(1)}, f32[64,128]{1,0:T(8,128)S(1)}, u32[]{:S(2)}, u32[]{:S(2)}) collective-permute-start(f32[64,128]{1,0:T(8,128)S(1)} %get-tuple-element.12.refs_3_), channel_id=1, source_target_pairs={{0,2},{1,3},{2,0},{3,1},{4,6},{5,7},{6,4},{7,5},{8,10},{9,11},{10,... | collective-permute-start | bytes 98312 | tf_op jit(solution)/shard_map/ppermute | solution.py:842
  11.3 0.3 %shard_map.78.parts_in = f32[3840,128]{1,0:T(8,128)S(1)} custom-call(f32[3840,128]{1,0:T(8,128)S(1)} %get-tuple-element.13.lifted), custom_call_target="tpu_custom_call" | custom-call | tf_op jit(solution)/shard_map/pallas_call | solution.py:372
  11.6 0.2 collective-permute-done.3.north.north_mask
  11.8 1.2 %shard_map.79 = (f32[3840,128]{1,0:T(8,128)S(1)}, f32[88,128]{1,0:T(8,128)S(1)}, f32[48,128]{1,0:T(8,128)S(1)}) custom-call(f32[3840,128]{1,0:T(8,128)S(1)} %shard_map.78.parts_in, f32[3840,128]{1,0:T(8,128)S(1)} %get-tuple-element.13.lifted, f32[10,8,128]{2,1,0:T(8,128)S(1)} %collective-permute-done.3.north.north_mask, ...), custom_call_target="tpu_custom_call", output_to_operand_aliasing={{0}: (0, {})} | custom-call | flops 20000000000 | bytes 8000000 | tf_op jit(solution)/shard_map/pallas_call | solution.py:447
  13.1 1.8 %collective-permute-start.6 = (f32[88,128]{1,0:T(8,128)S(1)}, f32[88,128]{1,0:T(8,128)S(1)}, u32[]{:S(2)}, u32[]{:S(2)}) collective-permute-start(f32[88,128]{1,0:T(8,128)S(1)} %get-tuple-element.17.refs_4_), channel_id=1, source_target_pairs={{0,7},{1,0},{2,1},{3,2},{4,3},{5,4},{6,5},{7,6},{8,15},{9,8},{10,9... | collective-permute-start | bytes 135176 | tf_op jit(solution)/shard_map/ppermute | solution.py:838
  14.9 0.5 %collective-permute-done.1.refs_1_ = f32[64,128]{1,0:T(8,128)S(1)} collective-permute-done((f32[64,128]{1,0:T(8,128)S(1)}, f32[64,128]{1,0:T(8,128)S(1)}, u32[]{:S(2)}, u32[]{:S(2)}) %collective-permute-start.1) | collective-permute-done | bytes 32800 | tf_op jit(solution)/shard_map/ppermute | solution.py:842
  15.4 3.0 %collective-permute-start.5 = (f32[256,128]{1,0:T(8,128)S(1)}, f32[256,128]{1,0:T(8,128)S(1)}, u32[]{:S(2)}, u32[]{:S(2)}) collective-permute-start(f32[256,128]{1,0:T(8,128)S(1)} %shard_map.80.refs_3_), channel_id=1, source_target_pairs={{0,24},{8,16},{16,8},{24,0},{1,25},{9,17},{17,9},{25,1},{2,26},{10... | collective-permute-start | bytes 393224 | tf_op jit(solution)/shard_map/ppermute | solution.py:842
  18.3 0.5 %collective-permute-start.8 = (f32[256,128]{1,0:T(8,128)S(1)}, f32[256,128]{1,0:T(8,128)S(1)}, u32[]{:S(2)}, u32[]{:S(2)}) collective-permute-start(f32[256,128]{1,0:T(8,128)S(1)} %shard_map.80.refs_3_), channel_id=1, source_target_pairs={{0,16},{8,24},{16,0},{24,8},{1,17},{9,25},{17,1},{25,9},{2,18},{10... | collective-permute-start | bytes 393224 | tf_op jit(solution)/shard_map/ppermute | solution.py:842
  18.8 0.1 collective-permute-start.9
  19.0 0.9 %collective-permute-done.7.west = f32[48,128]{1,0:T(8,128)S(1)} collective-permute-done((f32[48,128]{1,0:T(8,128)S(1)}, f32[48,128]{1,0:T(8,128)S(1)}, u32[]{:S(2)}, u32[]{:S(2)}) %collective-permute-start.7) | collective-permute-done | bytes 24608 | tf_op jit(solution)/shard_map/ppermute | solution.py:838
  19.9 2.2 %shard_map.81.refs_4_ = f32[4608,128]{1,0:T(8,128)S(1)} custom-call(f32[4,24,40,128]{3,2,1,0:T(8,128)S(1)} %bitcast.4, f32[3840,128]{1,0:T(8,128)S(1)} %get-tuple-element.18.flat, f32[88,128]{1,0:T(8,128)S(1)} %collective-permute-done.6.east, f32[48,128]{1,0:T(8,128)S(1)} %collective-permute-done.7.west, f32[2,8,128]{2,1,0:T(8,128)S(1)} %get-tuple-element.16.own_masks, ...), custom_call_target="tpu_custom_call" | custom-call | flops 8000000000 | bytes 8000000 | tf_op jit(solution)/shard_map/pallas_call | solution.py:701
  22.2 1.3 %shard_map.82 = f32[3,16,64,128]{3,2,1,0:T(8,128)} custom-call(f32[4,24,48,128]{3,2,1,0:T(8,128)S(1)} %bitcast.3), custom_call_target="tpu_custom_call" | custom-call | flops 4000000000 | bytes 8000000 | tf_op jit(solution)/shard_map/pallas_call | solution.py:724
  23.5 0.6 %collective-permute-start.10 = (f32[256,128]{1,0:T(8,128)S(1)}, f32[256,128]{1,0:T(8,128)S(1)}, u32[]{:S(2)}, u32[]{:S(2)}) collective-permute-start(f32[256,128]{1,0:T(8,128)S(1)} %collective-permute-done.5.refs_0_), channel_id=1, source_target_pairs={{0,1},{1,0},{2,3},{3,2},{4,5},{5,4},{6,7},{7,6},{8,9},{9,8},{10,11... | collective-permute-start | bytes 393224 | tf_op jit(solution)/shard_map/ppermute | solution.py:842
  24.1 0.0 collective-permute-start.11
  24.1 0.5 %collective-permute-start.12 = (f32[256,128]{1,0:T(8,128)S(1)}, f32[256,128]{1,0:T(8,128)S(1)}, u32[]{:S(2)}, u32[]{:S(2)}) collective-permute-start(f32[256,128]{1,0:T(8,128)S(1)} %collective-permute-done.9.refs_2_), channel_id=1, source_target_pairs={{0,1},{1,0},{2,3},{3,2},{4,5},{5,4},{6,7},{7,6},{8,9},{9,8},{10,11... | collective-permute-start | bytes 393224 | tf_op jit(solution)/shard_map/ppermute | solution.py:842
  24.6 0.3 %shard_map.83.refs_4_.own = f32[4,4,64,128]{3,2,1,0:T(8,128)S(1)} custom-call(f32[256,128]{1,0:T(8,128)S(1)} %collective-permute-done.5.refs_0_, f32[256,128]{1,0:T(8,128)S(1)} %collective-permute-done.8.refs_1_, f32[256,128]{1,0:T(8,128)S(1)} %collective-permute-done.9.refs_2_, f32[256,128]{1,0:T(8,128)S(1)} %shard_map.80.refs_3_, ...), custom_call_target="tpu_custom_call" | custom-call | tf_op jit(solution)/shard_map/pallas_call | solution.py:772
  24.9 0.1 collective-permute-done.10.refs_0_
  25.0 0.4 %collective-permute-done.11.refs_1_ = f32[256,128]{1,0:T(8,128)S(1)} collective-permute-done((f32[256,128]{1,0:T(8,128)S(1)}, f32[256,128]{1,0:T(8,128)S(1)}, u32[]{:S(2)}, u32[]{:S(2)}) %collective-permute-start.11) | collective-permute-done | bytes 131104 | tf_op jit(solution)/shard_map/ppermute | solution.py:842
  25.4 0.2 collective-permute-done.12.refs_2_
  25.6 0.3 %shard_map.84.other = f32[4,4,64,128]{3,2,1,0:T(8,128)S(1)} custom-call(f32[256,128]{1,0:T(8,128)S(1)} %collective-permute-done.10.refs_0_, f32[256,128]{1,0:T(8,128)S(1)} %collective-permute-done.11.refs_1_, f32[256,128]{1,0:T(8,128)S(1)} %collective-permute-done.12.refs_2_, f32[256,128]{1,0:T(8,128)S(1)} %collective-permute-done.13.refs_3_, ...), custom_call_target="tpu_custom_call" | custom-call | tf_op jit(solution)/shard_map/pallas_call | solution.py:772
  26.0 1.2 %shard_map.85 = f32[3,4,64,256]{3,2,1,0:T(8,128)} custom-call(f32[4,4,64,128]{3,2,1,0:T(8,128)S(1)} %shard_map.83.refs_4_.own, f32[4,4,64,128]{3,2,1,0:T(8,128)S(1)} %shard_map.84.other), custom_call_target="tpu_custom_call" | custom-call | tf_op jit(solution)/shard_map/pallas_call | solution.py:826
  (17 shorter events, 0.1 us)
Async XLA Ops:
  3.0 8.9 %collective-permute-start.4 = (f32[16,8,128]{2,1,0:T(8,128)S(1)}, f32[16,8,128]{2,1,0:T(8,128)S(1)}, u32[]{:S(2)}, u32[]{:S(2)}) collective-permute-start(f32[16,8,128]{2,1,0:T(8,128)S(1)} %get-tuple-element.15), channel_id=1, source_target_pairs={{0,24},{8,0},{16,8},{24,16},{1,25},{9,1},{17,9},{25,17},{2,26},{10... | collective-permute-start | bytes 196616 | tf_op jit(solution)/shard_map/ppermute | solution.py:838
  6.9 4.9 %collective-permute-start.3 = (f32[10,8,128]{2,1,0:T(8,128)S(1)}, f32[10,8,128]{2,1,0:T(8,128)S(1)}, u32[]{:S(2)}, u32[]{:S(2)}) collective-permute-start(f32[10,8,128]{2,1,0:T(8,128)S(1)} %get-tuple-element.14), channel_id=1, source_target_pairs={{0,8},{8,16},{16,24},{24,0},{1,9},{9,17},{17,25},{25,1},{2,10},{10... | collective-permute-start | bytes 122888 | tf_op jit(solution)/shard_map/ppermute | solution.py:838
  6.9 8.0 %collective-permute-start = (f32[64,128]{1,0:T(8,128)S(1)}, f32[64,128]{1,0:T(8,128)S(1)}, u32[]{:S(2)}, u32[]{:S(2)}) collective-permute-start(f32[64,128]{1,0:T(8,128)S(1)} %get-tuple-element.12.refs_3_), channel_id=1, source_target_pairs={{0,6},{1,7},{2,4},{3,5},{4,2},{5,3},{6,0},{7,1},{8,14},{9,15},{10,... | collective-permute-start | bytes 98312 | tf_op jit(solution)/shard_map/ppermute | solution.py:842
  10.5 4.8 %collective-permute-start.1 = (f32[64,128]{1,0:T(8,128)S(1)}, f32[64,128]{1,0:T(8,128)S(1)}, u32[]{:S(2)}, u32[]{:S(2)}) collective-permute-start(f32[64,128]{1,0:T(8,128)S(1)} %get-tuple-element.12.refs_3_), channel_id=1, source_target_pairs={{0,4},{1,5},{2,6},{3,7},{4,0},{5,1},{6,2},{7,3},{8,12},{9,13},{10,... | collective-permute-start | bytes 98312 | tf_op jit(solution)/shard_map/ppermute | solution.py:842
  10.5 4.8 %collective-permute-start.2 = (f32[64,128]{1,0:T(8,128)S(1)}, f32[64,128]{1,0:T(8,128)S(1)}, u32[]{:S(2)}, u32[]{:S(2)}) collective-permute-start(f32[64,128]{1,0:T(8,128)S(1)} %get-tuple-element.12.refs_3_), channel_id=1, source_target_pairs={{0,2},{1,3},{2,0},{3,1},{4,6},{5,7},{6,4},{7,5},{8,10},{9,11},{10,... | collective-permute-start | bytes 98312 | tf_op jit(solution)/shard_map/ppermute | solution.py:842
  13.1 6.9 %collective-permute-start.6 = (f32[88,128]{1,0:T(8,128)S(1)}, f32[88,128]{1,0:T(8,128)S(1)}, u32[]{:S(2)}, u32[]{:S(2)}) collective-permute-start(f32[88,128]{1,0:T(8,128)S(1)} %get-tuple-element.17.refs_4_), channel_id=1, source_target_pairs={{0,7},{1,0},{2,1},{3,2},{4,3},{5,4},{6,5},{7,6},{8,15},{9,8},{10,9... | collective-permute-start | bytes 135176 | tf_op jit(solution)/shard_map/ppermute | solution.py:838
  14.9 5.1 %copy-start = (bf16[1280,128]{1,0:T(8,128)(2,1)S(1)}, bf16[1280,128]{1,0:T(8,128)(2,1)}, u32[]{:S(2)}) copy-start(bf16[1280,128]{1,0:T(8,128)(2,1)} %constant.11.clone.narrow) | copy-start | bytes 983044
  14.9 5.1 %copy-start.1 = (bf16[528,256]{1,0:T(8,128)(2,1)S(1)}, bf16[528,256]{1,0:T(8,128)(2,1)}, u32[]{:S(2)}) copy-start(bf16[528,256]{1,0:T(8,128)(2,1)} %constant.10.clone.wide) | copy-start | bytes 811012
  14.9 5.0 %collective-permute-start.7 = (f32[48,128]{1,0:T(8,128)S(1)}, f32[48,128]{1,0:T(8,128)S(1)}, u32[]{:S(2)}, u32[]{:S(2)}) collective-permute-start(f32[48,128]{1,0:T(8,128)S(1)} %get-tuple-element.19), channel_id=1, source_target_pairs={{0,1},{1,2},{2,3},{3,4},{4,5},{5,6},{6,7},{7,0},{8,9},{9,10},{10,1... | collective-permute-start | bytes 73736 | tf_op jit(solution)/shard_map/ppermute | solution.py:838
  15.4 8.1 %collective-permute-start.5 = (f32[256,128]{1,0:T(8,128)S(1)}, f32[256,128]{1,0:T(8,128)S(1)}, u32[]{:S(2)}, u32[]{:S(2)}) collective-permute-start(f32[256,128]{1,0:T(8,128)S(1)} %shard_map.80.refs_3_), channel_id=1, source_target_pairs={{0,24},{8,16},{16,8},{24,0},{1,25},{9,17},{17,9},{25,1},{2,26},{10... | collective-permute-start | bytes 393224 | tf_op jit(solution)/shard_map/ppermute | solution.py:842
  18.3 5.8 %collective-permute-start.8 = (f32[256,128]{1,0:T(8,128)S(1)}, f32[256,128]{1,0:T(8,128)S(1)}, u32[]{:S(2)}, u32[]{:S(2)}) collective-permute-start(f32[256,128]{1,0:T(8,128)S(1)} %shard_map.80.refs_3_), channel_id=1, source_target_pairs={{0,16},{8,24},{16,0},{24,8},{1,17},{9,25},{17,1},{25,9},{2,18},{10... | collective-permute-start | bytes 393224 | tf_op jit(solution)/shard_map/ppermute | solution.py:842
  18.8 5.3 %collective-permute-start.9 = (f32[256,128]{1,0:T(8,128)S(1)}, f32[256,128]{1,0:T(8,128)S(1)}, u32[]{:S(2)}, u32[]{:S(2)}) collective-permute-start(f32[256,128]{1,0:T(8,128)S(1)} %shard_map.80.refs_3_), channel_id=1, source_target_pairs={{0,8},{8,0},{16,24},{24,16},{1,9},{9,1},{17,25},{25,17},{2,10},{10... | collective-permute-start | bytes 393224 | tf_op jit(solution)/shard_map/ppermute | solution.py:842
  19.9 5.0 %collective-permute-start.13 = (f32[256,128]{1,0:T(8,128)S(1)}, f32[256,128]{1,0:T(8,128)S(1)}, u32[]{:S(2)}, u32[]{:S(2)}) collective-permute-start(f32[256,128]{1,0:T(8,128)S(1)} %shard_map.80.refs_3_), channel_id=1, source_target_pairs={{0,1},{1,0},{2,3},{3,2},{4,5},{5,4},{6,7},{7,6},{8,9},{9,8},{10,11... | collective-permute-start | bytes 393224 | tf_op jit(solution)/shard_map/ppermute | solution.py:842
  23.5 1.6 %collective-permute-start.10 = (f32[256,128]{1,0:T(8,128)S(1)}, f32[256,128]{1,0:T(8,128)S(1)}, u32[]{:S(2)}, u32[]{:S(2)}) collective-permute-start(f32[256,128]{1,0:T(8,128)S(1)} %collective-permute-done.5.refs_0_), channel_id=1, source_target_pairs={{0,1},{1,0},{2,3},{3,2},{4,5},{5,4},{6,7},{7,6},{8,9},{9,8},{10,11... | collective-permute-start | bytes 393224 | tf_op jit(solution)/shard_map/ppermute | solution.py:842
  24.1 1.3 %collective-permute-start.11 = (f32[256,128]{1,0:T(8,128)S(1)}, f32[256,128]{1,0:T(8,128)S(1)}, u32[]{:S(2)}, u32[]{:S(2)}) collective-permute-start(f32[256,128]{1,0:T(8,128)S(1)} %collective-permute-done.8.refs_1_), channel_id=1, source_target_pairs={{0,1},{1,0},{2,3},{3,2},{4,5},{5,4},{6,7},{7,6},{8,9},{9,8},{10,11... | collective-permute-start | bytes 393224 | tf_op jit(solution)/shard_map/ppermute | solution.py:842
  24.1 1.5 %collective-permute-start.12 = (f32[256,128]{1,0:T(8,128)S(1)}, f32[256,128]{1,0:T(8,128)S(1)}, u32[]{:S(2)}, u32[]{:S(2)}) collective-permute-start(f32[256,128]{1,0:T(8,128)S(1)} %collective-permute-done.9.refs_2_), channel_id=1, source_target_pairs={{0,1},{1,0},{2,3},{3,2},{4,5},{5,4},{6,7},{7,6},{8,9},{9,8},{10,11... | collective-permute-start | bytes 393224 | tf_op jit(solution)/shard_map/ppermute | solution.py:842
